TPU v7x, 32 devices: a whole 2x2x4 slice. The times are simulated.
32 devices in a mesh: dp: 8 (over z, y), tensor: 4 (over x, core).
Axes of the slice: x: 2, y: 2, z: 4, core: 2. Of those that a mesh axis runs over, the one named last changes fastest.
Arguments:
- tokens: bfloat16 [16384, 768], P(('dp', 'tensor')), may hold values from -6 to 6
- doc_lengths: int32 [8, 8], P('dp'), may hold values from 1 to 1537, 2048 in all within a row
- key_mask: int32 [16384], P(('dp', 'tensor')), may hold values 0 or 1
- qkv_weight: bfloat16 [768, 3, 768], P(None, None, 'tensor'), may hold values from -0.21875 to 0.21875
- out_weight: bfloat16 [768, 768], P('tensor'), may hold values from -1.5 to 1.5
- gate_up_weight: bfloat16 [768, 2, 3072], P(None, None, 'tensor'), may hold values from -0.21875 to 0.21875
- down_weight: bfloat16 [3072, 768], P('tensor'), may hold values from -0.109375 to 0.109375
- norm1_gain: float32 [768], replicated, may hold values from 0.25 to 1.75
- norm1_bias: float32 [768], replicated, may hold values from -2 to 2
- norm2_gain: float32 [768], replicated, may hold values from 0.25 to 1.75
- norm2_bias: float32 [768], replicated, may hold values from -2 to 2
- out_grad: bfloat16 [16384, 768], P(('dp', 'tensor')), may hold values from -6 to 6
Outputs:
- output: bfloat16 [16384, 768], P(('dp', 'tensor'))
- input_grad: float32 [16384, 768], P(('dp', 'tensor'))
- qkv_grad: float32 [768, 3, 768], P('dp', None, 'tensor')
- out_proj_grad: float32 [768, 768], P('tensor', 'dp')
- gate_up_grad: float32 [768, 2, 3072], P('dp', None, 'tensor')
- down_grad: float32 [3072, 768], P('tensor', 'dp')
- norm1_gain_grad: float32 [768], replicated
- norm1_bias_grad: float32 [768], replicated
- norm2_gain_grad: float32 [768], replicated
- norm2_bias_grad: float32 [768], replicated
Inputs may be any that keep to these rules, and one draw needn't show every extreme that they name: `doc_lengths`: row g holds the lengths of the documents packed in order into group g; they sum to 2048, and the longest of every row has exactly 1537 tokens.
All inputs are finite; a program needn't handle non-finite values. No bound on the sum of `key_mask` on one device may be relied on, other than what follows from the above.
Results may differ from a plain program's by a relative error of at most 0.019.
Values may be sent and summed in bfloat16 or wider, within the bound.
No kernel may reach another device: no remote copies, remote signals or barrier semaphores. Data moves between devices by JAX's collectives and lax.ppermute only.
A program may use at most 128 MiB of HBM per device.

v0:
```python
import jax
import jax.numpy as jnp
from jax import lax
from jax.sharding import PartitionSpec as P

HD = 64


def rope_tables(position):
    half_size = HD // 2
    freqs = 1000.0 ** (-(jnp.arange(half_size, dtype=jnp.float32) * 2.0 / HD))
    angles = position.astype(jnp.float32)[:, None] * freqs[None, :]
    cosine_table = jnp.concatenate([jnp.cos(angles), jnp.cos(angles)], axis=1)
    sine_table = jnp.concatenate([jnp.sin(angles), jnp.sin(angles)], axis=1)
    return (cosine_table, sine_table)


def rotate(values, cosine_table, sine_table):
    half_size = HD // 2
    turned = jnp.concatenate([-values[..., half_size:], values[..., :half_size]], axis=-1)
    return values * cosine_table[:, None, :] + turned * sine_table[:, None, :]


def unrotate(grads, cosine_table, sine_table):
    half_size = HD // 2
    scaled = grads * sine_table[:, None, :]
    turned = jnp.concatenate([scaled[..., half_size:], -scaled[..., :half_size]], axis=-1)
    return grads * cosine_table[:, None, :] + turned


def layer_norm(hidden_in, gain, bias):
    centred = hidden_in - jnp.mean(hidden_in, axis=-1, keepdims=True)
    inverse = lax.rsqrt(jnp.mean(centred * centred, axis=-1, keepdims=True) + 1e-05)
    normed = centred * inverse
    return (normed * gain + bias, normed, inverse)


def norm_back(grad_out, normed, inverse, gain):
    scaled = grad_out * gain
    return inverse * (
        scaled
        - jnp.mean(scaled, axis=-1, keepdims=True)
        - normed * jnp.mean(scaled * normed, axis=-1, keepdims=True)
    )


def local(
    tokens,
    doc_lengths,
    key_mask,
    qkv_weight,
    out_weight,
    gate_up_weight,
    down_weight,
    norm1_gain,
    norm1_bias,
    norm2_gain,
    norm2_bias,
    out_grad,
):
    row_count = tokens.shape[0]
    group_rows = row_count * lax.axis_size("tensor")
    local_width = qkv_weight.shape[2]
    head_count = local_width // HD
    block_rows = min(512, group_rows)
    block_count = group_rows // block_rows
    score_scale = HD ** (-0.5)
    tokens_all, mask_all = (
        lax.all_gather(tokens, "tensor", axis=0, tiled=True),
        lax.all_gather(key_mask.astype(jnp.bfloat16), "tensor", axis=0, tiled=True),
    )
    places = jnp.arange(group_rows, dtype=jnp.int32)
    doc_ends = jnp.cumsum(doc_lengths[0])
    earlier = places[:, None] >= doc_ends[None, :]
    segment = jnp.sum(earlier.astype(jnp.int32), axis=1)
    position = places - jnp.sum(jnp.where(earlier, doc_lengths[0][None, :], 0), axis=1)
    key_valid = mask_all > 0.5
    cosine_table, sine_table = rope_tables(position)

    def project():
        qkv = jnp.einsum("td,dce->tce", tokens_all, qkv_weight, preferred_element_type=jnp.float32)
        queries = rotate(
            qkv[:, 0].reshape(group_rows, head_count, HD), cosine_table, sine_table
        ).astype(jnp.bfloat16)
        keys = rotate(
            qkv[:, 1].reshape(group_rows, head_count, HD), cosine_table, sine_table
        ).astype(jnp.bfloat16)
        values = qkv[:, 2].reshape(group_rows, head_count, HD).astype(jnp.bfloat16)
        return (queries, keys, values)

    def masked_scores(query_block, segment_block, place_block, keys):
        scores = (
            jnp.einsum("qhd,khd->hqk", query_block, keys, preferred_element_type=jnp.float32)
            * score_scale
        )
        allowed = (segment_block[:, None] == segment[None, :]) & (
            key_valid[None, :] | (place_block[:, None] == places[None, :])
        )
        return jnp.where(allowed[None], scores, -1e30)

    queries, keys, values = project()
    segment_blocks = segment.reshape(block_count, block_rows)
    place_blocks = places.reshape(block_count, block_rows)

    def forward_block(block_input):
        query_block, segment_block, place_block = block_input
        scores = masked_scores(query_block, segment_block, place_block, keys)
        highest = jnp.max(scores, axis=-1, keepdims=True)
        expo = jnp.exp(scores - highest)
        totals = jnp.sum(expo, axis=-1, keepdims=True)
        probs = (expo / totals).astype(jnp.bfloat16)
        result = jnp.einsum(
            "hqk,khd->qhd", probs, values, preferred_element_type=jnp.float32
        ).astype(jnp.bfloat16)
        return (result, (highest + jnp.log(totals))[..., 0])

    attended, log_sums = lax.map(
        forward_block,
        (queries.reshape(block_count, block_rows, head_count, HD), segment_blocks, place_blocks),
    )
    attended = attended.reshape(group_rows, local_width)
    attn_piece = lax.psum_scatter(
        jnp.dot(attended, out_weight, preferred_element_type=jnp.float32),
        "tensor",
        scatter_dimension=0,
        tiled=True,
    )
    middle, normed_one, inverse_one = layer_norm(
        tokens.astype(jnp.float32) + attn_piece, norm1_gain, norm1_bias
    )
    middle_low = lax.all_gather(middle.astype(jnp.bfloat16), "tensor", axis=0, tiled=True)
    gate_up = jnp.einsum(
        "td,dcf->tcf", middle_low, gate_up_weight, preferred_element_type=jnp.float32
    )
    hidden = (jax.nn.silu(gate_up[:, 0]) * gate_up[:, 1]).astype(jnp.bfloat16)
    second_in = middle + lax.psum_scatter(
        jnp.dot(hidden, down_weight, preferred_element_type=jnp.float32).astype(jnp.bfloat16),
        "tensor",
        scatter_dimension=0,
        tiled=True,
    ).astype(jnp.float32)
    result, normed_two, inverse_two = layer_norm(second_in, norm2_gain, norm2_bias)
    output = result.astype(jnp.bfloat16)
    grad_out = out_grad.astype(jnp.float32)
    gain_two_grad = jnp.sum(grad_out * normed_two, axis=0)
    bias_two_grad = jnp.sum(grad_out, axis=0)
    grad_second = norm_back(grad_out, normed_two, inverse_two, norm2_gain)
    grad_mlp_all = lax.all_gather(grad_second.astype(jnp.bfloat16), "tensor", axis=0, tiled=True)
    gate_up = jnp.einsum(
        "td,dcf->tcf", middle_low, gate_up_weight, preferred_element_type=jnp.float32
    )
    gate_val = gate_up[:, 0]
    up_val = gate_up[:, 1]
    sigma = jax.nn.sigmoid(gate_val)
    activ = gate_val * sigma
    hidden = (activ * up_val).astype(jnp.bfloat16)
    down_part_local = jnp.einsum(
        "tf,td->fd", hidden, grad_mlp_all, preferred_element_type=jnp.float32
    )
    grad_hidden = jnp.einsum(
        "td,fd->tf", grad_mlp_all, down_weight, preferred_element_type=jnp.float32
    )
    grad_gate = grad_hidden * up_val * sigma * (1.0 + gate_val * (1.0 - sigma))
    grad_up = grad_hidden * activ
    grad_gate_up = jnp.stack([grad_gate, grad_up], axis=1).astype(jnp.bfloat16)
    gate_up_local = jnp.einsum(
        "td,tcf->dcf", middle_low, grad_gate_up, preferred_element_type=jnp.float32
    )
    grad_middle = grad_second + lax.psum_scatter(
        jnp.einsum(
            "tcf,dcf->td", grad_gate_up, gate_up_weight, preferred_element_type=jnp.float32
        ).astype(jnp.bfloat16),
        "tensor",
        scatter_dimension=0,
        tiled=True,
    ).astype(jnp.float32)
    gain_one_grad = jnp.sum(grad_middle * normed_one, axis=0)
    bias_one_grad = jnp.sum(grad_middle, axis=0)
    grad_first = norm_back(grad_middle, normed_one, inverse_one, norm1_gain)
    grad_attn_all = lax.all_gather(grad_first.astype(jnp.bfloat16), "tensor", axis=0, tiled=True)
    out_proj_local = jnp.einsum(
        "te,td->ed", attended, grad_attn_all, preferred_element_type=jnp.float32
    )
    grad_attended = jnp.einsum(
        "td,ed->te", grad_attn_all, out_weight, preferred_element_type=jnp.float32
    ).astype(jnp.bfloat16)
    queries, keys, values = project()

    def backward_block(carry, block_input):
        key_total, value_total = carry
        query_block, segment_block, place_block, grad_block, lse_block = block_input
        scores = masked_scores(query_block, segment_block, place_block, keys)
        probs = jnp.exp(scores - lse_block[..., None])
        grad_probs = jnp.einsum(
            "qhd,khd->hqk", grad_block, values, preferred_element_type=jnp.float32
        )
        delta = jnp.sum(grad_probs * probs, axis=-1, keepdims=True)
        grad_scores = (probs * (grad_probs - delta)).astype(jnp.bfloat16)
        grad_query = (
            jnp.einsum("hqk,khd->qhd", grad_scores, keys, preferred_element_type=jnp.float32)
            * score_scale
        )
        key_total = (
            key_total
            + jnp.einsum(
                "hqk,qhd->khd", grad_scores, query_block, preferred_element_type=jnp.float32
            )
            * score_scale
        )
        value_total = value_total + jnp.einsum(
            "hqk,qhd->khd",
            probs.astype(jnp.bfloat16),
            grad_block,
            preferred_element_type=jnp.float32,
        )
        return ((key_total, value_total), grad_query.astype(jnp.bfloat16))

    zero_heads = jnp.zeros((group_rows, head_count, HD), jnp.float32)
    block_inputs = (
        queries.reshape(block_count, block_rows, head_count, HD),
        segment_blocks,
        place_blocks,
        grad_attended.reshape(block_count, block_rows, head_count, HD),
        log_sums,
    )
    (key_grad, value_grad), query_grad = lax.scan(
        backward_block, (zero_heads, zero_heads), block_inputs
    )
    query_grad = query_grad.reshape(group_rows, head_count, HD).astype(jnp.float32)
    key_grad = key_grad.astype(jnp.bfloat16).astype(jnp.float32)
    query_pre = unrotate(query_grad, cosine_table, sine_table).reshape(group_rows, local_width)
    key_pre = unrotate(key_grad, cosine_table, sine_table).reshape(group_rows, local_width)
    grad_qkv = jnp.stack(
        [query_pre, key_pre, value_grad.reshape(group_rows, local_width)], axis=1
    ).astype(jnp.bfloat16)
    qkv_local = jnp.einsum("td,tce->dce", tokens_all, grad_qkv, preferred_element_type=jnp.float32)
    input_grad = grad_first + lax.psum_scatter(
        jnp.einsum("tce,dce->td", grad_qkv, qkv_weight, preferred_element_type=jnp.float32).astype(
            jnp.bfloat16
        ),
        "tensor",
        scatter_dimension=0,
        tiled=True,
    ).astype(jnp.float32)
    qkv_part, out_part, gate_up_part, down_part = (
        lax.psum_scatter(qkv_local, "dp", scatter_dimension=0, tiled=True),
        lax.psum_scatter(out_proj_local, "dp", scatter_dimension=1, tiled=True),
        lax.psum_scatter(gate_up_local, "dp", scatter_dimension=0, tiled=True),
        lax.psum_scatter(down_part_local, "dp", scatter_dimension=1, tiled=True),
    )
    gain_one_sum, bias_one_sum, gain_two_sum, bias_two_sum = lax.psum(
        (gain_one_grad, bias_one_grad, gain_two_grad, bias_two_grad), ("dp", "tensor")
    )
    return (
        output,
        input_grad,
        qkv_part,
        out_part,
        gate_up_part,
        down_part,
        gain_one_sum,
        bias_one_sum,
        gain_two_sum,
        bias_two_sum,
    )


def solution(mesh):
    placed = (
        P(("dp", "tensor"), None),
        P("dp", None),
        P(("dp", "tensor")),
        P(None, None, "tensor"),
        P("tensor", None),
        P(None, None, "tensor"),
        P("tensor", None),
        P(),
        P(),
        P(),
        P(),
        P(("dp", "tensor"), None),
    )
    return jax.shard_map(
        local,
        mesh=mesh,
        in_specs=placed,
        out_specs=(
            P(("dp", "tensor"), None),
            P(("dp", "tensor"), None),
            P("dp", None, "tensor"),
            P("tensor", "dp"),
            P("dp", None, "tensor"),
            P("tensor", "dp"),
            P(),
            P(),
            P(),
            P(),
        ),
        check_vma=False,
    )
```

profile of v0, /device:TPU:0, one launch (start us, length us, event | category | flops | bytes accessed | tf_op | source)
XLA Modules:
  0.0 826.3 jit_solution(9589763561271944370)
XLA Ops:
  9.5 6.1 all-gather
  21.9 18.9 %all-gather.6.cloned.1.call-done = bf16[2048,768]{1,0:T(8,128)(2,1)} async-done(((bf16[512,768]{1,0:T(8,128)(2,1)}), bf16[2048,768]{1,0:T(8,128)(2,1)}) %all-gather.6.cloned.1.call-update) | async-done | bytes 3145744 | tf_op jit(solution)/shard_map/all_gather | solution.py:69
  63.4 90.5 %while.28 = (s32[]{:T(128)}, bf16[4,512,3,64]{1,3,2,0:T(8,128)(2,1)}, f32[4,3,512]{2,1,0:T(4,128)S(1)}, s32[4,512]{1,0:T(4,128)S(1)}, s32[2048]{0:T(1024)S(1)}, ...) while((s32[]{:T(128)}, ...), condition=%wide.region_6.7_spmd.clone, body=%wide.region_3.6_spmd.clone.sunk | while | flops 847346176 | bytes 47132832 | solution.py:117
  65.1 6.8 fusion.139
  71.9 6.8 fusion.140
  78.7 7.4 fusion.141
  87.6 6.8 fusion.139
  94.5 6.8 fusion.140
  101.3 7.4 fusion.141
  110.2 6.8 fusion.139
  117.0 6.8 fusion.140
  123.9 7.4 fusion.141
  132.8 6.8 fusion.139
  139.6 6.8 fusion.140
  146.5 7.4 fusion.141
  160.6 58.5 %reduce-scatter.13.cloned.1.call-done = f32[512,768]{1,0:T(8,128)} async-done(((f32[2048,768]{1,0:T(8,128)}), f32[512,768]{1,0:T(8,128)}) %reduce-scatter.13.cloned.1.call-update) | async-done | bytes 1572880 | tf_op jit(solution)/shard_map/reduce_scatter | solution.py:122
  223.6 28.4 %all-gather.8.cloned.1.call-done = bf16[2048,768]{1,0:T(8,128)(2,1)} async-done(((bf16[512,768]{1,0:T(8,128)(2,1)}), bf16[2048,768]{1,0:T(8,128)(2,1)}) %all-gather.8.cloned.1.call-update) | async-done | bytes 3145744 | tf_op jit(solution)/shard_map/all_gather | solution.py:131
  252.0 7.0 fusion.58
  269.3 38.1 %reduce-scatter.15.cloned.1.call-done = bf16[512,768]{1,0:T(8,128)(2,1)} async-done(((bf16[2048,768]{1,0:T(8,128)(2,1)}), bf16[512,768]{1,0:T(8,128)(2,1)}) %reduce-scatter.15.cloned.1.call-update) | async-done | bytes 786448 | tf_op jit(solution)/shard_map/reduce_scatter | solution.py:136
  314.2 28.2 %all-gather.10.cloned.1.call-done = bf16[2048,768]{1,0:T(8,128)(2,1)} async-done(((bf16[512,768]{1,0:T(8,128)(2,1)}), bf16[2048,768]{1,0:T(8,128)(2,1)}) %all-gather.10.cloned.1.call-update) | async-done | bytes 3145744 | tf_op jit(solution)/shard_map/all_gather | solution.py:148
  342.4 8.8 %fusion.60 = (bf16[2048,1,768]{2,0,1:T(8,128)(2,1)S(1)}, bf16[2048,1,768]{2,0,1:T(8,128)(2,1)S(1)}) fusion(f32[2048,2,768]{2,0,1:T(8,128)} %copy-done.12, bf16[2048,768]{1,0:T(8,128)(2,1)} %all-gather.10.cloned.1.call-done, bf16[768,768]{1,0:T(8,128)(2,1)} %param.22), kind=kOutput, calls=%fused_computation.79 | convolution fusion | flops 2436366336 | bytes 23199744 | tf_op jit(solution)/shard_map/td,fd->tf/dot_general | solution.py:160
  353.8 6.5 bitcast_convert_fusion.1
  360.3 38.1 %reduce-scatter.17.cloned.1.call-done = bf16[512,768]{1,0:T(8,128)(2,1)} async-done(((bf16[2048,768]{1,0:T(8,128)(2,1)}), bf16[512,768]{1,0:T(8,128)(2,1)}) %reduce-scatter.17.cloned.1.call-update) | async-done | bytes 786448 | tf_op jit(solution)/shard_map/reduce_scatter | solution.py:169
  403.7 9.8 %fusion.52 = f32[768,2,768]{2,0,1:T(8,128)} fusion(bf16[2048,1,768]{2,0,1:T(8,128)(2,1)} %copy-done.42, bf16[2048,1,768]{2,0,1:T(8,128)(2,1)} %copy-done.41, bf16[2048,768]{1,0:T(8,128)(2,1)} %all-gather.8.cloned.1.call-done), kind=kOutput, calls=%fused_computation.70 | convolution fusion | flops 4844421120 | bytes 14155776 | tf_op jit(solution)/shard_map/td,tcf->dcf/dot_general | solution.py:166
  413.6 18.7 %all-gather.12.cloned.1.call-done = bf16[2048,768]{1,0:T(8,128)(2,1)} async-done(((bf16[512,768]{1,0:T(8,128)(2,1)}), bf16[2048,768]{1,0:T(8,128)(2,1)}) %all-gather.12.cloned.1.call-update) | async-done | bytes 3145744 | tf_op jit(solution)/shard_map/all_gather | solution.py:180
  437.1 128.9 %while.29 = (s32[]{:T(128)}, f32[2048,3,64]{0,2,1:T(8,128)}, f32[2048,3,64]{0,2,1:T(8,128)}, bf16[4,512,3,64]{1,3,2,0:T(8,128)(2,1)}, bf16[4,512,3,64]{1,3,2,0:T...) while((s32[]{:T(128)}, f32[2048,3,64]{0,2,1:T(8,128)}, ...), condition=%wide.region_20.21_spmd.clone, body=%wide.region_18.20_spmd.clone.sunk | while | flops 2066807296 | bytes 150210928 | solution.py:226
  441.8 4.8 fusion.154
  446.6 5.8 multiply_reduce_fusion.7
  452.4 6.1 multiply_convert_fusion.5
  458.5 5.8 fusion.155
  472.4 6.2 fusion.154
  478.7 5.8 multiply_reduce_fusion.7
  484.4 6.1 multiply_convert_fusion.5
  490.5 5.9 fusion.155
  505.2 6.2 fusion.154
  511.4 5.8 multiply_reduce_fusion.7
  517.1 6.1 multiply_convert_fusion.5
  523.2 5.9 fusion.155
  537.8 6.2 fusion.154
  544.0 5.8 multiply_reduce_fusion.7
  549.7 6.1 multiply_convert_fusion.5
  555.8 5.8 fusion.155
  590.7 6.1 bitcast_convert_fusion
  598.7 5.9 fusion.93
  605.3 39.8 %all-reduce = (f32[768]{0:T(1024)}, f32[768]{0:T(1024)}, f32[768]{0:T(1024)}, f32[768]{0:T(1024)}) all-reduce(f32[768]{0:T(1024)S(1)} %copy-done.33, f32[768]{0:T(1024)S(1)} %copy-done.34, f32[768]{0:T(1024)S(1)} %copy-done.31, f32[768]{0:T(1024)S(1)} %copy-done.32), channel_id=1, replica_groups=mesh['dp'=8,'tensor'=4] {'dp','tensor'}, use_global_device_ids=true, to_apply=%region_27.28 | all-reduce | flops 3072 | bytes 24576 | tf_op jit(solution)/shard_map/psum | solution.py:251
  649.1 57.1 %reduce-scatter.25.cloned.1.call-done = f32[96,576]{1,0:T(8,128)} async-done(((f32[768,576]{1,0:T(8,128)}), f32[96,576]{1,0:T(8,128)}) %reduce-scatter.25.cloned.1.call-update) | async-done | bytes 221200
  708.3 37.5 %reduce-scatter.19.cloned.1.call-done = bf16[512,768]{1,0:T(8,128)(2,1)} async-done(((bf16[2048,768]{1,0:T(8,128)(2,1)}), bf16[512,768]{1,0:T(8,128)(2,1)}) %reduce-scatter.19.cloned.1.call-update) | async-done | bytes 786448 | tf_op jit(solution)/shard_map/reduce_scatter | solution.py:237
  748.8 70.3 %reduce-scatter.23.cloned.1.call-done = f32[768,96]{0,1:T(8,128)} async-done(((f32[768,768]{0,1:T(8,128)}), f32[768,96]{0,1:T(8,128)}) %reduce-scatter.23.cloned.1.call-update) | async-done | bytes 294928 | tf_op jit(solution)/shard_map/reduce_scatter | solution.py:249
  (263 shorter events, 147.8 us)
Async XLA Ops:
  7.2 244.8 %copy-start = (bf16[768,2,768]{2,1,0:T(2,128)(2,1)S(1)}, bf16[768,2,768]{2,1,0:T(2,128)(2,1)}, u32[]{:S(2)}) copy-start(bf16[768,2,768]{2,1,0:T(2,128)(2,1)} %param.21) | copy-start | bytes 7077892
  7.2 33.7 %all-gather.6.cloned.1.call-start = ((), (), s32[]{:S(2)}) async-start(), calls=%async_computation.8 | async-start | bytes 3932160 | tf_op jit(solution)/shard_map/all_gather | solution.py:69
  7.9 211.1 %reduce-scatter.13.cloned.1.call-start = ((), (), s32[]{:S(2)}) async-start(), calls=%async_computation.9 | async-start | bytes 7864320 | tf_op jit(solution)/shard_map/reduce_scatter | solution.py:122
  57.9 3.7 copy-start.10
  71.9 6.8 copy-start.9
  94.5 6.8 copy-start.9
  117.0 6.8 copy-start.9
  139.6 6.8 copy-start.9
  160.5 61.5 %copy-start.30 = (f32[768]{0:T(1024)S(1)}, f32[768]{0:T(1024)}, u32[]{:S(2)}) copy-start(f32[768]{0:T(1024)} %param.23) | copy-start | bytes 9220
  160.5 61.5 %copy-start.35 = (f32[768]{0:T(1024)S(1)}, f32[768]{0:T(1024)}, u32[]{:S(2)}) copy-start(f32[768]{0:T(1024)} %param.24) | copy-start | bytes 9220
  160.5 91.5 %all-gather.8.cloned.1.call-start = ((), (), s32[]{:S(2)}) async-start(), calls=%async_computation.10 | async-start | bytes 3932160 | tf_op jit(solution)/shard_map/all_gather | solution.py:131
  223.3 84.1 %reduce-scatter.15.cloned.1.call-start = ((), (), s32[]{:S(2)}) async-start(), calls=%async_computation.11 | async-start | bytes 3932160 | tf_op jit(solution)/shard_map/reduce_scatter | solution.py:136
  259.0 4.6 copy-start.12
  259.1 6.2 copy-start.40
  269.3 40.7 %copy-start.36 = (f32[768]{0:T(1024)S(1)}, f32[768]{0:T(1024)}, u32[]{:S(2)}) copy-start(f32[768]{0:T(1024)} %param.25) | copy-start | bytes 9220
  269.3 73.1 %all-gather.10.cloned.1.call-start = ((), (), s32[]{:S(2)}) async-start(), calls=%async_computation.12 | async-start | bytes 3932160 | tf_op jit(solution)/shard_map/all_gather | solution.py:148
  313.7 84.7 %reduce-scatter.17.cloned.1.call-start = ((), (), s32[]{:S(2)}) async-start(), calls=%async_computation.13 | async-start | bytes 3932160 | tf_op jit(solution)/shard_map/reduce_scatter | solution.py:169
  360.3 38.1 %copy-start.8 = (f32[512,768]{1,0:T(8,128)S(1)}, f32[512,768]{1,0:T(8,128)}, u32[]{:S(2)}) copy-start(f32[512,768]{1,0:T(8,128)} %copy-done.7) | copy-start | bytes 4718596
  360.3 72.0 %all-gather.12.cloned.1.call-start = ((), (), s32[]{:S(2)}) async-start(), calls=%async_computation.14 | async-start | bytes 3932160 | tf_op jit(solution)/shard_map/all_gather | solution.py:180
  398.4 3.2 copy-start.11
  398.4 3.2 copy-start.24
  403.6 241.6 %reduce-scatter.21.cloned.1.call-start = ((), (), s32[]{:S(2)}) async-start(), calls=%async_computation.16 | async-start | bytes 5308416 | tf_op jit(solution)/shard_map/reduce_scatter | solution.py:248
  413.5 234.0 %reduce-scatter.27.cloned.1.call-start = ((), (), s32[]{:S(2)}) async-start(), calls=%async_computation.19 | async-start | bytes 884736
  437.2 4.6 copy-start.4
  437.2 4.6 copy-start.20
  458.5 5.8 copy-start.2
  464.3 3.5 copy-start.5
  464.3 3.5 copy-start.21
  467.8 4.6 copy-start.4
  467.8 4.6 copy-start.20
  469.4 3.0 copy-start.3
  490.5 5.9 copy-start.2
  496.5 4.1 copy-start.5
  496.5 4.1 copy-start.21
  500.6 4.6 copy-start.4
  500.6 4.6 copy-start.20
  523.2 5.9 copy-start.2
  529.1 4.1 copy-start.5
  529.1 4.1 copy-start.21
  533.2 4.6 copy-start.4
  533.2 4.6 copy-start.20
  555.8 5.8 copy-start.2
  561.6 4.1 copy-start.5
  561.6 4.1 copy-start.21
  574.3 131.9 %reduce-scatter.25.cloned.1.call-start = ((), (), s32[]{:S(2)}) async-start(), calls=%async_computation.18 | async-start | bytes 2211840
  590.6 155.3 %reduce-scatter.19.cloned.1.call-start = ((), (), s32[]{:S(2)}) async-start(), calls=%async_computation.15 | async-start | bytes 3932160 | tf_op jit(solution)/shard_map/reduce_scatter | solution.py:237
  596.8 222.3 %reduce-scatter.23.cloned.1.call-start = ((), (), s32[]{:S(2)}) async-start(), calls=%async_computation.17 | async-start | bytes 2654208 | tf_op jit(solution)/shard_map/reduce_scatter | solution.py:249
  706.2 112.8 %copy-start.1 = (bf16[768,2,768]{2,1,0:T(2,128)(2,1)S(1)}, bf16[768,2,768]{2,1,0:T(2,128)(2,1)}, u32[]{:S(2)}) copy-start(bf16[768,2,768]{2,1,0:T(2,128)(2,1)} %param.21) | copy-start | bytes 7077892
  (28 other events, 52.2 us)
Sparse Core Ops, SparseCore 0:
  9.6 31.2 all-gather.5
  160.6 58.4 reduce-scatter.12
  223.4 28.5 all-gather.7
  269.4 37.9 reduce-scatter.14
  313.8 28.5 all-gather.9
  360.4 37.9 reduce-scatter.16
  403.7 28.5 all-gather.11
  436.4 95.3 reduce-scatter.20
  574.4 62.6 reduce-scatter.26
  640.5 65.6 reduce-scatter.24
  708.9 36.8 reduce-scatter.18
  749.8 69.1 reduce-scatter.22
where the time goes:
time: 834 us; the launch traced here: 826 us
  waiting for transfers between devices  395 us (47%)
  matrix products  218 us (26%)
  other arithmetic  109 us (13%)
  blocking collectives  45.9 us (6%)
  local copies, waits for them, and re-layouts  41.1 us (5%)
  between operations  15.1 us (2%)
    reduce_scatter x1, waiting for transfers between devices, local(): lax.psum_scatter(down_part_local, 'dp', scatter_dimension=1, tiled=True)  70.3 us
    reduce_scatter x1, waiting for transfers between devices, local(): lax.psum_scatter(jnp.dot(attended, out_weight, preferred_element_type=jnp...  58.5 us
    unnamed x14, waiting for transfers between devices  58 us
    psum x1, blocking collectives, local(): lax.psum((gain_one_grad, bias_one_grad, gain_two_grad, bias_two_grad), ('...  39.8 us
    dot_general x8, matrix products, masked_scores(): jnp.einsum('qhd,khd->hqk', query_block, keys, preferred_element_type=jnp....  39.3 us
    reduce_scatter x1, waiting for transfers between devices, local(): lax.psum_scatter(jnp.dot(hidden, down_weight, preferred_element_type=jnp....  38.1 us
    reduce_scatter x1, waiting for transfers between devices, local(): lax.psum_scatter(jnp.einsum('tcf,dcf->td', grad_gate_up, gate_up_weight,...  38.1 us
    reduce_scatter x1, waiting for transfers between devices, local(): lax.psum_scatter(jnp.einsum('tce,dce->td', grad_qkv, qkv_weight, preferre...  37.5 us
  transfers between devices with their start and end apart: 12, of which 10 were waited for; matrix products, arithmetic and copies ran while one was open for 23% of the time, Pallas kernels for 0%

commit v1 on v0

v1 whole, which is shorter than its diff:
```python
import functools

import jax
import jax.numpy as jnp
from jax import lax
from jax.experimental import pallas as pl
from jax.experimental.pallas import tpu as pltpu
from jax.sharding import PartitionSpec as P

HD = 64
F32 = jnp.float32
BF16 = jnp.bfloat16
BIG = -1e30
BLK = 256
WINDOWS = (640, 1664, 2048)
SCALE = 0.15
EXTRA = 16
NN = (((1,), (0,)), ((), ()))
NT = (((1,), (1,)), ((), ()))
TN = (((0,), (0,)), ((), ()))


def mm(a, b, dims=NN):
    return lax.dot_general(a, b, dims, preferred_element_type=F32)


class Order:
    def __init__(self):
        self.last = ()


ORDER = Order()


def run(kernel, us, mib, scalars, args, outs, scratch=(), awaits=(), carry=(), apart=()):
    in_vmem = pl.BlockSpec(memory_space=pltpu.VMEM)
    anywhere = pl.BlockSpec(memory_space=pl.ANY)
    awaits = (*awaits, *ORDER.last)
    n_in = len(scalars) + len(apart) + len(args)
    n_skip, n_out = len(awaits) + len(carry), len(outs)

    def body(*refs):
        rest = refs[n_in + n_skip :]
        kernel(*refs[:n_in], *rest[:n_out], *rest[n_out + len(carry) :])

    results = pl.pallas_call(
        body,
        in_specs=[pl.BlockSpec(memory_space=pltpu.SMEM)] * len(scalars)
        + [anywhere] * len(apart)
        + [in_vmem] * len(args)
        + [anywhere] * n_skip,
        out_specs=[in_vmem] * n_out + [anywhere] * len(carry),
        out_shape=[jax.ShapeDtypeStruct(*o) for o in outs] + [jax.ShapeDtypeStruct(c.shape, c.dtype) for c in carry],
        scratch_shapes=list(scratch),
        input_output_aliases={n_in + len(awaits) + i: n_out + i for i in range(len(carry))},
        compiler_params=pltpu.CompilerParams(vmem_limit_bytes=mib << 20),
        cost_estimate=pl.CostEstimate(flops=int(us * SCALE * 1.1e9), bytes_accessed=1 << 18, transcendentals=0),
    )(*scalars, *apart, *args, *awaits, *carry)
    ORDER.last = (min(results[:n_out], key=lambda r: r.size),)
    return results


def gate_kernel(out):
    out[...] = jnp.zeros(out.shape, F32)


def gate(*arrays, awaits=()):
    return run(gate_kernel, 0.1, 4, (), (), [((8, 128), F32)], awaits=awaits, carry=arrays)[1:]


def split3(v):
    top = v.astype(BF16).astype(F32)
    rest = v - top
    middle = rest.astype(BF16).astype(F32)
    return top, middle, rest - middle


def split_rows(value, first, second):
    half = first.shape[0]
    first[...] = value[0:half].astype(first.dtype)
    second[...] = value[half:].astype(second.dtype)


def transpose_into(dst, value, spots, cols):
    turned = value.T
    if spots is None:
        dst[:, cols] = turned
        return
    count = spots.shape[0]
    rows = turned.shape[0] // count
    for b in range(count):
        dst[pl.ds(pl.multiple_of(spots[b] * rows, rows), rows), cols] = turned[b * rows : (b + 1) * rows]


def transpose_kernel(fast, spots, at_ref, p0, p1, p2, p3, t0, t1, t2, t3, out, wo, sem):
    rows = out.shape[1] // 4
    part = wo.shape[0] // 4
    copies = []
    for n, p in enumerate((p0, p1, p2, p3)):
        spot = pl.ds(pl.multiple_of((at_ref[0] ^ n) * part, part), part)
        copies.append(pltpu.make_async_copy(p.at[pl.ds(p.shape[0] - part, part), :], wo.at[spot, :], sem.at[n]))
        copies[-1].start()
    for p, t in enumerate((t0, t1, t2, t3)):
        transpose_into(out, t[0:rows, :], spots if fast else None, slice(p * rows, (p + 1) * rows))
    for c in copies:
        c.wait()


def transposed(fast, spots, at, pieces, rows, parts, wo, awaits=()):
    width = pieces[0].shape[1]
    return run(
        functools.partial(transpose_kernel, fast),
        2,
        8,
        (spots, at),
        pieces,
        [((width, 4 * rows), BF16), (wo.shape, BF16)],
        [pltpu.SemaphoreType.DMA((4,))],
        awaits,
        apart=parts,
    )


def project_kernel(piece, sp_ref, freq_ref, tok_ref, w_ref, qt_ref, kt_ref, k_ref, vt_ref, cs_ref):
    n = tok_ref.shape[0] - EXTRA
    place = (sp_ref[8] ^ piece) * n + lax.broadcasted_iota(jnp.int32, (1, n), 1)
    seg = jnp.zeros((1, n), jnp.int32)
    pos = place
    end = 0
    for d in range(8):
        length = sp_ref[d]
        end = end + length
        past = place >= end
        seg += past.astype(jnp.int32)
        pos -= jnp.where(past, length, 0)
    angles = pos.astype(F32) * freq_ref[:, 0:1]
    cosine, sine = jnp.cos(angles), jnp.sin(angles)
    cs_ref[0:32, :] = cosine
    cs_ref[32:64, :] = sine
    idx = lax.broadcasted_iota(jnp.int32, (64, n), 0)
    which = jnp.where(idx < 19, idx - 8, idx - 19)
    bit = (jnp.broadcast_to(place, (64, n)) >> jnp.clip(which, 0, 10)) & 1
    flipped = jnp.where(idx < 19, bit, 1 - bit).astype(F32)
    same = (idx == seg).astype(F32)
    coded = (idx >= 8) & (idx < 30)
    invalid = 1.0 - tok_ref[n : n + EXTRA, 0:n].astype(F32)[0:1]
    q_tail = jnp.where(idx < 8, BIG * (1.0 - same), jnp.where(coded, BIG * flipped, 0.0))
    k_tail = jnp.where(idx < 8, same, jnp.where(coded, invalid * (1.0 - flipped), 0.0))
    k_tail = jnp.where((idx >= 32) & (idx < 35), 1.0, k_tail)
    v_tail = jnp.where(idx < 3, 1.0, 0.0)
    y = mm(w_ref[...], tok_ref[0:n, :], NT)

    def rotated(at):
        a, b = y[at : at + 32], y[at + 32 : at + 64]
        return jnp.concatenate([a * cosine - b * sine, b * cosine + a * sine], axis=0)

    for h in range(3):
        qt_ref[h] = jnp.concatenate([rotated(h * HD) * 0.125, q_tail], axis=0).astype(BF16)
        key = jnp.concatenate([rotated(192 + h * HD), k_tail], axis=0)
        kt_ref[h] = key.astype(BF16)
        k_ref[h] = key.T.astype(BF16)
        vt_ref[h] = jnp.concatenate([y[384 + h * HD : 448 + h * HD], v_tail], axis=0).astype(BF16)


def project(piece, sp, freqs, tok, w, awaits=(), carry=()):
    rows = tok.shape[0] - EXTRA
    wide, tall = ((3, 128, rows), BF16), ((3, rows, 128), BF16)
    return run(
        functools.partial(project_kernel, piece),
        2.5,
        10,
        (sp,),
        (freqs, tok, w),
        (wide, wide, tall, wide, ((HD, rows), F32)),
        awaits=awaits,
        carry=carry,
    )


def window_of(sp_ref, block, total):
    a = block * BLK
    b = a + BLK - 1
    first, last, end = 0, 0, 0
    for d in range(8):
        begin, end = end, end + sp_ref[d]
        first = jnp.where(begin <= a, begin, first)
        last = jnp.where(begin <= b, end, last)
    start = (first // 128) * 128
    kind = jnp.where(last - start <= WINDOWS[0], 0, jnp.where(last - start <= WINDOWS[1], 1, 2))
    size = jnp.where(kind == 0, WINDOWS[0], jnp.where(kind == 1, WINDOWS[1], WINDOWS[2]))
    return pl.multiple_of(jnp.minimum(start, total - size), 128), kind


def place_of(sp_ref, piece, rows):
    return pl.ds(pl.multiple_of((sp_ref[8] ^ piece) * rows, rows), rows)


def attend_kernel(base, sp_ref, qa, qb, k0, k1, k2, k3, v0, v1, v2, v3, oa, ob, ba, bb, k_scr, v_scr, s_scr, q_scr, o_scr):
    rows = qa.shape[2]
    total = 4 * rows
    for p, (k, v) in enumerate(((k0, v0), (k1, v1), (k2, v2), (k3, v3))):
        at = place_of(sp_ref, p, rows)
        k_scr[:, at, :] = k[...]
        v_scr[:, :, at] = v[...]
    for n in range(4):
        q_scr[n] = (qa, qb)[n // 2][:, :, (n % 2) * BLK : (n % 2 + 1) * BLK]

    def q_block(i, carry):
        start, kind = window_of(sp_ref, (base + i) ^ (2 * sp_ref[8]), total)

        def scores(h, size):
            s = mm(k_scr[h, pl.ds(start, size), :], q_scr[i, h])
            s_scr[h, 0:size, :] = s
            return jnp.max(s, axis=0, keepdims=True)

        def weigh(h, size, top):
            p = jnp.exp(s_scr[h, 0:size, :] - top).astype(BF16)
            acc = mm(v_scr[h, :, pl.ds(start, size)], p)
            norm = acc[64:65]
            o_scr[i, h * HD : (h + 1) * HD, :] = (acc[0:64] / norm).astype(BF16)
            parts = split3(-(top + jnp.log(norm)))
            q_scr[i, h, 96:112, :] = jnp.concatenate([*parts, jnp.zeros((13, BLK), F32)], axis=0).astype(BF16)

        for mode, size in enumerate(WINDOWS):

            @pl.when(kind == mode)
            def _():
                t0 = scores(0, size)
                t1 = scores(1, size)
                weigh(0, size, t0)
                t2 = scores(2, size)
                weigh(1, size, t1)
                weigh(2, size, t2)

        return carry

    lax.fori_loop(0, 4, q_block, 0)
    for n in range(4):
        at = slice((n % 2) * BLK, (n % 2 + 1) * BLK)
        (oa, ob)[n // 2][:, at] = o_scr[n]
        (ba, bb)[n // 2][:, :, at] = q_scr[n]


def attend(half, sp, qt, k, vt, awaits=(), carry=()):
    rows = qt[0].shape[2]
    total = 4 * rows
    out, back = ((3 * HD, rows), BF16), ((3, 128, rows), BF16)
    return run(
        functools.partial(attend_kernel, half * 4),
        8,
        18,
        (sp,),
        (qt[2 * half], qt[2 * half + 1], *k, *vt),
        (out, out, back, back),
        [
            pltpu.VMEM((3, total, 128), BF16),
            pltpu.VMEM((3, 128, total), BF16),
            pltpu.VMEM((3, total, BLK), F32),
            pltpu.VMEM((4, 3, 128, BLK), BF16),
            pltpu.VMEM((4, 3 * HD, BLK), BF16),
        ],
        awaits,
        carry,
    )


def attend_back_kernel(h, fast, sp_ref, spots, *refs):
    q_refs, kt_refs, k_refs, vt_refs, o_refs, d_refs = (refs[4 * n : 4 * n + 4] for n in range(6))
    n_given = (1, 4, 6)[h]
    cs_refs, tok_t, given, outs = refs[24:28], refs[28], refs[29 : 29 + n_given], refs[29 + n_given : -13]
    q_scr, do_scr, o_scr, kt_scr, k_scr, vt_scr, dq_scr, dk_scr, dv_scr, g_scr, tail_scr, eb_scr, sem = refs[-13:]
    rows = kt_refs[0].shape[2]
    total = 4 * rows
    head = pl.ds(h * HD, HD)
    copies = []
    for p in range(4):
        spot, at = place_of(sp_ref, p, rows), pl.ds(p * rows, rows)
        copies += [
            (kt_refs[p].at[h], kt_scr.at[:, spot]),
            (k_refs[p].at[h], k_scr.at[spot, :]),
            (vt_refs[p].at[h], vt_scr.at[:, spot]),
            (q_refs[p].at[h], q_scr.at[:, at]),
            (d_refs[p].at[head, :], do_scr.at[pl.ds(0, HD), at]),
            (o_refs[p].at[head, :], o_scr.at[:, at]),
            (d_refs[p].at[pl.ds(3 * HD, 16), :], tail_scr.at[p]),
        ]
    if h == 0:
        copies.append((d_refs[1].at[pl.ds(208, 576), :], eb_scr))
    copies = [pltpu.make_async_copy(src, dst, sem.at[n]) for n, (src, dst) in enumerate(copies)]
    for c in copies:
        c.start()
    dk_scr[...] = jnp.zeros(dk_scr.shape, F32)
    dv_scr[...] = jnp.zeros(dv_scr.shape, F32)
    for c in copies:
        c.wait()
    do_scr[64:128, :] = jnp.zeros((64, total), BF16)
    delta = jnp.sum(do_scr[0:64, :].astype(F32) * o_scr[...].astype(F32), axis=0, keepdims=True)
    do_scr[64:80, :] = jnp.concatenate([*split3(-delta), jnp.zeros((13, total), F32)], axis=0).astype(BF16)

    def q_block(i, carry):
        start, kind = window_of(sp_ref, i ^ (2 * sp_ref[8]), total)
        here = pl.ds(pl.multiple_of(i * BLK, BLK), BLK)
        for mode, size in enumerate(WINDOWS):

            @pl.when(kind == mode)
            def _():
                qt, dot = q_scr[:, here], do_scr[:, here]
                q, do = qt.astype(F32).T.astype(BF16), dot.astype(F32).T.astype(BF16)
                win = pl.ds(start, size)
                p = jnp.exp(mm(q, kt_scr[:, win]))
                ds = (p * mm(do, vt_scr[:, win])).astype(BF16)
                dv_scr[:, win] += mm(dot, p.astype(BF16))
                dk_scr[:, win] += mm(qt, ds)
                dq_scr[here, :] = mm(ds, k_scr[win, :])

        return carry

    lax.fori_loop(0, 8, q_block, 0)

    def unrotated(g, cosine, sine):
        g = g.astype(BF16).astype(F32)
        a, b = g[0:32], g[32:64]
        return jnp.concatenate([a * cosine + b * sine, b * cosine - a * sine], axis=0).astype(BF16)

    for p in range(4):
        at = slice(p * rows, (p + 1) * rows)
        cosine, sine = cs_refs[p][0:32, :], cs_refs[p][32:64, :]
        src = place_of(sp_ref, p, rows)
        g_scr[0:64, at] = unrotated(dq_scr[at, :].T[0:64] * 0.125, cosine, sine)
        g_scr[64:128, at] = unrotated(dk_scr[0:64, src], cosine, sine)
        g_scr[128:192, at] = dv_scr[0:64, src].astype(BF16)
    grad = mm(tok_t[...], g_scr[...], NT)
    heads = 3 * HD
    near, far, core = outs[0:3]
    near[...] = g_scr[:, 0:rows]
    far[0:heads, :] = g_scr[:, 2 * rows : 3 * rows]
    if h < 2:
        far[heads : 2 * heads, :] = g_scr[:, 3 * rows :]
    if h == 0:
        (ea,) = given
        grad_out, e_own, total = outs[3:]
        core[...] = g_scr[:, rows : 2 * rows]
        grad_out[...] = grad.astype(BF16)
        e = ea[...].astype(F32) + unpack_rows(eb_scr, 0, 2 * heads)
        e_own[...] = e[0:heads].astype(BF16)
        pack_rows(far, 2 * heads, e[heads:])
        sums = [tail_scr[p].astype(F32) for p in range(4)]
        joined = (sums[0] + sums[1]) + (sums[2] + sums[3])
        total[:, 0:512] = joined[0:4] + joined[4:8]
        total[:, 512:768] = (joined[8:12] + joined[12:16])[:, 0:256]
    elif h == 1:
        core_before, before, sum_own, sum_got = given
        first, second, total = outs[3:]
        core[0:heads, :] = core_before[...]
        core[heads:, :] = g_scr[:, rows : 2 * rows]
        split_rows(jnp.concatenate([before[...].astype(F32), grad], axis=1), first, second)
        total[...] = sum_own[...] + sum_got[...]
    else:
        core_before, far0, e_own, sum_own, sum_got, arrange = given
        first, second, total, cross = outs[3:]
        cross[...] = g_scr[:, 3 * rows :]
        core[0 : 2 * heads, :] = core_before[...]
        core[2 * heads : 3 * heads, :] = g_scr[:, rows : 2 * rows]
        core[3 * heads :, :] = far0[heads : 2 * heads, :]
        e = e_own[...].astype(F32) + unpack_rows(far0, 2 * heads, heads)
        if fast:
            transpose_into(eb_scr, e, spots, slice(None))
            e = eb_scr[...]
        else:
            e = mm(arrange[...], e.astype(BF16), NT)
        split_rows(jnp.concatenate([grad, e], axis=1), first, second)
        total[...] = sum_own[...] + sum_got[...]


def attend_back(h, fast, spots, sp, q, kt, k, vt, o, d, cs, tok_t, given, awaits=()):
    rows = kt[0].shape[2]
    total = 4 * rows
    width = tok_t.shape[0]
    heads = 3 * HD
    far = (2 * heads + 3 * heads // 2, 2 * heads, heads)[h]
    outs = [((heads, rows), BF16), ((far, rows), BF16), (((1, 2, 4)[h] * heads, rows), BF16)]
    if h == 0:
        outs += [((width, heads), BF16), ((heads, width), BF16)]
    else:
        outs += [((width // 2, 2 * heads), BF16)] * 2
    outs += [((4, width), F32)]
    if h == 2:
        outs += [((heads, rows), BF16)]
    return run(
        functools.partial(attend_back_kernel, h, fast),
        12,
        20,
        (sp, spots),
        (*cs, tok_t, *given),
        outs,
        [
            pltpu.VMEM((128, total), BF16),
            pltpu.VMEM((128, total), BF16),
            pltpu.VMEM((HD, total), BF16),
            pltpu.VMEM((128, total), BF16),
            pltpu.VMEM((total, 128), BF16),
            pltpu.VMEM((128, total), BF16),
            pltpu.VMEM((total, 128), F32),
            pltpu.VMEM((128, total), F32),
            pltpu.VMEM((128, total), F32),
            pltpu.VMEM((heads, total), BF16),
            pltpu.VMEM((4, 16, rows), BF16),
            pltpu.VMEM((3 * heads, rows), BF16) if h == 0 else pltpu.VMEM((width, heads), F32),
            pltpu.SemaphoreType.DMA((29,)),
        ],
        awaits,
        apart=(*q, *kt, *k, *vt, *o, *d),
    )


def norm_parts(h):
    centred = h - jnp.mean(h, axis=-1, keepdims=True)
    inverse = lax.rsqrt(jnp.mean(centred * centred, axis=-1, keepdims=True) + 1e-05)
    return centred * inverse, inverse


def norm_back(grad, normed, inverse, gain):
    scaled = grad * gain
    return inverse * (
        scaled
        - jnp.mean(scaled, axis=-1, keepdims=True)
        - normed * jnp.mean(scaled * normed, axis=-1, keepdims=True)
    )


def sigmoid(v):
    return 0.5 + 0.5 * jnp.tanh(0.5 * v)


def out_kernel(a0, a1, a2, a3, w0, w1, w2, w3, tok_ref, gain_ref, bias_ref, low_ref, xhat_ref, inv_ref):
    w = jnp.concatenate([w0[...], w1[...], w2[...], w3[...]], axis=0)
    for half in range(2):
        at = slice(half * BLK, (half + 1) * BLK)
        a = jnp.concatenate([a0[:, at], a1[:, at], a2[:, at], a3[:, at]], axis=0)
        normed, inverse = norm_parts(tok_ref[at, :].astype(F32) + mm(a, w, TN))
        xhat_ref[at, :] = normed
        inv_ref[at, :] = jnp.broadcast_to(inverse, (BLK, 128))
        low_ref[at, :] = (normed * gain_ref[...] + bias_ref[...]).astype(BF16)


def out_project(a, w, tok, gain, bias, awaits=()):
    rows, width = tok.shape
    return run(
        out_kernel,
        3,
        10,
        (),
        (*a, *w, tok, gain, bias),
        (((rows, width), BF16), ((rows, width), F32), ((rows, 128), F32)),
        awaits=awaits,
    )


def gather_weights(at_ref, parts, wgu, wd, sem):
    copies = []
    for n, part in enumerate(parts):
        dst = wgu if n < 4 else wd
        rows = dst.shape[0] // 4
        spot = pl.ds(pl.multiple_of((at_ref[0] ^ (n % 4)) * rows, rows), rows)
        copies.append(pltpu.make_async_copy(part.at[pl.ds(0, rows), :], dst.at[spot, :], sem.at[n]))
    for c in copies:
        c.start()
    return copies


def mlp_rows(x, wg, wu, down, da, db, hid):
    gate, up = mm(x, wg), mm(x, wu)
    s = sigmoid(gate)
    act = gate * s
    low = (act * up).astype(BF16)
    da[...] = (up * (s + act * (1.0 - s))).astype(BF16)
    db[...] = act.astype(BF16)
    if hid is not None:
        hid[...] = low
    return mm(low, down)


def mlp_own_kernel(ml1_ref, ml0, wgu, wd, acc, da, db, hid, ml1, sem):
    rows = ml0.shape[0]
    hidden = wd.shape[0]
    copy = pltpu.make_async_copy(ml1_ref, ml1, sem)
    copy.start()
    for block, x in enumerate((ml0, ml1)):
        if block:
            copy.wait()
        at = slice(block * rows, (block + 1) * rows)
        total = None
        for col in range(0, hidden, BLK):
            cols, ups = slice(col, col + BLK), slice(hidden + col, hidden + col + BLK)
            saved = [u.at[at, cols] for u in (da, db, hid)]
            part = mlp_rows(x[...], wgu[:, cols], wgu[:, ups], wd[cols, :], *saved)
            total = part if total is None else total + part
        acc[at, :] = total


def mlp_own(ml0, ml1, wgu, wd, awaits=()):
    rows, width = ml0.shape
    hidden = wd.shape[0]
    saved = ((2 * rows, hidden), BF16)
    return run(
        mlp_own_kernel,
        5,
        10,
        (),
        (ml0, wgu, wd),
        [((2 * rows, width), F32)] + [saved] * 3,
        [pltpu.VMEM((rows, width), BF16), pltpu.SemaphoreType.DMA],
        awaits,
        apart=(ml1,),
    )


def mlp_peer_kernel(at_ref, *refs):
    ml0, ml1, acc, own, sib, da, db, wgu, wd, sem = refs[8:]
    rows = ml0.shape[0]
    hidden = da.shape[1]
    for c in gather_weights(at_ref, refs[:8], wgu, wd, sem):
        c.wait()
    for block, x in enumerate((ml0, ml1)):
        at = slice(block * rows, (block + 1) * rows)
        total = acc[at, :]
        for col in range(0, hidden, BLK):
            cols, ups = slice(col, col + BLK), slice(hidden + col, hidden + col + BLK)
            saved = [u.at[at, cols] for u in (da, db)]
            total += mlp_rows(x[...], wgu[:, cols], wgu[:, ups], wd[cols, :], *saved, None)
        if block:
            sib[...] = total.astype(BF16)
        else:
            own[...] = total


def mlp_peer(at, ml0, ml1, acc, parts, awaits=()):
    rows, width = ml0.shape
    hidden = parts[0].shape[1] // 2
    saved = ((2 * rows, hidden), BF16)
    return run(
        mlp_peer_kernel,
        6,
        13,
        (at,),
        (ml0, ml1, acc),
        [((rows, width), F32), ((rows, width), BF16)] + [saved] * 2,
        [pltpu.VMEM((width, 2 * hidden), BF16), pltpu.VMEM((hidden, width), BF16), pltpu.SemaphoreType.DMA((8,))],
        awaits,
        apart=parts,
    )


def copies_of(src, dst, sem, rows=128):
    copies = []
    for n in range(src.shape[0] // rows):
        at = pl.ds(n * rows, rows)
        copies.append(pltpu.make_async_copy(src.at[at, :], dst.at[at, :], sem.at[n]))
        copies[-1].start()
    return copies


def mid_kernel(
    got, xhat_ref, own_ref, go_ref, g1, b1, g2, b2, out_ref, dh_ref, dm_ref, sums_ref, got_ref, sem
):
    gain_sum, bias_sum = 0.0, 0.0
    copies = copies_of(got, got_ref, sem)
    for start in range(0, xhat_ref.shape[0], 128):
        at = slice(start, start + 128)
        copies[start // 128].wait()
        mid = xhat_ref[at, :] * g1[...] + b1[...]
        normed, inverse = norm_parts(mid + (own_ref[at, :] + got_ref[at, :].astype(F32)))
        out_ref[at, :] = (normed * g2[...] + b2[...]).astype(BF16)
        grad = go_ref[at, :].astype(F32)
        dh = norm_back(grad, normed, inverse, g2[...])
        dh_ref[at, :] = dh
        dm_ref[at, :] = dh.astype(BF16)
        gain_sum += jnp.sum(grad * normed, axis=0, keepdims=True)
        bias_sum += jnp.sum(grad, axis=0, keepdims=True)
    sums_ref[0:1, :] = gain_sum
    sums_ref[1:2, :] = bias_sum


def mid_norm(xhat, own, got, out_grad, g1, b1, g2, b2, awaits=()):
    rows, width = xhat.shape
    return run(
        mid_kernel,
        3,
        8,
        (),
        (xhat, own, out_grad, g1, b1, g2, b2),
        (((rows, width), BF16), ((rows, width), F32), ((rows, width), BF16), ((2, width), F32)),
        [pltpu.VMEM((rows, width), BF16), pltpu.SemaphoreType.DMA((rows // 128,))],
        awaits,
        apart=(got,),
    )


def mlp_back_kernel(at_ref, *refs):
    dm1_ref, dm0, wgu, wd, da_o, db_o, da_p, db_p, own, sib, dg_o, du_o, wgu_p, wd_p, dm1, sem = refs[8:]
    rows = dm0.shape[0]
    hidden = wd.shape[0]
    first = pltpu.make_async_copy(dm1_ref, dm1, sem.at[8])
    first.start()
    copies = gather_weights(at_ref, refs[:8], wgu_p, wd_p, sem)

    def part_of(x, at, cols, wg, wu, down, da, db, keep):
        dhid = mm(x[...], down, NT)
        dgate = (dhid * da[at, cols].astype(F32)).astype(BF16)
        dup = (dhid * db[at, cols].astype(F32)).astype(BF16)
        if keep:
            dg_o[at, cols] = dgate
            du_o[at, cols] = dup
        return mm(dgate, wg, NT) + mm(dup, wu, NT)

    totals = [None, None]
    for peer, (gu, down, da, db) in enumerate(((wgu, wd, da_o, db_o), (wgu_p, wd_p, da_p, db_p))):
        for block, x in enumerate((dm0, dm1)):
            if block and not peer:
                first.wait()
            at = slice(block * rows, (block + 1) * rows)
            for col in range(0, hidden, BLK):
                cols, ups = slice(col, col + BLK), slice(hidden + col, hidden + col + BLK)
                part = part_of(x, at, cols, gu[:, cols], gu[:, ups], down[cols, :], da, db, not peer)
                totals[block] = part if totals[block] is None else totals[block] + part
        if not peer:
            for c in copies:
                c.wait()
    own[...] = totals[0]
    sib[...] = totals[1].astype(BF16)


def mlp_backward(at, dm0, dm1, wgu, wd, parts, da_o, db_o, da_p, db_p, awaits=()):
    rows, width = dm0.shape
    hidden = wd.shape[0]
    saved = ((2 * rows, hidden), BF16)
    return run(
        mlp_back_kernel,
        11,
        18,
        (at,),
        (dm0, wgu, wd, da_o, db_o, da_p, db_p),
        [((rows, width), F32), ((rows, width), BF16)] + [saved] * 2,
        [
            pltpu.VMEM((width, 2 * hidden), BF16),
            pltpu.VMEM((hidden, width), BF16),
            pltpu.VMEM((rows, width), BF16),
            pltpu.SemaphoreType.DMA((9,)),
        ],
        awaits,
        apart=(*parts, dm1),
    )


def first_norm_kernel(
    got_ref, dh2, own, xhat, inv, g1, sums2, a0, a1, a2, a3, w0, w1, w2, w3,
    dh1, d0, d1, d2, d3, ea, dat_scr, got, sem,
):
    gain_sum, bias_sum = 0.0, 0.0
    copies = copies_of(got_ref, got, sem)
    for start in range(0, dh2.shape[0], 128):
        at = slice(start, start + 128)
        copies[start // 128].wait()
        dmid = dh2[at, :] + (own[at, :] + got[at, :].astype(F32))
        normed = xhat[at, :]
        gain_sum += jnp.sum(dmid * normed, axis=0, keepdims=True)
        bias_sum += jnp.sum(dmid, axis=0, keepdims=True)
        grad = norm_back(dmid, normed, inv[at, 0:1], g1[...])
        dh1[at, :] = grad
        dat_scr[at, :] = grad.astype(BF16)
    sums = jnp.concatenate([gain_sum, bias_sum, sums2[...]], axis=0)
    high = sums.astype(BF16).astype(F32)
    both = jnp.concatenate([high, sums - high], axis=0)
    rest = jnp.concatenate([both[:, 512:], jnp.zeros((8, dh2.shape[0] - 256), F32)], axis=1)
    tail = jnp.concatenate([both[:, 0:512], rest], axis=0).astype(BF16)
    dat = dat_scr[...]
    for w, d in ((w0, d0), (w1, d1), (w2, d2), (w3, d3)):
        d[0:192, :] = mm(w[...], dat, NT).astype(BF16)
        d[192:208, :] = tail
    ea[...] = mm(jnp.concatenate([a0[...], a2[...]], axis=0), dat).astype(BF16)
    pack_rows(d1, 208, mm(jnp.concatenate([a1[...], a3[...]], axis=0), dat))


def pack_rows(dst, start, value):
    n = value.shape[0]
    rest = value[:, 512:]
    dst[start : start + n, :] = value[:, 0:512].astype(dst.dtype)
    dst[start + n : start + n + n // 2, :] = jnp.concatenate([rest[0 : n // 2], rest[n // 2 :]], axis=1).astype(dst.dtype)


def unpack_rows(src, start, n):
    rest = src[start + n : start + n + n // 2, :].astype(F32)
    rest = jnp.concatenate([rest[:, 0:256], rest[:, 256:]], axis=0)
    return jnp.concatenate([src[start : start + n, :].astype(F32), rest], axis=1)


def first_norm_back(dh2, own, got, xhat, inv, g1, sums2, a, w, awaits=()):
    rows, width = dh2.shape
    heads = a[0].shape[0]
    d = ((heads + 16, rows), BF16)
    return run(
        first_norm_kernel,
        5,
        12,
        (),
        (dh2, own, xhat, inv, g1, sums2, *a, *w),
        [((rows, width), F32), d, ((4 * heads + 16, rows), BF16), d, d, ((2 * heads, width), BF16)],
        [pltpu.VMEM((rows, width), BF16), pltpu.VMEM((rows, width), BF16), pltpu.SemaphoreType.DMA((rows // 128,))],
        awaits,
        apart=(got,),
    )


def far_kernel(
    fast, spots, dm0, dm1, dm2, dm3, ml2, ml3, wgu, wd, hid_o, first, second, dg, du, dmt, hids
):
    rows = dm0.shape[0]
    hidden = wd.shape[0]
    for p, u in enumerate((dm0, dm1, dm2, dm3)):
        transpose_into(dmt, u[...], spots if fast else None, slice(p * rows, (p + 1) * rows))
    for col in range(0, hidden, BLK):
        cols, ups = slice(col, col + BLK), slice(hidden + col, hidden + col + BLK)
        hids[0 : 2 * rows, :] = hid_o[:, cols]
        for block, (x, dm) in enumerate(((ml2, dm2), (ml3, dm3))):
            at = slice(block * rows, (block + 1) * rows)
            gate, up, dhid = mm(x[...], wgu[:, cols]), mm(x[...], wgu[:, ups]), mm(dm[...], wd[cols, :], NT)
            s = sigmoid(gate)
            act = gate * s
            hids[(2 + block) * rows : (3 + block) * rows, :] = (act * up).astype(BF16)
            dg[at, cols] = (dhid * (up * (s + act * (1.0 - s)))).astype(BF16)
            du[at, cols] = (dhid * act).astype(BF16)
        split_rows(mm(dmt[...], hids[...]), first.at[:, cols], second.at[:, cols])


def far_rows(fast, spots, dm, ml, wgu, wd, hid, awaits=(), carry=()):
    rows, width = dm[0].shape
    hidden = wd.shape[0]
    return run(
        functools.partial(far_kernel, fast),
        8,
        14,
        (spots,),
        (*dm, *ml, wgu, wd, hid),
        [((width // 2, hidden), BF16)] * 2 + [((2 * rows, hidden), BF16)] * 2,
        [pltpu.VMEM((width, 4 * rows), BF16), pltpu.VMEM((4 * rows, BLK), BF16)],
        awaits,
        carry,
    )


def weight_kernel(fast, spots, ml0, ml1, ml2, ml3, dg_o, du_o, dg_f, du_f, first, second, mlt):
    rows = ml0.shape[0]
    hidden = dg_o.shape[1]
    for p, u in enumerate((ml0, ml1, ml2, ml3)):
        transpose_into(mlt, u[...], spots if fast else None, slice(p * rows, (p + 1) * rows))
    for n, (near, far) in enumerate(((dg_o, dg_f), (du_o, du_f))):
        cols = slice(n * hidden, (n + 1) * hidden)
        grad = mm(mlt[:, 0 : 2 * rows], near[...]) + mm(mlt[:, 2 * rows :], far[...])
        split_rows(grad, first.at[:, cols], second.at[:, cols])


def weight_grads(fast, spots, ml, near, far, awaits=()):
    rows, width = ml[0].shape
    hidden = near[0].shape[1]
    return run(
        functools.partial(weight_kernel, fast),
        6,
        14,
        (spots,),
        (*ml, *near, *far),
        [((width // 2, 2 * hidden), BF16)] * 2,
        [pltpu.VMEM((width, 4 * rows), BF16)],
        awaits,
    )


def input_kernel(dh1, n0, n1, n2, core, core1, f0, f1, f2, x2, w0, w1, w2, w3, out):
    rows = n0.shape[1]
    heads = 3 * HD
    sources = (
        ((n0, 0), (n1, 0), (n2, 0)),
        ((core, 0), (core, heads), (core, 2 * heads)),
        ((f0, 0), (f1, 0), (f2, 0)),
        ((core, 3 * heads), (core1, heads), (x2, 0)),
    )
    for half in range(rows // BLK):
        at = slice(half * BLK, (half + 1) * BLK)
        total = dh1[at, :]
        for source, w in zip(sources, (w0, w1, w2, w3)):
            cat = jnp.concatenate([ref[start : start + heads, at] for ref, start in source], axis=0)
            parts = [w[c * heads + h * HD : c * heads + (h + 1) * HD, :] for h in range(3) for c in range(3)]
            total += mm(cat, jnp.concatenate(parts, axis=0), TN)
        out[at, :] = total


def input_back(dh1, near, core, core1, far, far2, weights, awaits=()):
    args = (dh1, *near, core, core1, *far, far2, *weights)
    return run(input_kernel, 4, 12, (), args, [(dh1.shape, F32)], awaits=awaits)[0]


def swap(v, bit, axis="tensor"):
    n = lax.axis_size(axis)
    return lax.ppermute(v, axis, [(i, i ^ bit) for i in range(n)])


def bits_of(n):
    return n.bit_length() - 1


def spots_of(order, n):
    block = jnp.arange(n, dtype=jnp.int32) ^ lax.axis_index("dp")
    spot = jnp.zeros((n,), jnp.int32)
    for s, bit in enumerate(order):
        spot = spot + (((block >> bit) & 1) << (len(order) - 1 - s))
    return spot


def last_kernel(chains, kind, *refs):
    count = sum(chains)
    parts, outs, scrs, sem = refs[:count], refs[count:-count - 1], refs[-count - 1 : -1], refs[-1]
    copies = []
    for n, (part, scr) in enumerate(zip(parts, scrs)):
        copies.append(pltpu.make_async_copy(part.at[pl.ds(0, scr.shape[0]), :], scr, sem.at[n]))
        copies[-1].start()
    for c in copies:
        c.wait()
    sums, at = [], 0
    for length in chains:
        sums.append(sum(scr[...].astype(F32) for scr in scrs[at : at + length]))
        at += length
    if kind == "mlp":
        gu, down = outs
        half = gu.shape[2]
        gu[:, 0, :] = sums[0][:, 0:half]
        gu[:, 1, :] = sums[0][:, half:]
        down[...] = sums[1]
    else:
        qkv, out = outs
        total = jnp.concatenate([sums[0], sums[1]], axis=1)
        if len(sums) > 2:
            total += sums[2]
        for c in range(3):
            qkv[c] = jnp.concatenate([total[:, (3 * h + c) * HD : (3 * h + c + 1) * HD] for h in range(3)], axis=1)
        out[...] = total[:, 9 * HD :].T


def last_sums(kind, rows, chains, outs):
    parts = [part for chain in chains for part in chain]
    return run(
        functools.partial(last_kernel, [len(chain) for chain in chains], kind),
        2,
        8,
        (),
        (),
        outs,
        [pltpu.VMEM((rows, part.shape[1]), BF16) for part in parts] + [pltpu.SemaphoreType.DMA((len(parts),))],
        apart=parts,
    )


class scatter_steps:
    def __init__(self, first, second, order):
        self.first, self.parts, self.order, self.step = first, [first], order, 0
        self.sent = second

    def advance(self):
        self.parts.append(swap(self.sent, 1 << self.order[self.step], "dp"))
        self.step += 1
        if self.step < len(self.order):
            length = self.parts[-1].shape[0]
            self.sent = sum(u[length // 2 : length].astype(F32) for u in self.parts).astype(BF16)
        return self.parts[-1]

    def all_parts(self):
        while self.step < len(self.order):
            self.advance()
        return self.parts


def joined_steps(one, two):
    order, both = one.order, []
    for step in range(1, len(order)):
        length = (both or one.parts)[-1].shape[0] // 2
        at = slice(length, 2 * length)
        sent = jnp.concatenate([sum(u[at].astype(F32) for u in chain.parts) for chain in (one, two)], axis=1)
        both.append(swap(sum((u[at].astype(F32) for u in both), sent).astype(BF16), 1 << order[step], "dp"))
    return one.parts, two.parts, both


def first_sums(chains, rows):
    sums = [sum(part[0:rows].astype(F32) for part in chain) for chain in chains]
    if len(sums) == 3:
        return jnp.concatenate(sums[0:2], axis=1) + sums[2]
    return sums


def quarter_of(w):
    rows = w.shape[0] // 4
    return lax.dynamic_slice_in_dim(w, (lax.axis_index("dp") % 4) * rows, rows, axis=0)


def local(
    tokens,
    doc_lengths,
    key_mask,
    qkv_weight,
    out_weight,
    gate_up_weight,
    down_weight,
    norm1_gain,
    norm1_bias,
    norm2_gain,
    norm2_bias,
    out_grad,
):
    rows, width = tokens.shape
    flags = jnp.pad(key_mask.astype(BF16).reshape(1, rows), ((0, EXTRA - 1), (0, width - rows)))
    tok0 = jnp.concatenate([tokens, flags], axis=0)
    tok1 = swap(tok0, 1)
    tok2 = swap(tok0, 2)
    sp = jnp.concatenate([doc_lengths[0], lax.axis_index("tensor").reshape(1)]).astype(jnp.int32)
    quarter = (lax.axis_index("dp") % 4).reshape(1).astype(jnp.int32)
    freqs = 1000.0 ** (-(jnp.arange(HD // 2, dtype=F32) * 2.0 / HD))
    freqs = jnp.broadcast_to(freqs[:, None], (HD // 2, 128))
    wt = jnp.transpose(qkv_weight, (1, 2, 0)).reshape(-1, width)

    n_dp = lax.axis_size("dp")
    fast = (width // n_dp) % 16 == 0
    order = list(range(bits_of(n_dp)))
    order_d = order[1:2] + order[0:1] + order[2:]
    spots, spots_d = spots_of(order, n_dp), spots_of(order_d, n_dp)

    def arranged(v, at):
        if fast:
            return v
        blocks = v.reshape(v.shape[0], n_dp, width // n_dp)
        return jnp.take(blocks, jnp.argsort(at), axis=1).reshape(v.shape)

    ORDER.last = ()
    wo0 = out_weight
    wo1 = swap(wo0, 1)
    wgu = gate_up_weight.reshape(width, -1)
    part_a = jnp.concatenate([quarter_of(down_weight), quarter_of(out_weight)], axis=0)
    part_b = quarter_of(wgu)
    pa0 = swap(part_a, 2)

    proj = [project(0, sp, freqs, tok0, wt), project(1, sp, freqs, tok1, wt, awaits=(part_a, part_b))]
    (tok2,) = gate(tok2)
    tok3 = swap(tok2, 1)
    tok = (tok0, tok1, tok2, tok3)
    *more, part_b = project(2, sp, freqs, tok2, wt, carry=(part_b,))
    proj.append(more)
    pb0 = swap(part_b, 2)
    proj.append(project(3, sp, freqs, tok3, wt))
    qt, kt, k, vt, cs = zip(*proj)
    o2, o3, q2, q3 = attend(1, sp, qt, k, vt, (wo1,))
    o2, o3 = gate(o2, o3, awaits=(pa0,))
    pa1, pa2, pa3 = swap(pa0, 1, "dp"), swap(pa0, 2, "dp"), swap(pa0, 3, "dp")
    g2, g3 = swap(o2, 2), swap(o3, 3)
    o0, o1, q0, q1 = attend(0, sp, qt, k, vt)
    o1, pb0 = gate(o1, pb0)
    g1 = swap(o1, 1)
    tok_t, wo2 = transposed(
        fast, spots, quarter, [arranged(u, spots) for u in tok], rows, (pa0, pa1, pa2, pa3), wo0
    )
    wo3 = swap(wo2, 1)
    wo = (wo0, wo1, wo2, wo3)

    gain1, bias1, gain2, bias2 = (u.reshape(1, width) for u in (norm1_gain, norm1_bias, norm2_gain, norm2_bias))
    ml0, xhat1, inv1 = out_project((o0, g1, g2, g3), wo, tokens, gain1, bias1)
    ml0, pb0 = gate(ml0, pb0)
    pb1, pb2, pb3 = swap(pb0, 1, "dp"), swap(pb0, 2, "dp"), swap(pb0, 3, "dp")
    ml1, ml2 = swap(ml0, 1), swap(ml0, 2)
    acc, da_o, db_o, hid_o = mlp_own(ml0, ml1, wgu, down_weight)
    parts = (pb0, pb1, pb2, pb3, pa0, pa1, pa2, pa3)
    own, sib, da_p, db_p = mlp_peer(quarter, ml0, ml1, acc, parts)
    output, dh2, dm0, sums2 = mid_norm(xhat1, own, swap(sib, 1), out_grad, gain1, bias1, gain2, bias2)
    dm0, ml2 = gate(dm0, ml2)
    dm1, dm2 = swap(dm0, 1), swap(dm0, 2)
    ml3 = swap(ml2, 1)
    own, sib, dg_o, du_o = mlp_backward(quarter, dm0, dm1, wgu, down_weight, parts, da_o, db_o, da_p, db_p)
    (sib,) = gate(sib, awaits=(ml3,))
    dh1, d0, d1, d2, d3, ea = first_norm_back(
        dh2, own, swap(sib, 1), xhat1, inv1, gain1, sums2, (o0, g1, g2, g3), wo, (dm2,)
    )
    d1, d2, d3 = gate(d1, d2, d3)
    dm3 = swap(dm2, 1)
    d = (d0, swap(d1, 1), swap(d2, 2), swap(d3, 3))
    ml = [arranged(u, spots) for u in (ml0, ml1, ml2, ml3)]
    dm = [arranged(u, spots_d) for u in (dm0, dm1, dm2, dm3)]
    d_first, d_second, dg_f, du_f = far_rows(fast, spots_d, dm, ml[2:], wgu, down_weight, hid_o)
    wt0 = wt
    d_second, wt = gate(d_second, wt, awaits=d[1:])
    dn = scatter_steps(d_first, d_second, order_d)
    dn1 = dn.advance()
    wt1, wt2 = swap(wt0, 1), swap(wt, 2)
    gu_first, gu_second = weight_grads(fast, spots, ml, (dg_o, du_o), (dg_f, du_f))
    (gu_second,) = gate(gu_second, awaits=(wt1,))
    gu = scatter_steps(gu_first, gu_second, order)
    gu1 = gu.advance()

    arrange = jnp.zeros((8, 128), BF16)
    if not fast:
        column = jnp.arange(width)
        target = spots[column // (width // n_dp)] * (width // n_dp) + column % (width // n_dp)
        arrange = (column[:, None] == target[None, :]).astype(BF16)
    back = functools.partial(
        attend_back,
        fast=fast,
        spots=spots,
        sp=sp,
        q=(q0, q1, q2, q3),
        kt=kt,
        k=k,
        vt=vt,
        o=(o0, o1, o2, o3),
        d=d,
        cs=cs,
        tok_t=tok_t,
    )
    near0, far0, core0, grad0, e_own, sums = back(0, given=(ea,))
    far0, sums = gate(far0, sums, awaits=(dn1,))
    got0, dn2 = swap(far0, 2), dn.advance()
    sum_bits = [*order[1:], 0]
    sums_got = swap(sums, 1 << sum_bits[0], "dp")
    near1, far1, core1, first, second, sums = back(1, given=(core0, grad0, sums, sums_got))
    far1, second, sums = gate(far1, second, sums, awaits=(gu1, wt2))
    c1 = scatter_steps(first, second, order)
    c1_got, gu2 = c1.advance(), gu.advance()
    got1 = swap(far1, 2)
    sums_got = swap(sums, 1 << sum_bits[1], "dp")
    near2, far2, core2, first, second, sums, cross2 = back(
        2, given=(core1, got0, e_own, sums, sums_got, arrange)
    )
    far2, core2, second, sums, cross2, wt2 = gate(
        far2, core2, second, sums, cross2, wt2, awaits=(c1_got, gu2, got1, dn2)
    )
    c2 = scatter_steps(first, second, order)
    c2.advance()
    wt3 = swap(wt2, 1)
    for bit in sum_bits[2:]:
        sums = sums + swap(sums, 1 << bit, "dp")
    gu, dn, attention = gu.all_parts(), dn.all_parts(), joined_steps(c1, c2)
    core, core1 = swap(core2, 1), swap(got1, 1)
    got2, x2 = swap(far2, 2), swap(cross2, 3)
    input_grad = input_back(dh1, (near0, near1, near2), core, core1, (got0, got1, got2), x2, (wt, wt1, wt2, wt3))
    shard = width // n_dp
    if fast:
        hidden = down_weight.shape[0]
        gu_part, down_part = last_sums("mlp", shard, (gu, dn), [((shard, 2, hidden), F32), ((shard, hidden), F32)])
        qkv_part, out_part = last_sums(
            "attention", shard, attention, [((3, shard, 3 * HD), F32), ((3 * HD, shard), F32)]
        )
        qkv_part = jnp.transpose(qkv_part, (1, 0, 2))
    else:
        gu_part, down_part = first_sums((gu, dn), shard)
        gu_part = gu_part.reshape(shard, 2, -1)
        total = first_sums(attention, shard)
        out_part = total[:, 9 * HD :].T
        qkv_part = jnp.transpose(total[:, 0 : 9 * HD].reshape(shard, 3, 3, HD), (0, 2, 1, 3)).reshape(shard, 3, 3 * HD)
    return (
        output,
        input_grad,
        qkv_part,
        out_part,
        gu_part,
        down_part.T,
        sums[0],
        sums[1],
        sums[2],
        sums[3],
    )


def solution(mesh):
    placed = (
        P(("dp", "tensor"), None),
        P("dp", None),
        P(("dp", "tensor")),
        P(None, None, "tensor"),
        P("tensor", None),
        P(None, None, "tensor"),
        P("tensor", None),
        P(),
        P(),
        P(),
        P(),
        P(("dp", "tensor"), None),
    )
    return jax.shard_map(
        local,
        mesh=mesh,
        in_specs=placed,
        out_specs=(
            P(("dp", "tensor"), None),
            P(("dp", "tensor"), None),
            P("dp", None, "tensor"),
            P("tensor", "dp"),
            P("dp", None, "tensor"),
            P("tensor", "dp"),
            P(),
            P(),
            P(),
            P(),
        ),
        check_vma=False,
    )
```

time: 834 us -> 289 us (0.35)
  waiting for transfers between devices: 395 us -> 105 us
  matrix products: 218 us -> 0 us
  Pallas kernels: 0 us -> 120 us
  other arithmetic: 109 us -> 1.63 us
  blocking collectives: 45.9 us -> 0 us
  starting transfers between devices: 1.46 us -> 45.1 us
  local copies, waits for them, and re-layouts: 41.1 us -> 11.6 us
  between operations: 15.1 us -> 1.81 us
    reduce_scatter x6 -> x0, waiting for transfers between devices: 242 us -> none  [the longest x1 70.3 us: local(): lax.psum_scatter(down_part_local, 'dp', scatter_dimension=1, tiled=True)]
    dot_general x38 -> x0, matrix products: 211 us -> none  [the longest x8 39.3 us: masked_scores(): jnp.einsum('qhd,khd->hqk', query_block, keys, preferred_element_type=jnp....]
    pallas_call x0 -> x33, Pallas kernels: none -> 120 us  [run(): pl.pallas_call(body, in_specs=[pl.BlockSpec(memory_space=pltpu.SMEM)] * l...]
    ppermute x0 -> x49, waiting for transfers between devices: none -> 105 us  [swap(): return lax.ppermute(v, axis, [(i, i ^ bit) for i in range(n)])]
    all_gather x4 -> x0, waiting for transfers between devices: 94.2 us -> none  [the longest x1 28.4 us: local(): lax.all_gather(middle.astype(jnp.bfloat16), 'tensor', axis=0, tiled=True)]
    unnamed x14 -> x0, waiting for transfers between devices: 58 us -> none
    ppermute x0 -> x49, starting transfers between devices: none -> 45.1 us  [swap(): return lax.ppermute(v, axis, [(i, i ^ bit) for i in range(n)])]
    psum x1 -> x0, blocking collectives: 39.8 us -> none  [local(): lax.psum((gain_one_grad, bias_one_grad, gain_two_grad, bias_two_grad), ('...]
  transfers between devices with their start and end apart: 12 -> 49, of which waited for: 10 -> 19; matrix products, arithmetic and copies ran while one was open for 23% -> 1% of each run, Pallas kernels for 0% -> 36%
where the time goes in v1:
time: 289 us; the launch traced here: 284 us
  Pallas kernels  120 us (42%)
  waiting for transfers between devices  105 us (36%)
  starting transfers between devices  45.1 us (16%)
  local copies, waits for them, and re-layouts  11.6 us (4%)
    pallas_call x33, Pallas kernels, run(): pl.pallas_call(body, in_specs=[pl.BlockSpec(memory_space=pltpu.SMEM)] * l...  120 us
    ppermute x49, waiting for transfers between devices, swap(): return lax.ppermute(v, axis, [(i, i ^ bit) for i in range(n)])  105 us
    ppermute x49, starting transfers between devices, swap(): return lax.ppermute(v, axis, [(i, i ^ bit) for i in range(n)])  45.1 us
    unnamed x52, local copies, waits for them, and re-layouts  10.8 us
  transfers between devices with their start and end apart: 49, of which 19 were waited for; matrix products, arithmetic and copies ran while one was open for 1% of the time, Pallas kernels for 36%

profile of v1, /device:TPU:0, one launch (start us, length us, event | category | flops | bytes accessed | tf_op | source)
XLA Modules:
  0.0 284.3 jit_solution(3523862489964178976)
XLA Ops:
  3.5 2.5 collective-permute-start.1
  6.0 2.1 copy.50
  8.3 2.2 shard_map.195
  10.7 2.1 shard_map.196
  12.8 12.2 %collective-permute-done.1.refs_1_ = bf16[528,768]{1,0:T(8,128)(2,1)} collective-permute-done((bf16[528,768]{1,0:T(8,128)(2,1)}, bf16[528,768]{1,0:T(8,128)(2,1)}, u32[]{:S(2)}, u32[]{:S(2)}) %collective-permute-start.1) | collective-permute-done | bytes 811040 | tf_op jit(solution)/shard_map/ppermute | solution.py:803
  25.0 1.7 collective-permute-start.3
  26.7 2.1 shard_map.198
  29.2 7.1 %collective-permute-done.3.refs_0_.refs_2_.refs_5_ = bf16[240,768]{1,0:T(8,128)(2,1)S(1)} collective-permute-done((bf16[240,768]{1,0:T(8,128)(2,1)S(1)}, bf16[240,768]{1,0:T(8,128)(2,1)S(1)}, u32[]{:S(2)}, u32[]{:S(2)}) %collective-permute-start.3) | collective-permute-done | bytes 368672 | tf_op jit(solution)/shard_map/ppermute | solution.py:803
  36.4 1.8 collective-permute-start.10
  39.9 1.5 shard_map.199
  41.4 7.1 %shard_map.200 = (bf16[192,512]{1,0:T(8,128)(2,1)S(1)}, bf16[192,512]{1,0:T(8,128)(2,1)S(1)}, bf16[3,128,512]{2,1,0:T(8,128)(2,1)S(1)}, bf16[3,128,512]{2,1,0:T(8,128)(2,1)S(1)}) custom-call(s32[9]{0:T(128)S(1)} %pad_add_fusion.refs_0_, bf16[3,128,512]{2,1,0:T(8,128)(2,1)S(1)} %get-tuple-element.149.refs_1_, ...), custom_call_target="tpu_custom_call" | custom-call | flops 1320000000 | bytes 262144 | tf_op jit(solution)/shard_map/pallas_call | solution.py:46
  48.5 7.6 %shard_map.202 = (bf16[192,512]{1,0:T(8,128)(2,1)S(1)}, bf16[192,512]{1,0:T(8,128)(2,1)S(1)}, bf16[3,128,512]{2,1,0:T(8,128)(2,1)S(1)}, bf16[3,128,512]{2,1,0:T(8,128)(2,1)S(1)}) custom-call(s32[9]{0:T(128)S(1)} %pad_add_fusion.refs_0_, bf16[3,128,512]{2,1,0:T(8,128)(2,1)S(1)} %get-tuple-element.134.refs_1_, ...), custom_call_target="tpu_custom_call" | custom-call | flops 1320000000 | bytes 262144 | tf_op jit(solution)/shard_map/pallas_call | solution.py:46
  56.8 3.1 %shard_map.204 = (bf16[768,2048]{1,0:T(8,128)(2,1)S(1)}, bf16[192,768]{1,0:T(8,128)(2,1)S(1)}) custom-call(s32[8]{0:T(128)S(1)} %add_add_fusion.1.refs_0_.refs_1_, s32[1]{0:T(128)} %bitcast.refs_1_.refs_0_, bf16[240,768]{1,0:T(8,128)(2,1)S(1)} %collective-permute-done.3.refs_0_.refs_2_.refs_5_, bf16[240,768]{1,0:T(8,128)(2,1)S(1)} %collective-permute-done.9.refs_3_.refs_6_, ...), custom_call_target="tpu_custom_call" | custom-call | flops 330000000 | bytes 262144 | tf_op jit(solution)/shard_map/pallas_call | solution.py:46
  62.0 6.2 %collective-permute-done.7.refs_2_.refs_9_ = bf16[192,512]{1,0:T(8,128)(2,1)S(1)} collective-permute-done((bf16[192,512]{1,0:T(8,128)(2,1)S(1)}, bf16[192,512]{1,0:T(8,128)(2,1)S(1)}, u32[]{:S(2)}, u32[]{:S(2)}) %collective-permute-start.7) | collective-permute-done | bytes 196640 | tf_op jit(solution)/shard_map/ppermute | solution.py:803
  68.2 2.5 collective-permute-done.8.refs_3_.refs_10_
  76.1 5.0 %shard_map.207 = (f32[1024,768]{1,0:T(8,128)S(1)}, bf16[1024,768]{1,0:T(8,128)(2,1)S(1)}, bf16[1024,768]{1,0:T(8,128)(2,1)S(1)}, bf16[1024,768]{1,0:T(8,128)(2,1)S(1)}) custom-call(bf16[512,768]{1,0:T(8,128)(2,1)S(1)} %collective-permute-done.16.refs_0_.refs_10_.refs_2_, bf16[512,768]{1,0:T(8,128)(2,1)S(1)} %get-tuple-element.167.refs_1_.refs_9_, ...), custom_call_target="tpu_custom_call" | custom-call | flops 825000000 | bytes 262144 | tf_op jit(solution)/shard_map/pallas_call | solution.py:46
  81.1 6.8 %collective-permute-done.13.refs_2_ = bf16[192,1536]{1,0:T(8,128)(2,1)S(1)} collective-permute-done((bf16[192,1536]{1,0:T(8,128)(2,1)S(1)}, bf16[192,1536]{1,0:T(8,128)(2,1)S(1)}, u32[]{:S(2)}, u32[]{:S(2)}) %collective-permute-start.13) | collective-permute-done | bytes 589856 | tf_op jit(solution)/shard_map/ppermute | solution.py:803
  88.0 2.1 collective-permute-done.14.refs_3_
  90.0 11.8 %collective-permute-done.15.refs_4_ = bf16[192,1536]{1,0:T(8,128)(2,1)S(1)} collective-permute-done((bf16[192,1536]{1,0:T(8,128)(2,1)S(1)}, bf16[192,1536]{1,0:T(8,128)(2,1)S(1)}, u32[]{:S(2)}, u32[]{:S(2)}) %collective-permute-start.15) | collective-permute-done | bytes 589856 | tf_op jit(solution)/shard_map/ppermute | solution.py:803
  101.8 5.3 %shard_map.208 = (f32[512,768]{1,0:T(8,128)S(1)}, bf16[512,768]{1,0:T(8,128)(2,1)S(1)}, bf16[1024,768]{1,0:T(8,128)(2,1)S(1)}, bf16[1024,768]{1,0:T(8,128)(2,1)S(1)}) custom-call(s32[1]{0:T(128)} %bitcast.refs_1_.refs_0_, bf16[192,1536]{1,0:T(8,128)(2,1)S(1)} %get-tuple-element.166.refs_1_, bf16[192,1536]{1,0:T(8,128)(2,1)S(1)} %collective-permute-done.13.refs_2_, ...), custom_call_target="tpu_custom_call" | custom-call | flops 990000000 | bytes 262144 | tf_op jit(solution)/shard_map/pallas_call | solution.py:46
  111.7 3.4 %shard_map.209 = (bf16[512,768]{1,0:T(8,128)(2,1)}, f32[512,768]{1,0:T(8,128)S(1)}, bf16[512,768]{1,0:T(8,128)(2,1)S(1)}, f32[2,768]{1,0:T(2,128)S(1)}) custom-call(bf16[512,768]{1,0:T(8,128)(2,1)S(1)} %collective-permute-done.17.refs_0_, f32[512,768]{1,0:T(8,128)S(1)} %get-tuple-element.171.refs_1_.refs_3_, ...), custom_call_target="tpu_custom_call" | custom-call | flops 495000000 | bytes 262144 | tf_op jit(solution)/shard_map/pallas_call | solution.py:46
  115.2 14.2 %collective-permute-done.18.refs_2_ = bf16[512,768]{1,0:T(8,128)(2,1)S(1)} collective-permute-done((bf16[512,768]{1,0:T(8,128)(2,1)S(1)}, bf16[512,768]{1,0:T(8,128)(2,1)S(1)}, u32[]{:S(2)}, u32[]{:S(2)}) %collective-permute-start.18) | collective-permute-done | bytes 786464 | tf_op jit(solution)/shard_map/ppermute | solution.py:803
  131.7 13.1 %shard_map.211 = (f32[512,768]{1,0:T(8,128)S(1)}, bf16[512,768]{1,0:T(8,128)(2,1)S(1)}, bf16[1024,768]{1,0:T(8,128)(2,1)S(1)}, bf16[1024,768]{1,0:T(8,128)(2,1)S(1)}) custom-call(s32[1]{0:T(128)} %bitcast.refs_1_.refs_0_, bf16[192,1536]{1,0:T(8,128)(2,1)S(1)} %get-tuple-element.166.refs_1_, bf16[192,1536]{1,0:T(8,128)(2,1)S(1)} %collective-permute-done.13.refs_2_, ...), custom_call_target="tpu_custom_call" | custom-call | flops 1815000064 | bytes 262144 | tf_op jit(solution)/shard_map/pallas_call | solution.py:46
  146.1 3.3 %collective-permute-done.22.refs_15_.refs_3_ = bf16[512,768]{1,0:T(8,128)(2,1)S(1)} collective-permute-done((bf16[512,768]{1,0:T(8,128)(2,1)S(1)}, bf16[512,768]{1,0:T(8,128)(2,1)S(1)}, u32[]{:S(2)}, u32[]{:S(2)}) %collective-permute-start.22) | collective-permute-done | bytes 786464 | tf_op jit(solution)/shard_map/ppermute | solution.py:803
  149.9 4.2 %shard_map.213 = (f32[512,768]{1,0:T(8,128)S(1)}, bf16[208,512]{1,0:T(8,128)(2,1)S(1)}, bf16[784,512]{1,0:T(8,128)(2,1)S(1)}, bf16[208,512]{1,0:T(8,128)(2,1)S(1...) custom-call(bf16[512,768]{1,0:T(8,128)(2,1)S(1)} %collective-permute-done.21.refs_0_, ...), custom_call_target="tpu_custom_call" | custom-call | flops 825000000 | bytes 262144 | tf_op jit(solution)/shard_map/pallas_call | solution.py:46
  154.2 1.5 collective-permute-start.24
  156.0 7.5 %shard_map.215 = (bf16[384,768]{1,0:T(8,128)(2,1)S(1)}, bf16[384,768]{1,0:T(8,128)(2,1)S(1)}, bf16[1024,768]{1,0:T(8,128)(2,1)S(1)}, bf16[1024,768]{1,0:T(8,128)(2,1)S(1)}) custom-call(s32[8]{0:T(128)S(1)} %add_add_fusion.refs_0_, bf16[512,768]{1,0:T(8,128)(2,1)S(1)} %get-tuple-element.177.refs_10_.refs_1_, ...), custom_call_target="tpu_custom_call" | custom-call | flops 1320000000 | bytes 262144 | tf_op jit(solution)/shard_map/pallas_call | solution.py:46
  163.6 2.3 collective-permute-done.25.refs_2_.refs_25_
  167.4 6.7 %shard_map.217 = (bf16[384,1536]{1,0:T(8,128)(2,1)S(1)}, bf16[384,1536]{1,0:T(8,128)(2,1)S(1)}) custom-call(s32[8]{0:T(128)S(1)} %add_add_fusion.1.refs_0_.refs_1_, bf16[512,768]{1,0:T(8,128)(2,1)S(1)} %get-tuple-element.167.refs_1_.refs_9_, bf16[512,768]{1,0:T(8,128)(2,1)S(1)} %collective-permute-done.16.refs_0_.refs_10_.refs_2_, ...), custom_call_target="tpu_custom_call" | custom-call | flops 990000000 | bytes 262144 | tf_op jit(solution)/shard_map/pallas_call | solution.py:46
  176.5 13.3 %shard_map.219 = (bf16[192,512]{1,0:T(8,128)(2,1)S(1)}, bf16[672,512]{1,0:T(8,128)(2,1)S(1)}, bf16[192,512]{1,0:T(8,128)(2,1)S(1)}, bf16[768,192]{1,0:T(8,128)(2...) custom-call(s32[9]{0:T(128)S(1)} %pad_add_fusion.refs_0_, s32[8]{0:T(128)S(1)} %add_add_fusion.1.refs_0_.refs_1_, ...), custom_call_target="tpu_custom_call" | custom-call | flops 1980000000 | bytes 262144 | tf_op jit(solution)/shard_map/pallas_call | solution.py:46
  189.8 1.5 collective-permute-start.32
  194.6 8.3 %collective-permute-done.31.refs_0_.refs_1_ = bf16[384,1536]{1,0:T(8,128)(2,1)S(1)} collective-permute-done((bf16[384,1536]{1,0:T(8,128)(2,1)S(1)}, bf16[384,1536]{1,0:T(8,128)(2,1)S(1)}, u32[]{:S(2)}, u32[]{:S(2)}) %collective-permute-start.31) | collective-permute-done | bytes 1179680 | tf_op jit(solution)/shard_map/ppermute | solution.py:803
  203.1 1.6 collective-permute-start.35
  204.7 13.1 %shard_map.221 = (bf16[192,512]{1,0:T(8,128)(2,1)S(1)}, bf16[384,512]{1,0:T(8,128)(2,1)S(1)}, bf16[384,512]{1,0:T(8,128)(2,1)S(1)}, bf16[384,384]{1,0:T(8,128)(2...) custom-call(s32[9]{0:T(128)S(1)} %pad_add_fusion.refs_0_, s32[8]{0:T(128)S(1)} %add_add_fusion.1.refs_0_.refs_1_, ...), custom_call_target="tpu_custom_call" | custom-call | flops 1980000000 | bytes 262144 | tf_op jit(solution)/shard_map/pallas_call | solution.py:46
  217.8 2.5 collective-permute-start.33
  220.4 1.5 collective-permute-start.36
  222.9 4.3 %collective-permute-done.30.refs_32_.refs_6_ = bf16[672,512]{1,0:T(8,128)(2,1)S(1)} collective-permute-done((bf16[672,512]{1,0:T(8,128)(2,1)S(1)}, bf16[672,512]{1,0:T(8,128)(2,1)S(1)}, u32[]{:S(2)}, u32[]{:S(2)}) %collective-permute-start.30) | collective-permute-done | bytes 688160 | tf_op jit(solution)/shard_map/ppermute | solution.py:803
  227.2 13.3 %shard_map.223 = (bf16[192,512]{1,0:T(8,128)(2,1)S(1)}, bf16[192,512]{1,0:T(8,128)(2,1)S(1)}, bf16[768,512]{1,0:T(8,128)(2,1)S(1)}, bf16[384,384]{1,0:T(8,128)(2...) custom-call(s32[9]{0:T(128)S(1)} %pad_add_fusion.refs_0_, ...), custom_call_target="tpu_custom_call" | custom-call | flops 1980000000 | bytes 262144 | tf_op jit(solution)/shard_map/pallas_call | solution.py:46
  243.4 4.1 %collective-permute-done.43.refs_3_ = bf16[384,384]{1,0:T(8,128)(2,1)S(1)} collective-permute-done((bf16[384,384]{1,0:T(8,128)(2,1)S(1)}, bf16[384,384]{1,0:T(8,128)(2,1)S(1)}, u32[]{:S(2)}, u32[]{:S(2)}) %collective-permute-start.43) | collective-permute-done | bytes 294944 | tf_op jit(solution)/shard_map/ppermute | solution.py:803
  247.7 1.6 collective-permute-start.40
  249.3 4.2 %collective-permute-done.40.refs_8_ = bf16[192,512]{1,0:T(8,128)(2,1)S(1)} collective-permute-done((bf16[192,512]{1,0:T(8,128)(2,1)S(1)}, bf16[192,512]{1,0:T(8,128)(2,1)S(1)}, u32[]{:S(2)}, u32[]{:S(2)}) %collective-permute-start.40) | collective-permute-done | bytes 196640 | tf_op jit(solution)/shard_map/ppermute | solution.py:803
  253.5 3.1 %collective-permute-start.46 = (bf16[96,1536]{1,0:T(8,128)(2,1)S(1)}, bf16[96,1536]{1,0:T(8,128)(2,1)S(1)}, u32[]{:S(2)}, u32[]{:S(2)}) collective-permute-start(bf16[96,1536]{1,0:T(8,128)(2,1)S(1)} %add_convert_fusion.1), channel_id=1, source_target_pairs={{0,16},{4,20},{8,24},{12,28},{16,0},{20,4},{24,8},{28,12},{1,17},{... | collective-permute-start | bytes 884744 | tf_op jit(solution)/shard_map/ppermute | solution.py:803
  256.6 7.1 %collective-permute-done.41.refs_9_ = bf16[192,512]{1,0:T(8,128)(2,1)S(1)} collective-permute-done((bf16[192,512]{1,0:T(8,128)(2,1)S(1)}, bf16[192,512]{1,0:T(8,128)(2,1)S(1)}, u32[]{:S(2)}, u32[]{:S(2)}) %collective-permute-start.41) | collective-permute-done | bytes 196640 | tf_op jit(solution)/shard_map/ppermute | solution.py:803
  263.7 3.0 %collective-permute-start.47 = (bf16[96,768]{1,0:T(8,128)(2,1)S(1)}, bf16[96,768]{1,0:T(8,128)(2,1)S(1)}, u32[]{:S(2)}, u32[]{:S(2)}) collective-permute-start(bf16[96,768]{1,0:T(8,128)(2,1)S(1)} %add_convert_fusion.3), channel_id=1, source_target_pairs={{0,16},{4,20},{8,24},{12,28},{16,0},{20,4},{24,8},{28,12},{1,17},{... | collective-permute-start | bytes 442376 | tf_op jit(solution)/shard_map/ppermute | solution.py:803
  267.4 3.8 %shard_map.225.refs_8_ = f32[512,768]{1,0:T(8,128)} custom-call(f32[512,768]{1,0:T(8,128)S(1)} %get-tuple-element.188.refs_0_, bf16[192,512]{1,0:T(8,128)(2,1)S(1)} %get-tuple-element.218.refs_1_, bf16[192,512]{1,0:T(8,128)(2,1)S(1)} %get-tuple-element.226.refs_2_, bf16[192,512]{1,0:T(8,128)(2,1)S(1)} %get-tuple-element.237.refs_3_, ...), custom_call_target="tpu_custom_call" | custom-call | flops 660000000 | bytes 262144 | tf_op jit(solution)/shard_map/pallas_call | solution.py:46
  271.2 6.4 %collective-permute-done.47.refs_7_ = bf16[96,768]{1,0:T(8,128)(2,1)S(1)} collective-permute-done((bf16[96,768]{1,0:T(8,128)(2,1)S(1)}, bf16[96,768]{1,0:T(8,128)(2,1)S(1)}, u32[]{:S(2)}, u32[]{:S(2)}) %collective-permute-start.47) | collective-permute-done | bytes 147488 | tf_op jit(solution)/shard_map/ppermute | solution.py:803
  279.0 2.2 shard_map.226
  282.2 1.7 shard_map.227
  (164 shorter events, 36.8 us)
Async XLA Ops:
  3.0 7.7 %collective-permute-start = (bf16[528,768]{1,0:T(8,128)(2,1)}, bf16[528,768]{1,0:T(8,128)(2,1)}, u32[]{:S(2)}, u32[]{:S(2)}) collective-permute-start(bf16[528,768]{1,0:T(8,128)(2,1)} %fusion.1.refs_2_.refs_6_), channel_id=1, source_target_pairs={{0,1},{1,0},{2,3},{3,2},{4,5},{5,4},{6,7},{7,6},{8,9},{9,8},{10,11... | collective-permute-start | bytes 2433032 | tf_op jit(solution)/shard_map/ppermute | solution.py:803
  3.5 21.5 %collective-permute-start.1 = (bf16[528,768]{1,0:T(8,128)(2,1)}, bf16[528,768]{1,0:T(8,128)(2,1)}, u32[]{:S(2)}, u32[]{:S(2)}) collective-permute-start(bf16[528,768]{1,0:T(8,128)(2,1)} %fusion.1.refs_2_.refs_6_), channel_id=1, source_target_pairs={{0,2},{1,3},{2,0},{3,1},{4,6},{5,7},{6,4},{7,5},{8,10},{9,11},{10,... | collective-permute-start | bytes 2433032 | tf_op jit(solution)/shard_map/ppermute | solution.py:803
  25.0 14.6 %collective-permute-start.2 = (bf16[528,768]{1,0:T(8,128)(2,1)}, bf16[528,768]{1,0:T(8,128)(2,1)S(1)}, u32[]{:S(2)}, u32[]{:S(2)}) collective-permute-start(bf16[528,768]{1,0:T(8,128)(2,1)} %get-tuple-element.140.refs_2_.refs_8_), channel_id=1, source_target_pairs={{0,1},{1,0},{2,3},{3,2},{4,5},{5,4},{6,7},{7,6},{8,9},{9,8},{10,11... | collective-permute-start | bytes 2433032 | tf_op jit(solution)/shard_map/ppermute | solution.py:803
  25.0 11.4 %collective-permute-start.3 = (bf16[240,768]{1,0:T(8,128)(2,1)S(1)}, bf16[240,768]{1,0:T(8,128)(2,1)S(1)}, u32[]{:S(2)}, u32[]{:S(2)}) collective-permute-start(bf16[240,768]{1,0:T(8,128)(2,1)S(1)} %pad_maximum_fusion.refs_4_), channel_id=1, source_target_pairs={{0,2},{1,3},{2,0},{3,1},{4,6},{5,7},{6,4},{7,5},{8,10},{9,11},{10,... | collective-permute-start | bytes 1105928 | tf_op jit(solution)/shard_map/ppermute | solution.py:803
  28.9 27.2 %collective-permute-start.5 = (bf16[192,1536]{1,0:T(8,128)(2,1)S(1)}, bf16[192,1536]{1,0:T(8,128)(2,1)S(1)}, u32[]{:S(2)}, u32[]{:S(2)}) collective-permute-start(bf16[192,1536]{1,0:T(8,128)(2,1)S(1)} %get-tuple-element.157), channel_id=1, source_target_pairs={{0,2},{1,3},{2,0},{3,1},{4,6},{5,7},{6,4},{7,5},{8,10},{9,11},{10,... | collective-permute-start | bytes 1769480 | tf_op jit(solution)/shard_map/ppermute | solution.py:803
  29.2 12.2 %collective-permute-start.4 = (bf16[192,768]{1,0:T(8,128)(2,1)S(1)}, bf16[192,768]{1,0:T(8,128)(2,1)S(1)}, u32[]{:S(2)}, u32[]{:S(2)}) collective-permute-start(bf16[192,768]{1,0:T(8,128)(2,1)S(1)} %copy-done.14), channel_id=1, source_target_pairs={{0,1},{1,0},{2,3},{3,2},{4,5},{5,4},{6,7},{7,6},{8,9},{9,8},{10,11... | collective-permute-start | bytes 884744 | tf_op jit(solution)/shard_map/ppermute | solution.py:803
  36.4 19.7 %collective-permute-start.10 = (bf16[240,768]{1,0:T(8,128)(2,1)S(1)}, bf16[240,768]{1,0:T(8,128)(2,1)S(1)}, u32[]{:S(2)}, u32[]{:S(2)}) collective-permute-start(bf16[240,768]{1,0:T(8,128)(2,1)S(1)} %collective-permute-done.3.refs_0_.refs_2_.refs_5_), channel_id=1, source_target_pairs={{0,8},{4,12},{8,0},{12,4},{16,24},{20,28},{24,16},{28,20},{1,9},{5... | collective-permute-start | bytes 1105928 | tf_op jit(solution)/shard_map/ppermute | solution.py:803
  38.2 17.9 %collective-permute-start.11 = (bf16[240,768]{1,0:T(8,128)(2,1)S(1)}, bf16[240,768]{1,0:T(8,128)(2,1)S(1)}, u32[]{:S(2)}, u32[]{:S(2)}) collective-permute-start(bf16[240,768]{1,0:T(8,128)(2,1)S(1)} %collective-permute-done.3.refs_0_.refs_2_.refs_5_), channel_id=1, source_target_pairs={{0,12},{4,8},{8,4},{12,0},{16,28},{20,24},{24,20},{28,16},{1,13},{... | collective-permute-start | bytes 1105928 | tf_op jit(solution)/shard_map/ppermute | solution.py:803
  39.6 17.2 %collective-permute-start.9 = (bf16[240,768]{1,0:T(8,128)(2,1)S(1)}, bf16[240,768]{1,0:T(8,128)(2,1)S(1)}, u32[]{:S(2)}, u32[]{:S(2)}) collective-permute-start(bf16[240,768]{1,0:T(8,128)(2,1)S(1)} %collective-permute-done.3.refs_0_.refs_2_.refs_5_), channel_id=1, source_target_pairs={{0,4},{4,0},{8,12},{12,8},{16,20},{20,16},{24,28},{28,24},{1,5},{5... | collective-permute-start | bytes 1105928 | tf_op jit(solution)/shard_map/ppermute | solution.py:803
  59.9 10.8 %collective-permute-start.12 = (bf16[192,768]{1,0:T(8,128)(2,1)S(1)}, bf16[192,768]{1,0:T(8,128)(2,1)S(1)}, u32[]{:S(2)}, u32[]{:S(2)}) collective-permute-start(bf16[192,768]{1,0:T(8,128)(2,1)S(1)} %get-tuple-element.162.refs_6_.refs_11_.refs_13_), channel_id=1, source_target_pairs={{0,1},{1,0},{2,3},{3,2},{4,5},{5,4},{6,7},{7,6},{8,9},{9,8},{10,11... | collective-permute-start | bytes 884744 | tf_op jit(solution)/shard_map/ppermute | solution.py:803
  60.5 7.8 %collective-permute-start.7 = (bf16[192,512]{1,0:T(8,128)(2,1)S(1)}, bf16[192,512]{1,0:T(8,128)(2,1)S(1)}, u32[]{:S(2)}, u32[]{:S(2)}) collective-permute-start(bf16[192,512]{1,0:T(8,128)(2,1)S(1)} %get-tuple-element.159.refs_20_), channel_id=1, source_target_pairs={{0,2},{1,3},{2,0},{3,1},{4,6},{5,7},{6,4},{7,5},{8,10},{9,11},{10,... | collective-permute-start | bytes 589832 | tf_op jit(solution)/shard_map/ppermute | solution.py:803
  62.0 8.7 %collective-permute-start.8 = (bf16[192,512]{1,0:T(8,128)(2,1)S(1)}, bf16[192,512]{1,0:T(8,128)(2,1)S(1)}, u32[]{:S(2)}, u32[]{:S(2)}) collective-permute-start(bf16[192,512]{1,0:T(8,128)(2,1)S(1)} %get-tuple-element.160.refs_21_), channel_id=1, source_target_pairs={{0,3},{1,2},{2,1},{3,0},{4,7},{5,6},{6,5},{7,4},{8,11},{9,10},{10,... | collective-permute-start | bytes 589832 | tf_op jit(solution)/shard_map/ppermute | solution.py:803
  71.9 4.3 %collective-permute-start.16 = (bf16[512,768]{1,0:T(8,128)(2,1)S(1)}, bf16[512,768]{1,0:T(8,128)(2,1)S(1)}, u32[]{:S(2)}, u32[]{:S(2)}) collective-permute-start(bf16[512,768]{1,0:T(8,128)(2,1)S(1)} %get-tuple-element.167.refs_1_.refs_9_), channel_id=1, source_target_pairs={{0,1},{1,0},{2,3},{3,2},{4,5},{5,4},{6,7},{7,6},{8,9},{9,8},{10,11... | collective-permute-start | bytes 2359304 | tf_op jit(solution)/shard_map/ppermute | solution.py:803
  72.7 15.3 %collective-permute-start.13 = (bf16[192,1536]{1,0:T(8,128)(2,1)S(1)}, bf16[192,1536]{1,0:T(8,128)(2,1)S(1)}, u32[]{:S(2)}, u32[]{:S(2)}) collective-permute-start(bf16[192,1536]{1,0:T(8,128)(2,1)S(1)} %get-tuple-element.166.refs_1_), channel_id=1, source_target_pairs={{0,4},{4,0},{8,12},{12,8},{16,20},{20,16},{24,28},{28,24},{1,5},{5... | collective-permute-start | bytes 1769480 | tf_op jit(solution)/shard_map/ppermute | solution.py:803
  73.8 16.2 %collective-permute-start.14 = (bf16[192,1536]{1,0:T(8,128)(2,1)S(1)}, bf16[192,1536]{1,0:T(8,128)(2,1)S(1)}, u32[]{:S(2)}, u32[]{:S(2)}) collective-permute-start(bf16[192,1536]{1,0:T(8,128)(2,1)S(1)} %get-tuple-element.166.refs_1_), channel_id=1, source_target_pairs={{0,8},{4,12},{8,0},{12,4},{16,24},{20,28},{24,16},{28,20},{1,9},{5... | collective-permute-start | bytes 1769480 | tf_op jit(solution)/shard_map/ppermute | solution.py:803
  75.0 26.8 %collective-permute-start.15 = (bf16[192,1536]{1,0:T(8,128)(2,1)S(1)}, bf16[192,1536]{1,0:T(8,128)(2,1)S(1)}, u32[]{:S(2)}, u32[]{:S(2)}) collective-permute-start(bf16[192,1536]{1,0:T(8,128)(2,1)S(1)} %get-tuple-element.166.refs_1_), channel_id=1, source_target_pairs={{0,12},{4,8},{8,4},{12,0},{16,28},{20,24},{24,20},{28,16},{1,13},{... | collective-permute-start | bytes 1769480 | tf_op jit(solution)/shard_map/ppermute | solution.py:803
  109.4 2.3 collective-permute-start.17
  109.4 20.0 %collective-permute-start.18 = (bf16[512,768]{1,0:T(8,128)(2,1)S(1)}, bf16[512,768]{1,0:T(8,128)(2,1)S(1)}, u32[]{:S(2)}, u32[]{:S(2)}) collective-permute-start(bf16[512,768]{1,0:T(8,128)(2,1)S(1)} %get-tuple-element.167.refs_1_.refs_9_), channel_id=1, source_target_pairs={{0,2},{1,3},{2,0},{3,1},{4,6},{5,7},{6,4},{7,5},{8,10},{9,11},{10,... | collective-permute-start | bytes 2359304 | tf_op jit(solution)/shard_map/ppermute | solution.py:803
  129.4 2.3 collective-permute-start.20
  129.4 15.4 %collective-permute-start.19 = (bf16[512,768]{1,0:T(8,128)(2,1)S(1)}, bf16[512,768]{1,0:T(8,128)(2,1)S(1)}, u32[]{:S(2)}, u32[]{:S(2)}) collective-permute-start(bf16[512,768]{1,0:T(8,128)(2,1)S(1)} %get-tuple-element.176.refs_5_.refs_3_), channel_id=1, source_target_pairs={{0,1},{1,0},{2,3},{3,2},{4,5},{5,4},{6,7},{7,6},{8,9},{9,8},{10,11... | collective-permute-start | bytes 2359304 | tf_op jit(solution)/shard_map/ppermute | solution.py:803
  129.9 19.4 %collective-permute-start.22 = (bf16[512,768]{1,0:T(8,128)(2,1)S(1)}, bf16[512,768]{1,0:T(8,128)(2,1)S(1)}, u32[]{:S(2)}, u32[]{:S(2)}) collective-permute-start(bf16[512,768]{1,0:T(8,128)(2,1)S(1)} %get-tuple-element.177.refs_10_.refs_1_), channel_id=1, source_target_pairs={{0,2},{1,3},{2,0},{3,1},{4,6},{5,7},{6,4},{7,5},{8,10},{9,11},{10,... | collective-permute-start | bytes 2359304 | tf_op jit(solution)/shard_map/ppermute | solution.py:803
  146.0 3.9 %collective-permute-start.21 = (bf16[512,768]{1,0:T(8,128)(2,1)S(1)}, bf16[512,768]{1,0:T(8,128)(2,1)S(1)}, u32[]{:S(2)}, u32[]{:S(2)}) collective-permute-start(bf16[512,768]{1,0:T(8,128)(2,1)S(1)} %get-tuple-element.185), channel_id=1, source_target_pairs={{0,1},{1,0},{2,3},{3,2},{4,5},{5,4},{6,7},{7,6},{8,9},{9,8},{10,11... | collective-permute-start | bytes 2359304 | tf_op jit(solution)/shard_map/ppermute | solution.py:803
  149.3 6.7 %collective-permute-start.27 = (bf16[512,768]{1,0:T(8,128)(2,1)S(1)}, bf16[512,768]{1,0:T(8,128)(2,1)S(1)}, u32[]{:S(2)}, u32[]{:S(2)}) collective-permute-start(bf16[512,768]{1,0:T(8,128)(2,1)S(1)} %collective-permute-done.22.refs_15_.refs_3_), channel_id=1, source_target_pairs={{0,1},{1,0},{2,3},{3,2},{4,5},{5,4},{6,7},{7,6},{8,9},{9,8},{10,11... | collective-permute-start | bytes 2359304 | tf_op jit(solution)/shard_map/ppermute | solution.py:803
  149.4 14.2 %collective-permute-start.26 = (bf16[576,768]{1,0:T(8,128)(2,1)S(1)}, bf16[576,768]{1,0:T(8,128)(2,1)S(1)}, u32[]{:S(2)}, u32[]{:S(2)}) collective-permute-start(bf16[576,768]{1,0:T(8,128)(2,1)S(1)} %bitcast.14), channel_id=1, source_target_pairs={{0,1},{1,0},{2,3},{3,2},{4,5},{5,4},{6,7},{7,6},{8,9},{9,8},{10,11... | collective-permute-start | bytes 2654216 | tf_op jit(solution)/shard_map/ppermute | solution.py:803
  154.1 11.9 %collective-permute-start.23 = (bf16[784,512]{1,0:T(8,128)(2,1)S(1)}, bf16[784,512]{1,0:T(8,128)(2,1)S(1)}, u32[]{:S(2)}, u32[]{:S(2)}) collective-permute-start(bf16[784,512]{1,0:T(8,128)(2,1)S(1)} %get-tuple-element.201), channel_id=1, source_target_pairs={{0,1},{1,0},{2,3},{3,2},{4,5},{5,4},{6,7},{7,6},{8,9},{9,8},{10,11... | collective-permute-start | bytes 2408456 | tf_op jit(solution)/shard_map/ppermute | solution.py:803
  154.2 9.4 %collective-permute-start.24 = (bf16[208,512]{1,0:T(8,128)(2,1)S(1)}, bf16[208,512]{1,0:T(8,128)(2,1)S(1)}, u32[]{:S(2)}, u32[]{:S(2)}) collective-permute-start(bf16[208,512]{1,0:T(8,128)(2,1)S(1)} %get-tuple-element.202), channel_id=1, source_target_pairs={{0,2},{1,3},{2,0},{3,1},{4,6},{5,7},{6,4},{7,5},{8,10},{9,11},{10,... | collective-permute-start | bytes 638984 | tf_op jit(solution)/shard_map/ppermute | solution.py:803
  155.7 10.2 %collective-permute-start.25 = (bf16[208,512]{1,0:T(8,128)(2,1)S(1)}, bf16[208,512]{1,0:T(8,128)(2,1)S(1)}, u32[]{:S(2)}, u32[]{:S(2)}) collective-permute-start(bf16[208,512]{1,0:T(8,128)(2,1)S(1)} %get-tuple-element.203), channel_id=1, source_target_pairs={{0,3},{1,2},{2,1},{3,0},{4,7},{5,6},{6,5},{7,4},{8,11},{9,10},{10,... | collective-permute-start | bytes 638984 | tf_op jit(solution)/shard_map/ppermute | solution.py:803
  174.1 28.9 %collective-permute-start.31 = (bf16[384,1536]{1,0:T(8,128)(2,1)S(1)}, bf16[384,1536]{1,0:T(8,128)(2,1)S(1)}, u32[]{:S(2)}, u32[]{:S(2)}) collective-permute-start(bf16[384,1536]{1,0:T(8,128)(2,1)S(1)} %get-tuple-element.230), channel_id=1, source_target_pairs={{0,4},{4,0},{8,12},{12,8},{16,20},{20,16},{24,28},{28,24},{1,5},{5... | collective-permute-start | bytes 3538952 | tf_op jit(solution)/shard_map/ppermute | solution.py:803
  175.3 16.1 %collective-permute-start.28 = (bf16[384,768]{1,0:T(8,128)(2,1)S(1)}, bf16[384,768]{1,0:T(8,128)(2,1)S(1)}, u32[]{:S(2)}, u32[]{:S(2)}) collective-permute-start(bf16[384,768]{1,0:T(8,128)(2,1)S(1)} %get-tuple-element.221), channel_id=1, source_target_pairs={{0,8},{4,12},{8,0},{12,4},{16,24},{20,28},{24,16},{28,20},{1,9},{5... | collective-permute-start | bytes 1769480 | tf_op jit(solution)/shard_map/ppermute | solution.py:803
  189.8 28.0 %collective-permute-start.32 = (bf16[576,768]{1,0:T(8,128)(2,1)S(1)}, bf16[576,768]{1,0:T(8,128)(2,1)S(1)}, u32[]{:S(2)}, u32[]{:S(2)}) collective-permute-start(bf16[576,768]{1,0:T(8,128)(2,1)S(1)} %get-tuple-element.231.refs_10_), channel_id=1, source_target_pairs={{0,2},{1,3},{2,0},{3,1},{4,6},{5,7},{6,4},{7,5},{8,10},{9,11},{10,... | collective-permute-start | bytes 2654216 | tf_op jit(solution)/shard_map/ppermute | solution.py:803
  191.4 30.4 %collective-permute-start.37 = (bf16[192,768]{1,0:T(8,128)(2,1)S(1)}, bf16[192,768]{1,0:T(8,128)(2,1)S(1)}, u32[]{:S(2)}, u32[]{:S(2)}) collective-permute-start(bf16[192,768]{1,0:T(8,128)(2,1)S(1)} %add_convert_fusion.2), channel_id=1, source_target_pairs={{0,4},{4,0},{8,12},{12,8},{16,20},{20,16},{24,28},{28,24},{1,5},{5... | collective-permute-start | bytes 884744 | tf_op jit(solution)/shard_map/ppermute | solution.py:803
  192.8 12.0 %collective-permute-start.29 = (f32[4,768]{1,0:T(4,128)S(1)}, f32[4,768]{1,0:T(4,128)S(1)}, u32[]{:S(2)}, u32[]{:S(2)}) collective-permute-start(f32[4,768]{1,0:T(4,128)S(1)} %get-tuple-element.224.refs_33_), channel_id=1, source_target_pairs={{0,8},{4,12},{8,0},{12,4},{16,24},{20,28},{24,16},{28,20},{1,9},{5... | collective-permute-start | bytes 36872 | tf_op jit(solution)/shard_map/ppermute | solution.py:803
  193.1 34.1 %collective-permute-start.30 = (bf16[672,512]{1,0:T(8,128)(2,1)S(1)}, bf16[672,512]{1,0:T(8,128)(2,1)S(1)}, u32[]{:S(2)}, u32[]{:S(2)}) collective-permute-start(bf16[672,512]{1,0:T(8,128)(2,1)S(1)} %get-tuple-element.228), channel_id=1, source_target_pairs={{0,2},{1,3},{2,0},{3,1},{4,6},{5,7},{6,4},{7,5},{8,10},{9,11},{10,... | collective-permute-start | bytes 2064392 | tf_op jit(solution)/shard_map/ppermute | solution.py:803
  203.1 37.4 %collective-permute-start.35 = (bf16[192,1536]{1,0:T(8,128)(2,1)S(1)}, bf16[192,1536]{1,0:T(8,128)(2,1)S(1)}, u32[]{:S(2)}, u32[]{:S(2)}) collective-permute-start(bf16[192,1536]{1,0:T(8,128)(2,1)S(1)} %add_convert_fusion), channel_id=1, source_target_pairs={{0,8},{4,12},{8,0},{12,4},{16,24},{20,28},{24,16},{28,20},{1,9},{5... | collective-permute-start | bytes 1769480 | tf_op jit(solution)/shard_map/ppermute | solution.py:803
  217.8 5.0 %collective-permute-start.33 = (f32[4,768]{1,0:T(4,128)S(1)}, f32[4,768]{1,0:T(4,128)S(1)}, u32[]{:S(2)}, u32[]{:S(2)}) collective-permute-start(f32[4,768]{1,0:T(4,128)S(1)} %get-tuple-element.235.refs_34_), channel_id=1, source_target_pairs={{0,16},{4,20},{8,24},{12,28},{16,0},{20,4},{24,8},{28,12},{1,17},{... | collective-permute-start | bytes 36872 | tf_op jit(solution)/shard_map/ppermute | solution.py:803
  220.4 20.1 %collective-permute-start.36 = (bf16[384,512]{1,0:T(8,128)(2,1)S(1)}, bf16[384,512]{1,0:T(8,128)(2,1)S(1)}, u32[]{:S(2)}, u32[]{:S(2)}) collective-permute-start(bf16[384,512]{1,0:T(8,128)(2,1)S(1)} %get-tuple-element.239), channel_id=1, source_target_pairs={{0,2},{1,3},{2,0},{3,1},{4,6},{5,7},{6,4},{7,5},{8,10},{9,11},{10,... | collective-permute-start | bytes 1179656 | tf_op jit(solution)/shard_map/ppermute | solution.py:803
  221.9 18.6 %collective-permute-start.34 = (bf16[384,384]{1,0:T(8,128)(2,1)S(1)}, bf16[384,384]{1,0:T(8,128)(2,1)S(1)}, u32[]{:S(2)}, u32[]{:S(2)}) collective-permute-start(bf16[384,384]{1,0:T(8,128)(2,1)S(1)} %get-tuple-element.238), channel_id=1, source_target_pairs={{0,4},{4,0},{8,12},{12,8},{16,20},{20,16},{24,28},{28,24},{1,5},{5... | collective-permute-start | bytes 884744 | tf_op jit(solution)/shard_map/ppermute | solution.py:803
  240.5 6.9 %collective-permute-start.43 = (bf16[384,384]{1,0:T(8,128)(2,1)S(1)}, bf16[384,384]{1,0:T(8,128)(2,1)S(1)}, u32[]{:S(2)}, u32[]{:S(2)}) collective-permute-start(bf16[384,384]{1,0:T(8,128)(2,1)S(1)} %get-tuple-element.252), channel_id=1, source_target_pairs={{0,4},{4,0},{8,12},{12,8},{16,20},{20,16},{24,28},{28,24},{1,5},{5... | collective-permute-start | bytes 884744 | tf_op jit(solution)/shard_map/ppermute | solution.py:803
  241.9 24.8 %collective-permute-start.39 = (bf16[384,512]{1,0:T(8,128)(2,1)S(1)}, bf16[384,512]{1,0:T(8,128)(2,1)S(1)}, u32[]{:S(2)}, u32[]{:S(2)}) collective-permute-start(bf16[384,512]{1,0:T(8,128)(2,1)S(1)} %collective-permute-done.36.refs_2_.refs_7_), channel_id=1, source_target_pairs={{0,1},{1,0},{2,3},{3,2},{4,5},{5,4},{6,7},{7,6},{8,9},{9,8},{10,11... | collective-permute-start | bytes 1179656 | tf_op jit(solution)/shard_map/ppermute | solution.py:803
  242.0 5.8 %collective-permute-start.48 = (f32[4,768]{1,0:T(4,128)S(1)}, f32[4,768]{1,0:T(4,128)S(1)}, u32[]{:S(2)}, u32[]{:S(2)}) collective-permute-start(f32[4,768]{1,0:T(4,128)S(1)} %get-tuple-element.257), channel_id=1, source_target_pairs={{0,4},{4,0},{8,12},{12,8},{16,20},{20,16},{24,28},{28,24},{1,5},{5... | collective-permute-start | bytes 36872 | tf_op jit(solution)/shard_map/ppermute | solution.py:803
  242.8 24.5 %collective-permute-start.42 = (bf16[576,768]{1,0:T(8,128)(2,1)S(1)}, bf16[576,768]{1,0:T(8,128)(2,1)S(1)}, u32[]{:S(2)}, u32[]{:S(2)}) collective-permute-start(bf16[576,768]{1,0:T(8,128)(2,1)S(1)} %get-tuple-element.248.refs_12_), channel_id=1, source_target_pairs={{0,1},{1,0},{2,3},{3,2},{4,5},{5,4},{6,7},{7,6},{8,9},{9,8},{10,11... | collective-permute-start | bytes 2654216 | tf_op jit(solution)/shard_map/ppermute | solution.py:803
  243.0 24.3 %collective-permute-start.38 = (bf16[768,512]{1,0:T(8,128)(2,1)S(1)}, bf16[768,512]{1,0:T(8,128)(2,1)S(1)}, u32[]{:S(2)}, u32[]{:S(2)}) collective-permute-start(bf16[768,512]{1,0:T(8,128)(2,1)S(1)} %get-tuple-element.245), channel_id=1, source_target_pairs={{0,1},{1,0},{2,3},{3,2},{4,5},{5,4},{6,7},{7,6},{8,9},{9,8},{10,11... | collective-permute-start | bytes 2359304 | tf_op jit(solution)/shard_map/ppermute | solution.py:803
  247.5 9.0 %collective-permute-start.44 = (bf16[192,768]{1,0:T(8,128)(2,1)S(1)}, bf16[192,768]{1,0:T(8,128)(2,1)S(1)}, u32[]{:S(2)}, u32[]{:S(2)}) collective-permute-start(bf16[192,768]{1,0:T(8,128)(2,1)S(1)} %pad_maximum_fusion.1), channel_id=1, source_target_pairs={{0,8},{4,12},{8,0},{12,4},{16,24},{20,28},{24,16},{28,20},{1,9},{5... | collective-permute-start | bytes 884744 | tf_op jit(solution)/shard_map/ppermute | solution.py:803
  247.7 5.7 %collective-permute-start.40 = (bf16[192,512]{1,0:T(8,128)(2,1)S(1)}, bf16[192,512]{1,0:T(8,128)(2,1)S(1)}, u32[]{:S(2)}, u32[]{:S(2)}) collective-permute-start(bf16[192,512]{1,0:T(8,128)(2,1)S(1)} %get-tuple-element.246), channel_id=1, source_target_pairs={{0,2},{1,3},{2,0},{3,1},{4,6},{5,7},{6,4},{7,5},{8,10},{9,11},{10,... | collective-permute-start | bytes 589832 | tf_op jit(solution)/shard_map/ppermute | solution.py:803
  253.5 24.1 %collective-permute-start.46 = (bf16[96,1536]{1,0:T(8,128)(2,1)S(1)}, bf16[96,1536]{1,0:T(8,128)(2,1)S(1)}, u32[]{:S(2)}, u32[]{:S(2)}) collective-permute-start(bf16[96,1536]{1,0:T(8,128)(2,1)S(1)} %add_convert_fusion.1), channel_id=1, source_target_pairs={{0,16},{4,20},{8,24},{12,28},{16,0},{20,4},{24,8},{28,12},{1,17},{... | collective-permute-start | bytes 884744 | tf_op jit(solution)/shard_map/ppermute | solution.py:803
  256.5 7.1 %collective-permute-start.41 = (bf16[192,512]{1,0:T(8,128)(2,1)S(1)}, bf16[192,512]{1,0:T(8,128)(2,1)S(1)}, u32[]{:S(2)}, u32[]{:S(2)}) collective-permute-start(bf16[192,512]{1,0:T(8,128)(2,1)S(1)} %get-tuple-element.247), channel_id=1, source_target_pairs={{0,3},{1,2},{2,1},{3,0},{4,7},{5,6},{6,5},{7,4},{8,11},{9,10},{10,... | collective-permute-start | bytes 589832 | tf_op jit(solution)/shard_map/ppermute | solution.py:803
  263.7 13.9 %collective-permute-start.47 = (bf16[96,768]{1,0:T(8,128)(2,1)S(1)}, bf16[96,768]{1,0:T(8,128)(2,1)S(1)}, u32[]{:S(2)}, u32[]{:S(2)}) collective-permute-start(bf16[96,768]{1,0:T(8,128)(2,1)S(1)} %add_convert_fusion.3), channel_id=1, source_target_pairs={{0,16},{4,20},{8,24},{12,28},{16,0},{20,4},{24,8},{28,12},{1,17},{... | collective-permute-start | bytes 442376 | tf_op jit(solution)/shard_map/ppermute | solution.py:803
  266.7 14.5 %collective-permute-start.45 = (bf16[96,768]{1,0:T(8,128)(2,1)S(1)}, bf16[96,768]{1,0:T(8,128)(2,1)S(1)}, u32[]{:S(2)}, u32[]{:S(2)}) collective-permute-start(bf16[96,768]{1,0:T(8,128)(2,1)S(1)} %fusion.2), channel_id=1, source_target_pairs={{0,16},{4,20},{8,24},{12,28},{16,0},{20,4},{24,8},{28,12},{1,17},{... | collective-permute-start | bytes 442376 | tf_op jit(solution)/shard_map/ppermute | solution.py:803
  (24 other events, 199.7 us)

commit v2 on v1

--- a/solution.py
+++ b/solution.py
@@ -32,7 +32,7 @@
 ORDER = Order()
 
 
-def run(kernel, us, mib, scalars, args, outs, scratch=(), awaits=(), carry=(), apart=()):
+def run(kernel, us, mib, scalars, args, outs, scratch=(), awaits=(), carry=(), apart=(), hbm=()):
     in_vmem = pl.BlockSpec(memory_space=pltpu.VMEM)
     anywhere = pl.BlockSpec(memory_space=pl.ANY)
     awaits = (*awaits, *ORDER.last)
@@ -49,7 +49,8 @@
         + [anywhere] * len(apart)
         + [in_vmem] * len(args)
         + [anywhere] * n_skip,
-        out_specs=[in_vmem] * n_out + [anywhere] * len(carry),
+        out_specs=[pl.BlockSpec(memory_space=pltpu.HBM) if n in hbm else in_vmem for n in range(n_out)]
+        + [anywhere] * len(carry),
         out_shape=[jax.ShapeDtypeStruct(*o) for o in outs] + [jax.ShapeDtypeStruct(c.shape, c.dtype) for c in carry],
         scratch_shapes=list(scratch),
         input_output_aliases={n_in + len(awaits) + i: n_out + i for i in range(len(carry))},
@@ -66,6 +67,33 @@
 
 def gate(*arrays, awaits=()):
     return run(gate_kernel, 0.1, 4, (), (), [((8, 128), F32)], awaits=awaits, carry=arrays)[1:]
+
+
+def park_kernel(places, *refs):
+    count = len(places)
+    copies = []
+    for n, (first, rows) in enumerate(places):
+        src = refs[n] if rows is None else refs[n].at[pl.ds(first, rows), :]
+        copies.append(pltpu.make_async_copy(src, refs[count + n], refs[-1].at[n]))
+        copies[-1].start()
+    for c in copies:
+        c.wait()
+
+
+def park(arrays, halves=()):
+    places = [(0, None) for _ in arrays] + [(n * (u.shape[0] // 2), u.shape[0] // 2) for u, n in halves]
+    outs = [(u.shape, u.dtype) for u in arrays] + [((u.shape[0] // 2, u.shape[1]), u.dtype) for u, n in halves]
+    return run(
+        functools.partial(park_kernel, places),
+        3,
+        4,
+        (),
+        (),
+        outs,
+        [pltpu.SemaphoreType.DMA((len(outs),))],
+        apart=(*arrays, *[u for u, n in halves]),
+        hbm=range(len(outs)),
+    )
 
 
 def split3(v):
@@ -92,33 +120,32 @@
         dst[pl.ds(pl.multiple_of(spots[b] * rows, rows), rows), cols] = turned[b * rows : (b + 1) * rows]
 
 
-def transpose_kernel(fast, spots, at_ref, p0, p1, p2, p3, t0, t1, t2, t3, out, wo, sem):
+def transpose_kernel(fast, spots, t0, t1, t2, t3, out):
     rows = out.shape[1] // 4
-    part = wo.shape[0] // 4
+    for p, t in enumerate((t0, t1, t2, t3)):
+        transpose_into(out, t[0:rows, :], spots if fast else None, slice(p * rows, (p + 1) * rows))
+
+
+def transposed(fast, spots, pieces, rows):
+    width = pieces[0].shape[1]
+    return run(functools.partial(transpose_kernel, fast), 2, 8, (spots,), pieces, [((width, 4 * rows), BF16)])[0]
+
+
+def together_kernel(at_ref, p0, p1, p2, p3, out, sem):
+    part = out.shape[0] // 4
     copies = []
     for n, p in enumerate((p0, p1, p2, p3)):
         spot = pl.ds(pl.multiple_of((at_ref[0] ^ n) * part, part), part)
-        copies.append(pltpu.make_async_copy(p.at[pl.ds(p.shape[0] - part, part), :], wo.at[spot, :], sem.at[n]))
+        copies.append(pltpu.make_async_copy(p.at[pl.ds(p.shape[0] - part, part), :], out.at[spot, :], sem.at[n]))
         copies[-1].start()
-    for p, t in enumerate((t0, t1, t2, t3)):
-        transpose_into(out, t[0:rows, :], spots if fast else None, slice(p * rows, (p + 1) * rows))
     for c in copies:
         c.wait()
 
 
-def transposed(fast, spots, at, pieces, rows, parts, wo, awaits=()):
-    width = pieces[0].shape[1]
-    return run(
-        functools.partial(transpose_kernel, fast),
-        2,
-        8,
-        (spots, at),
-        pieces,
-        [((width, 4 * rows), BF16), (wo.shape, BF16)],
-        [pltpu.SemaphoreType.DMA((4,))],
-        awaits,
-        apart=parts,
-    )
+def together(at, parts, shape, awaits=()):
+    return run(
+        together_kernel, 1, 4, (at,), (), [(shape, BF16)], [pltpu.SemaphoreType.DMA((4,))], awaits, apart=parts
+    )[0]
 
 
 def project_kernel(piece, sp_ref, freq_ref, tok_ref, w_ref, qt_ref, kt_ref, k_ref, vt_ref, cs_ref):
@@ -266,9 +293,9 @@
 
 def attend_back_kernel(h, fast, sp_ref, spots, *refs):
     q_refs, kt_refs, k_refs, vt_refs, o_refs, d_refs = (refs[4 * n : 4 * n + 4] for n in range(6))
-    n_given = (1, 4, 6)[h]
-    cs_refs, tok_t, given, outs = refs[24:28], refs[28], refs[29 : 29 + n_given], refs[29 + n_given : -13]
-    q_scr, do_scr, o_scr, kt_scr, k_scr, vt_scr, dq_scr, dk_scr, dv_scr, g_scr, tail_scr, eb_scr, sem = refs[-13:]
+    n_given = (1, 2, 4)[h]
+    cs_refs, tok_t, given, outs = refs[24:28], refs[28], refs[29 : 29 + n_given], refs[29 + n_given : -12]
+    q_scr, do_scr, o_scr, kt_scr, k_scr, vt_scr, dq_scr, dk_scr, dv_scr, g_scr, eb_scr, sem = refs[-12:]
     rows = kt_refs[0].shape[2]
     total = 4 * rows
     head = pl.ds(h * HD, HD)
@@ -282,7 +309,6 @@
             (q_refs[p].at[h], q_scr.at[:, at]),
             (d_refs[p].at[head, :], do_scr.at[pl.ds(0, HD), at]),
             (o_refs[p].at[head, :], o_scr.at[:, at]),
-            (d_refs[p].at[pl.ds(3 * HD, 16), :], tail_scr.at[p]),
         ]
     if h == 0:
         copies.append((d_refs[1].at[pl.ds(208, 576), :], eb_scr))
@@ -334,31 +360,24 @@
     near, far, core = outs[0:3]
     near[...] = g_scr[:, 0:rows]
     far[0:heads, :] = g_scr[:, 2 * rows : 3 * rows]
-    if h < 2:
-        far[heads : 2 * heads, :] = g_scr[:, 3 * rows :]
+    far[heads : 2 * heads, :] = g_scr[:, 3 * rows :]
     if h == 0:
         (ea,) = given
-        grad_out, e_own, total = outs[3:]
+        grad_out, e_own = outs[3:]
         core[...] = g_scr[:, rows : 2 * rows]
         grad_out[...] = grad.astype(BF16)
         e = ea[...].astype(F32) + unpack_rows(eb_scr, 0, 2 * heads)
         e_own[...] = e[0:heads].astype(BF16)
         pack_rows(far, 2 * heads, e[heads:])
-        sums = [tail_scr[p].astype(F32) for p in range(4)]
-        joined = (sums[0] + sums[1]) + (sums[2] + sums[3])
-        total[:, 0:512] = joined[0:4] + joined[4:8]
-        total[:, 512:768] = (joined[8:12] + joined[12:16])[:, 0:256]
     elif h == 1:
-        core_before, before, sum_own, sum_got = given
-        first, second, total = outs[3:]
+        core_before, before = given
+        first, second = outs[3:]
         core[0:heads, :] = core_before[...]
         core[heads:, :] = g_scr[:, rows : 2 * rows]
         split_rows(jnp.concatenate([before[...].astype(F32), grad], axis=1), first, second)
-        total[...] = sum_own[...] + sum_got[...]
     else:
-        core_before, far0, e_own, sum_own, sum_got, arrange = given
-        first, second, total, cross = outs[3:]
-        cross[...] = g_scr[:, 3 * rows :]
+        core_before, far0, e_own, arrange = given
+        first, second = outs[3:]
         core[0 : 2 * heads, :] = core_before[...]
         core[2 * heads : 3 * heads, :] = g_scr[:, rows : 2 * rows]
         core[3 * heads :, :] = far0[heads : 2 * heads, :]
@@ -369,7 +388,6 @@
         else:
             e = mm(arrange[...], e.astype(BF16), NT)
         split_rows(jnp.concatenate([grad, e], axis=1), first, second)
-        total[...] = sum_own[...] + sum_got[...]
 
 
 def attend_back(h, fast, spots, sp, q, kt, k, vt, o, d, cs, tok_t, given, awaits=()):
@@ -377,15 +395,12 @@
     total = 4 * rows
     width = tok_t.shape[0]
     heads = 3 * HD
-    far = (2 * heads + 3 * heads // 2, 2 * heads, heads)[h]
+    far = (2 * heads + 3 * heads // 2, 2 * heads, 2 * heads)[h]
     outs = [((heads, rows), BF16), ((far, rows), BF16), (((1, 2, 4)[h] * heads, rows), BF16)]
     if h == 0:
         outs += [((width, heads), BF16), ((heads, width), BF16)]
     else:
         outs += [((width // 2, 2 * heads), BF16)] * 2
-    outs += [((4, width), F32)]
-    if h == 2:
-        outs += [((heads, rows), BF16)]
     return run(
         functools.partial(attend_back_kernel, h, fast),
         12,
@@ -404,9 +419,8 @@
             pltpu.VMEM((128, total), F32),
             pltpu.VMEM((128, total), F32),
             pltpu.VMEM((heads, total), BF16),
-            pltpu.VMEM((4, 16, rows), BF16),
             pltpu.VMEM((3 * heads, rows), BF16) if h == 0 else pltpu.VMEM((width, heads), F32),
-            pltpu.SemaphoreType.DMA((29,)),
+            pltpu.SemaphoreType.DMA((25,)),
         ],
         awaits,
         apart=(*q, *kt, *k, *vt, *o, *d),
@@ -432,7 +446,7 @@
     return 0.5 + 0.5 * jnp.tanh(0.5 * v)
 
 
-def out_kernel(a0, a1, a2, a3, w0, w1, w2, w3, tok_ref, gain_ref, bias_ref, low_ref, xhat_ref, inv_ref):
+def out_kernel(a0, a1, a2, a3, w0, w1, w2, w3, tok_ref, gain_ref, bias_ref, low_ref, xhat_ref, inv_ref, *halves):
     w = jnp.concatenate([w0[...], w1[...], w2[...], w3[...]], axis=0)
     for half in range(2):
         at = slice(half * BLK, (half + 1) * BLK)
@@ -440,7 +454,9 @@
         normed, inverse = norm_parts(tok_ref[at, :].astype(F32) + mm(a, w, TN))
         xhat_ref[at, :] = normed
         inv_ref[at, :] = jnp.broadcast_to(inverse, (BLK, 128))
-        low_ref[at, :] = (normed * gain_ref[...] + bias_ref[...]).astype(BF16)
+        low = (normed * gain_ref[...] + bias_ref[...]).astype(BF16)
+        low_ref[at, :] = low
+        halves[half][...] = low
 
 
 def out_project(a, w, tok, gain, bias, awaits=()):
@@ -451,18 +467,27 @@
         10,
         (),
         (*a, *w, tok, gain, bias),
-        (((rows, width), BF16), ((rows, width), F32), ((rows, 128), F32)),
+        (((rows, width), BF16), ((rows, width), F32), ((rows, 128), F32), *[((rows // 2, width), BF16)] * 2),
         awaits=awaits,
     )
+
+
+PART_PLACES = (
+    *((0, n, 0, 2) for n in range(3)),
+    (0, 3, 0, 1),
+    (0, 3, 1, 1),
+    *((1, n, 0, 2) for n in range(4)),
+)
 
 
 def gather_weights(at_ref, parts, wgu, wd, sem):
     copies = []
-    for n, part in enumerate(parts):
-        dst = wgu if n < 4 else wd
-        rows = dst.shape[0] // 4
-        spot = pl.ds(pl.multiple_of((at_ref[0] ^ (n % 4)) * rows, rows), rows)
-        copies.append(pltpu.make_async_copy(part.at[pl.ds(0, rows), :], dst.at[spot, :], sem.at[n]))
+    for n, (part, (which, quarter, first, count)) in enumerate(zip(parts, PART_PLACES)):
+        dst = (wgu, wd)[which]
+        half = dst.shape[0] // 8
+        spot = pl.multiple_of((at_ref[0] ^ quarter) * (2 * half) + first * half, half)
+        src = part.at[pl.ds(0, count * half), :]
+        copies.append(pltpu.make_async_copy(src, dst.at[pl.ds(spot, count * half), :], sem.at[n]))
     for c in copies:
         c.start()
     return copies
@@ -480,14 +505,17 @@
     return mm(low, down)
 
 
-def mlp_own_kernel(ml1_ref, ml0, wgu, wd, acc, da, db, hid, ml1, sem):
+def mlp_own_kernel(half0, half1, ml0, wgu, wd, acc, da, db, hid, ml1, sem):
     rows = ml0.shape[0]
     hidden = wd.shape[0]
-    copy = pltpu.make_async_copy(ml1_ref, ml1, sem)
-    copy.start()
+    copies = []
+    for n, half in enumerate((half0, half1)):
+        copies.append(pltpu.make_async_copy(half, ml1.at[pl.ds(n * (rows // 2), rows // 2), :], sem.at[n]))
+        copies[-1].start()
     for block, x in enumerate((ml0, ml1)):
         if block:
-            copy.wait()
+            for c in copies:
+                c.wait()
         at = slice(block * rows, (block + 1) * rows)
         total = None
         for col in range(0, hidden, BLK):
@@ -498,7 +526,7 @@
         acc[at, :] = total
 
 
-def mlp_own(ml0, ml1, wgu, wd, awaits=()):
+def mlp_own(ml0, halves, wgu, wd, awaits=()):
     rows, width = ml0.shape
     hidden = wd.shape[0]
     saved = ((2 * rows, hidden), BF16)
@@ -508,18 +536,19 @@
         10,
         (),
         (ml0, wgu, wd),
-        [((2 * rows, width), F32)] + [saved] * 3,
-        [pltpu.VMEM((rows, width), BF16), pltpu.SemaphoreType.DMA],
+        [((2 * rows, width), F32)] + [saved] * 3 + [((rows, width), BF16)],
+        [pltpu.SemaphoreType.DMA((2,))],
         awaits,
-        apart=(ml1,),
+        apart=halves,
     )
 
 
 def mlp_peer_kernel(at_ref, *refs):
-    ml0, ml1, acc, own, sib, da, db, wgu, wd, sem = refs[8:]
+    n_parts = len(PART_PLACES)
+    ml0, ml1, acc, own, sib, da, db, wgu, wd, sem = refs[n_parts:]
     rows = ml0.shape[0]
     hidden = da.shape[1]
-    for c in gather_weights(at_ref, refs[:8], wgu, wd, sem):
+    for c in gather_weights(at_ref, refs[:n_parts], wgu, wd, sem):
         c.wait()
     for block, x in enumerate((ml0, ml1)):
         at = slice(block * rows, (block + 1) * rows)
@@ -545,7 +574,7 @@
         (at,),
         (ml0, ml1, acc),
         [((rows, width), F32), ((rows, width), BF16)] + [saved] * 2,
-        [pltpu.VMEM((width, 2 * hidden), BF16), pltpu.VMEM((hidden, width), BF16), pltpu.SemaphoreType.DMA((8,))],
+        [pltpu.VMEM((width, 2 * hidden), BF16), pltpu.VMEM((hidden, width), BF16), pltpu.SemaphoreType.DMA((len(parts),))],
         awaits,
         apart=parts,
     )
@@ -597,12 +626,13 @@
 
 
 def mlp_back_kernel(at_ref, *refs):
-    dm1_ref, dm0, wgu, wd, da_o, db_o, da_p, db_p, own, sib, dg_o, du_o, wgu_p, wd_p, dm1, sem = refs[8:]
+    n_parts = len(PART_PLACES)
+    dm1_ref, dm0, wgu, wd, da_o, db_o, da_p, db_p, own, sib, dg_o, du_o, wgu_p, wd_p, dm1, sem = refs[n_parts:]
     rows = dm0.shape[0]
     hidden = wd.shape[0]
-    first = pltpu.make_async_copy(dm1_ref, dm1, sem.at[8])
+    first = pltpu.make_async_copy(dm1_ref, dm1, sem.at[n_parts])
     first.start()
-    copies = gather_weights(at_ref, refs[:8], wgu_p, wd_p, sem)
+    copies = gather_weights(at_ref, refs[:n_parts], wgu_p, wd_p, sem)
 
     def part_of(x, at, cols, wg, wu, down, da, db, keep):
         dhid = mm(x[...], down, NT)
@@ -645,7 +675,7 @@
             pltpu.VMEM((width, 2 * hidden), BF16),
             pltpu.VMEM((hidden, width), BF16),
             pltpu.VMEM((rows, width), BF16),
-            pltpu.SemaphoreType.DMA((9,)),
+            pltpu.SemaphoreType.DMA((len(parts) + 1,)),
         ],
         awaits,
         apart=(*parts, dm1),
@@ -748,54 +778,142 @@
     )
 
 
-def weight_kernel(fast, spots, ml0, ml1, ml2, ml3, dg_o, du_o, dg_f, du_f, first, second, mlt):
+def weight_kernel(
+    fast, spots, spots_d, d0, d1, d2, d3, ml0, ml1, ml2, ml3, dg, du, dg_f, du_f,
+    g_first, g_second, u_first, u_second, total, mlt, mlt_d, tail_scr, sem,
+):
     rows = ml0.shape[0]
-    hidden = dg_o.shape[1]
+    copies = [
+        pltpu.make_async_copy(d.at[pl.ds(3 * HD, 16), :], tail_scr.at[p], sem.at[p]) for p, d in enumerate((d0, d1, d2, d3))
+    ]
+    for c in copies:
+        c.start()
     for p, u in enumerate((ml0, ml1, ml2, ml3)):
-        transpose_into(mlt, u[...], spots if fast else None, slice(p * rows, (p + 1) * rows))
-    for n, (near, far) in enumerate(((dg_o, dg_f), (du_o, du_f))):
-        cols = slice(n * hidden, (n + 1) * hidden)
-        grad = mm(mlt[:, 0 : 2 * rows], near[...]) + mm(mlt[:, 2 * rows :], far[...])
-        split_rows(grad, first.at[:, cols], second.at[:, cols])
-
-
-def weight_grads(fast, spots, ml, near, far, awaits=()):
+        cols = slice(p * rows, (p + 1) * rows)
+        transpose_into(mlt, u[...], spots if fast else None, cols)
+        transpose_into(mlt_d, u[...], spots_d if fast else None, cols)
+    for turned, near, far, first, second in (
+        (mlt, dg, dg_f, g_first, g_second),
+        (mlt_d, du, du_f, u_first, u_second),
+    ):
+        split_rows(mm(turned[:, 0 : 2 * rows], near[...]) + mm(turned[:, 2 * rows :], far[...]), first, second)
+    for c in copies:
+        c.wait()
+    sums = [tail_scr[p].astype(F32) for p in range(4)]
+    joined = (sums[0] + sums[1]) + (sums[2] + sums[3])
+    total[:, 0:512] = joined[0:4] + joined[4:8]
+    total[:, 512:768] = (joined[8:12] + joined[12:16])[:, 0:256]
+
+
+def weight_grads(fast, spots, spots_d, d, ml, near, far, awaits=()):
     rows, width = ml[0].shape
     hidden = near[0].shape[1]
     return run(
         functools.partial(weight_kernel, fast),
         6,
+        16,
+        (spots, spots_d),
+        (*ml, *near, *far),
+        [((width // 2, hidden), BF16)] * 4 + [((4, width), F32)],
+        [
+            *[pltpu.VMEM((width, 4 * rows), BF16)] * 2,
+            pltpu.VMEM((4, 16, rows), BF16),
+            pltpu.SemaphoreType.DMA((4,)),
+        ],
+        awaits,
+        apart=d,
+    )
+
+
+def join_kernel(core, got1, got2, out, sem):
+    heads = 3 * HD
+    pieces = ((core, 0, 4 * heads), (got1, heads, heads), (got2, heads, heads))
+    copies, at = [], 0
+    for n, (src, start, count) in enumerate(pieces):
+        copies.append(pltpu.make_async_copy(src.at[pl.ds(start, count), :], out.at[pl.ds(at, count), :], sem.at[n]))
+        copies[-1].start()
+        at += count
+    for c in copies:
+        c.wait()
+
+
+def join(core, got1, got2):
+    return run(
+        join_kernel,
+        1,
+        4,
+        (),
+        (),
+        [((18 * HD, core.shape[1]), BF16)],
+        [pltpu.SemaphoreType.DMA((3,))],
+        apart=(core, got1, got2),
+    )[0]
+
+
+def by_heads(w):
+    heads = 3 * HD
+    return jnp.concatenate([w[c * heads + h * HD : c * heads + (h + 1) * HD, :] for h in range(3) for c in range(3)], axis=0)
+
+
+def near_kernel(f0, f1, f2, dh1, n0, n1, n2, w0, w2, out, far, sem):
+    heads = 3 * HD
+    copies = []
+    for n, f in enumerate((f0, f1, f2)):
+        spot = pl.ds(n * heads, heads)
+        copies.append(pltpu.make_async_copy(f.at[pl.ds(0, heads), :], far.at[spot, :], sem.at[n]))
+        copies[-1].start()
+    near = jnp.concatenate([n0[...], n1[...], n2[...]], axis=0)
+    out[...] = dh1[...] + mm(near, by_heads(w0), TN)
+    for c in copies:
+        c.wait()
+    out[...] += mm(far[...], by_heads(w2), TN)
+
+
+def input_near(dh1, near, far, w0, w2):
+    return run(
+        near_kernel,
+        3,
+        12,
+        (),
+        (dh1, *near, w0, w2),
+        [(dh1.shape, F32)],
+        [pltpu.VMEM((9 * HD, dh1.shape[0]), BF16), pltpu.SemaphoreType.DMA((3,))],
+        apart=far,
+    )[0]
+
+
+def input_kernel(core_ref, before, w1, w3, out, core, total, sem):
+    arrival = pltpu.make_async_copy(core_ref, core, sem.at[0])
+    arrival.start()
+    w = jnp.concatenate([by_heads(w1), by_heads(w3)], axis=0)
+    arrival.wait()
+    copies = []
+    for half in range(before.shape[0] // BLK):
+        at = slice(half * BLK, (half + 1) * BLK)
+        total[at, :] = before[at, :] + mm(core[:, at], w, TN)
+        spot = pl.ds(half * BLK, BLK)
+        copies.append(pltpu.make_async_copy(total.at[spot, :], out.at[spot, :], sem.at[1 + half]))
+        copies[-1].start()
+    for c in copies:
+        c.wait()
+
+
+def input_back(before, core, w1, w3):
+    return run(
+        input_kernel,
+        3,
         14,
-        (spots,),
-        (*ml, *near, *far),
-        [((width // 2, 2 * hidden), BF16)] * 2,
-        [pltpu.VMEM((width, 4 * rows), BF16)],
-        awaits,
-    )
-
-
-def input_kernel(dh1, n0, n1, n2, core, core1, f0, f1, f2, x2, w0, w1, w2, w3, out):
-    rows = n0.shape[1]
-    heads = 3 * HD
-    sources = (
-        ((n0, 0), (n1, 0), (n2, 0)),
-        ((core, 0), (core, heads), (core, 2 * heads)),
-        ((f0, 0), (f1, 0), (f2, 0)),
-        ((core, 3 * heads), (core1, heads), (x2, 0)),
-    )
-    for half in range(rows // BLK):
-        at = slice(half * BLK, (half + 1) * BLK)
-        total = dh1[at, :]
-        for source, w in zip(sources, (w0, w1, w2, w3)):
-            cat = jnp.concatenate([ref[start : start + heads, at] for ref, start in source], axis=0)
-            parts = [w[c * heads + h * HD : c * heads + (h + 1) * HD, :] for h in range(3) for c in range(3)]
-            total += mm(cat, jnp.concatenate(parts, axis=0), TN)
-        out[at, :] = total
-
-
-def input_back(dh1, near, core, core1, far, far2, weights, awaits=()):
-    args = (dh1, *near, core, core1, *far, far2, *weights)
-    return run(input_kernel, 4, 12, (), args, [(dh1.shape, F32)], awaits=awaits)[0]
+        (),
+        (before, w1, w3),
+        [(before.shape, F32)],
+        [
+            pltpu.VMEM(core.shape, BF16),
+            pltpu.VMEM(before.shape, F32),
+            pltpu.SemaphoreType.DMA((1 + before.shape[0] // BLK,)),
+        ],
+        apart=(core,),
+        hbm=(0,),
+    )[0]
 
 
 def swap(v, bit, axis="tensor"):
@@ -830,15 +948,15 @@
         at += length
     if kind == "mlp":
         gu, down = outs
-        half = gu.shape[2]
-        gu[:, 0, :] = sums[0][:, 0:half]
-        gu[:, 1, :] = sums[0][:, half:]
-        down[...] = sums[1]
+        width = down.shape[1]
+        if len(sums) > 3:
+            sums = [u + sums[3][:, n * width : (n + 1) * width] for n, u in enumerate(sums[0:3])]
+        gu[:, 0, :] = sums[0]
+        gu[:, 1, :] = sums[1]
+        down[...] = sums[2]
     else:
         qkv, out = outs
-        total = jnp.concatenate([sums[0], sums[1]], axis=1)
-        if len(sums) > 2:
-            total += sums[2]
+        total = jnp.concatenate(sums, axis=1)
         for c in range(3):
             qkv[c] = jnp.concatenate([total[:, (3 * h + c) * HD : (3 * h + c + 1) * HD] for h in range(3)], axis=1)
         out[...] = total[:, 9 * HD :].T
@@ -866,10 +984,13 @@
     def advance(self):
         self.parts.append(swap(self.sent, 1 << self.order[self.step], "dp"))
         self.step += 1
+        self.next_sent()
+        return self.parts[-1]
+
+    def next_sent(self):
         if self.step < len(self.order):
             length = self.parts[-1].shape[0]
             self.sent = sum(u[length // 2 : length].astype(F32) for u in self.parts).astype(BF16)
-        return self.parts[-1]
 
     def all_parts(self):
         while self.step < len(self.order):
@@ -877,21 +998,17 @@
         return self.parts
 
 
-def joined_steps(one, two):
-    order, both = one.order, []
-    for step in range(1, len(order)):
-        length = (both or one.parts)[-1].shape[0] // 2
-        at = slice(length, 2 * length)
-        sent = jnp.concatenate([sum(u[at].astype(F32) for u in chain.parts) for chain in (one, two)], axis=1)
-        both.append(swap(sum((u[at].astype(F32) for u in both), sent).astype(BF16), 1 << order[step], "dp"))
-    return one.parts, two.parts, both
+def advance_together(chains):
+    bits = {chain.order[chain.step] for chain in chains}
+    if len(bits) > 1 or any(chain.step < len(chain.order) - 1 for chain in chains):
+        return None
+    for chain in chains:
+        chain.step += 1
+    return swap(jnp.concatenate([chain.sent for chain in chains], axis=1), 1 << bits.pop(), "dp")
 
 
 def first_sums(chains, rows):
-    sums = [sum(part[0:rows].astype(F32) for part in chain) for chain in chains]
-    if len(sums) == 3:
-        return jnp.concatenate(sums[0:2], axis=1) + sums[2]
-    return sums
+    return [sum(part[0:rows].astype(F32) for part in chain) for chain in chains]
 
 
 def quarter_of(w):
@@ -938,13 +1055,13 @@
 
     ORDER.last = ()
     wo0 = out_weight
-    wo1 = swap(wo0, 1)
+    wo1, wt1 = swap(wo0, 1), swap(wt, 1)
     wgu = gate_up_weight.reshape(width, -1)
     part_a = jnp.concatenate([quarter_of(down_weight), quarter_of(out_weight)], axis=0)
     part_b = quarter_of(wgu)
     pa0 = swap(part_a, 2)
 
-    proj = [project(0, sp, freqs, tok0, wt), project(1, sp, freqs, tok1, wt, awaits=(part_a, part_b))]
+    proj = [project(0, sp, freqs, tok0, wt), project(1, sp, freqs, tok1, wt, awaits=(part_a, part_b, wt1))]
     (tok2,) = gate(tok2)
     tok3 = swap(tok2, 1)
     tok = (tok0, tok1, tok2, tok3)
@@ -954,26 +1071,32 @@
     proj.append(project(3, sp, freqs, tok3, wt))
     qt, kt, k, vt, cs = zip(*proj)
     o2, o3, q2, q3 = attend(1, sp, qt, k, vt, (wo1,))
-    o2, o3 = gate(o2, o3, awaits=(pa0,))
+    o2, pa0 = gate(o2, pa0)
     pa1, pa2, pa3 = swap(pa0, 1, "dp"), swap(pa0, 2, "dp"), swap(pa0, 3, "dp")
-    g2, g3 = swap(o2, 2), swap(o3, 3)
+    g2 = swap(o2, 2)
     o0, o1, q0, q1 = attend(0, sp, qt, k, vt)
-    o1, pb0 = gate(o1, pb0)
+    o1, o3 = gate(o1, o3, awaits=(pb0,))
+    g3 = swap(o3, 3)
+    tok_t = transposed(fast, spots, [arranged(u, spots) for u in tok], rows)
+    (o1,) = gate(o1, awaits=(g2,))
     g1 = swap(o1, 1)
-    tok_t, wo2 = transposed(
-        fast, spots, quarter, [arranged(u, spots) for u in tok], rows, (pa0, pa1, pa2, pa3), wo0
-    )
+    wo2 = together(quarter, (pa0, pa1, pa2, pa3), wo0.shape, (g3, g1))
+    wo2, pb0 = gate(wo2, pb0)
     wo3 = swap(wo2, 1)
+    pb1, pb2 = swap(pb0, 1, "dp"), swap(pb0, 2, "dp")
     wo = (wo0, wo1, wo2, wo3)
 
     gain1, bias1, gain2, bias2 = (u.reshape(1, width) for u in (norm1_gain, norm1_bias, norm2_gain, norm2_bias))
-    ml0, xhat1, inv1 = out_project((o0, g1, g2, g3), wo, tokens, gain1, bias1)
-    ml0, pb0 = gate(ml0, pb0)
-    pb1, pb2, pb3 = swap(pb0, 1, "dp"), swap(pb0, 2, "dp"), swap(pb0, 3, "dp")
-    ml1, ml2 = swap(ml0, 1), swap(ml0, 2)
-    acc, da_o, db_o, hid_o = mlp_own(ml0, ml1, wgu, down_weight)
-    parts = (pb0, pb1, pb2, pb3, pa0, pa1, pa2, pa3)
+    ml0, xhat1, inv1, *halves = out_project((o0, g1, g2, g3), wo, tokens, gain1, bias1)
+    acc, da_o, db_o, hid_o, ml1 = mlp_own(ml0, [swap(u, 1) for u in halves], wgu, down_weight)
+    (ml0,) = gate(ml0)
+    ml2 = swap(ml0, 2)
+    kept = park((*kt, *k, *vt, q0, q1, q2, q3, tok_t))
+    kt, k, vt, (q0, q1, q2, q3, tok_t) = kept[0:4], kept[4:8], kept[8:12], kept[12:17]
+    half2, half1 = park((), ((pb2, 0), (pb1, 1)))
+    parts = (pb0, pb1, pb2, swap(half2, 1, "dp"), swap(half1, 2, "dp"), pa0, pa1, pa2, pa3)
     own, sib, da_p, db_p = mlp_peer(quarter, ml0, ml1, acc, parts)
+    (sib,) = gate(sib, awaits=(ml2,))
     output, dh2, dm0, sums2 = mid_norm(xhat1, own, swap(sib, 1), out_grad, gain1, bias1, gain2, bias2)
     dm0, ml2 = gate(dm0, ml2)
     dm1, dm2 = swap(dm0, 1), swap(dm0, 2)
@@ -989,15 +1112,19 @@
     ml = [arranged(u, spots) for u in (ml0, ml1, ml2, ml3)]
     dm = [arranged(u, spots_d) for u in (dm0, dm1, dm2, dm3)]
     d_first, d_second, dg_f, du_f = far_rows(fast, spots_d, dm, ml[2:], wgu, down_weight, hid_o)
-    wt0 = wt
     d_second, wt = gate(d_second, wt, awaits=d[1:])
     dn = scatter_steps(d_first, d_second, order_d)
     dn1 = dn.advance()
-    wt1, wt2 = swap(wt0, 1), swap(wt, 2)
-    gu_first, gu_second = weight_grads(fast, spots, ml, (dg_o, du_o), (dg_f, du_f))
-    (gu_second,) = gate(gu_second, awaits=(wt1,))
-    gu = scatter_steps(gu_first, gu_second, order)
-    gu1 = gu.advance()
+    wt2 = swap(wt, 2)
+    g_first, g_second, u_first, u_second, sums = weight_grads(
+        fast, spots, spots_d, d, ml, (dg_o, du_o), (dg_f, du_f)
+    )
+    g_second, u_second, sums, dn.parts[-1] = gate(g_second, u_second, sums, dn1)
+    dn.next_sent()
+    dn2 = dn.advance()
+    sums_got = swap(sums, 2, "dp")
+    gg, gu = scatter_steps(g_first, g_second, order), scatter_steps(u_first, u_second, order_d)
+    gg1, gu1 = gg.advance(), gu.advance()
 
     arrange = jnp.zeros((8, 128), BF16)
     if not fast:
@@ -1018,44 +1145,60 @@
         cs=cs,
         tok_t=tok_t,
     )
-    near0, far0, core0, grad0, e_own, sums = back(0, given=(ea,))
-    far0, sums = gate(far0, sums, awaits=(dn1,))
-    got0, dn2 = swap(far0, 2), dn.advance()
-    sum_bits = [*order[1:], 0]
-    sums_got = swap(sums, 1 << sum_bits[0], "dp")
-    near1, far1, core1, first, second, sums = back(1, given=(core0, grad0, sums, sums_got))
-    far1, second, sums = gate(far1, second, sums, awaits=(gu1, wt2))
+    near0, far0, core0, grad0, e_own = back(0, given=(ea,))
+    far0, dn.parts[-1], gg.parts[-1], gu.parts[-1], wt2, sums_got = gate(far0, dn2, gg1, gu1, wt2, sums_got)
+    for chain in (dn, gg, gu):
+        chain.next_sent()
+    got0, gg2, gu2 = swap(far0, 2), gg.advance(), gu.advance()
+    wt3 = swap(wt2, 1)
+    sums = sums + sums_got
+    sums_got = swap(sums, 4, "dp") if n_dp > 4 else sums_got
+    near1, far1, core1, first, second = back(1, given=(core0, grad0))
+    far1, second, gg.parts[-1], gu.parts[-1], sums_got = gate(far1, second, gg2, gu2, sums_got, awaits=(wt3,))
+    for chain in (gg, gu):
+        chain.next_sent()
     c1 = scatter_steps(first, second, order)
-    c1_got, gu2 = c1.advance(), gu.advance()
+    c1_got, mlp3 = c1.advance(), advance_together((gg, gu, dn))
     got1 = swap(far1, 2)
-    sums_got = swap(sums, 1 << sum_bits[1], "dp")
-    near2, far2, core2, first, second, sums, cross2 = back(
-        2, given=(core1, got0, e_own, sums, sums_got, arrange)
-    )
-    far2, core2, second, sums, cross2, wt2 = gate(
-        far2, core2, second, sums, cross2, wt2, awaits=(c1_got, gu2, got1, dn2)
-    )
+    sums = sums + sums_got
+    sums_got = swap(sums, 1, "dp")
+    near2, far2, core2, first, second = back(2, given=(core1, got0, e_own, arrange))
+    far2, second, c1.parts[-1], sums_got = gate(far2, second, c1_got, sums_got, awaits=(got1,) if mlp3 is None else (got1, mlp3))
+    c1.next_sent()
+    sums = sums + sums_got
+    bit = 8
+    while bit < n_dp:
+        sums = sums + swap(sums, bit, "dp")
+        bit *= 2
     c2 = scatter_steps(first, second, order)
-    c2.advance()
-    wt3 = swap(wt2, 1)
-    for bit in sum_bits[2:]:
-        sums = sums + swap(sums, 1 << bit, "dp")
-    gu, dn, attention = gu.all_parts(), dn.all_parts(), joined_steps(c1, c2)
-    core, core1 = swap(core2, 1), swap(got1, 1)
-    got2, x2 = swap(far2, 2), swap(cross2, 3)
-    input_grad = input_back(dh1, (near0, near1, near2), core, core1, (got0, got1, got2), x2, (wt, wt1, wt2, wt3))
+    c2_got, c1_got, got2 = c2.advance(), c1.advance(), swap(far2, 2)
+    c2.parts[-1], c1.parts[-1] = gate(c2_got, c1_got)
+    c2.next_sent()
+    c1.next_sent()
+    c2_got, c1_got = c2.advance(), c1.advance()
+    core = swap(join(core2, got1, got2), 1)
+    input_grad = input_near(dh1, (near0, near1, near2), (got0, got1, got2), wt, wt2)
+    c2.parts[-1], c1.parts[-1] = gate(c2_got, c1_got)
+    c2.next_sent()
+    c1.next_sent()
+    mlp = [chain.all_parts() for chain in (gg, gu, dn)]
+    attention = (c1.all_parts(), c2.all_parts())
+    if mlp3 is not None:
+        mlp.append([mlp3])
     shard = width // n_dp
     if fast:
         hidden = down_weight.shape[0]
-        gu_part, down_part = last_sums("mlp", shard, (gu, dn), [((shard, 2, hidden), F32), ((shard, hidden), F32)])
+        gu_part, down_part = last_sums("mlp", shard, mlp, [((shard, 2, hidden), F32), ((shard, hidden), F32)])
+        input_grad = input_back(input_grad, core, wt1, wt3)
         qkv_part, out_part = last_sums(
             "attention", shard, attention, [((3, shard, 3 * HD), F32), ((3 * HD, shard), F32)]
         )
         qkv_part = jnp.transpose(qkv_part, (1, 0, 2))
     else:
-        gu_part, down_part = first_sums((gu, dn), shard)
-        gu_part = gu_part.reshape(shard, 2, -1)
-        total = first_sums(attention, shard)
+        input_grad = input_back(input_grad, core, wt1, wt3)
+        gg, gu, down_part = first_sums(mlp, shard)
+        gu_part = jnp.stack([gg, gu], axis=1)
+        total = jnp.concatenate(first_sums(attention, shard), axis=1)
         out_part = total[:, 9 * HD :].T
         qkv_part = jnp.transpose(total[:, 0 : 9 * HD].reshape(shard, 3, 3, HD), (0, 2, 1, 3)).reshape(shard, 3, 3 * HD)
     return (

time: 289 us -> 250 us (0.87)
  waiting for transfers between devices: 105 us -> 62.8 us
  Pallas kernels: 120 us -> 126 us
  local copies, waits for them, and re-layouts: 11.6 us -> 7.32 us
    ppermute x49 -> x52, waiting for transfers between devices: 105 us -> 62.8 us  [swap(): return lax.ppermute(v, axis, [(i, i ^ bit) for i in range(n)])]
    pallas_call x33 -> x43, Pallas kernels: 120 us -> 126 us  [run(): pl.pallas_call(body, in_specs=[pl.BlockSpec(memory_space=pltpu.SMEM)] * l...]
    unnamed x52 -> x35, local copies, waits for them, and re-layouts: 10.8 us -> 6.5 us
    ppermute x49 -> x52, starting transfers between devices: 45.1 us -> 45.5 us  [swap(): return lax.ppermute(v, axis, [(i, i ^ bit) for i in range(n)])]
  transfers between devices with their start and end apart: 49 -> 52, of which waited for: 19 -> 21; matrix products, arithmetic and copies ran while one was open for 1% -> 2% of each run, Pallas kernels for 36% -> 48%
where the time goes in v2:
time: 250 us; the launch traced here: 246 us
  Pallas kernels  126 us (50%)
  waiting for transfers between devices  62.8 us (25%)
  starting transfers between devices  45.5 us (18%)
  local copies, waits for them, and re-layouts  7.32 us (3%)
    pallas_call x43, Pallas kernels, run(): pl.pallas_call(body, in_specs=[pl.BlockSpec(memory_space=pltpu.SMEM)] * l...  126 us
    ppermute x52, waiting for transfers between devices, swap(): return lax.ppermute(v, axis, [(i, i ^ bit) for i in range(n)])  62.8 us
    ppermute x52, starting transfers between devices, swap(): return lax.ppermute(v, axis, [(i, i ^ bit) for i in range(n)])  45.5 us
    unnamed x35, local copies, waits for them, and re-layouts  6.5 us
  transfers between devices with their start and end apart: 52, of which 21 were waited for; matrix products, arithmetic and copies ran while one was open for 2% of the time, Pallas kernels for 48%

profile of v2, /device:TPU:0, one launch (start us, length us, event | category | flops | bytes accessed | tf_op | source)
XLA Modules:
  0.0 245.6 jit_solution(666005493628464412)
XLA Ops:
  3.5 2.9 %collective-permute-start.2 = (bf16[528,768]{1,0:T(8,128)(2,1)}, bf16[528,768]{1,0:T(8,128)(2,1)}, u32[]{:S(2)}, u32[]{:S(2)}) collective-permute-start(bf16[528,768]{1,0:T(8,128)(2,1)} %fusion.1.refs_2_.refs_1_), channel_id=1, source_target_pairs={{0,2},{1,3},{2,0},{3,1},{4,6},{5,7},{6,4},{7,5},{8,10},{9,11},{10,... | collective-permute-start | bytes 2433032 | tf_op jit(solution)/shard_map/ppermute | solution.py:921
  6.3 2.1 copy.64
  8.7 2.2 shard_map.195
  11.1 2.1 shard_map.196
  13.2 11.8 %collective-permute-done.2.refs_1_ = bf16[528,768]{1,0:T(8,128)(2,1)} collective-permute-done((bf16[528,768]{1,0:T(8,128)(2,1)}, bf16[528,768]{1,0:T(8,128)(2,1)}, u32[]{:S(2)}, u32[]{:S(2)}) %collective-permute-start.2) | collective-permute-done | bytes 811040 | tf_op jit(solution)/shard_map/ppermute | solution.py:921
  25.5 1.7 collective-permute-start.5
  27.3 2.1 shard_map.198
  31.3 7.0 %shard_map.200 = (bf16[192,512]{1,0:T(8,128)(2,1)S(1)}, bf16[192,512]{1,0:T(8,128)(2,1)S(1)}, bf16[3,128,512]{2,1,0:T(8,128)(2,1)S(1)}, bf16[3,128,512]{2,1,0:T(8,128)(2,1)S(1)}) custom-call(s32[9]{0:T(128)S(1)} %pad_add_fusion.refs_0_, bf16[3,128,512]{2,1,0:T(8,128)(2,1)S(1)} %get-tuple-element.187.refs_1_, ...), custom_call_target="tpu_custom_call" | custom-call | flops 1320000000 | bytes 262144 | tf_op jit(solution)/shard_map/pallas_call | solution.py:46
  38.4 1.8 collective-permute-start.10
  40.2 2.3 collective-permute-start.11
  42.5 1.5 collective-permute-start.6
  44.1 7.2 %shard_map.202 = (bf16[192,512]{1,0:T(8,128)(2,1)S(1)}, bf16[192,512]{1,0:T(8,128)(2,1)S(1)}, bf16[3,128,512]{2,1,0:T(8,128)(2,1)S(1)}, bf16[3,128,512]{2,1,0:T(8,128)(2,1)S(1)}) custom-call(s32[9]{0:T(128)S(1)} %pad_add_fusion.refs_0_, bf16[3,128,512]{2,1,0:T(8,128)(2,1)S(1)} %get-tuple-element.172.refs_1_, ...), custom_call_target="tpu_custom_call" | custom-call | flops 1320000000 | bytes 262144 | tf_op jit(solution)/shard_map/pallas_call | solution.py:46
  51.4 2.6 %shard_map.204.refs_1_.refs_16_ = bf16[768,2048]{1,0:T(8,128)(2,1)S(1)} custom-call(s32[8]{0:T(128)S(1)} %add_add_fusion.1.refs_0_.refs_1_, bf16[528,768]{1,0:T(8,128)(2,1)} %fusion.1.refs_2_.refs_1_, bf16[528,768]{1,0:T(8,128)(2,1)} %collective-permute-done.refs_2_, bf16[528,768]{1,0:T(8,128)(2,1)} %get-tuple-element.178.refs_2_.refs_3_, ...), custom_call_target="tpu_custom_call" | custom-call | flops 330000000 | bytes 262144 | tf_op jit(solution)/shard_map/pallas_call | solution.py:46
  54.3 3.0 %collective-permute-done.9.refs_5_.refs_3_.refs_10_ = bf16[192,512]{1,0:T(8,128)(2,1)S(1)} collective-permute-done((bf16[192,512]{1,0:T(8,128)(2,1)S(1)}, bf16[192,512]{1,0:T(8,128)(2,1)S(1)}, u32[]{:S(2)}, u32[]{:S(2)}) %collective-permute-start.9) | collective-permute-done | bytes 196640 | tf_op jit(solution)/shard_map/ppermute | solution.py:921
  63.7 1.7 collective-permute-start.18
  65.5 5.4 %shard_map.209 = (f32[1024,768]{1,0:T(8,128)S(1)}, bf16[1024,768]{1,0:T(8,128)(2,1)S(1)}, bf16[1024,768]{1,0:T(8,128)(2,1)S(1)}, bf16[1024,768]{1,0:T(8,128)(2,1)S(1)}, bf16[512,768]{1,0:T(8,128)(2,1)S(1)}) custom-call(bf16[256,768]{1,0:T(8,128)(2,1)S(1)} %collective-permute-done.14.refs_0_, bf16[256,768]{1,0:T(8,128)(2,1)S(1)} %collective-permute-done.15.refs_1_, ...), custom_call_target="tpu_custom_call" | custom-call | flops 825000000 | bytes 262144 | tf_op jit(solution)/shard_map/pallas_call | solution.py:46
  71.7 3.6 %shard_map.211 = (bf16[3,128,512]{2,1,0:T(8,128)(2,1)S(1)}, bf16[3,128,512]{2,1,0:T(8,128)(2,1)S(1)}, bf16[3,128,512]{2,1,0:T(8,128)(2,1)S(1)}, bf16[3,128,512]{...) custom-call(bf16[3,128,512]{2,1,0:T(8,128)(2,1)S(1)} %get-tuple-elem, ...), custom_call_target="tpu_custom_call" | custom-call | flops 495000000 | bytes 262144 | tf_op jit(solution)/shard_map/pallas_call | solution.py:46
  75.2 2.4 collective-permute-done.17.refs_1_.refs_2_
  79.5 1.7 collective-permute-start.20
  81.3 5.6 %collective-permute-done.19.refs_4_ = bf16[96,1536]{1,0:T(8,128)(2,1)S(1)} collective-permute-done((bf16[96,1536]{1,0:T(8,128)(2,1)S(1)}, bf16[96,1536]{1,0:T(8,128)(2,1)S(1)}, u32[]{:S(2)}, u32[]{:S(2)}) %collective-permute-start.19) | collective-permute-done | bytes 294944 | tf_op jit(solution)/shard_map/ppermute | solution.py:921
  87.2 5.3 %shard_map.213 = (f32[512,768]{1,0:T(8,128)S(1)}, bf16[512,768]{1,0:T(8,128)(2,1)S(1)}, bf16[1024,768]{1,0:T(8,128)(2,1)S(1)}, bf16[1024,768]{1,0:T(8,128)(2,1)S(1)}) custom-call(s32[1]{0:T(128)} %bitcast.5.refs_0_, bf16[192,1536]{1,0:T(8,128)(2,1)S(1)} %get-tuple-element.211.refs_1_, bf16[192,1536]{1,0:T(8,128)(2,1)S(1)} %collective-permute-done.17.refs_1_.refs_2_, ...), custom_call_target="tpu_custom_call" | custom-call | flops 990000000 | bytes 262144 | tf_op jit(solution)/shard_map/pallas_call | solution.py:46
  93.3 1.7 collective-permute-done.21.refs_0_
  95.0 3.5 %shard_map.215 = (bf16[512,768]{1,0:T(8,128)(2,1)}, f32[512,768]{1,0:T(8,128)S(1)}, bf16[512,768]{1,0:T(8,128)(2,1)S(1)}, f32[2,768]{1,0:T(2,128)S(1)}) custom-call(bf16[512,768]{1,0:T(8,128)(2,1)S(1)} %collective-permute-done.21.refs_0_, f32[512,768]{1,0:T(8,128)S(1)} %get-tuple-element.228.refs_1_.refs_3_, ...), custom_call_target="tpu_custom_call" | custom-call | flops 495000000 | bytes 262144 | tf_op jit(solution)/shard_map/pallas_call | solution.py:46
  100.8 13.1 %shard_map.217 = (f32[512,768]{1,0:T(8,128)S(1)}, bf16[512,768]{1,0:T(8,128)(2,1)S(1)}, bf16[1024,768]{1,0:T(8,128)(2,1)S(1)}, bf16[1024,768]{1,0:T(8,128)(2,1)S(1)}) custom-call(s32[1]{0:T(128)} %bitcast.5.refs_0_, bf16[192,1536]{1,0:T(8,128)(2,1)S(1)} %get-tuple-element.211.refs_1_, bf16[192,1536]{1,0:T(8,128)(2,1)S(1)} %collective-permute-done.17.refs_1_.refs_2_, ...), custom_call_target="tpu_custom_call" | custom-call | flops 1815000064 | bytes 262144 | tf_op jit(solution)/shard_map/pallas_call | solution.py:46
  114.2 4.4 %collective-permute-done.25.refs_15_.refs_3_ = bf16[512,768]{1,0:T(8,128)(2,1)S(1)} collective-permute-done((bf16[512,768]{1,0:T(8,128)(2,1)S(1)}, bf16[512,768]{1,0:T(8,128)(2,1)S(1)}, u32[]{:S(2)}, u32[]{:S(2)}) %collective-permute-start.25) | collective-permute-done | bytes 786464 | tf_op jit(solution)/shard_map/ppermute | solution.py:921
  118.6 4.2 %shard_map.219 = (f32[512,768]{1,0:T(8,128)S(1)}, bf16[208,512]{1,0:T(8,128)(2,1)S(1)}, bf16[784,512]{1,0:T(8,128)(2,1)S(1)}, bf16[208,512]{1,0:T(8,128)(2,1)S(1...) custom-call(bf16[512,768]{1,0:T(8,128)(2,1)S(1)} %collective-permute-done.24.refs_0_, ...), custom_call_target="tpu_custom_call" | custom-call | flops 825000000 | bytes 262144 | tf_op jit(solution)/shard_map/pallas_call | solution.py:46
  124.9 7.6 %shard_map.221 = (bf16[384,768]{1,0:T(8,128)(2,1)S(1)}, bf16[384,768]{1,0:T(8,128)(2,1)S(1)}, bf16[1024,768]{1,0:T(8,128)(2,1)S(1)}, bf16[1024,768]{1,0:T(8,128)(2,1)S(1)}) custom-call(s32[8]{0:T(128)S(1)} %add_add_fusion.refs_0_.refs_1_, bf16[512,768]{1,0:T(8,128)(2,1)S(1)} %get-tuple-element.249.refs_11_.refs_1_, ...), custom_call_target="tpu_custom_call" | custom-call | flops 1320000000 | bytes 262144 | tf_op jit(solution)/shard_map/pallas_call | solution.py:46
  132.5 1.9 collective-permute-done.28.refs_2_.refs_5_.refs_25_
  134.4 1.7 collective-permute-start.30
  136.8 7.2 %shard_map.223 = (bf16[384,768]{1,0:T(8,128)(2,1)S(1)}, bf16[384,768]{1,0:T(8,128)(2,1)S(1)}, bf16[384,768]{1,0:T(8,128)(2,1)S(1)}, bf16[384,768]{1,0:T(8,128)(2,1)S(1)}, f32[4,768]{1,0:T(4,128)S(1)}) custom-call(s32[8]{0:T(128)S(1)} %add_add_fusion.1.refs_0_.refs_1_, s32[8]{0:T(128)S(1)} %add_add_fusion.refs_0_.refs_1_, ...), custom_call_target="tpu_custom_call" | custom-call | flops 990000000 | bytes 262144 | tf_op jit(solution)/shard_map/pallas_call | solution.py:46
  144.0 6.2 %collective-permute-done.30.refs_4_ = bf16[384,768]{1,0:T(8,128)(2,1)S(1)} collective-permute-done((bf16[384,768]{1,0:T(8,128)(2,1)S(1)}, bf16[384,768]{1,0:T(8,128)(2,1)S(1)}, u32[]{:S(2)}, u32[]{:S(2)}) %collective-permute-start.30) | collective-permute-done | bytes 589856 | tf_op jit(solution)/shard_map/ppermute | solution.py:921
  151.7 1.7 collective-permute-start.33
  154.5 12.7 %shard_map.225 = (bf16[192,512]{1,0:T(8,128)(2,1)S(1)}, bf16[672,512]{1,0:T(8,128)(2,1)S(1)}, bf16[192,512]{1,0:T(8,128)(2,1)S(1)}, bf16[768,192]{1,0:T(8,128)(2,1)S(1)}, bf16[192,768]{1,0:T(8,128)(2,1)S(1)}) custom-call(s32[9]{0:T(128)S(1)} %pad_add_fusion.refs_0_, s32[8]{0:T(128)S(1)} %add_add_fusion.1.refs_0_.refs_1_, ...), custom_call_target="tpu_custom_call" | custom-call | flops 1980000000 | bytes 262144 | tf_op jit(solution)/shard_map/pallas_call | solution.py:46
  167.3 4.4 %collective-permute-done.31.refs_2_ = bf16[192,768]{1,0:T(8,128)(2,1)S(1)} collective-permute-done((bf16[192,768]{1,0:T(8,128)(2,1)S(1)}, bf16[192,768]{1,0:T(8,128)(2,1)S(1)}, u32[]{:S(2)}, u32[]{:S(2)}) %collective-permute-start.31) | collective-permute-done | bytes 294944 | tf_op jit(solution)/shard_map/ppermute | solution.py:921
  171.7 2.7 %collective-permute-start.40 = (f32[4,768]{1,0:T(4,128)S(1)}, f32[4,768]{1,0:T(4,128)S(1)}, u32[]{:S(2)}, u32[]{:S(2)}) collective-permute-start(f32[4,768]{1,0:T(4,128)S(1)} %add.92), channel_id=1, source_target_pairs={{0,16},{4,20},{8,24},{12,28},{16,0},{20,4},{24,8},{28,12},{1,17},{... | collective-permute-start | bytes 36872 | tf_op jit(solution)/shard_map/ppermute | solution.py:921
  176.0 1.8 collective-permute-start.38
  178.7 12.8 %shard_map.227 = (bf16[192,512]{1,0:T(8,128)(2,1)S(1)}, bf16[384,512]{1,0:T(8,128)(2,1)S(1)}, bf16[384,512]{1,0:T(8,128)(2,1)S(1)}, bf16[384,384]{1,0:T(8,128)(2,1)S(1)}, bf16[384,384]{1,0:T(8,128)(2,1)S(1)}) custom-call(s32[9]{0:T(128)S(1)} %pad_add_fusion.refs_0_, s32[8]{0:T(128)S(1)} %add_add_fusion.1.refs_0_.refs_1_, ...), custom_call_target="tpu_custom_call" | custom-call | flops 1980000000 | bytes 262144 | tf_op jit(solution)/shard_map/pallas_call | solution.py:46
  194.0 1.7 collective-permute-start.44
  196.1 12.5 %shard_map.229 = (bf16[192,512]{1,0:T(8,128)(2,1)S(1)}, bf16[384,512]{1,0:T(8,128)(2,1)S(1)}, bf16[768,512]{1,0:T(8,128)(2,1)S(1)}, bf16[384,384]{1,0:T(8,128)(2,1)S(1)}, bf16[384,384]{1,0:T(8,128)(2,1)S(1)}) custom-call(s32[9]{0:T(128)S(1)} %pad_add_fusion.refs_0_, s32[8]{0:T(128)S(1)} %add_add_fusion.1.refs_0_.refs_1_, ...), custom_call_target="tpu_custom_call" | custom-call | flops 1980000000 | bytes 262144 | tf_op jit(solution)/shard_map/pallas_call | solution.py:46
  208.7 5.3 %collective-permute-done.42.refs_1_.refs_9_ = bf16[96,2304]{1,0:T(8,128)(2,1)S(1)} collective-permute-done((bf16[96,2304]{1,0:T(8,128)(2,1)S(1)}, bf16[96,2304]{1,0:T(8,128)(2,1)S(1)}, u32[]{:S(2)}, u32[]{:S(2)}) %collective-permute-start.42) | collective-permute-done | bytes 442400 | tf_op jit(solution)/shard_map/ppermute | solution.py:921
  215.9 5.1 %collective-permute-done.47.refs_2_ = bf16[192,384]{1,0:T(8,128)(2,1)S(1)} collective-permute-done((bf16[192,384]{1,0:T(8,128)(2,1)S(1)}, bf16[192,384]{1,0:T(8,128)(2,1)S(1)}, u32[]{:S(2)}, u32[]{:S(2)}) %collective-permute-start.47) | collective-permute-done | bytes 147488 | tf_op jit(solution)/shard_map/ppermute | solution.py:921
  221.1 2.6 %collective-permute-done.46.refs_1_ = bf16[384,384]{1,0:T(8,128)(2,1)S(1)} collective-permute-done((bf16[384,384]{1,0:T(8,128)(2,1)S(1)}, bf16[384,384]{1,0:T(8,128)(2,1)S(1)}, u32[]{:S(2)}, u32[]{:S(2)}) %collective-permute-start.46) | collective-permute-done | bytes 294944 | tf_op jit(solution)/shard_map/ppermute | solution.py:921
  225.2 1.7 collective-permute-start.49
  227.5 2.8 %shard_map.233.refs_0_.refs_1_ = f32[512,768]{1,0:T(8,128)S(1)} custom-call(bf16[672,512]{1,0:T(8,128)(2,1)S(1)} %collective-permute-done.36.refs_32_.refs_0_, bf16[384,512]{1,0:T(8,128)(2,1)S(1)} %collective-permute-done.41.refs_0_.refs_1_, bf16[384,512]{1,0:T(8,128)(2,1)S(1)} %collective-permute-done.45.refs_2_, ...), custom_call_target="tpu_custom_call" | custom-call | flops 495000000 | bytes 262144 | tf_op jit(solution)/shard_map/pallas_call | solution.py:46
  230.8 2.2 collective-permute-done.49.refs_1_
  234.2 3.2 %shard_map.235 = (f32[96,2,768]{2,1,0:T(2,128)}, f32[96,768]{1,0:T(8,128)}) custom-call(bf16[384,768]{1,0:T(8,128)(2,1)S(1)} %get-tuple-element.300.refs_0_, bf16[384,768]{1,0:T(8,128)(2,1)S(1)} %get-tuple-element.301.refs_1_, bf16[192,768]{1,0:T(8,128)(2,1)S(1)} %get-tuple-element.308.refs_2_, bf16[384,768]{1,0:T(8,128)(2,1)S(1)} %get-tuple-element.302.refs_3_, ...), custom_call_target="tpu_custom_call" | custom-call | flops 330000000 | bytes 262144 | tf_op jit(solution)/shard_map/pallas_call | solution.py:46
  238.4 3.7 %shard_map.236.refs_8_ = f32[512,768]{1,0:T(8,128)} custom-call(bf16[1152,512]{1,0:T(8,128)(2,1)S(1)} %collective-permute-done.48.refs_0_, f32[512,768]{1,0:T(8,128)S(1)} %shard_map.233.refs_0_.refs_1_, bf16[576,768]{1,0:T(8,128)(2,1)} %collective-permute-done.1.refs_6_.refs_2_, bf16[576,768]{1,0:T(8,128)(2,1)S(1)} %collective-permute-done.37.refs_0_.refs_3_, ...), custom_call_target="tpu_custom_call" | custom-call | flops 495000000 | bytes 262144 | tf_op jit(solution)/shard_map/pallas_call | solution.py:46
  243.5 1.7 shard_map.237
  (165 shorter events, 37.2 us)
Async XLA Ops:
  1.9 9.2 %collective-permute-start.1 = (bf16[576,768]{1,0:T(8,128)(2,1)S(1)}, bf16[576,768]{1,0:T(8,128)(2,1)}, u32[]{:S(2)}, u32[]{:S(2)}) collective-permute-start(bf16[576,768]{1,0:T(8,128)(2,1)S(1)} %bitcast.10), channel_id=1, source_target_pairs={{0,1},{1,0},{2,3},{3,2},{4,5},{5,4},{6,7},{7,6},{8,9},{9,8},{10,11... | collective-permute-start | bytes 2654216 | tf_op jit(solution)/shard_map/ppermute | solution.py:921
  3.3 7.7 %collective-permute-start = (bf16[528,768]{1,0:T(8,128)(2,1)}, bf16[528,768]{1,0:T(8,128)(2,1)}, u32[]{:S(2)}, u32[]{:S(2)}) collective-permute-start(bf16[528,768]{1,0:T(8,128)(2,1)} %fusion.1.refs_2_.refs_1_), channel_id=1, source_target_pairs={{0,1},{1,0},{2,3},{3,2},{4,5},{5,4},{6,7},{7,6},{8,9},{9,8},{10,11... | collective-permute-start | bytes 2433032 | tf_op jit(solution)/shard_map/ppermute | solution.py:921
  3.5 21.5 %collective-permute-start.2 = (bf16[528,768]{1,0:T(8,128)(2,1)}, bf16[528,768]{1,0:T(8,128)(2,1)}, u32[]{:S(2)}, u32[]{:S(2)}) collective-permute-start(bf16[528,768]{1,0:T(8,128)(2,1)} %fusion.1.refs_2_.refs_1_), channel_id=1, source_target_pairs={{0,2},{1,3},{2,0},{3,1},{4,6},{5,7},{6,4},{7,5},{8,10},{9,11},{10,... | collective-permute-start | bytes 2433032 | tf_op jit(solution)/shard_map/ppermute | solution.py:921
  25.0 4.7 %collective-permute-start.3 = (bf16[528,768]{1,0:T(8,128)(2,1)}, bf16[528,768]{1,0:T(8,128)(2,1)S(1)}, u32[]{:S(2)}, u32[]{:S(2)}) collective-permute-start(bf16[528,768]{1,0:T(8,128)(2,1)} %get-tuple-element.178.refs_2_.refs_3_), channel_id=1, source_target_pairs={{0,1},{1,0},{2,3},{3,2},{4,5},{5,4},{6,7},{7,6},{8,9},{9,8},{10,11... | collective-permute-start | bytes 2433032 | tf_op jit(solution)/shard_map/ppermute | solution.py:921
  25.0 6.3 %collective-permute-start.4 = (bf16[192,768]{1,0:T(8,128)(2,1)S(1)}, bf16[192,768]{1,0:T(8,128)(2,1)S(1)}, u32[]{:S(2)}, u32[]{:S(2)}) collective-permute-start(bf16[192,768]{1,0:T(8,128)(2,1)S(1)} %copy-done.4), channel_id=1, source_target_pairs={{0,1},{1,0},{2,3},{3,2},{4,5},{5,4},{6,7},{7,6},{8,9},{9,8},{10,11... | collective-permute-start | bytes 884744 | tf_op jit(solution)/shard_map/ppermute | solution.py:921
  25.5 12.8 %collective-permute-start.5 = (bf16[240,768]{1,0:T(8,128)(2,1)S(1)}, bf16[240,768]{1,0:T(8,128)(2,1)S(1)}, u32[]{:S(2)}, u32[]{:S(2)}) collective-permute-start(bf16[240,768]{1,0:T(8,128)(2,1)S(1)} %pad_maximum_fusion.1.refs_4_), channel_id=1, source_target_pairs={{0,2},{1,3},{2,0},{3,1},{4,6},{5,7},{6,4},{7,5},{8,10},{9,11},{10,... | collective-permute-start | bytes 1105928 | tf_op jit(solution)/shard_map/ppermute | solution.py:921
  29.4 21.9 %collective-permute-start.7 = (bf16[192,1536]{1,0:T(8,128)(2,1)S(1)}, bf16[192,1536]{1,0:T(8,128)(2,1)S(1)}, u32[]{:S(2)}, u32[]{:S(2)}) collective-permute-start(bf16[192,1536]{1,0:T(8,128)(2,1)S(1)} %get-tuple-element.194), channel_id=1, source_target_pairs={{0,2},{1,3},{2,0},{3,1},{4,6},{5,7},{6,4},{7,5},{8,10},{9,11},{10,... | collective-permute-start | bytes 1769480 | tf_op jit(solution)/shard_map/ppermute | solution.py:921
  38.4 18.9 %collective-permute-start.10 = (bf16[240,768]{1,0:T(8,128)(2,1)S(1)}, bf16[240,768]{1,0:T(8,128)(2,1)S(1)}, u32[]{:S(2)}, u32[]{:S(2)}) collective-permute-start(bf16[240,768]{1,0:T(8,128)(2,1)S(1)} %get-tuple-element.201.refs_1_.refs_6_), channel_id=1, source_target_pairs={{0,4},{4,0},{8,12},{12,8},{16,20},{20,16},{24,28},{28,24},{1,5},{5... | collective-permute-start | bytes 1105928 | tf_op jit(solution)/shard_map/ppermute | solution.py:921
  40.2 17.0 %collective-permute-start.11 = (bf16[240,768]{1,0:T(8,128)(2,1)S(1)}, bf16[240,768]{1,0:T(8,128)(2,1)S(1)}, u32[]{:S(2)}, u32[]{:S(2)}) collective-permute-start(bf16[240,768]{1,0:T(8,128)(2,1)S(1)} %get-tuple-element.201.refs_1_.refs_6_), channel_id=1, source_target_pairs={{0,8},{4,12},{8,0},{12,4},{16,24},{20,28},{24,16},{28,20},{1,9},{5... | collective-permute-start | bytes 1105928 | tf_op jit(solution)/shard_map/ppermute | solution.py:921
  42.5 15.8 %collective-permute-start.12 = (bf16[240,768]{1,0:T(8,128)(2,1)S(1)}, bf16[240,768]{1,0:T(8,128)(2,1)S(1)}, u32[]{:S(2)}, u32[]{:S(2)}) collective-permute-start(bf16[240,768]{1,0:T(8,128)(2,1)S(1)} %get-tuple-element.201.refs_1_.refs_6_), channel_id=1, source_target_pairs={{0,12},{4,8},{8,4},{12,0},{16,28},{20,24},{24,20},{28,16},{1,13},{... | collective-permute-start | bytes 1105928 | tf_op jit(solution)/shard_map/ppermute | solution.py:921
  42.5 11.5 %collective-permute-start.6 = (bf16[192,512]{1,0:T(8,128)(2,1)S(1)}, bf16[192,512]{1,0:T(8,128)(2,1)S(1)}, u32[]{:S(2)}, u32[]{:S(2)}) collective-permute-start(bf16[192,512]{1,0:T(8,128)(2,1)S(1)} %get-tuple-element.193.refs_20_), channel_id=1, source_target_pairs={{0,2},{1,3},{2,0},{3,1},{4,6},{5,7},{6,4},{7,5},{8,10},{9,11},{10,... | collective-permute-start | bytes 589832 | tf_op jit(solution)/shard_map/ppermute | solution.py:921
  51.3 5.9 %collective-permute-start.9 = (bf16[192,512]{1,0:T(8,128)(2,1)S(1)}, bf16[192,512]{1,0:T(8,128)(2,1)S(1)}, u32[]{:S(2)}, u32[]{:S(2)}) collective-permute-start(bf16[192,512]{1,0:T(8,128)(2,1)S(1)} %get-tuple-element.200.refs_21_), channel_id=1, source_target_pairs={{0,3},{1,2},{2,1},{3,0},{4,7},{5,6},{6,5},{7,4},{8,11},{9,10},{10,... | collective-permute-start | bytes 589832 | tf_op jit(solution)/shard_map/ppermute | solution.py:921
  54.0 4.3 %collective-permute-start.8 = (bf16[192,512]{1,0:T(8,128)(2,1)S(1)}, bf16[192,512]{1,0:T(8,128)(2,1)S(1)}, u32[]{:S(2)}, u32[]{:S(2)}) collective-permute-start(bf16[192,512]{1,0:T(8,128)(2,1)S(1)} %get-tuple-element.199.refs_19_), channel_id=1, source_target_pairs={{0,1},{1,0},{2,3},{3,2},{4,5},{5,4},{6,7},{7,6},{8,9},{9,8},{10,11... | collective-permute-start | bytes 589832 | tf_op jit(solution)/shard_map/ppermute | solution.py:921
  61.6 3.8 %collective-permute-start.14 = (bf16[256,768]{1,0:T(8,128)(2,1)S(1)}, bf16[256,768]{1,0:T(8,128)(2,1)S(1)}, u32[]{:S(2)}, u32[]{:S(2)}) collective-permute-start(bf16[256,768]{1,0:T(8,128)(2,1)S(1)} %get-tuple-element.205), channel_id=1, source_target_pairs={{0,1},{1,0},{2,3},{3,2},{4,5},{5,4},{6,7},{7,6},{8,9},{9,8},{10,11... | collective-permute-start | bytes 1179656 | tf_op jit(solution)/shard_map/ppermute | solution.py:921
  62.2 15.4 %collective-permute-start.17 = (bf16[192,1536]{1,0:T(8,128)(2,1)S(1)}, bf16[192,1536]{1,0:T(8,128)(2,1)S(1)}, u32[]{:S(2)}, u32[]{:S(2)}) collective-permute-start(bf16[192,1536]{1,0:T(8,128)(2,1)S(1)} %get-tuple-element.211.refs_1_), channel_id=1, source_target_pairs={{0,4},{4,0},{8,12},{12,8},{16,20},{20,16},{24,28},{28,24},{1,5},{5... | collective-permute-start | bytes 1769480 | tf_op jit(solution)/shard_map/ppermute | solution.py:921
  63.7 15.1 %collective-permute-start.18 = (bf16[192,1536]{1,0:T(8,128)(2,1)S(1)}, bf16[192,1536]{1,0:T(8,128)(2,1)S(1)}, u32[]{:S(2)}, u32[]{:S(2)}) collective-permute-start(bf16[192,1536]{1,0:T(8,128)(2,1)S(1)} %get-tuple-element.211.refs_1_), channel_id=1, source_target_pairs={{0,8},{4,12},{8,0},{12,4},{16,24},{20,28},{24,16},{28,20},{1,9},{5... | collective-permute-start | bytes 1769480 | tf_op jit(solution)/shard_map/ppermute | solution.py:921
  70.8 21.7 %collective-permute-start.16 = (bf16[512,768]{1,0:T(8,128)(2,1)S(1)}, bf16[512,768]{1,0:T(8,128)(2,1)S(1)}, u32[]{:S(2)}, u32[]{:S(2)}) collective-permute-start(bf16[512,768]{1,0:T(8,128)(2,1)S(1)} %get-tuple-element.210.refs_10_.refs_6_), channel_id=1, source_target_pairs={{0,2},{1,3},{2,0},{3,1},{4,6},{5,7},{6,4},{7,5},{8,10},{9,11},{10,... | collective-permute-start | bytes 2359304 | tf_op jit(solution)/shard_map/ppermute | solution.py:921
  78.9 8.0 %collective-permute-start.19 = (bf16[96,1536]{1,0:T(8,128)(2,1)S(1)}, bf16[96,1536]{1,0:T(8,128)(2,1)S(1)}, u32[]{:S(2)}, u32[]{:S(2)}) collective-permute-start(bf16[96,1536]{1,0:T(8,128)(2,1)S(1)} %get-tuple-element.222.refs_13_), channel_id=1, source_target_pairs={{0,4},{4,0},{8,12},{12,8},{16,20},{20,16},{24,28},{28,24},{1,5},{5... | collective-permute-start | bytes 884744 | tf_op jit(solution)/shard_map/ppermute | solution.py:921
  79.5 7.7 %collective-permute-start.20 = (bf16[96,1536]{1,0:T(8,128)(2,1)S(1)}, bf16[96,1536]{1,0:T(8,128)(2,1)S(1)}, u32[]{:S(2)}, u32[]{:S(2)}) collective-permute-start(bf16[96,1536]{1,0:T(8,128)(2,1)S(1)} %get-tuple-element.223), channel_id=1, source_target_pairs={{0,8},{4,12},{8,0},{12,4},{16,24},{20,28},{24,16},{28,20},{1,9},{5... | collective-permute-start | bytes 884744 | tf_op jit(solution)/shard_map/ppermute | solution.py:921
  98.7 15.3 %collective-permute-start.22 = (bf16[512,768]{1,0:T(8,128)(2,1)S(1)}, bf16[512,768]{1,0:T(8,128)(2,1)S(1)}, u32[]{:S(2)}, u32[]{:S(2)}) collective-permute-start(bf16[512,768]{1,0:T(8,128)(2,1)S(1)} %get-tuple-element.248.refs_5_.refs_8_), channel_id=1, source_target_pairs={{0,1},{1,0},{2,3},{3,2},{4,5},{5,4},{6,7},{7,6},{8,9},{9,8},{10,11... | collective-permute-start | bytes 2359304 | tf_op jit(solution)/shard_map/ppermute | solution.py:921
  99.0 19.6 %collective-permute-start.25 = (bf16[512,768]{1,0:T(8,128)(2,1)S(1)}, bf16[512,768]{1,0:T(8,128)(2,1)S(1)}, u32[]{:S(2)}, u32[]{:S(2)}) collective-permute-start(bf16[512,768]{1,0:T(8,128)(2,1)S(1)} %get-tuple-element.249.refs_11_.refs_1_), channel_id=1, source_target_pairs={{0,2},{1,3},{2,0},{3,1},{4,6},{5,7},{6,4},{7,5},{8,10},{9,11},{10,... | collective-permute-start | bytes 2359304 | tf_op jit(solution)/shard_map/ppermute | solution.py:921
  114.0 4.6 %collective-permute-start.24 = (bf16[512,768]{1,0:T(8,128)(2,1)S(1)}, bf16[512,768]{1,0:T(8,128)(2,1)S(1)}, u32[]{:S(2)}, u32[]{:S(2)}) collective-permute-start(bf16[512,768]{1,0:T(8,128)(2,1)S(1)} %get-tuple-element.257), channel_id=1, source_target_pairs={{0,1},{1,0},{2,3},{3,2},{4,5},{5,4},{6,7},{7,6},{8,9},{9,8},{10,11... | collective-permute-start | bytes 2359304 | tf_op jit(solution)/shard_map/ppermute | solution.py:921
  118.6 6.3 %collective-permute-start.29 = (bf16[512,768]{1,0:T(8,128)(2,1)S(1)}, bf16[512,768]{1,0:T(8,128)(2,1)S(1)}, u32[]{:S(2)}, u32[]{:S(2)}) collective-permute-start(bf16[512,768]{1,0:T(8,128)(2,1)S(1)} %collective-permute-done.25.refs_15_.refs_3_), channel_id=1, source_target_pairs={{0,1},{1,0},{2,3},{3,2},{4,5},{5,4},{6,7},{7,6},{8,9},{9,8},{10,11... | collective-permute-start | bytes 2359304 | tf_op jit(solution)/shard_map/ppermute | solution.py:921
  122.9 11.5 %collective-permute-start.26 = (bf16[784,512]{1,0:T(8,128)(2,1)S(1)}, bf16[784,512]{1,0:T(8,128)(2,1)S(1)}, u32[]{:S(2)}, u32[]{:S(2)}) collective-permute-start(bf16[784,512]{1,0:T(8,128)(2,1)S(1)} %get-tuple-element.264), channel_id=1, source_target_pairs={{0,1},{1,0},{2,3},{3,2},{4,5},{5,4},{6,7},{7,6},{8,9},{9,8},{10,11... | collective-permute-start | bytes 2408456 | tf_op jit(solution)/shard_map/ppermute | solution.py:921
  123.4 9.0 %collective-permute-start.27 = (bf16[208,512]{1,0:T(8,128)(2,1)S(1)}, bf16[208,512]{1,0:T(8,128)(2,1)S(1)}, u32[]{:S(2)}, u32[]{:S(2)}) collective-permute-start(bf16[208,512]{1,0:T(8,128)(2,1)S(1)} %get-tuple-element.265), channel_id=1, source_target_pairs={{0,2},{1,3},{2,0},{3,1},{4,6},{5,7},{6,4},{7,5},{8,10},{9,11},{10,... | collective-permute-start | bytes 638984 | tf_op jit(solution)/shard_map/ppermute | solution.py:921
  124.7 9.6 %collective-permute-start.28 = (bf16[208,512]{1,0:T(8,128)(2,1)S(1)}, bf16[208,512]{1,0:T(8,128)(2,1)S(1)}, u32[]{:S(2)}, u32[]{:S(2)}) collective-permute-start(bf16[208,512]{1,0:T(8,128)(2,1)S(1)} %get-tuple-element.266), channel_id=1, source_target_pairs={{0,3},{1,2},{2,1},{3,0},{4,7},{5,6},{6,5},{7,4},{8,11},{9,10},{10,... | collective-permute-start | bytes 638984 | tf_op jit(solution)/shard_map/ppermute | solution.py:921
  134.4 15.9 %collective-permute-start.30 = (bf16[384,768]{1,0:T(8,128)(2,1)S(1)}, bf16[384,768]{1,0:T(8,128)(2,1)S(1)}, u32[]{:S(2)}, u32[]{:S(2)}) collective-permute-start(bf16[384,768]{1,0:T(8,128)(2,1)S(1)} %get-tuple-element.281), channel_id=1, source_target_pairs={{0,8},{4,12},{8,0},{12,4},{16,24},{20,28},{24,16},{28,20},{1,9},{5... | collective-permute-start | bytes 1769480 | tf_op jit(solution)/shard_map/ppermute | solution.py:921
  136.1 35.6 %collective-permute-start.34 = (bf16[576,768]{1,0:T(8,128)(2,1)S(1)}, bf16[576,768]{1,0:T(8,128)(2,1)S(1)}, u32[]{:S(2)}, u32[]{:S(2)}) collective-permute-start(bf16[576,768]{1,0:T(8,128)(2,1)S(1)} %get-tuple-element.290.refs_7_), channel_id=1, source_target_pairs={{0,2},{1,3},{2,0},{3,1},{4,6},{5,7},{6,4},{7,5},{8,10},{9,11},{10,... | collective-permute-start | bytes 2654216 | tf_op jit(solution)/shard_map/ppermute | solution.py:921
  150.3 21.4 %collective-permute-start.32 = (bf16[384,768]{1,0:T(8,128)(2,1)S(1)}, bf16[384,768]{1,0:T(8,128)(2,1)S(1)}, u32[]{:S(2)}, u32[]{:S(2)}) collective-permute-start(bf16[384,768]{1,0:T(8,128)(2,1)S(1)} %get-tuple-element.288), channel_id=1, source_target_pairs={{0,4},{4,0},{8,12},{12,8},{16,20},{20,16},{24,28},{28,24},{1,5},{5... | collective-permute-start | bytes 1769480 | tf_op jit(solution)/shard_map/ppermute | solution.py:921
  151.7 20.0 %collective-permute-start.33 = (bf16[384,768]{1,0:T(8,128)(2,1)S(1)}, bf16[384,768]{1,0:T(8,128)(2,1)S(1)}, u32[]{:S(2)}, u32[]{:S(2)}) collective-permute-start(bf16[384,768]{1,0:T(8,128)(2,1)S(1)} %get-tuple-element.289), channel_id=1, source_target_pairs={{0,8},{4,12},{8,0},{12,4},{16,24},{20,28},{24,16},{28,20},{1,9},{5... | collective-permute-start | bytes 1769480 | tf_op jit(solution)/shard_map/ppermute | solution.py:921
  153.5 18.2 %collective-permute-start.31 = (bf16[192,768]{1,0:T(8,128)(2,1)S(1)}, bf16[192,768]{1,0:T(8,128)(2,1)S(1)}, u32[]{:S(2)}, u32[]{:S(2)}) collective-permute-start(bf16[192,768]{1,0:T(8,128)(2,1)S(1)} %add_convert_fusion.2), channel_id=1, source_target_pairs={{0,4},{4,0},{8,12},{12,8},{16,20},{20,16},{24,28},{28,24},{1,5},{5... | collective-permute-start | bytes 884744 | tf_op jit(solution)/shard_map/ppermute | solution.py:921
  154.2 13.0 %collective-permute-start.35 = (f32[4,768]{1,0:T(4,128)S(1)}, f32[4,768]{1,0:T(4,128)S(1)}, u32[]{:S(2)}, u32[]{:S(2)}) collective-permute-start(f32[4,768]{1,0:T(4,128)S(1)} %get-tuple-element.291), channel_id=1, source_target_pairs={{0,8},{4,12},{8,0},{12,4},{16,24},{20,28},{24,16},{28,20},{1,9},{5... | collective-permute-start | bytes 36872 | tf_op jit(solution)/shard_map/ppermute | solution.py:921
  171.7 19.8 %collective-permute-start.40 = (f32[4,768]{1,0:T(4,128)S(1)}, f32[4,768]{1,0:T(4,128)S(1)}, u32[]{:S(2)}, u32[]{:S(2)}) collective-permute-start(f32[4,768]{1,0:T(4,128)S(1)} %add.92), channel_id=1, source_target_pairs={{0,16},{4,20},{8,24},{12,28},{16,0},{20,4},{24,8},{28,12},{1,17},{... | collective-permute-start | bytes 36872 | tf_op jit(solution)/shard_map/ppermute | solution.py:921
  174.4 17.1 %collective-permute-start.37 = (bf16[576,768]{1,0:T(8,128)(2,1)S(1)}, bf16[576,768]{1,0:T(8,128)(2,1)S(1)}, u32[]{:S(2)}, u32[]{:S(2)}) collective-permute-start(bf16[576,768]{1,0:T(8,128)(2,1)S(1)} %get-tuple-element.296.refs_8_), channel_id=1, source_target_pairs={{0,1},{1,0},{2,3},{3,2},{4,5},{5,4},{6,7},{7,6},{8,9},{9,8},{10,11... | collective-permute-start | bytes 2654216 | tf_op jit(solution)/shard_map/ppermute | solution.py:921
  174.5 17.0 %collective-permute-start.39 = (bf16[192,768]{1,0:T(8,128)(2,1)S(1)}, bf16[192,768]{1,0:T(8,128)(2,1)S(1)}, u32[]{:S(2)}, u32[]{:S(2)}) collective-permute-start(bf16[192,768]{1,0:T(8,128)(2,1)S(1)} %add_convert_fusion), channel_id=1, source_target_pairs={{0,4},{4,0},{8,12},{12,8},{16,20},{20,16},{24,28},{28,24},{1,5},{5... | collective-permute-start | bytes 884744 | tf_op jit(solution)/shard_map/ppermute | solution.py:921
  176.0 15.5 %collective-permute-start.38 = (bf16[192,768]{1,0:T(8,128)(2,1)S(1)}, bf16[192,768]{1,0:T(8,128)(2,1)S(1)}, u32[]{:S(2)}, u32[]{:S(2)}) collective-permute-start(bf16[192,768]{1,0:T(8,128)(2,1)S(1)} %add_convert_fusion.1), channel_id=1, source_target_pairs={{0,8},{4,12},{8,0},{12,4},{16,24},{20,28},{24,16},{28,20},{1,9},{5... | collective-permute-start | bytes 884744 | tf_op jit(solution)/shard_map/ppermute | solution.py:921
  177.9 18.2 %collective-permute-start.36 = (bf16[672,512]{1,0:T(8,128)(2,1)S(1)}, bf16[672,512]{1,0:T(8,128)(2,1)S(1)}, u32[]{:S(2)}, u32[]{:S(2)}) collective-permute-start(bf16[672,512]{1,0:T(8,128)(2,1)S(1)} %get-tuple-element.294), channel_id=1, source_target_pairs={{0,2},{1,3},{2,0},{3,1},{4,6},{5,7},{6,4},{7,5},{8,10},{9,11},{10,... | collective-permute-start | bytes 2064392 | tf_op jit(solution)/shard_map/ppermute | solution.py:921
  191.7 22.2 %collective-permute-start.42 = (bf16[96,2304]{1,0:T(8,128)(2,1)S(1)}, bf16[96,2304]{1,0:T(8,128)(2,1)S(1)}, u32[]{:S(2)}, u32[]{:S(2)}) collective-permute-start(bf16[96,2304]{1,0:T(8,128)(2,1)S(1)} %pad_maximum_fusion), channel_id=1, source_target_pairs={{0,16},{4,20},{8,24},{12,28},{16,0},{20,4},{24,8},{28,12},{1,17},{... | collective-permute-start | bytes 1327112 | tf_op jit(solution)/shard_map/ppermute | solution.py:921
  192.4 16.2 %collective-permute-start.41 = (bf16[384,512]{1,0:T(8,128)(2,1)S(1)}, bf16[384,512]{1,0:T(8,128)(2,1)S(1)}, u32[]{:S(2)}, u32[]{:S(2)}) collective-permute-start(bf16[384,512]{1,0:T(8,128)(2,1)S(1)} %get-tuple-element.307), channel_id=1, source_target_pairs={{0,2},{1,3},{2,0},{3,1},{4,6},{5,7},{6,4},{7,5},{8,10},{9,11},{10,... | collective-permute-start | bytes 1179656 | tf_op jit(solution)/shard_map/ppermute | solution.py:921
  193.7 14.9 %collective-permute-start.43 = (bf16[384,384]{1,0:T(8,128)(2,1)S(1)}, bf16[384,384]{1,0:T(8,128)(2,1)S(1)}, u32[]{:S(2)}, u32[]{:S(2)}) collective-permute-start(bf16[384,384]{1,0:T(8,128)(2,1)S(1)} %get-tuple-element.314), channel_id=1, source_target_pairs={{0,4},{4,0},{8,12},{12,8},{16,20},{20,16},{24,28},{28,24},{1,5},{5... | collective-permute-start | bytes 884744 | tf_op jit(solution)/shard_map/ppermute | solution.py:921
  194.0 14.6 %collective-permute-start.44 = (f32[4,768]{1,0:T(4,128)S(1)}, f32[4,768]{1,0:T(4,128)S(1)}, u32[]{:S(2)}, u32[]{:S(2)}) collective-permute-start(f32[4,768]{1,0:T(4,128)S(1)} %add.99), channel_id=1, source_target_pairs={{0,4},{4,0},{8,12},{12,8},{16,20},{20,16},{24,28},{28,24},{1,5},{5... | collective-permute-start | bytes 36872 | tf_op jit(solution)/shard_map/ppermute | solution.py:921
  213.9 10.4 %collective-permute-start.45 = (bf16[384,512]{1,0:T(8,128)(2,1)S(1)}, bf16[384,512]{1,0:T(8,128)(2,1)S(1)}, u32[]{:S(2)}, u32[]{:S(2)}) collective-permute-start(bf16[384,512]{1,0:T(8,128)(2,1)S(1)} %get-tuple-element.316), channel_id=1, source_target_pairs={{0,2},{1,3},{2,0},{3,1},{4,6},{5,7},{6,4},{7,5},{8,10},{9,11},{10,... | collective-permute-start | bytes 1179656 | tf_op jit(solution)/shard_map/ppermute | solution.py:921
  215.2 8.5 %collective-permute-start.46 = (bf16[384,384]{1,0:T(8,128)(2,1)S(1)}, bf16[384,384]{1,0:T(8,128)(2,1)S(1)}, u32[]{:S(2)}, u32[]{:S(2)}) collective-permute-start(bf16[384,384]{1,0:T(8,128)(2,1)S(1)} %get-tuple-element.318), channel_id=1, source_target_pairs={{0,4},{4,0},{8,12},{12,8},{16,20},{20,16},{24,28},{28,24},{1,5},{5... | collective-permute-start | bytes 884744 | tf_op jit(solution)/shard_map/ppermute | solution.py:921
  215.8 5.2 %collective-permute-start.47 = (bf16[192,384]{1,0:T(8,128)(2,1)S(1)}, bf16[192,384]{1,0:T(8,128)(2,1)S(1)}, u32[]{:S(2)}, u32[]{:S(2)}) collective-permute-start(bf16[192,384]{1,0:T(8,128)(2,1)S(1)} %add_convert_fusion.4), channel_id=1, source_target_pairs={{0,8},{4,12},{8,0},{12,4},{16,24},{20,28},{24,16},{28,20},{1,9},{5... | collective-permute-start | bytes 442376 | tf_op jit(solution)/shard_map/ppermute | solution.py:921
  224.9 12.5 %collective-permute-start.48 = (bf16[1152,512]{1,0:T(8,128)(2,1)S(1)}, bf16[1152,512]{1,0:T(8,128)(2,1)S(1)}, u32[]{:S(2)}, u32[]{:S(2)}) collective-permute-start(bf16[1152,512]{1,0:T(8,128)(2,1)S(1)} %shard_map.232.refs_9_), channel_id=1, source_target_pairs={{0,1},{1,0},{2,3},{3,2},{4,5},{5,4},{6,7},{7,6},{8,9},{9,8},{10,11... | collective-permute-start | bytes 3538952 | tf_op jit(solution)/shard_map/ppermute | solution.py:921
  225.1 5.8 %collective-permute-start.50 = (bf16[96,384]{1,0:T(8,128)(2,1)S(1)}, bf16[96,384]{1,0:T(8,128)(2,1)S(1)}, u32[]{:S(2)}, u32[]{:S(2)}) collective-permute-start(bf16[96,384]{1,0:T(8,128)(2,1)S(1)} %add_convert_fusion.9), channel_id=1, source_target_pairs={{0,16},{4,20},{8,24},{12,28},{16,0},{20,4},{24,8},{28,12},{1,17},{... | collective-permute-start | bytes 221192 | tf_op jit(solution)/shard_map/ppermute | solution.py:921
  225.2 7.9 %collective-permute-start.49 = (bf16[192,384]{1,0:T(8,128)(2,1)S(1)}, bf16[192,384]{1,0:T(8,128)(2,1)S(1)}, u32[]{:S(2)}, u32[]{:S(2)}) collective-permute-start(bf16[192,384]{1,0:T(8,128)(2,1)S(1)} %add_convert_fusion.3), channel_id=1, source_target_pairs={{0,8},{4,12},{8,0},{12,4},{16,24},{20,28},{24,16},{28,20},{1,9},{5... | collective-permute-start | bytes 442376 | tf_op jit(solution)/shard_map/ppermute | solution.py:921
  233.1 8.9 %collective-permute-start.51 = (bf16[96,384]{1,0:T(8,128)(2,1)S(1)}, bf16[96,384]{1,0:T(8,128)(2,1)S(1)}, u32[]{:S(2)}, u32[]{:S(2)}) collective-permute-start(bf16[96,384]{1,0:T(8,128)(2,1)S(1)} %add_convert_fusion.8), channel_id=1, source_target_pairs={{0,16},{4,20},{8,24},{12,28},{16,0},{20,4},{24,8},{28,12},{1,17},{... | collective-permute-start | bytes 221192 | tf_op jit(solution)/shard_map/ppermute | solution.py:921
  (19 other events, 47.7 us)

commit v3 on v2

--- a/solution.py
+++ b/solution.py
@@ -120,32 +120,19 @@
         dst[pl.ds(pl.multiple_of(spots[b] * rows, rows), rows), cols] = turned[b * rows : (b + 1) * rows]
 
 
-def transpose_kernel(fast, spots, t0, t1, t2, t3, out):
-    rows = out.shape[1] // 4
-    for p, t in enumerate((t0, t1, t2, t3)):
-        transpose_into(out, t[0:rows, :], spots if fast else None, slice(p * rows, (p + 1) * rows))
+def transpose_kernel(fast, *refs):
+    count = (len(refs) - 4) // 2
+    spots, tokens, outs = refs[:count], refs[count : count + 4], refs[count + 4 :]
+    rows = outs[0].shape[1] // 4
+    for p, t in enumerate(tokens):
+        for spot, out in zip(spots, outs):
+            transpose_into(out, t[0:rows, :], spot if fast else None, slice(p * rows, (p + 1) * rows))
 
 
 def transposed(fast, spots, pieces, rows):
     width = pieces[0].shape[1]
-    return run(functools.partial(transpose_kernel, fast), 2, 8, (spots,), pieces, [((width, 4 * rows), BF16)])[0]
-
-
-def together_kernel(at_ref, p0, p1, p2, p3, out, sem):
-    part = out.shape[0] // 4
-    copies = []
-    for n, p in enumerate((p0, p1, p2, p3)):
-        spot = pl.ds(pl.multiple_of((at_ref[0] ^ n) * part, part), part)
-        copies.append(pltpu.make_async_copy(p.at[pl.ds(p.shape[0] - part, part), :], out.at[spot, :], sem.at[n]))
-        copies[-1].start()
-    for c in copies:
-        c.wait()
-
-
-def together(at, parts, shape, awaits=()):
-    return run(
-        together_kernel, 1, 4, (at,), (), [(shape, BF16)], [pltpu.SemaphoreType.DMA((4,))], awaits, apart=parts
-    )[0]
+    outs = [((width, 4 * rows), BF16)] * len(spots)
+    return run(functools.partial(transpose_kernel, fast), 2, 8, spots, pieces, outs)
 
 
 def project_kernel(piece, sp_ref, freq_ref, tok_ref, w_ref, qt_ref, kt_ref, k_ref, vt_ref, cs_ref):
@@ -472,12 +459,7 @@
     )
 
 
-PART_PLACES = (
-    *((0, n, 0, 2) for n in range(3)),
-    (0, 3, 0, 1),
-    (0, 3, 1, 1),
-    *((1, n, 0, 2) for n in range(4)),
-)
+PART_PLACES = ((0, 0, 0, 2), (0, 1, 0, 2), (0, 2, 0, 2), (0, 3, 0, 1), (0, 3, 1, 1)) + tuple((1, n, 0, 2) for n in range(4))
 
 
 def gather_weights(at_ref, parts, wgu, wd, sem):
@@ -485,9 +467,8 @@
     for n, (part, (which, quarter, first, count)) in enumerate(zip(parts, PART_PLACES)):
         dst = (wgu, wd)[which]
         half = dst.shape[0] // 8
-        spot = pl.multiple_of((at_ref[0] ^ quarter) * (2 * half) + first * half, half)
-        src = part.at[pl.ds(0, count * half), :]
-        copies.append(pltpu.make_async_copy(src, dst.at[pl.ds(spot, count * half), :], sem.at[n]))
+        spot = pl.ds(pl.multiple_of((at_ref[0] ^ quarter) * (2 * half) + first * half, half), count * half)
+        copies.append(pltpu.make_async_copy(part, dst.at[spot, :], sem.at[n]))
     for c in copies:
         c.start()
     return copies
@@ -627,7 +608,7 @@
 
 def mlp_back_kernel(at_ref, *refs):
     n_parts = len(PART_PLACES)
-    dm1_ref, dm0, wgu, wd, da_o, db_o, da_p, db_p, own, sib, dg_o, du_o, wgu_p, wd_p, dm1, sem = refs[n_parts:]
+    dm1_ref, dm0, wgu, wd, da_o, db_o, da_p, db_p, own, sib0, sib1, dg_o, du_o, wgu_p, wd_p, dm1, sem = refs[n_parts:]
     rows = dm0.shape[0]
     hidden = wd.shape[0]
     first = pltpu.make_async_copy(dm1_ref, dm1, sem.at[n_parts])
@@ -657,7 +638,8 @@
             for c in copies:
                 c.wait()
     own[...] = totals[0]
-    sib[...] = totals[1].astype(BF16)
+    sib0[...] = totals[1][0 : rows // 2].astype(BF16)
+    sib1[...] = totals[1][rows // 2 :].astype(BF16)
 
 
 def mlp_backward(at, dm0, dm1, wgu, wd, parts, da_o, db_o, da_p, db_p, awaits=()):
@@ -670,7 +652,7 @@
         18,
         (at,),
         (dm0, wgu, wd, da_o, db_o, da_p, db_p),
-        [((rows, width), F32), ((rows, width), BF16)] + [saved] * 2,
+        [((rows, width), F32)] + [((rows // 2, width), BF16)] * 2 + [saved] * 2,
         [
             pltpu.VMEM((width, 2 * hidden), BF16),
             pltpu.VMEM((hidden, width), BF16),
@@ -683,11 +665,12 @@
 
 
 def first_norm_kernel(
-    got_ref, dh2, own, xhat, inv, g1, sums2, a0, a1, a2, a3, w0, w1, w2, w3,
+    got_ref, got_late, dh2, own, xhat, inv, g1, sums2, a0, a1, a2, a3, w0, w1, w2, w3,
     dh1, d0, d1, d2, d3, ea, dat_scr, got, sem,
 ):
     gain_sum, bias_sum = 0.0, 0.0
-    copies = copies_of(got_ref, got, sem)
+    half = got_ref.shape[0]
+    copies = copies_of(got_ref, got, sem) + copies_of(got_late, got.at[pl.ds(half, half), :], sem.at[pl.ds(half // 128, half // 128)])
     for start in range(0, dh2.shape[0], 128):
         at = slice(start, start + 128)
         copies[start // 128].wait()
@@ -737,17 +720,20 @@
         [((rows, width), F32), d, ((4 * heads + 16, rows), BF16), d, d, ((2 * heads, width), BF16)],
         [pltpu.VMEM((rows, width), BF16), pltpu.VMEM((rows, width), BF16), pltpu.SemaphoreType.DMA((rows // 128,))],
         awaits,
-        apart=(got,),
+        apart=got,
     )
 
 
 def far_kernel(
-    fast, spots, dm0, dm1, dm2, dm3, ml2, ml3, wgu, wd, hid_o, first, second, dg, du, dmt, hids
+    fast, spots_a, spots_b, dm0, dm1, dm2, dm3, ml2, ml3, wgu, wd, hid_o,
+    a_first, a_second, b_first, b_second, dg, du, dmt_a, dmt_b, hids,
 ):
     rows = dm0.shape[0]
     hidden = wd.shape[0]
     for p, u in enumerate((dm0, dm1, dm2, dm3)):
-        transpose_into(dmt, u[...], spots if fast else None, slice(p * rows, (p + 1) * rows))
+        cols = slice(p * rows, (p + 1) * rows)
+        transpose_into(dmt_a, u[...], spots_a if fast else None, cols)
+        transpose_into(dmt_b, u[...], spots_b if fast else None, cols)
     for col in range(0, hidden, BLK):
         cols, ups = slice(col, col + BLK), slice(hidden + col, hidden + col + BLK)
         hids[0 : 2 * rows, :] = hid_o[:, cols]
@@ -759,30 +745,35 @@
             hids[(2 + block) * rows : (3 + block) * rows, :] = (act * up).astype(BF16)
             dg[at, cols] = (dhid * (up * (s + act * (1.0 - s)))).astype(BF16)
             du[at, cols] = (dhid * act).astype(BF16)
-        split_rows(mm(dmt[...], hids[...]), first.at[:, cols], second.at[:, cols])
-
-
-def far_rows(fast, spots, dm, ml, wgu, wd, hid, awaits=(), carry=()):
+        for turned, first, second, start in ((dmt_a, a_first, a_second, 0), (dmt_b, b_first, b_second, hidden // 2)):
+            lo, hi = max(col, start), min(col + BLK, start + hidden // 2)
+            if lo < hi:
+                there = slice(lo - start, hi - start)
+                split_rows(mm(turned[...], hids[:, lo - col : hi - col]), first.at[:, there], second.at[:, there])
+
+
+def far_rows(fast, spots, dm, ml, wgu, wd, hid, awaits=()):
     rows, width = dm[0].shape
     hidden = wd.shape[0]
+    half = ((width // 2, hidden // 2), BF16)
     return run(
         functools.partial(far_kernel, fast),
         8,
-        14,
-        (spots,),
+        18,
+        spots,
         (*dm, *ml, wgu, wd, hid),
-        [((width // 2, hidden), BF16)] * 2 + [((2 * rows, hidden), BF16)] * 2,
-        [pltpu.VMEM((width, 4 * rows), BF16), pltpu.VMEM((4 * rows, BLK), BF16)],
+        [half] * 4 + [((2 * rows, hidden), BF16)] * 2,
+        [*[pltpu.VMEM((width, 4 * rows), BF16)] * 2, pltpu.VMEM((4 * rows, BLK), BF16)],
         awaits,
-        carry,
     )
 
 
 def weight_kernel(
-    fast, spots, spots_d, d0, d1, d2, d3, ml0, ml1, ml2, ml3, dg, du, dg_f, du_f,
-    g_first, g_second, u_first, u_second, total, mlt, mlt_d, tail_scr, sem,
+    fast, spots_a, spots_b, d0, d1, d2, d3, ml0, ml1, ml2, ml3, dg, du, dg_f, du_f, da_first, da_second, db_first,
+    db_second, a_first, a_second, b_first, b_second, total, mlt_a, mlt_b, tail_scr, sem,
 ):
     rows = ml0.shape[0]
+    hidden = dg.shape[1]
     copies = [
         pltpu.make_async_copy(d.at[pl.ds(3 * HD, 16), :], tail_scr.at[p], sem.at[p]) for p, d in enumerate((d0, d1, d2, d3))
     ]
@@ -790,13 +781,14 @@
         c.start()
     for p, u in enumerate((ml0, ml1, ml2, ml3)):
         cols = slice(p * rows, (p + 1) * rows)
-        transpose_into(mlt, u[...], spots if fast else None, cols)
-        transpose_into(mlt_d, u[...], spots_d if fast else None, cols)
-    for turned, near, far, first, second in (
-        (mlt, dg, dg_f, g_first, g_second),
-        (mlt_d, du, du_f, u_first, u_second),
-    ):
-        split_rows(mm(turned[:, 0 : 2 * rows], near[...]) + mm(turned[:, 2 * rows :], far[...]), first, second)
+        transpose_into(mlt_a, u[...], spots_a if fast else None, cols)
+        transpose_into(mlt_b, u[...], spots_b if fast else None, cols)
+    for src, dst in ((da_first, a_first), (da_second, a_second), (db_first, b_first), (db_second, b_second)):
+        dst[:, hidden:] = src[...]
+    wide = slice(0, hidden)
+    for turned, near, far, first, second in ((mlt_a, dg, dg_f, a_first, a_second), (mlt_b, du, du_f, b_first, b_second)):
+        grad = mm(turned[:, 0 : 2 * rows], near[...]) + mm(turned[:, 2 * rows :], far[...])
+        split_rows(grad, first.at[:, wide], second.at[:, wide])
     for c in copies:
         c.wait()
     sums = [tail_scr[p].astype(F32) for p in range(4)]
@@ -805,16 +797,17 @@
     total[:, 512:768] = (joined[8:12] + joined[12:16])[:, 0:256]
 
 
-def weight_grads(fast, spots, spots_d, d, ml, near, far, awaits=()):
+def weight_grads(fast, spots, d, ml, near, far, down, awaits=()):
     rows, width = ml[0].shape
     hidden = near[0].shape[1]
+    chain = ((width // 2, hidden + hidden // 2), BF16)
     return run(
         functools.partial(weight_kernel, fast),
         6,
         16,
-        (spots, spots_d),
-        (*ml, *near, *far),
-        [((width // 2, hidden), BF16)] * 4 + [((4, width), F32)],
+        spots,
+        (*ml, *near, *far, *down),
+        [chain] * 4 + [((4, width), F32)],
         [
             *[pltpu.VMEM((width, 4 * rows), BF16)] * 2,
             pltpu.VMEM((4, 16, rows), BF16),
@@ -914,6 +907,10 @@
         apart=(core,),
         hbm=(0,),
     )[0]
+
+
+def split_halves(v):
+    return v[0 : v.shape[0] // 2], v[v.shape[0] // 2 :]
 
 
 def swap(v, bit, axis="tensor"):
@@ -949,14 +946,18 @@
     if kind == "mlp":
         gu, down = outs
         width = down.shape[1]
-        if len(sums) > 3:
-            sums = [u + sums[3][:, n * width : (n + 1) * width] for n, u in enumerate(sums[0:3])]
-        gu[:, 0, :] = sums[0]
-        gu[:, 1, :] = sums[1]
-        down[...] = sums[2]
+        one, two = sums[0:2]
+        if len(sums) > 2:
+            one += sums[2][:, 0 : one.shape[1]]
+            two += sums[2][:, one.shape[1] :]
+        gu[:, 0, :] = one[:, 0:width]
+        gu[:, 1, :] = two[:, 0:width]
+        down[...] = jnp.concatenate([one[:, width:], two[:, width:]], axis=1)
     else:
         qkv, out = outs
-        total = jnp.concatenate(sums, axis=1)
+        total = jnp.concatenate(sums[0:2], axis=1)
+        if len(sums) > 2:
+            total += sums[2]
         for c in range(3):
             qkv[c] = jnp.concatenate([total[:, (3 * h + c) * HD : (3 * h + c + 1) * HD] for h in range(3)], axis=1)
         out[...] = total[:, 9 * HD :].T
@@ -1044,8 +1045,8 @@
     n_dp = lax.axis_size("dp")
     fast = (width // n_dp) % 16 == 0
     order = list(range(bits_of(n_dp)))
-    order_d = order[1:2] + order[0:1] + order[2:]
-    spots, spots_d = spots_of(order, n_dp), spots_of(order_d, n_dp)
+    order_b = order[1:2] + order[0:1] + order[2:]
+    spots, spots_b = (spots_of(u, n_dp) for u in (order, order_b))
 
     def arranged(v, at):
         if fast:
@@ -1057,74 +1058,72 @@
     wo0 = out_weight
     wo1, wt1 = swap(wo0, 1), swap(wt, 1)
     wgu = gate_up_weight.reshape(width, -1)
-    part_a = jnp.concatenate([quarter_of(down_weight), quarter_of(out_weight)], axis=0)
-    part_b = quarter_of(wgu)
-    pa0 = swap(part_a, 2)
+    part_a, part_b = quarter_of(down_weight), quarter_of(wgu)
 
     proj = [project(0, sp, freqs, tok0, wt), project(1, sp, freqs, tok1, wt, awaits=(part_a, part_b, wt1))]
     (tok2,) = gate(tok2)
     tok3 = swap(tok2, 1)
+    wo2 = swap(wo0, 2)
     tok = (tok0, tok1, tok2, tok3)
-    *more, part_b = project(2, sp, freqs, tok2, wt, carry=(part_b,))
+    *more, part_a = project(2, sp, freqs, tok2, wt, carry=(part_a,))
+    proj.append(more)
+    pa0 = swap(part_a, 2)
+    *more, part_b = project(3, sp, freqs, tok3, wt, carry=(part_b,))
     proj.append(more)
     pb0 = swap(part_b, 2)
-    proj.append(project(3, sp, freqs, tok3, wt))
     qt, kt, k, vt, cs = zip(*proj)
     o2, o3, q2, q3 = attend(1, sp, qt, k, vt, (wo1,))
-    o2, pa0 = gate(o2, pa0)
+    o2, o3, wo2, pa0 = gate(o2, o3, wo2, pa0)
     pa1, pa2, pa3 = swap(pa0, 1, "dp"), swap(pa0, 2, "dp"), swap(pa0, 3, "dp")
     g2 = swap(o2, 2)
     o0, o1, q0, q1 = attend(0, sp, qt, k, vt)
-    o1, o3 = gate(o1, o3, awaits=(pb0,))
-    g3 = swap(o3, 3)
-    tok_t = transposed(fast, spots, [arranged(u, spots) for u in tok], rows)
-    (o1,) = gate(o1, awaits=(g2,))
-    g1 = swap(o1, 1)
-    wo2 = together(quarter, (pa0, pa1, pa2, pa3), wo0.shape, (g3, g1))
-    wo2, pb0 = gate(wo2, pb0)
-    wo3 = swap(wo2, 1)
+    o1, o3, pb0, wo2 = gate(o1, o3, pb0, wo2, awaits=(g2, pa1, pa2, pa3))
+    g1, g3, wo3 = swap(o1, 1), swap(o3, 3), swap(wo2, 1)
+    wo = (wo0, wo1, wo2, wo3)
     pb1, pb2 = swap(pb0, 1, "dp"), swap(pb0, 2, "dp")
-    wo = (wo0, wo1, wo2, wo3)
+    toks = transposed(fast, (spots_b, spots), tok, rows)
+    if not fast:
+        toks = [arranged(toks[0].T, u).T for u in (spots_b, spots)]
+    (g3,) = gate(g3)
 
     gain1, bias1, gain2, bias2 = (u.reshape(1, width) for u in (norm1_gain, norm1_bias, norm2_gain, norm2_bias))
     ml0, xhat1, inv1, *halves = out_project((o0, g1, g2, g3), wo, tokens, gain1, bias1)
     acc, da_o, db_o, hid_o, ml1 = mlp_own(ml0, [swap(u, 1) for u in halves], wgu, down_weight)
-    (ml0,) = gate(ml0)
+    half2, half1 = park((), ((pb2, 0), (pb1, 1)))
+    half2, half1, ml0 = gate(half2, half1, ml0)
+    parts = (pb0, pb1, pb2, swap(half2, 1, "dp"), swap(half1, 2, "dp"), pa0, pa1, pa2, pa3)
     ml2 = swap(ml0, 2)
-    kept = park((*kt, *k, *vt, q0, q1, q2, q3, tok_t))
-    kt, k, vt, (q0, q1, q2, q3, tok_t) = kept[0:4], kept[4:8], kept[8:12], kept[12:17]
-    half2, half1 = park((), ((pb2, 0), (pb1, 1)))
-    parts = (pb0, pb1, pb2, swap(half2, 1, "dp"), swap(half1, 2, "dp"), pa0, pa1, pa2, pa3)
+    kept = park((*kt, *k, *vt, q0, q1, q2, q3, *toks))
+    kt, k, vt, (q0, q1, q2, q3, *toks) = kept[0:4], kept[4:8], kept[8:12], kept[12:18]
     own, sib, da_p, db_p = mlp_peer(quarter, ml0, ml1, acc, parts)
     (sib,) = gate(sib, awaits=(ml2,))
     output, dh2, dm0, sums2 = mid_norm(xhat1, own, swap(sib, 1), out_grad, gain1, bias1, gain2, bias2)
     dm0, ml2 = gate(dm0, ml2)
     dm1, dm2 = swap(dm0, 1), swap(dm0, 2)
     ml3 = swap(ml2, 1)
-    own, sib, dg_o, du_o = mlp_backward(quarter, dm0, dm1, wgu, down_weight, parts, da_o, db_o, da_p, db_p)
-    (sib,) = gate(sib, awaits=(ml3,))
+    own, sib0, sib1, dg_o, du_o = mlp_backward(quarter, dm0, dm1, wgu, down_weight, parts, da_o, db_o, da_p, db_p)
+    sib0, sib1 = gate(sib0, sib1, awaits=(ml3,))
     dh1, d0, d1, d2, d3, ea = first_norm_back(
-        dh2, own, swap(sib, 1), xhat1, inv1, gain1, sums2, (o0, g1, g2, g3), wo, (dm2,)
-    )
-    d1, d2, d3 = gate(d1, d2, d3)
+        dh2, own, (swap(sib0, 1), swap(sib1, 1)), xhat1, inv1, gain1, sums2, (o0, g1, g2, g3), wo
+    )
+    d1, d2, d3, dm2 = gate(d1, d2, d3, dm2)
     dm3 = swap(dm2, 1)
     d = (d0, swap(d1, 1), swap(d2, 2), swap(d3, 3))
-    ml = [arranged(u, spots) for u in (ml0, ml1, ml2, ml3)]
-    dm = [arranged(u, spots_d) for u in (dm0, dm1, dm2, dm3)]
-    d_first, d_second, dg_f, du_f = far_rows(fast, spots_d, dm, ml[2:], wgu, down_weight, hid_o)
-    d_second, wt = gate(d_second, wt, awaits=d[1:])
-    dn = scatter_steps(d_first, d_second, order_d)
-    dn1 = dn.advance()
+    ml, dm, both = (ml0, ml1, ml2, ml3), (dm0, dm1, dm2, dm3), (spots, spots_b)
+    *down, dg_f, du_f = far_rows(fast, both, dm, ml[2:], wgu, down_weight, hid_o)
+    (wt,) = gate(wt, awaits=d[1:])
     wt2 = swap(wt, 2)
-    g_first, g_second, u_first, u_second, sums = weight_grads(
-        fast, spots, spots_d, d, ml, (dg_o, du_o), (dg_f, du_f)
-    )
-    g_second, u_second, sums, dn.parts[-1] = gate(g_second, u_second, sums, dn1)
-    dn.next_sent()
-    dn2 = dn.advance()
-    sums_got = swap(sums, 2, "dp")
-    gg, gu = scatter_steps(g_first, g_second, order), scatter_steps(u_first, u_second, order_d)
-    gg1, gu1 = gg.advance(), gu.advance()
+    a_first, a_second, b_first, b_second, sums = weight_grads(
+        fast, both, d, ml, (dg_o, du_o), (dg_f, du_f), down
+    )
+    if not fast:
+        a_first, a_second = split_halves(arranged(jnp.concatenate([a_first, a_second]).T, spots).T)
+        b_first, b_second = split_halves(arranged(jnp.concatenate([b_first, b_second]).T, spots_b).T)
+    a_second, b_second, sums = gate(a_second, b_second, sums)
+    sum_bits = order[2:3] + order[1::-1] + order[3:]
+    sums_got = swap(sums, 1 << sum_bits[0], "dp")
+    chain_a, chain_b = scatter_steps(a_first, a_second, order), scatter_steps(b_first, b_second, order_b)
+    a_got, b_got = chain_a.advance(), chain_b.advance()
 
     arrange = jnp.zeros((8, 128), BF16)
     if not fast:
@@ -1143,61 +1142,60 @@
         o=(o0, o1, o2, o3),
         d=d,
         cs=cs,
-        tok_t=tok_t,
-    )
-    near0, far0, core0, grad0, e_own = back(0, given=(ea,))
-    far0, dn.parts[-1], gg.parts[-1], gu.parts[-1], wt2, sums_got = gate(far0, dn2, gg1, gu1, wt2, sums_got)
-    for chain in (dn, gg, gu):
+    )
+    near0, far0, core0, grad0, e_own = back(0, tok_t=toks[0], given=(ea,))
+    far0, chain_a.parts[-1], chain_b.parts[-1], wt2, sums_got = gate(far0, a_got, b_got, wt2, sums_got)
+    for chain in (chain_a, chain_b):
         chain.next_sent()
-    got0, gg2, gu2 = swap(far0, 2), gg.advance(), gu.advance()
+    a_got, b_got, got0 = chain_a.advance(), chain_b.advance(), swap(far0, 2)
+    sums = sums + sums_got
+    sums_got = swap(sums, 1 << sum_bits[1], "dp")
+    near1, far1, core1, first, second = back(1, tok_t=toks[0], given=(core0, grad0))
+    far1, second, chain_a.parts[-1], chain_b.parts[-1], sums_got, wt2 = gate(far1, second, a_got, b_got, sums_got, wt2)
+    for chain in (chain_a, chain_b):
+        chain.next_sent()
+    c1 = scatter_steps(first, second, order_b)
+    c1_got, mlp3 = c1.advance(), advance_together((chain_a, chain_b))
     wt3 = swap(wt2, 1)
-    sums = sums + sums_got
-    sums_got = swap(sums, 4, "dp") if n_dp > 4 else sums_got
-    near1, far1, core1, first, second = back(1, given=(core0, grad0))
-    far1, second, gg.parts[-1], gu.parts[-1], sums_got = gate(far1, second, gg2, gu2, sums_got, awaits=(wt3,))
-    for chain in (gg, gu):
-        chain.next_sent()
-    c1 = scatter_steps(first, second, order)
-    c1_got, mlp3 = c1.advance(), advance_together((gg, gu, dn))
     got1 = swap(far1, 2)
     sums = sums + sums_got
-    sums_got = swap(sums, 1, "dp")
-    near2, far2, core2, first, second = back(2, given=(core1, got0, e_own, arrange))
-    far2, second, c1.parts[-1], sums_got = gate(far2, second, c1_got, sums_got, awaits=(got1,) if mlp3 is None else (got1, mlp3))
+    sums_got = swap(sums, 1 << sum_bits[2], "dp")
+    near2, far2, core2, first, second = back(2, tok_t=toks[1], given=(core1, got0, e_own, arrange))
+    far2, second, c1.parts[-1], sums_got = gate(far2, second, c1_got, sums_got, awaits=(got1, wt3))
     c1.next_sent()
     sums = sums + sums_got
-    bit = 8
-    while bit < n_dp:
-        sums = sums + swap(sums, bit, "dp")
-        bit *= 2
+    for bit in sum_bits[3:]:
+        sums = sums + swap(sums, 1 << bit, "dp")
     c2 = scatter_steps(first, second, order)
     c2_got, c1_got, got2 = c2.advance(), c1.advance(), swap(far2, 2)
-    c2.parts[-1], c1.parts[-1] = gate(c2_got, c1_got)
+    (c2.parts[-1],) = gate(c2_got)
     c2.next_sent()
-    c1.next_sent()
-    c2_got, c1_got = c2.advance(), c1.advance()
+    c2_got = c2.advance()
+    mlp, shard = [chain_a.all_parts(), chain_b.all_parts()], width // n_dp
+    if mlp3 is not None:
+        mlp.append([mlp3])
+    if fast:
+        hidden = down_weight.shape[0]
+        gu_part, down_part = last_sums("mlp", shard, mlp, [((shard, 2, hidden), F32), ((shard, hidden), F32)])
     core = swap(join(core2, got1, got2), 1)
     input_grad = input_near(dh1, (near0, near1, near2), (got0, got1, got2), wt, wt2)
     c2.parts[-1], c1.parts[-1] = gate(c2_got, c1_got)
     c2.next_sent()
     c1.next_sent()
-    mlp = [chain.all_parts() for chain in (gg, gu, dn)]
-    attention = (c1.all_parts(), c2.all_parts())
-    if mlp3 is not None:
-        mlp.append([mlp3])
-    shard = width // n_dp
+    both = advance_together((c1, c2))
+    attention = [c1.all_parts(), c2.all_parts()]
+    if both is not None:
+        attention.append([both])
+    input_grad = input_back(input_grad, core, wt1, wt3)
     if fast:
-        hidden = down_weight.shape[0]
-        gu_part, down_part = last_sums("mlp", shard, mlp, [((shard, 2, hidden), F32), ((shard, hidden), F32)])
-        input_grad = input_back(input_grad, core, wt1, wt3)
         qkv_part, out_part = last_sums(
             "attention", shard, attention, [((3, shard, 3 * HD), F32), ((3 * HD, shard), F32)]
         )
         qkv_part = jnp.transpose(qkv_part, (1, 0, 2))
     else:
-        input_grad = input_back(input_grad, core, wt1, wt3)
-        gg, gu, down_part = first_sums(mlp, shard)
-        gu_part = jnp.stack([gg, gu], axis=1)
+        one, two = first_sums(mlp, shard)
+        gu_part = jnp.stack([one[:, 0:width], two[:, 0:width]], axis=1)
+        down_part = jnp.concatenate([one[:, width:], two[:, width:]], axis=1)
         total = jnp.concatenate(first_sums(attention, shard), axis=1)
         out_part = total[:, 9 * HD :].T
         qkv_part = jnp.transpose(total[:, 0 : 9 * HD].reshape(shard, 3, 3, HD), (0, 2, 1, 3)).reshape(shard, 3, 3 * HD)

time: 250 us -> 243 us (0.972)
  waiting for transfers between devices: 62.8 us -> 47.1 us
  local copies, waits for them, and re-layouts: 7.32 us -> 11.5 us
  Pallas kernels: 126 us -> 130 us
    ppermute x52 -> x51, waiting for transfers between devices: 62.8 us -> 47.1 us  [swap(): return lax.ppermute(v, axis, [(i, i ^ bit) for i in range(n)])]
    unnamed x35 -> x52, local copies, waits for them, and re-layouts: 6.5 us -> 10.7 us
    pallas_call x43 -> x41, Pallas kernels: 126 us -> 130 us  [run(): pl.pallas_call(body, in_specs=[pl.BlockSpec(memory_space=pltpu.SMEM)] * l...]
    ppermute x52 -> x51, starting transfers between devices: 45.5 us -> 46.7 us  [swap(): return lax.ppermute(v, axis, [(i, i ^ bit) for i in range(n)])]
  transfers between devices with their start and end apart: 52 -> 51, of which waited for: 21 -> 23; matrix products, arithmetic and copies ran while one was open for 2% -> 2% of each run, Pallas kernels for 48% -> 49%
where the time goes in v3:
time: 243 us; the launch traced here: 239 us
  Pallas kernels  130 us (53%)
  waiting for transfers between devices  47.1 us (19%)
  starting transfers between devices  46.7 us (19%)
  local copies, waits for them, and re-layouts  11.5 us (5%)
    pallas_call x41, Pallas kernels, run(): pl.pallas_call(body, in_specs=[pl.BlockSpec(memory_space=pltpu.SMEM)] * l...  130 us
    ppermute x51, waiting for transfers between devices, swap(): return lax.ppermute(v, axis, [(i, i ^ bit) for i in range(n)])  47.1 us
    ppermute x51, starting transfers between devices, swap(): return lax.ppermute(v, axis, [(i, i ^ bit) for i in range(n)])  46.7 us
    unnamed x52, local copies, waits for them, and re-layouts  10.7 us
  transfers between devices with their start and end apart: 51, of which 23 were waited for; matrix products, arithmetic and copies ran while one was open for 2% of the time, Pallas kernels for 49%

profile of v3, /device:TPU:0, one launch (start us, length us, event | category | flops | bytes accessed | tf_op | source)
XLA Modules:
  0.0 238.8 jit_solution(10848689406872380495)
XLA Ops:
  3.5 2.9 %collective-permute-start.2 = (bf16[528,768]{1,0:T(8,128)(2,1)}, bf16[528,768]{1,0:T(8,128)(2,1)}, u32[]{:S(2)}, u32[]{:S(2)}) collective-permute-start(bf16[528,768]{1,0:T(8,128)(2,1)} %fusion.1.refs_2_), channel_id=1, source_target_pairs={{0,2},{1,3},{2,0},{3,1},{4,6},{5,7},{6,4},{7,5},{8,10},{9,11},{10,... | collective-permute-start | bytes 2433032 | tf_op jit(solution)/shard_map/ppermute | solution.py:918
  6.3 2.1 copy.68
  8.6 2.2 shard_map.195
  11.0 2.2 shard_map.196
  13.2 11.8 %collective-permute-done.2.refs_1_ = bf16[528,768]{1,0:T(8,128)(2,1)} collective-permute-done((bf16[528,768]{1,0:T(8,128)(2,1)}, bf16[528,768]{1,0:T(8,128)(2,1)}, u32[]{:S(2)}, u32[]{:S(2)}) %collective-permute-start.2) | collective-permute-done | bytes 811040 | tf_op jit(solution)/shard_map/ppermute | solution.py:918
  25.5 1.7 collective-permute-start.5
  27.3 2.1 shard_map.198
  29.7 1.5 shard_map.199
  31.2 1.8 collective-permute-start.11
  33.1 7.8 %shard_map.200 = (bf16[192,512]{1,0:T(8,128)(2,1)S(1)}, bf16[192,512]{1,0:T(8,128)(2,1)S(1)}, bf16[3,128,512]{2,1,0:T(8,128)(2,1)S(1)}, bf16[3,128,512]{2,1,0:T(8,128)(2,1)S(1)}) custom-call(s32[9]{0:T(128)S(1)} %pad_add_fusion.refs_0_, bf16[3,128,512]{2,1,0:T(8,128)(2,1)S(1)} %get-tuple-element.185.refs_1_, ...), custom_call_target="tpu_custom_call" | custom-call | flops 1320000000 | bytes 262144 | tf_op jit(solution)/shard_map/pallas_call | solution.py:46
  41.7 2.8 %collective-permute-start.10 = (bf16[192,768]{1,0:T(8,128)(2,1)S(1)}, bf16[192,768]{1,0:T(8,128)(2,1)S(1)}, u32[]{:S(2)}, u32[]{:S(2)}) collective-permute-start(bf16[192,768]{1,0:T(8,128)(2,1)S(1)} %get-tuple-element.201.refs_6_), channel_id=1, source_target_pairs={{0,12},{4,8},{8,4},{12,0},{16,28},{20,24},{24,20},{28,16},{1,13},{... | collective-permute-start | bytes 884744 | tf_op jit(solution)/shard_map/ppermute | solution.py:918
  45.2 1.7 collective-permute-start.7
  46.9 6.8 %shard_map.202 = (bf16[192,512]{1,0:T(8,128)(2,1)S(1)}, bf16[192,512]{1,0:T(8,128)(2,1)S(1)}, bf16[3,128,512]{2,1,0:T(8,128)(2,1)S(1)}, bf16[3,128,512]{2,1,0:T(8,128)(2,1)S(1)}) custom-call(s32[9]{0:T(128)S(1)} %pad_add_fusion.refs_0_, bf16[3,128,512]{2,1,0:T(8,128)(2,1)S(1)} %get-tuple-element.202.refs_1_, ...), custom_call_target="tpu_custom_call" | custom-call | flops 1320000000 | bytes 262144 | tf_op jit(solution)/shard_map/pallas_call | solution.py:46
  53.8 3.9 %collective-permute-done.7.refs_0_.refs_2_.refs_10_ = bf16[192,512]{1,0:T(8,128)(2,1)S(1)} collective-permute-done((bf16[192,512]{1,0:T(8,128)(2,1)S(1)}, bf16[192,512]{1,0:T(8,128)(2,1)S(1)}, u32[]{:S(2)}, u32[]{:S(2)}) %collective-permute-start.7) | collective-permute-done | bytes 196640 | tf_op jit(solution)/shard_map/ppermute | solution.py:918
  57.8 1.9 collective-permute-start.15
  59.7 1.6 collective-permute-start.12
  61.3 1.5 collective-permute-start.13
  62.9 3.4 %shard_map.204 = (bf16[768,2048]{1,0:T(8,128)(2,1)S(1)}, bf16[768,2048]{1,0:T(8,128)(2,1)S(1)}) custom-call(s32[8]{0:T(128)S(1)} %add_add_fusion.1.refs_0_.refs_1_, s32[8]{0:T(128)S(1)} %add_add_fusion.refs_1_.refs_0_, bf16[528,768]{1,0:T(8,128)(2,1)} %fusion.1.refs_2_, bf16[528,768]{1,0:T(8,128)(2,1)} %collective-permute-done.refs_2_.refs_3_, ...), custom_call_target="tpu_custom_call" | custom-call | flops 330000000 | bytes 262144 | tf_op jit(solution)/shard_map/pallas_call | solution.py:46
  71.0 5.4 %shard_map.207 = (f32[1024,768]{1,0:T(8,128)S(1)}, bf16[1024,768]{1,0:T(8,128)(2,1)S(1)}, bf16[1024,768]{1,0:T(8,128)(2,1)S(1)}, bf16[1024,768]{1,0:T(8,128)(2,1)S(1)}, bf16[512,768]{1,0:T(8,128)(2,1)S(1)}) custom-call(bf16[256,768]{1,0:T(8,128)(2,1)S(1)} %collective-permute-done.17.refs_0_, bf16[256,768]{1,0:T(8,128)(2,1)S(1)} %collective-permute-done.18.refs_1_, ...), custom_call_target="tpu_custom_call" | custom-call | flops 825000000 | bytes 262144 | tf_op jit(solution)/shard_map/pallas_call | solution.py:46
  79.3 1.6 collective-permute-start.21
  80.8 3.8 %shard_map.210 = (bf16[3,128,512]{2,1,0:T(8,128)(2,1)S(1)}, bf16[3,128,512]{2,1,0:T(8,128)(2,1)S(1)}, bf16[3,128,512]{2,1,0:T(8,128)(2,1)S(1)}, bf16[3,128,512]{...) custom-call(bf16[3,128,512]{2,1,0:T(8,128)(2,1)S(1)} %get-tuple-elem, ...), custom_call_target="tpu_custom_call" | custom-call | flops 495000000 | bytes 262144 | tf_op jit(solution)/shard_map/pallas_call | solution.py:46
  84.6 1.6 copy-done.4
  88.0 5.3 %shard_map.211 = (f32[512,768]{1,0:T(8,128)S(1)}, bf16[512,768]{1,0:T(8,128)(2,1)S(1)}, bf16[1024,768]{1,0:T(8,128)(2,1)S(1)}, bf16[1024,768]{1,0:T(8,128)(2,1)S(1)}) custom-call(s32[1]{0:T(128)} %bitcast.5.refs_0_, bf16[192,1536]{1,0:T(8,128)(2,1)S(1)} %get-tuple-element.210.refs_1_, bf16[192,1536]{1,0:T(8,128)(2,1)S(1)} %collective-permute-done.13.refs_1_.refs_2_, ...), custom_call_target="tpu_custom_call" | custom-call | flops 990000000 | bytes 262144 | tf_op jit(solution)/shard_map/pallas_call | solution.py:46
  93.3 3.8 %collective-permute-done.19.refs_0_.refs_2_ = bf16[512,768]{1,0:T(8,128)(2,1)S(1)} collective-permute-done((bf16[512,768]{1,0:T(8,128)(2,1)S(1)}, bf16[512,768]{1,0:T(8,128)(2,1)S(1)}, u32[]{:S(2)}, u32[]{:S(2)}) %collective-permute-start.19) | collective-permute-done | bytes 786464 | tf_op jit(solution)/shard_map/ppermute | solution.py:918
  97.8 1.7 collective-permute-done.22.refs_0_
  99.5 3.5 %shard_map.213 = (bf16[512,768]{1,0:T(8,128)(2,1)}, f32[512,768]{1,0:T(8,128)S(1)}, bf16[512,768]{1,0:T(8,128)(2,1)S(1)}, f32[2,768]{1,0:T(2,128)S(1)}) custom-call(bf16[512,768]{1,0:T(8,128)(2,1)S(1)} %collective-permute-done.22.refs_0_, f32[512,768]{1,0:T(8,128)S(1)} %get-tuple-element.243.refs_1_.refs_4_, ...), custom_call_target="tpu_custom_call" | custom-call | flops 495000000 | bytes 262144 | tf_op jit(solution)/shard_map/pallas_call | solution.py:46
  105.3 13.1 %shard_map.215 = (f32[512,768]{1,0:T(8,128)S(1)}, bf16[256,768]{1,0:T(8,128)(2,1)S(1)}, bf16[256,768]{1,0:T(8,128)(2,1)S(1)}, bf16[1024,768]{1,0:T(8,128)(2,1)S(1)}, bf16[1024,768]{1,0:T(8,128)(2,1)S(1)}) custom-call(s32[1]{0:T(128)} %bitcast.5.refs_0_, bf16[192,1536]{1,0:T(8,128)(2,1)S(1)} %get-tuple-element.210.refs_1_, ...), custom_call_target="tpu_custom_call" | custom-call | flops 1815000064 | bytes 262144 | tf_op jit(solution)/shard_map/pallas_call | solution.py:46
  120.9 4.2 %shard_map.217 = (f32[512,768]{1,0:T(8,128)S(1)}, bf16[208,512]{1,0:T(8,128)(2,1)S(1)}, bf16[784,512]{1,0:T(8,128)(2,1)S(1)}, bf16[208,512]{1,0:T(8,128)(2,1)S(1...) custom-call(bf16[256,768]{1,0:T(8,128)(2,1)S(1)} %collective-permute-done.25.refs_0_, ...), custom_call_target="tpu_custom_call" | custom-call | flops 825000000 | bytes 262144 | tf_op jit(solution)/shard_map/pallas_call | solution.py:46
  127.5 8.7 %shard_map.219 = (bf16[384,384]{1,0:T(8,128)(2,1)S(1)}, bf16[384,384]{1,0:T(8,128)(2,1)S(1)}, bf16[384,384]{1,0:T(8,128)(2,1)S(1)}, bf16[384,384]{1,0:T(8,128)(2...) custom-call(s32[8]{0:T(128)S(1)} %add_add_fusion.refs_1_.refs_0_, ...), custom_call_target="tpu_custom_call" | custom-call | flops 1320000000 | bytes 262144 | tf_op jit(solution)/shard_map/pallas_call | solution.py:46
  137.6 7.3 %shard_map.221 = (bf16[384,1152]{1,0:T(8,128)(2,1)S(1)}, bf16[384,1152]{1,0:T(8,128)(2,1)S(1)}, bf16[384,1152]{1,0:T(8,128)(2,1)S(1)}, bf16[384,1152]{1,0:T(8,128)(2,1)S(1)}, f32[4,768]{1,0:T(4,128)S(1)}) custom-call(s32[8]{0:T(128)S(1)} %add_add_fusion.refs_1_.refs_0_, s32[8]{0:T(128)S(1)} %add_add_fusion.1.refs_0_.refs_1_, ...), custom_call_target="tpu_custom_call" | custom-call | flops 990000000 | bytes 262144 | tf_op jit(solution)/shard_map/pallas_call | solution.py:46
  145.5 1.5 collective-permute-start.33
  148.5 2.6 %collective-permute-start.35 = (f32[4,768]{1,0:T(4,128)S(1)}, f32[4,768]{1,0:T(4,128)S(1)}, u32[]{:S(2)}, u32[]{:S(2)}) collective-permute-start(f32[4,768]{1,0:T(4,128)S(1)} %get-tuple-element.310), channel_id=1, source_target_pairs={{0,16},{4,20},{8,24},{12,28},{16,0},{20,4},{24,8},{28,12},{1,17},{... | collective-permute-start | bytes 36872 | tf_op jit(solution)/shard_map/ppermute | solution.py:918
  151.1 13.2 %shard_map.223 = (bf16[192,512]{1,0:T(8,128)(2,1)S(1)}, bf16[672,512]{1,0:T(8,128)(2,1)S(1)}, bf16[192,512]{1,0:T(8,128)(2,1)S(1)}, bf16[768,192]{1,0:T(8,128)(2,1)S(1)}, bf16[192,768]{1,0:T(8,128)(2,1)S(1)}) custom-call(s32[9]{0:T(128)S(1)} %pad_add_fusion.refs_0_, s32[8]{0:T(128)S(1)} %add_add_fusion.refs_1_.refs_0_, ...), custom_call_target="tpu_custom_call" | custom-call | flops 1980000000 | bytes 262144 | tf_op jit(solution)/shard_map/pallas_call | solution.py:46
  164.3 2.1 collective-permute-done.35.refs_5_
  169.2 2.7 %collective-permute-start.37 = (bf16[192,1152]{1,0:T(8,128)(2,1)S(1)}, bf16[192,1152]{1,0:T(8,128)(2,1)S(1)}, u32[]{:S(2)}, u32[]{:S(2)}) collective-permute-start(bf16[192,1152]{1,0:T(8,128)(2,1)S(1)} %add_convert_fusion.1), channel_id=1, source_target_pairs={{0,8},{4,12},{8,0},{12,4},{16,24},{20,28},{24,16},{28,20},{1,9},{5... | collective-permute-start | bytes 1327112 | tf_op jit(solution)/shard_map/ppermute | solution.py:918
  172.9 13.2 %shard_map.225 = (bf16[192,512]{1,0:T(8,128)(2,1)S(1)}, bf16[384,512]{1,0:T(8,128)(2,1)S(1)}, bf16[384,512]{1,0:T(8,128)(2,1)S(1)}, bf16[384,384]{1,0:T(8,128)(2,1)S(1)}, bf16[384,384]{1,0:T(8,128)(2,1)S(1)}) custom-call(s32[9]{0:T(128)S(1)} %pad_add_fusion.refs_0_, s32[8]{0:T(128)S(1)} %add_add_fusion.refs_1_.refs_0_, ...), custom_call_target="tpu_custom_call" | custom-call | flops 1980000000 | bytes 262144 | tf_op jit(solution)/shard_map/pallas_call | solution.py:46
  187.8 1.9 collective-permute-start.42
  189.9 1.6 collective-permute-start.45
  191.5 12.9 %shard_map.227 = (bf16[192,512]{1,0:T(8,128)(2,1)S(1)}, bf16[384,512]{1,0:T(8,128)(2,1)S(1)}, bf16[768,512]{1,0:T(8,128)(2,1)S(1)}, bf16[384,384]{1,0:T(8,128)(2,1)S(1)}, bf16[384,384]{1,0:T(8,128)(2,1)S(1)}) custom-call(s32[9]{0:T(128)S(1)} %pad_add_fusion.refs_0_, s32[8]{0:T(128)S(1)} %add_add_fusion.refs_1_.refs_0_, ...), custom_call_target="tpu_custom_call" | custom-call | flops 1980000000 | bytes 262144 | tf_op jit(solution)/shard_map/pallas_call | solution.py:46
  204.5 1.5 collective-permute-start.44
  206.1 8.3 %collective-permute-done.46.refs_1_ = bf16[384,384]{1,0:T(8,128)(2,1)S(1)} collective-permute-done((bf16[384,384]{1,0:T(8,128)(2,1)S(1)}, bf16[384,384]{1,0:T(8,128)(2,1)S(1)}, u32[]{:S(2)}, u32[]{:S(2)}) %collective-permute-start.46) | collective-permute-done | bytes 294944 | tf_op jit(solution)/shard_map/ppermute | solution.py:918
  214.4 3.2 %shard_map.230 = (f32[96,2,768]{2,1,0:T(2,128)}, f32[96,768]{1,0:T(8,128)}) custom-call(bf16[384,1152]{1,0:T(8,128)(2,1)S(1)} %get-tuple-element.318.refs_0_, bf16[384,1152]{1,0:T(8,128)(2,1)S(1)} %get-tuple-element.319.refs_1_, bf16[192,1152]{1,0:T(8,128)(2,1)S(1)} %get-tuple-element.334.refs_2_, bf16[384,1152]{1,0:T(8,128)(2,1)S(1)} %get-tuple-element.320.refs_3_, ...), custom_call_target="tpu_custom_call" | custom-call | flops 330000000 | bytes 262144 | tf_op jit(solution)/shard_map/pallas_call | solution.py:46
  219.6 1.7 collective-permute-start.48
  221.4 2.8 %shard_map.232.refs_0_.refs_1_ = f32[512,768]{1,0:T(8,128)S(1)} custom-call(bf16[672,512]{1,0:T(8,128)(2,1)S(1)} %collective-permute-done.36.refs_32_.refs_0_, bf16[384,512]{1,0:T(8,128)(2,1)S(1)} %collective-permute-done.40.refs_0_.refs_1_, bf16[384,512]{1,0:T(8,128)(2,1)S(1)} %collective-permute-done.44.refs_2_, f32[512,768]{1,0:T(8,128)S(1)} %copy-done.9, ...), custom_call_target="tpu_custom_call" | custom-call | flops 495000000 | bytes 262144 | tf_op jit(solution)/shard_map/pallas_call | solution.py:46
  225.8 1.6 collective-permute-start.50
  228.0 3.7 %shard_map.234.refs_7_ = f32[512,768]{1,0:T(8,128)} custom-call(bf16[1152,512]{1,0:T(8,128)(2,1)S(1)} %collective-permute-done.47.refs_0_, f32[512,768]{1,0:T(8,128)S(1)} %shard_map.232.refs_0_.refs_1_, bf16[576,768]{1,0:T(8,128)(2,1)} %collective-permute-done.1.refs_6_.refs_2_, bf16[576,768]{1,0:T(8,128)(2,1)S(1)} %collective-permute-done.41.refs_1_.refs_3_, ...), custom_call_target="tpu_custom_call" | custom-call | flops 495000000 | bytes 262144 | tf_op jit(solution)/shard_map/pallas_call | solution.py:46
  231.7 3.6 %collective-permute-done.50.refs_6_ = bf16[96,768]{1,0:T(8,128)(2,1)S(1)} collective-permute-done((bf16[96,768]{1,0:T(8,128)(2,1)S(1)}, bf16[96,768]{1,0:T(8,128)(2,1)S(1)}, u32[]{:S(2)}, u32[]{:S(2)}) %collective-permute-start.50) | collective-permute-done | bytes 147488 | tf_op jit(solution)/shard_map/ppermute | solution.py:918
  236.6 1.7 shard_map.235
  (175 shorter events, 37.4 us)
Async XLA Ops:
  1.9 9.1 %collective-permute-start.1 = (bf16[576,768]{1,0:T(8,128)(2,1)S(1)}, bf16[576,768]{1,0:T(8,128)(2,1)}, u32[]{:S(2)}, u32[]{:S(2)}) collective-permute-start(bf16[576,768]{1,0:T(8,128)(2,1)S(1)} %bitcast.10), channel_id=1, source_target_pairs={{0,1},{1,0},{2,3},{3,2},{4,5},{5,4},{6,7},{7,6},{8,9},{9,8},{10,11... | collective-permute-start | bytes 2654216 | tf_op jit(solution)/shard_map/ppermute | solution.py:918
  3.3 7.6 %collective-permute-start = (bf16[528,768]{1,0:T(8,128)(2,1)}, bf16[528,768]{1,0:T(8,128)(2,1)}, u32[]{:S(2)}, u32[]{:S(2)}) collective-permute-start(bf16[528,768]{1,0:T(8,128)(2,1)} %fusion.1.refs_2_), channel_id=1, source_target_pairs={{0,1},{1,0},{2,3},{3,2},{4,5},{5,4},{6,7},{7,6},{8,9},{9,8},{10,11... | collective-permute-start | bytes 2433032 | tf_op jit(solution)/shard_map/ppermute | solution.py:918
  3.5 21.5 %collective-permute-start.2 = (bf16[528,768]{1,0:T(8,128)(2,1)}, bf16[528,768]{1,0:T(8,128)(2,1)}, u32[]{:S(2)}, u32[]{:S(2)}) collective-permute-start(bf16[528,768]{1,0:T(8,128)(2,1)} %fusion.1.refs_2_), channel_id=1, source_target_pairs={{0,2},{1,3},{2,0},{3,1},{4,6},{5,7},{6,4},{7,5},{8,10},{9,11},{10,... | collective-permute-start | bytes 2433032 | tf_op jit(solution)/shard_map/ppermute | solution.py:918
  25.0 4.7 %collective-permute-start.3 = (bf16[528,768]{1,0:T(8,128)(2,1)}, bf16[528,768]{1,0:T(8,128)(2,1)S(1)}, u32[]{:S(2)}, u32[]{:S(2)}) collective-permute-start(bf16[528,768]{1,0:T(8,128)(2,1)} %get-tuple-element.183.refs_2_.refs_4_), channel_id=1, source_target_pairs={{0,1},{1,0},{2,3},{3,2},{4,5},{5,4},{6,7},{7,6},{8,9},{9,8},{10,11... | collective-permute-start | bytes 2433032 | tf_op jit(solution)/shard_map/ppermute | solution.py:918
  25.0 8.1 %collective-permute-start.4 = (bf16[192,768]{1,0:T(8,128)(2,1)S(1)}, bf16[192,768]{1,0:T(8,128)(2,1)S(1)}, u32[]{:S(2)}, u32[]{:S(2)}) collective-permute-start(bf16[192,768]{1,0:T(8,128)(2,1)S(1)} %copy-done.12), channel_id=1, source_target_pairs={{0,1},{1,0},{2,3},{3,2},{4,5},{5,4},{6,7},{7,6},{8,9},{9,8},{10,11... | collective-permute-start | bytes 884744 | tf_op jit(solution)/shard_map/ppermute | solution.py:918
  25.5 15.4 %collective-permute-start.5 = (bf16[192,768]{1,0:T(8,128)(2,1)S(1)}, bf16[192,768]{1,0:T(8,128)(2,1)S(1)}, u32[]{:S(2)}, u32[]{:S(2)}) collective-permute-start(bf16[192,768]{1,0:T(8,128)(2,1)S(1)} %copy-done.12), channel_id=1, source_target_pairs={{0,2},{1,3},{2,0},{3,1},{4,6},{5,7},{6,4},{7,5},{8,10},{9,11},{10,... | collective-permute-start | bytes 884744 | tf_op jit(solution)/shard_map/ppermute | solution.py:918
  29.4 12.3 %collective-permute-start.6 = (bf16[192,768]{1,0:T(8,128)(2,1)S(1)}, bf16[192,768]{1,0:T(8,128)(2,1)S(1)}, u32[]{:S(2)}, u32[]{:S(2)}) collective-permute-start(bf16[192,768]{1,0:T(8,128)(2,1)S(1)} %get-tuple-element.199), channel_id=1, source_target_pairs={{0,2},{1,3},{2,0},{3,1},{4,6},{5,7},{6,4},{7,5},{8,10},{9,11},{10,... | collective-permute-start | bytes 884744 | tf_op jit(solution)/shard_map/ppermute | solution.py:918
  31.2 26.4 %collective-permute-start.11 = (bf16[192,1536]{1,0:T(8,128)(2,1)S(1)}, bf16[192,1536]{1,0:T(8,128)(2,1)S(1)}, u32[]{:S(2)}, u32[]{:S(2)}) collective-permute-start(bf16[192,1536]{1,0:T(8,128)(2,1)S(1)} %get-tuple-element.208), channel_id=1, source_target_pairs={{0,2},{1,3},{2,0},{3,1},{4,6},{5,7},{6,4},{7,5},{8,10},{9,11},{10,... | collective-permute-start | bytes 1769480 | tf_op jit(solution)/shard_map/ppermute | solution.py:918
  41.7 16.0 %collective-permute-start.10 = (bf16[192,768]{1,0:T(8,128)(2,1)S(1)}, bf16[192,768]{1,0:T(8,128)(2,1)S(1)}, u32[]{:S(2)}, u32[]{:S(2)}) collective-permute-start(bf16[192,768]{1,0:T(8,128)(2,1)S(1)} %get-tuple-element.201.refs_6_), channel_id=1, source_target_pairs={{0,12},{4,8},{8,4},{12,0},{16,28},{20,24},{24,20},{28,16},{1,13},{... | collective-permute-start | bytes 884744 | tf_op jit(solution)/shard_map/ppermute | solution.py:918
  44.5 13.2 %collective-permute-start.8 = (bf16[192,768]{1,0:T(8,128)(2,1)S(1)}, bf16[192,768]{1,0:T(8,128)(2,1)S(1)}, u32[]{:S(2)}, u32[]{:S(2)}) collective-permute-start(bf16[192,768]{1,0:T(8,128)(2,1)S(1)} %get-tuple-element.201.refs_6_), channel_id=1, source_target_pairs={{0,4},{4,0},{8,12},{12,8},{16,20},{20,16},{24,28},{28,24},{1,5},{5... | collective-permute-start | bytes 884744 | tf_op jit(solution)/shard_map/ppermute | solution.py:918
  45.0 12.7 %collective-permute-start.9 = (bf16[192,768]{1,0:T(8,128)(2,1)S(1)}, bf16[192,768]{1,0:T(8,128)(2,1)S(1)}, u32[]{:S(2)}, u32[]{:S(2)}) collective-permute-start(bf16[192,768]{1,0:T(8,128)(2,1)S(1)} %get-tuple-element.201.refs_6_), channel_id=1, source_target_pairs={{0,8},{4,12},{8,0},{12,4},{16,24},{20,28},{24,16},{28,20},{1,9},{5... | collective-permute-start | bytes 884744 | tf_op jit(solution)/shard_map/ppermute | solution.py:918
  45.2 12.5 %collective-permute-start.7 = (bf16[192,512]{1,0:T(8,128)(2,1)S(1)}, bf16[192,512]{1,0:T(8,128)(2,1)S(1)}, u32[]{:S(2)}, u32[]{:S(2)}) collective-permute-start(bf16[192,512]{1,0:T(8,128)(2,1)S(1)} %get-tuple-element.200.refs_20_), channel_id=1, source_target_pairs={{0,2},{1,3},{2,0},{3,1},{4,6},{5,7},{6,4},{7,5},{8,10},{9,11},{10,... | collective-permute-start | bytes 589832 | tf_op jit(solution)/shard_map/ppermute | solution.py:918
  57.7 8.7 %collective-permute-start.16 = (bf16[192,768]{1,0:T(8,128)(2,1)S(1)}, bf16[192,768]{1,0:T(8,128)(2,1)S(1)}, u32[]{:S(2)}, u32[]{:S(2)}) collective-permute-start(bf16[192,768]{1,0:T(8,128)(2,1)S(1)} %get-tuple-element.216.refs_6_.refs_14_), channel_id=1, source_target_pairs={{0,1},{1,0},{2,3},{3,2},{4,5},{5,4},{6,7},{7,6},{8,9},{9,8},{10,11... | collective-permute-start | bytes 884744 | tf_op jit(solution)/shard_map/ppermute | solution.py:918
  57.8 8.5 %collective-permute-start.15 = (bf16[192,512]{1,0:T(8,128)(2,1)S(1)}, bf16[192,512]{1,0:T(8,128)(2,1)S(1)}, u32[]{:S(2)}, u32[]{:S(2)}) collective-permute-start(bf16[192,512]{1,0:T(8,128)(2,1)S(1)} %get-tuple-element.214.refs_21_), channel_id=1, source_target_pairs={{0,3},{1,2},{2,1},{3,0},{4,7},{5,6},{6,5},{7,4},{8,11},{9,10},{10,... | collective-permute-start | bytes 589832 | tf_op jit(solution)/shard_map/ppermute | solution.py:918
  59.6 6.7 %collective-permute-start.14 = (bf16[192,512]{1,0:T(8,128)(2,1)S(1)}, bf16[192,512]{1,0:T(8,128)(2,1)S(1)}, u32[]{:S(2)}, u32[]{:S(2)}) collective-permute-start(bf16[192,512]{1,0:T(8,128)(2,1)S(1)} %get-tuple-element.211.refs_19_), channel_id=1, source_target_pairs={{0,1},{1,0},{2,3},{3,2},{4,5},{5,4},{6,7},{7,6},{8,9},{9,8},{10,11... | collective-permute-start | bytes 589832 | tf_op jit(solution)/shard_map/ppermute | solution.py:918
  59.7 16.7 %collective-permute-start.12 = (bf16[192,1536]{1,0:T(8,128)(2,1)S(1)}, bf16[192,1536]{1,0:T(8,128)(2,1)S(1)}, u32[]{:S(2)}, u32[]{:S(2)}) collective-permute-start(bf16[192,1536]{1,0:T(8,128)(2,1)S(1)} %get-tuple-element.210.refs_1_), channel_id=1, source_target_pairs={{0,8},{4,12},{8,0},{12,4},{16,24},{20,28},{24,16},{28,20},{1,9},{5... | collective-permute-start | bytes 1769480 | tf_op jit(solution)/shard_map/ppermute | solution.py:918
  61.3 15.4 %collective-permute-start.13 = (bf16[192,1536]{1,0:T(8,128)(2,1)S(1)}, bf16[192,1536]{1,0:T(8,128)(2,1)S(1)}, u32[]{:S(2)}, u32[]{:S(2)}) collective-permute-start(bf16[192,1536]{1,0:T(8,128)(2,1)S(1)} %get-tuple-element.210.refs_1_), channel_id=1, source_target_pairs={{0,4},{4,0},{8,12},{12,8},{16,20},{20,16},{24,28},{28,24},{1,5},{5... | collective-permute-start | bytes 1769480 | tf_op jit(solution)/shard_map/ppermute | solution.py:918
  68.7 2.3 collective-permute-start.18
  77.5 19.6 %collective-permute-start.19 = (bf16[512,768]{1,0:T(8,128)(2,1)S(1)}, bf16[512,768]{1,0:T(8,128)(2,1)S(1)}, u32[]{:S(2)}, u32[]{:S(2)}) collective-permute-start(bf16[512,768]{1,0:T(8,128)(2,1)S(1)} %get-tuple-element.225.refs_10_.refs_6_), channel_id=1, source_target_pairs={{0,2},{1,3},{2,0},{3,1},{4,6},{5,7},{6,4},{7,5},{8,10},{9,11},{10,... | collective-permute-start | bytes 2359304 | tf_op jit(solution)/shard_map/ppermute | solution.py:918
  78.1 8.8 %collective-permute-start.20 = (bf16[96,1536]{1,0:T(8,128)(2,1)S(1)}, bf16[96,1536]{1,0:T(8,128)(2,1)S(1)}, u32[]{:S(2)}, u32[]{:S(2)}) collective-permute-start(bf16[96,1536]{1,0:T(8,128)(2,1)S(1)} %get-tuple-element.226), channel_id=1, source_target_pairs={{0,4},{4,0},{8,12},{12,8},{16,20},{20,16},{24,28},{28,24},{1,5},{5... | collective-permute-start | bytes 884744 | tf_op jit(solution)/shard_map/ppermute | solution.py:918
  79.3 8.7 %collective-permute-start.21 = (bf16[96,1536]{1,0:T(8,128)(2,1)S(1)}, bf16[96,1536]{1,0:T(8,128)(2,1)S(1)}, u32[]{:S(2)}, u32[]{:S(2)}) collective-permute-start(bf16[96,1536]{1,0:T(8,128)(2,1)S(1)} %get-tuple-element.227), channel_id=1, source_target_pairs={{0,8},{4,12},{8,0},{12,4},{16,24},{20,28},{24,16},{28,20},{1,9},{5... | collective-permute-start | bytes 884744 | tf_op jit(solution)/shard_map/ppermute | solution.py:918
  97.1 2.4 collective-permute-start.22
  102.9 2.4 collective-permute-start.24
  103.1 15.4 %collective-permute-start.23 = (bf16[512,768]{1,0:T(8,128)(2,1)S(1)}, bf16[512,768]{1,0:T(8,128)(2,1)S(1)}, u32[]{:S(2)}, u32[]{:S(2)}) collective-permute-start(bf16[512,768]{1,0:T(8,128)(2,1)S(1)} %get-tuple-element.263.refs_6_.refs_8_), channel_id=1, source_target_pairs={{0,1},{1,0},{2,3},{3,2},{4,5},{5,4},{6,7},{7,6},{8,9},{9,8},{10,11... | collective-permute-start | bytes 2359304 | tf_op jit(solution)/shard_map/ppermute | solution.py:918
  103.5 21.6 %collective-permute-start.27 = (bf16[512,768]{1,0:T(8,128)(2,1)S(1)}, bf16[512,768]{1,0:T(8,128)(2,1)S(1)}, u32[]{:S(2)}, u32[]{:S(2)}) collective-permute-start(bf16[512,768]{1,0:T(8,128)(2,1)S(1)} %get-tuple-element.264.refs_11_.refs_2_), channel_id=1, source_target_pairs={{0,2},{1,3},{2,0},{3,1},{4,6},{5,7},{6,4},{7,5},{8,10},{9,11},{10,... | collective-permute-start | bytes 2359304 | tf_op jit(solution)/shard_map/ppermute | solution.py:918
  125.2 2.4 collective-permute-start.31
  125.4 11.4 %collective-permute-start.28 = (bf16[784,512]{1,0:T(8,128)(2,1)S(1)}, bf16[784,512]{1,0:T(8,128)(2,1)S(1)}, u32[]{:S(2)}, u32[]{:S(2)}) collective-permute-start(bf16[784,512]{1,0:T(8,128)(2,1)S(1)} %get-tuple-element.281), channel_id=1, source_target_pairs={{0,1},{1,0},{2,3},{3,2},{4,5},{5,4},{6,7},{7,6},{8,9},{9,8},{10,11... | collective-permute-start | bytes 2408456 | tf_op jit(solution)/shard_map/ppermute | solution.py:918
  125.7 10.5 %collective-permute-start.29 = (bf16[208,512]{1,0:T(8,128)(2,1)S(1)}, bf16[208,512]{1,0:T(8,128)(2,1)S(1)}, u32[]{:S(2)}, u32[]{:S(2)}) collective-permute-start(bf16[208,512]{1,0:T(8,128)(2,1)S(1)} %get-tuple-element.282), channel_id=1, source_target_pairs={{0,2},{1,3},{2,0},{3,1},{4,6},{5,7},{6,4},{7,5},{8,10},{9,11},{10,... | collective-permute-start | bytes 638984 | tf_op jit(solution)/shard_map/ppermute | solution.py:918
  126.3 10.5 %collective-permute-start.30 = (bf16[208,512]{1,0:T(8,128)(2,1)S(1)}, bf16[208,512]{1,0:T(8,128)(2,1)S(1)}, u32[]{:S(2)}, u32[]{:S(2)}) collective-permute-start(bf16[208,512]{1,0:T(8,128)(2,1)S(1)} %get-tuple-element.283), channel_id=1, source_target_pairs={{0,3},{1,2},{2,1},{3,0},{4,7},{5,6},{6,5},{7,4},{8,11},{9,10},{10,... | collective-permute-start | bytes 638984 | tf_op jit(solution)/shard_map/ppermute | solution.py:918
  144.9 22.0 %collective-permute-start.32 = (bf16[384,1152]{1,0:T(8,128)(2,1)S(1)}, bf16[384,1152]{1,0:T(8,128)(2,1)S(1)}, u32[]{:S(2)}, u32[]{:S(2)}) collective-permute-start(bf16[384,1152]{1,0:T(8,128)(2,1)S(1)} %get-tuple-element.307), channel_id=1, source_target_pairs={{0,4},{4,0},{8,12},{12,8},{16,20},{20,16},{24,28},{28,24},{1,5},{5... | collective-permute-start | bytes 2654216 | tf_op jit(solution)/shard_map/ppermute | solution.py:918
  145.5 21.9 %collective-permute-start.33 = (bf16[384,1152]{1,0:T(8,128)(2,1)S(1)}, bf16[384,1152]{1,0:T(8,128)(2,1)S(1)}, u32[]{:S(2)}, u32[]{:S(2)}) collective-permute-start(bf16[384,1152]{1,0:T(8,128)(2,1)S(1)} %get-tuple-element.308), channel_id=1, source_target_pairs={{0,8},{4,12},{8,0},{12,4},{16,24},{20,28},{24,16},{28,20},{1,9},{5... | collective-permute-start | bytes 2654216 | tf_op jit(solution)/shard_map/ppermute | solution.py:918
  147.0 21.3 %collective-permute-start.34 = (bf16[576,768]{1,0:T(8,128)(2,1)S(1)}, bf16[576,768]{1,0:T(8,128)(2,1)S(1)}, u32[]{:S(2)}, u32[]{:S(2)}) collective-permute-start(bf16[576,768]{1,0:T(8,128)(2,1)S(1)} %get-tuple-element.309.refs_7_), channel_id=1, source_target_pairs={{0,2},{1,3},{2,0},{3,1},{4,6},{5,7},{6,4},{7,5},{8,10},{9,11},{10,... | collective-permute-start | bytes 2654216 | tf_op jit(solution)/shard_map/ppermute | solution.py:918
  148.5 17.9 %collective-permute-start.35 = (f32[4,768]{1,0:T(4,128)S(1)}, f32[4,768]{1,0:T(4,128)S(1)}, u32[]{:S(2)}, u32[]{:S(2)}) collective-permute-start(f32[4,768]{1,0:T(4,128)S(1)} %get-tuple-element.310), channel_id=1, source_target_pairs={{0,16},{4,20},{8,24},{12,28},{16,0},{20,4},{24,8},{28,12},{1,17},{... | collective-permute-start | bytes 36872 | tf_op jit(solution)/shard_map/ppermute | solution.py:918
  168.5 17.6 %collective-permute-start.38 = (bf16[192,1152]{1,0:T(8,128)(2,1)S(1)}, bf16[192,1152]{1,0:T(8,128)(2,1)S(1)}, u32[]{:S(2)}, u32[]{:S(2)}) collective-permute-start(bf16[192,1152]{1,0:T(8,128)(2,1)S(1)} %add_convert_fusion), channel_id=1, source_target_pairs={{0,4},{4,0},{8,12},{12,8},{16,20},{20,16},{24,28},{28,24},{1,5},{5... | collective-permute-start | bytes 1327112 | tf_op jit(solution)/shard_map/ppermute | solution.py:918
  169.2 16.9 %collective-permute-start.37 = (bf16[192,1152]{1,0:T(8,128)(2,1)S(1)}, bf16[192,1152]{1,0:T(8,128)(2,1)S(1)}, u32[]{:S(2)}, u32[]{:S(2)}) collective-permute-start(bf16[192,1152]{1,0:T(8,128)(2,1)S(1)} %add_convert_fusion.1), channel_id=1, source_target_pairs={{0,8},{4,12},{8,0},{12,4},{16,24},{20,28},{24,16},{28,20},{1,9},{5... | collective-permute-start | bytes 1327112 | tf_op jit(solution)/shard_map/ppermute | solution.py:918
  171.9 14.2 %collective-permute-start.39 = (f32[4,768]{1,0:T(4,128)S(1)}, f32[4,768]{1,0:T(4,128)S(1)}, u32[]{:S(2)}, u32[]{:S(2)}) collective-permute-start(f32[4,768]{1,0:T(4,128)S(1)} %add.77), channel_id=1, source_target_pairs={{0,8},{4,12},{8,0},{12,4},{16,24},{20,28},{24,16},{28,20},{1,9},{5... | collective-permute-start | bytes 36872 | tf_op jit(solution)/shard_map/ppermute | solution.py:918
  172.0 17.9 %collective-permute-start.36 = (bf16[672,512]{1,0:T(8,128)(2,1)S(1)}, bf16[672,512]{1,0:T(8,128)(2,1)S(1)}, u32[]{:S(2)}, u32[]{:S(2)}) collective-permute-start(bf16[672,512]{1,0:T(8,128)(2,1)S(1)} %get-tuple-element.313), channel_id=1, source_target_pairs={{0,2},{1,3},{2,0},{3,1},{4,6},{5,7},{6,4},{7,5},{8,10},{9,11},{10,... | collective-permute-start | bytes 2064392 | tf_op jit(solution)/shard_map/ppermute | solution.py:918
  186.2 18.3 %collective-permute-start.43 = (f32[4,768]{1,0:T(4,128)S(1)}, f32[4,768]{1,0:T(4,128)S(1)}, u32[]{:S(2)}, u32[]{:S(2)}) collective-permute-start(f32[4,768]{1,0:T(4,128)S(1)} %add.78), channel_id=1, source_target_pairs={{0,4},{4,0},{8,12},{12,8},{16,20},{20,16},{24,28},{28,24},{1,5},{5... | collective-permute-start | bytes 36872 | tf_op jit(solution)/shard_map/ppermute | solution.py:918
  187.3 17.2 %collective-permute-start.41 = (bf16[576,768]{1,0:T(8,128)(2,1)S(1)}, bf16[576,768]{1,0:T(8,128)(2,1)S(1)}, u32[]{:S(2)}, u32[]{:S(2)}) collective-permute-start(bf16[576,768]{1,0:T(8,128)(2,1)S(1)} %get-tuple-element.327.refs_8_), channel_id=1, source_target_pairs={{0,1},{1,0},{2,3},{3,2},{4,5},{5,4},{6,7},{7,6},{8,9},{9,8},{10,11... | collective-permute-start | bytes 2654216 | tf_op jit(solution)/shard_map/ppermute | solution.py:918
  187.3 17.2 %collective-permute-start.40 = (bf16[384,512]{1,0:T(8,128)(2,1)S(1)}, bf16[384,512]{1,0:T(8,128)(2,1)S(1)}, u32[]{:S(2)}, u32[]{:S(2)}) collective-permute-start(bf16[384,512]{1,0:T(8,128)(2,1)S(1)} %get-tuple-element.326), channel_id=1, source_target_pairs={{0,2},{1,3},{2,0},{3,1},{4,6},{5,7},{6,4},{7,5},{8,10},{9,11},{10,... | collective-permute-start | bytes 1179656 | tf_op jit(solution)/shard_map/ppermute | solution.py:918
  187.8 16.7 %collective-permute-start.42 = (bf16[384,384]{1,0:T(8,128)(2,1)S(1)}, bf16[384,384]{1,0:T(8,128)(2,1)S(1)}, u32[]{:S(2)}, u32[]{:S(2)}) collective-permute-start(bf16[384,384]{1,0:T(8,128)(2,1)S(1)} %get-tuple-element.331), channel_id=1, source_target_pairs={{0,8},{4,12},{8,0},{12,4},{16,24},{20,28},{24,16},{28,20},{1,9},{5... | collective-permute-start | bytes 884744 | tf_op jit(solution)/shard_map/ppermute | solution.py:918
  189.9 24.4 %collective-permute-start.45 = (bf16[96,2304]{1,0:T(8,128)(2,1)S(1)}, bf16[96,2304]{1,0:T(8,128)(2,1)S(1)}, u32[]{:S(2)}, u32[]{:S(2)}) collective-permute-start(bf16[96,2304]{1,0:T(8,128)(2,1)S(1)} %pad_maximum_fusion), channel_id=1, source_target_pairs={{0,16},{4,20},{8,24},{12,28},{16,0},{20,4},{24,8},{28,12},{1,17},{... | collective-permute-start | bytes 1327112 | tf_op jit(solution)/shard_map/ppermute | solution.py:918
  204.5 13.0 %collective-permute-start.44 = (bf16[384,512]{1,0:T(8,128)(2,1)S(1)}, bf16[384,512]{1,0:T(8,128)(2,1)S(1)}, u32[]{:S(2)}, u32[]{:S(2)}) collective-permute-start(bf16[384,512]{1,0:T(8,128)(2,1)S(1)} %get-tuple-element.333), channel_id=1, source_target_pairs={{0,2},{1,3},{2,0},{3,1},{4,6},{5,7},{6,4},{7,5},{8,10},{9,11},{10,... | collective-permute-start | bytes 1179656 | tf_op jit(solution)/shard_map/ppermute | solution.py:918
  206.1 8.3 %collective-permute-start.46 = (bf16[384,384]{1,0:T(8,128)(2,1)S(1)}, bf16[384,384]{1,0:T(8,128)(2,1)S(1)}, u32[]{:S(2)}, u32[]{:S(2)}) collective-permute-start(bf16[384,384]{1,0:T(8,128)(2,1)S(1)} %get-tuple-element.337), channel_id=1, source_target_pairs={{0,4},{4,0},{8,12},{12,8},{16,20},{20,16},{24,28},{28,24},{1,5},{5... | collective-permute-start | bytes 884744 | tf_op jit(solution)/shard_map/ppermute | solution.py:918
  219.1 8.9 %collective-permute-start.47 = (bf16[1152,512]{1,0:T(8,128)(2,1)S(1)}, bf16[1152,512]{1,0:T(8,128)(2,1)S(1)}, u32[]{:S(2)}, u32[]{:S(2)}) collective-permute-start(bf16[1152,512]{1,0:T(8,128)(2,1)S(1)} %shard_map.231.refs_9_), channel_id=1, source_target_pairs={{0,1},{1,0},{2,3},{3,2},{4,5},{5,4},{6,7},{7,6},{8,9},{9,8},{10,11... | collective-permute-start | bytes 3538952 | tf_op jit(solution)/shard_map/ppermute | solution.py:918
  219.2 6.3 %collective-permute-start.49 = (bf16[192,384]{1,0:T(8,128)(2,1)S(1)}, bf16[192,384]{1,0:T(8,128)(2,1)S(1)}, u32[]{:S(2)}, u32[]{:S(2)}) collective-permute-start(bf16[192,384]{1,0:T(8,128)(2,1)S(1)} %add_convert_fusion.4), channel_id=1, source_target_pairs={{0,4},{4,0},{8,12},{12,8},{16,20},{20,16},{24,28},{28,24},{1,5},{5... | collective-permute-start | bytes 442376 | tf_op jit(solution)/shard_map/ppermute | solution.py:918
  219.6 6.0 %collective-permute-start.48 = (bf16[192,384]{1,0:T(8,128)(2,1)S(1)}, bf16[192,384]{1,0:T(8,128)(2,1)S(1)}, u32[]{:S(2)}, u32[]{:S(2)}) collective-permute-start(bf16[192,384]{1,0:T(8,128)(2,1)S(1)} %add_convert_fusion.5), channel_id=1, source_target_pairs={{0,8},{4,12},{8,0},{12,4},{16,24},{20,28},{24,16},{28,20},{1,9},{5... | collective-permute-start | bytes 442376 | tf_op jit(solution)/shard_map/ppermute | solution.py:918
  225.8 9.5 %collective-permute-start.50 = (bf16[96,768]{1,0:T(8,128)(2,1)S(1)}, bf16[96,768]{1,0:T(8,128)(2,1)S(1)}, u32[]{:S(2)}, u32[]{:S(2)}) collective-permute-start(bf16[96,768]{1,0:T(8,128)(2,1)S(1)} %pad_maximum_fusion.1), channel_id=1, source_target_pairs={{0,16},{4,20},{8,24},{12,28},{16,0},{20,4},{24,8},{28,12},{1,17},{... | collective-permute-start | bytes 442376 | tf_op jit(solution)/shard_map/ppermute | solution.py:918
  (26 other events, 112.8 us)

commit v4 on v3

--- a/solution.py
+++ b/solution.py
@@ -524,41 +524,51 @@
     )
 
 
-def mlp_peer_kernel(at_ref, *refs):
+def mlp_chunks(x, total, wgu, wd, da, db):
+    hidden = wd.shape[0]
+    for col in range(0, hidden, BLK):
+        cols, ups = slice(col, col + BLK), slice(hidden + col, hidden + col + BLK)
+        total += mlp_rows(x[...], wgu[:, cols], wgu[:, ups], wd[cols, :], da.at[:, cols], db.at[:, cols], None)
+    return total
+
+
+def mlp_far_kernel(at_ref, *refs):
     n_parts = len(PART_PLACES)
-    ml0, ml1, acc, own, sib, da, db, wgu, wd, sem = refs[n_parts:]
-    rows = ml0.shape[0]
-    hidden = da.shape[1]
+    ml1, acc, sib0, sib1, da, db, wgu, wd, sem = refs[n_parts:]
+    rows = ml1.shape[0]
     for c in gather_weights(at_ref, refs[:n_parts], wgu, wd, sem):
         c.wait()
-    for block, x in enumerate((ml0, ml1)):
-        at = slice(block * rows, (block + 1) * rows)
-        total = acc[at, :]
-        for col in range(0, hidden, BLK):
-            cols, ups = slice(col, col + BLK), slice(hidden + col, hidden + col + BLK)
-            saved = [u.at[at, cols] for u in (da, db)]
-            total += mlp_rows(x[...], wgu[:, cols], wgu[:, ups], wd[cols, :], *saved, None)
-        if block:
-            sib[...] = total.astype(BF16)
-        else:
-            own[...] = total
-
-
-def mlp_peer(at, ml0, ml1, acc, parts, awaits=()):
-    rows, width = ml0.shape
+    total = mlp_chunks(ml1, acc[rows:, :], wgu, wd, da, db)
+    sib0[...] = total[0 : rows // 2].astype(BF16)
+    sib1[...] = total[rows // 2 :].astype(BF16)
+
+
+def mlp_far(at, ml1, acc, parts, awaits=()):
+    rows, width = ml1.shape
     hidden = parts[0].shape[1] // 2
-    saved = ((2 * rows, hidden), BF16)
-    return run(
-        mlp_peer_kernel,
-        6,
-        13,
+    return run(
+        mlp_far_kernel,
+        4,
+        10,
         (at,),
-        (ml0, ml1, acc),
-        [((rows, width), F32), ((rows, width), BF16)] + [saved] * 2,
-        [pltpu.VMEM((width, 2 * hidden), BF16), pltpu.VMEM((hidden, width), BF16), pltpu.SemaphoreType.DMA((len(parts),))],
+        (ml1, acc),
+        [((rows // 2, width), BF16)] * 2
+        + [((rows, hidden), BF16)] * 2
+        + [((width, 2 * hidden), BF16), ((hidden, width), BF16)],
+        [pltpu.SemaphoreType.DMA((len(parts),))],
         awaits,
         apart=parts,
     )
+
+
+def mlp_last_kernel(ml0, acc, wgu, wd, own, da, db):
+    own[...] = mlp_chunks(ml0, acc[0 : ml0.shape[0], :], wgu, wd, da, db)
+
+
+def mlp_last(ml0, acc, wgu, wd):
+    rows, width = ml0.shape
+    saved = ((rows, wd.shape[0]), BF16)
+    return run(mlp_last_kernel, 3, 10, (), (ml0, acc, wgu, wd), [((rows, width), F32), saved, saved])
 
 
 def copies_of(src, dst, sem, rows=128):
@@ -571,10 +581,12 @@
 
 
 def mid_kernel(
-    got, xhat_ref, own_ref, go_ref, g1, b1, g2, b2, out_ref, dh_ref, dm_ref, sums_ref, got_ref, sem
+    got, got_late, xhat_ref, own_ref, go_ref, g1, b1, g2, b2, out_ref, dh_ref, dm_ref, sums_ref, got_ref, sem
 ):
     gain_sum, bias_sum = 0.0, 0.0
+    half = got.shape[0]
     copies = copies_of(got, got_ref, sem)
+    copies += copies_of(got_late, got_ref.at[pl.ds(half, half), :], sem.at[pl.ds(half // 128, half // 128)])
     for start in range(0, xhat_ref.shape[0], 128):
         at = slice(start, start + 128)
         copies[start // 128].wait()
@@ -602,66 +614,67 @@
         (((rows, width), BF16), ((rows, width), F32), ((rows, width), BF16), ((2, width), F32)),
         [pltpu.VMEM((rows, width), BF16), pltpu.SemaphoreType.DMA((rows // 128,))],
         awaits,
-        apart=(got,),
-    )
-
-
-def mlp_back_kernel(at_ref, *refs):
-    n_parts = len(PART_PLACES)
-    dm1_ref, dm0, wgu, wd, da_o, db_o, da_p, db_p, own, sib0, sib1, dg_o, du_o, wgu_p, wd_p, dm1, sem = refs[n_parts:]
-    rows = dm0.shape[0]
+        apart=got,
+    )
+
+
+def mlp_back_chunks(x, total, wgu, wd, da, db, at, dg=None, du=None):
     hidden = wd.shape[0]
-    first = pltpu.make_async_copy(dm1_ref, dm1, sem.at[n_parts])
-    first.start()
-    copies = gather_weights(at_ref, refs[:n_parts], wgu_p, wd_p, sem)
-
-    def part_of(x, at, cols, wg, wu, down, da, db, keep):
-        dhid = mm(x[...], down, NT)
+    for col in range(0, hidden, BLK):
+        cols, ups = slice(col, col + BLK), slice(hidden + col, hidden + col + BLK)
+        dhid = mm(x[...], wd[cols, :], NT)
         dgate = (dhid * da[at, cols].astype(F32)).astype(BF16)
         dup = (dhid * db[at, cols].astype(F32)).astype(BF16)
-        if keep:
-            dg_o[at, cols] = dgate
-            du_o[at, cols] = dup
-        return mm(dgate, wg, NT) + mm(dup, wu, NT)
-
-    totals = [None, None]
-    for peer, (gu, down, da, db) in enumerate(((wgu, wd, da_o, db_o), (wgu_p, wd_p, da_p, db_p))):
-        for block, x in enumerate((dm0, dm1)):
-            if block and not peer:
-                first.wait()
-            at = slice(block * rows, (block + 1) * rows)
-            for col in range(0, hidden, BLK):
-                cols, ups = slice(col, col + BLK), slice(hidden + col, hidden + col + BLK)
-                part = part_of(x, at, cols, gu[:, cols], gu[:, ups], down[cols, :], da, db, not peer)
-                totals[block] = part if totals[block] is None else totals[block] + part
-        if not peer:
-            for c in copies:
-                c.wait()
-    own[...] = totals[0]
-    sib0[...] = totals[1][0 : rows // 2].astype(BF16)
-    sib1[...] = totals[1][rows // 2 :].astype(BF16)
-
-
-def mlp_backward(at, dm0, dm1, wgu, wd, parts, da_o, db_o, da_p, db_p, awaits=()):
+        if dg is not None:
+            dg[:, cols] = dgate
+            du[:, cols] = dup
+        part = mm(dgate, wgu[:, cols], NT) + mm(dup, wgu[:, ups], NT)
+        total = part if total is None else total + part
+    return total
+
+
+def back_own_kernel(dm0, wgu, wd, da, db, acc, dg, du):
+    acc[...] = mlp_back_chunks(dm0, None, wgu, wd, da, db, slice(0, dm0.shape[0]), dg, du)
+
+
+def back_own(dm0, wgu, wd, da, db):
     rows, width = dm0.shape
-    hidden = wd.shape[0]
-    saved = ((2 * rows, hidden), BF16)
-    return run(
-        mlp_back_kernel,
-        11,
-        18,
-        (at,),
-        (dm0, wgu, wd, da_o, db_o, da_p, db_p),
-        [((rows, width), F32)] + [((rows // 2, width), BF16)] * 2 + [saved] * 2,
-        [
-            pltpu.VMEM((width, 2 * hidden), BF16),
-            pltpu.VMEM((hidden, width), BF16),
-            pltpu.VMEM((rows, width), BF16),
-            pltpu.SemaphoreType.DMA((len(parts) + 1,)),
-        ],
-        awaits,
-        apart=(*parts, dm1),
-    )
+    saved = ((rows, wd.shape[0]), BF16)
+    return run(back_own_kernel, 3, 10, (), (dm0, wgu, wd, da, db), [((rows, width), F32), saved, saved])
+
+
+def back_far_kernel(dm1_ref, wgu, wd, wgu_p, wd_p, da_o, db_o, da_p, db_p, sib0, sib1, dg, du, dm1, sem):
+    rows = dm1.shape[0]
+    copy = pltpu.make_async_copy(dm1_ref, dm1, sem)
+    copy.start()
+    copy.wait()
+    total = mlp_back_chunks(dm1, None, wgu, wd, da_o, db_o, slice(rows, 2 * rows), dg, du)
+    total = mlp_back_chunks(dm1, total, wgu_p, wd_p, da_p, db_p, slice(0, rows))
+    sib0[...] = total[0 : rows // 2].astype(BF16)
+    sib1[...] = total[rows // 2 :].astype(BF16)
+
+
+def back_far(dm1, wgu, wd, wgu_p, wd_p, da_o, db_o, da_p, db_p):
+    rows, width = dm1.shape
+    saved = ((rows, wd.shape[0]), BF16)
+    return run(
+        back_far_kernel,
+        6,
+        12,
+        (),
+        (wgu, wd, wgu_p, wd_p, da_o, db_o, da_p, db_p),
+        [((rows // 2, width), BF16)] * 2 + [saved, saved],
+        [pltpu.VMEM((rows, width), BF16), pltpu.SemaphoreType.DMA],
+        apart=(dm1,),
+    )
+
+
+def back_last_kernel(dm0, acc, wgu, wd, da, db, own):
+    own[...] = mlp_back_chunks(dm0, acc[...], wgu, wd, da, db, slice(0, dm0.shape[0]))
+
+
+def back_last(dm0, acc, wgu, wd, da, db):
+    return run(back_last_kernel, 3, 10, (), (dm0, acc, wgu, wd, da, db), [(acc.shape, F32)])[0]
 
 
 def first_norm_kernel(
@@ -769,11 +782,11 @@
 
 
 def weight_kernel(
-    fast, spots_a, spots_b, d0, d1, d2, d3, ml0, ml1, ml2, ml3, dg, du, dg_f, du_f, da_first, da_second, db_first,
+    fast, spots_a, spots_b, d0, d1, d2, d3, ml0, ml1, ml2, ml3, dg0, dg1, du0, du1, dg_f, du_f, da_first, da_second, db_first,
     db_second, a_first, a_second, b_first, b_second, total, mlt_a, mlt_b, tail_scr, sem,
 ):
     rows = ml0.shape[0]
-    hidden = dg.shape[1]
+    hidden = dg0.shape[1]
     copies = [
         pltpu.make_async_copy(d.at[pl.ds(3 * HD, 16), :], tail_scr.at[p], sem.at[p]) for p, d in enumerate((d0, d1, d2, d3))
     ]
@@ -784,17 +797,27 @@
         transpose_into(mlt_a, u[...], spots_a if fast else None, cols)
         transpose_into(mlt_b, u[...], spots_b if fast else None, cols)
     for src, dst in ((da_first, a_first), (da_second, a_second), (db_first, b_first), (db_second, b_second)):
-        dst[:, hidden:] = src[...]
+        dst[0 : src.shape[0], hidden:] = src[...]
     wide = slice(0, hidden)
-    for turned, near, far, first, second in ((mlt_a, dg, dg_f, a_first, a_second), (mlt_b, du, du_f, b_first, b_second)):
-        grad = mm(turned[:, 0 : 2 * rows], near[...]) + mm(turned[:, 2 * rows :], far[...])
-        split_rows(grad, first.at[:, wide], second.at[:, wide])
+    half = a_first.shape[0]
+    for turned, near, late, far, first, second in (
+        (mlt_a, dg0, dg1, dg_f, a_first, a_second),
+        (mlt_b, du0, du1, du_f, b_first, b_second),
+    ):
+        grad = mm(turned[:, 0:rows], near[...]) + mm(turned[:, rows : 2 * rows], late[...])
+        grad += mm(turned[:, 2 * rows :], far[...])
+        split_rows(grad, first.at[:, wide], second.at[0:half, wide])
     for c in copies:
         c.wait()
     sums = [tail_scr[p].astype(F32) for p in range(4)]
     joined = (sums[0] + sums[1]) + (sums[2] + sums[3])
-    total[:, 0:512] = joined[0:4] + joined[4:8]
-    total[:, 512:768] = (joined[8:12] + joined[12:16])[:, 0:256]
+    whole = jnp.concatenate([joined[0:4] + joined[4:8], (joined[8:12] + joined[12:16])[:, 0:256]], axis=1)
+    high = whole.astype(BF16).astype(F32)
+    low = (whole - high).astype(BF16).astype(F32)
+    total[...] = high + low
+    rest = jnp.zeros((8, hidden), F32)
+    a_second[half : half + EXTRA, wide] = jnp.concatenate([high, low, rest], axis=0).astype(BF16)
+    a_second[half : half + EXTRA, hidden:] = jnp.zeros((EXTRA, a_second.shape[1] - hidden), BF16)
 
 
 def weight_grads(fast, spots, d, ml, near, far, down, awaits=()):
@@ -807,7 +830,7 @@
         16,
         spots,
         (*ml, *near, *far, *down),
-        [chain] * 4 + [((4, width), F32)],
+        [chain, ((width // 2 + EXTRA, hidden + hidden // 2), BF16), chain, chain, ((4, width), F32)],
         [
             *[pltpu.VMEM((width, 4 * rows), BF16)] * 2,
             pltpu.VMEM((4, 16, rows), BF16),
@@ -977,21 +1000,41 @@
     )
 
 
+def in_two(v):
+    high = lax.reduce_precision(v, 8, 7)
+    low = lax.reduce_precision(v - high, 8, 7)
+    return jnp.concatenate([high, low], axis=0), high + low
+
+
 class scatter_steps:
-    def __init__(self, first, second, order):
-        self.first, self.parts, self.order, self.step = first, [first], order, 0
-        self.sent = second
+    def __init__(self, first, second, order, ride=None):
+        self.parts, self.order, self.step = [first], order, 0
+        self.sent, self.ride, self.base = second, ride, None
+        self.extra = 0 if ride is None else EXTRA
 
     def advance(self):
+        self.base = self.ride
         self.parts.append(swap(self.sent, 1 << self.order[self.step], "dp"))
         self.step += 1
         self.next_sent()
         return self.parts[-1]
 
+    def carried(self, got):
+        n, width = self.base.shape
+        rows = got[got.shape[0] - EXTRA : got.shape[0] - EXTRA + 2 * n, 0:width].astype(F32)
+        return self.base + (rows[0:n] + rows[n:])
+
     def next_sent(self):
+        if self.extra:
+            self.ride = self.carried(self.parts[-1])
         if self.step < len(self.order):
-            length = self.parts[-1].shape[0]
-            self.sent = sum(u[length // 2 : length].astype(F32) for u in self.parts).astype(BF16)
+            length = self.parts[-1].shape[0] - self.extra
+            sent = sum(u[length // 2 : length].astype(F32) for u in self.parts)
+            if self.extra:
+                rows, self.ride = in_two(self.ride)
+                padding = ((0, EXTRA - rows.shape[0]), (0, sent.shape[1] - rows.shape[1]))
+                sent = jnp.concatenate([sent, jnp.pad(rows, padding)], axis=0)
+            self.sent = sent.astype(BF16)
 
     def all_parts(self):
         while self.step < len(self.order):
@@ -1003,9 +1046,13 @@
     bits = {chain.order[chain.step] for chain in chains}
     if len(bits) > 1 or any(chain.step < len(chain.order) - 1 for chain in chains):
         return None
+    tall = max(chain.sent.shape[0] for chain in chains)
+    sent = [jnp.pad(chain.sent, ((0, tall - chain.sent.shape[0]), (0, 0))) for chain in chains]
+    got = swap(jnp.concatenate(sent, axis=1), 1 << bits.pop(), "dp")
     for chain in chains:
         chain.step += 1
-    return swap(jnp.concatenate([chain.sent for chain in chains], axis=1), 1 << bits.pop(), "dp")
+        chain.base = chain.ride
+    return got
 
 
 def first_sums(chains, rows):
@@ -1058,53 +1105,55 @@
     wo0 = out_weight
     wo1, wt1 = swap(wo0, 1), swap(wt, 1)
     wgu = gate_up_weight.reshape(width, -1)
-    part_a, part_b = quarter_of(down_weight), quarter_of(wgu)
+    part_b = quarter_of(wgu)
+    part_a = jnp.concatenate([quarter_of(down_weight), wo0], axis=0)
 
     proj = [project(0, sp, freqs, tok0, wt), project(1, sp, freqs, tok1, wt, awaits=(part_a, part_b, wt1))]
-    (tok2,) = gate(tok2)
-    tok3 = swap(tok2, 1)
-    wo2 = swap(wo0, 2)
+    tok2, part_b = gate(tok2, part_b)
+    tok3, pb0 = swap(tok2, 1), swap(part_b, 2)
     tok = (tok0, tok1, tok2, tok3)
-    *more, part_a = project(2, sp, freqs, tok2, wt, carry=(part_a,))
+    proj.append(project(2, sp, freqs, tok2, wt))
+    *more, part_a = project(3, sp, freqs, tok3, wt, carry=(part_a,))
     proj.append(more)
     pa0 = swap(part_a, 2)
-    *more, part_b = project(3, sp, freqs, tok3, wt, carry=(part_b,))
-    proj.append(more)
-    pb0 = swap(part_b, 2)
     qt, kt, k, vt, cs = zip(*proj)
     o2, o3, q2, q3 = attend(1, sp, qt, k, vt, (wo1,))
-    o2, o3, wo2, pa0 = gate(o2, o3, wo2, pa0)
+    o2, pb0 = gate(o2, pb0)
+    pb1, pb2, g2 = swap(pb0, 1, "dp"), swap(pb0, 2, "dp"), swap(o2, 2)
+    o0, o1, q0, q1 = attend(0, sp, qt, k, vt)
+    half2, half1 = park((), ((pb2, 0), (pb1, 1)))
+    half2, half1, o3, pa0 = gate(half2, half1, o3, pa0)
+    g3, pb3 = swap(o3, 3), (swap(half2, 1, "dp"), swap(half1, 2, "dp"))
+    (tok_t,) = transposed(fast, (spots,), tok, rows)
+    if not fast:
+        tok_t = arranged(tok_t.T, spots).T
+    pa0, wo2 = park((), ((pa0, 0), (pa0, 1)))
+    o1, pa0, wo2 = gate(o1, pa0, wo2, awaits=(g2, g3, *pb3))
+    g1, wo3 = swap(o1, 1), swap(wo2, 1)
     pa1, pa2, pa3 = swap(pa0, 1, "dp"), swap(pa0, 2, "dp"), swap(pa0, 3, "dp")
-    g2 = swap(o2, 2)
-    o0, o1, q0, q1 = attend(0, sp, qt, k, vt)
-    o1, o3, pb0, wo2 = gate(o1, o3, pb0, wo2, awaits=(g2, pa1, pa2, pa3))
-    g1, g3, wo3 = swap(o1, 1), swap(o3, 3), swap(wo2, 1)
     wo = (wo0, wo1, wo2, wo3)
-    pb1, pb2 = swap(pb0, 1, "dp"), swap(pb0, 2, "dp")
-    toks = transposed(fast, (spots_b, spots), tok, rows)
-    if not fast:
-        toks = [arranged(toks[0].T, u).T for u in (spots_b, spots)]
-    (g3,) = gate(g3)
 
     gain1, bias1, gain2, bias2 = (u.reshape(1, width) for u in (norm1_gain, norm1_bias, norm2_gain, norm2_bias))
     ml0, xhat1, inv1, *halves = out_project((o0, g1, g2, g3), wo, tokens, gain1, bias1)
+    ml2 = swap(ml0, 2)
     acc, da_o, db_o, hid_o, ml1 = mlp_own(ml0, [swap(u, 1) for u in halves], wgu, down_weight)
-    half2, half1 = park((), ((pb2, 0), (pb1, 1)))
-    half2, half1, ml0 = gate(half2, half1, ml0)
-    parts = (pb0, pb1, pb2, swap(half2, 1, "dp"), swap(half1, 2, "dp"), pa0, pa1, pa2, pa3)
-    ml2 = swap(ml0, 2)
-    kept = park((*kt, *k, *vt, q0, q1, q2, q3, *toks))
-    kt, k, vt, (q0, q1, q2, q3, *toks) = kept[0:4], kept[4:8], kept[8:12], kept[12:18]
-    own, sib, da_p, db_p = mlp_peer(quarter, ml0, ml1, acc, parts)
-    (sib,) = gate(sib, awaits=(ml2,))
-    output, dh2, dm0, sums2 = mid_norm(xhat1, own, swap(sib, 1), out_grad, gain1, bias1, gain2, bias2)
+    parts = (pb0, pb1, pb2, *pb3, pa0, pa1, pa2, pa3)
+    kept = park((*kt, *k, *vt, q0, q1, q2, q3, tok_t))
+    kt, k, vt, (q0, q1, q2, q3, tok_t) = kept[0:4], kept[4:8], kept[8:12], kept[12:17]
+    sib0, sib1, da_1, db_1, wgu_p, wd_p = mlp_far(quarter, ml1, acc, parts)
+    own, da_0, db_0 = mlp_last(ml0, acc, wgu_p, wd_p)
+    gate(awaits=(ml2,))
+    output, dh2, dm0, sums2 = mid_norm(
+        xhat1, own, (swap(sib0, 1), swap(sib1, 1)), out_grad, gain1, bias1, gain2, bias2
+    )
     dm0, ml2 = gate(dm0, ml2)
     dm1, dm2 = swap(dm0, 1), swap(dm0, 2)
     ml3 = swap(ml2, 1)
-    own, sib0, sib1, dg_o, du_o = mlp_backward(quarter, dm0, dm1, wgu, down_weight, parts, da_o, db_o, da_p, db_p)
-    sib0, sib1 = gate(sib0, sib1, awaits=(ml3,))
+    acc, dg_0, du_0 = back_own(dm0, wgu, down_weight, da_o, db_o)
+    sib0, sib1, dg_1, du_1 = back_far(dm1, wgu, down_weight, wgu_p, wd_p, da_o, db_o, da_1, db_1)
+    own = back_last(dm0, acc, wgu_p, wd_p, da_0, db_0)
     dh1, d0, d1, d2, d3, ea = first_norm_back(
-        dh2, own, (swap(sib0, 1), swap(sib1, 1)), xhat1, inv1, gain1, sums2, (o0, g1, g2, g3), wo
+        dh2, own, (swap(sib0, 1), swap(sib1, 1)), xhat1, inv1, gain1, sums2, (o0, g1, g2, g3), wo, (ml3,)
     )
     d1, d2, d3, dm2 = gate(d1, d2, d3, dm2)
     dm3 = swap(dm2, 1)
@@ -1114,15 +1163,16 @@
     (wt,) = gate(wt, awaits=d[1:])
     wt2 = swap(wt, 2)
     a_first, a_second, b_first, b_second, sums = weight_grads(
-        fast, both, d, ml, (dg_o, du_o), (dg_f, du_f), down
+        fast, both, d, ml, (dg_0, dg_1, du_0, du_1), (dg_f, du_f), down
     )
     if not fast:
-        a_first, a_second = split_halves(arranged(jnp.concatenate([a_first, a_second]).T, spots).T)
+        tail = a_second[width // 2 :]
+        a_first, a_second = split_halves(arranged(jnp.concatenate([a_first, a_second[0 : width // 2]]).T, spots).T)
+        a_second = jnp.concatenate([a_second, tail])
         b_first, b_second = split_halves(arranged(jnp.concatenate([b_first, b_second]).T, spots_b).T)
-    a_second, b_second, sums = gate(a_second, b_second, sums)
-    sum_bits = order[2:3] + order[1::-1] + order[3:]
-    sums_got = swap(sums, 1 << sum_bits[0], "dp")
-    chain_a, chain_b = scatter_steps(a_first, a_second, order), scatter_steps(b_first, b_second, order_b)
+    a_second, b_second = gate(a_second, b_second)
+    chain_a = scatter_steps(a_first, a_second, order, sums)
+    chain_b = scatter_steps(b_first, b_second, order_b)
     a_got, b_got = chain_a.advance(), chain_b.advance()
 
     arrange = jnp.zeros((8, 128), BF16)
@@ -1142,52 +1192,49 @@
         o=(o0, o1, o2, o3),
         d=d,
         cs=cs,
-    )
-    near0, far0, core0, grad0, e_own = back(0, tok_t=toks[0], given=(ea,))
-    far0, chain_a.parts[-1], chain_b.parts[-1], wt2, sums_got = gate(far0, a_got, b_got, wt2, sums_got)
+        tok_t=tok_t,
+    )
+    near0, far0, core0, grad0, e_own = back(0, given=(ea,))
+    far0, chain_a.parts[-1], chain_b.parts[-1], wt2 = gate(far0, a_got, b_got, wt2)
     for chain in (chain_a, chain_b):
         chain.next_sent()
     a_got, b_got, got0 = chain_a.advance(), chain_b.advance(), swap(far0, 2)
-    sums = sums + sums_got
-    sums_got = swap(sums, 1 << sum_bits[1], "dp")
-    near1, far1, core1, first, second = back(1, tok_t=toks[0], given=(core0, grad0))
-    far1, second, chain_a.parts[-1], chain_b.parts[-1], sums_got, wt2 = gate(far1, second, a_got, b_got, sums_got, wt2)
+    near1, far1, core1, first, second = back(1, given=(core0, grad0))
+    far1, second, chain_a.parts[-1], chain_b.parts[-1], wt2 = gate(far1, second, a_got, b_got, wt2)
     for chain in (chain_a, chain_b):
         chain.next_sent()
-    c1 = scatter_steps(first, second, order_b)
+    c1 = scatter_steps(first, second, order)
     c1_got, mlp3 = c1.advance(), advance_together((chain_a, chain_b))
     wt3 = swap(wt2, 1)
     got1 = swap(far1, 2)
-    sums = sums + sums_got
-    sums_got = swap(sums, 1 << sum_bits[2], "dp")
-    near2, far2, core2, first, second = back(2, tok_t=toks[1], given=(core1, got0, e_own, arrange))
-    far2, second, c1.parts[-1], sums_got = gate(far2, second, c1_got, sums_got, awaits=(got1, wt3))
+    near2, far2, core2, first, second = back(2, given=(core1, got0, e_own, arrange))
+    far2, second, c1.parts[-1] = gate(far2, second, c1_got, awaits=(got1, wt3))
     c1.next_sent()
-    sums = sums + sums_got
-    for bit in sum_bits[3:]:
-        sums = sums + swap(sums, 1 << bit, "dp")
     c2 = scatter_steps(first, second, order)
-    c2_got, c1_got, got2 = c2.advance(), c1.advance(), swap(far2, 2)
-    (c2.parts[-1],) = gate(c2_got)
+    c2_got, got2 = c2.advance(), swap(far2, 2)
+    c2.parts[-1], *late = gate(c2_got, *([] if mlp3 is None else [mlp3]))
     c2.next_sent()
-    c2_got = c2.advance()
+    c2_got, c1_got = c2.advance(), c1.advance()
     mlp, shard = [chain_a.all_parts(), chain_b.all_parts()], width // n_dp
     if mlp3 is not None:
         mlp.append([mlp3])
-    if fast:
-        hidden = down_weight.shape[0]
-        gu_part, down_part = last_sums("mlp", shard, mlp, [((shard, 2, hidden), F32), ((shard, hidden), F32)])
     core = swap(join(core2, got1, got2), 1)
     input_grad = input_near(dh1, (near0, near1, near2), (got0, got1, got2), wt, wt2)
     c2.parts[-1], c1.parts[-1] = gate(c2_got, c1_got)
     c2.next_sent()
     c1.next_sent()
+    if late:
+        chain_a.ride = chain_a.carried(late[0])
+        mlp[-1] = late
     both = advance_together((c1, c2))
     attention = [c1.all_parts(), c2.all_parts()]
     if both is not None:
         attention.append([both])
     input_grad = input_back(input_grad, core, wt1, wt3)
+    sums = chain_a.ride
     if fast:
+        hidden = down_weight.shape[0]
+        gu_part, down_part = last_sums("mlp", shard, mlp, [((shard, 2, hidden), F32), ((shard, hidden), F32)])
         qkv_part, out_part = last_sums(
             "attention", shard, attention, [((3, shard, 3 * HD), F32), ((3 * HD, shard), F32)]
         )

time: 243 us -> 235 us (0.967)
  starting transfers between devices: 46.7 us -> 39.7 us
  local copies, waits for them, and re-layouts: 11.5 us -> 7.71 us
  waiting for transfers between devices: 47.1 us -> 50.2 us
    ppermute x51 -> x48, starting transfers between devices: 46.7 us -> 39.7 us  [swap(): return lax.ppermute(v, axis, [(i, i ^ bit) for i in range(n)])]
    unnamed x52 -> x31, local copies, waits for them, and re-layouts: 10.7 us -> 6.91 us
    ppermute x51 -> x48, waiting for transfers between devices: 47.1 us -> 50.2 us  [swap(): return lax.ppermute(v, axis, [(i, i ^ bit) for i in range(n)])]
    pallas_call x41 -> x43, Pallas kernels: 130 us -> 129 us  [run(): pl.pallas_call(body, in_specs=[pl.BlockSpec(memory_space=pltpu.SMEM)] * l...]
  transfers between devices with their start and end apart: 51 -> 48, of which waited for: 23 -> 17; matrix products, arithmetic and copies ran while one was open for 2% -> 2% of each run, Pallas kernels for 49% -> 50%
where the time goes in v4:
time: 235 us; the launch traced here: 230 us
  Pallas kernels  129 us (55%)
  waiting for transfers between devices  50.2 us (21%)
  starting transfers between devices  39.7 us (17%)
  local copies, waits for them, and re-layouts  7.71 us (3%)
    pallas_call x43, Pallas kernels, run(): pl.pallas_call(body, in_specs=[pl.BlockSpec(memory_space=pltpu.SMEM)] * l...  129 us
    ppermute x48, waiting for transfers between devices, swap(): return lax.ppermute(v, axis, [(i, i ^ bit) for i in range(n)])  50.2 us
    ppermute x48, starting transfers between devices, swap(): return lax.ppermute(v, axis, [(i, i ^ bit) for i in range(n)])  39.7 us
    unnamed x31, local copies, waits for them, and re-layouts  6.91 us
  transfers between devices with their start and end apart: 48, of which 17 were waited for; matrix products, arithmetic and copies ran while one was open for 2% of the time, Pallas kernels for 50%

profile of v4, /device:TPU:0, one launch (start us, length us, event | category | flops | bytes accessed | tf_op | source)
XLA Modules:
  0.0 230.5 jit_solution(15599444343560912286)
XLA Ops:
  3.5 2.9 %collective-permute-start.2 = (bf16[528,768]{1,0:T(8,128)(2,1)}, bf16[528,768]{1,0:T(8,128)(2,1)}, u32[]{:S(2)}, u32[]{:S(2)}) collective-permute-start(bf16[528,768]{1,0:T(8,128)(2,1)} %fusion.2.refs_2_.refs_1_), channel_id=1, source_target_pairs={{0,2},{1,3},{2,0},{3,1},{4,6},{5,7},{6,4},{7,5},{8,10},{9,11},{10,... | collective-permute-start | bytes 2433032 | tf_op jit(solution)/shard_map/ppermute | solution.py:941
  6.3 2.1 copy.59
  8.6 2.3 shard_map.195
  11.1 2.1 shard_map.196
  13.2 11.8 %collective-permute-done.2.refs_1_ = bf16[528,768]{1,0:T(8,128)(2,1)} collective-permute-done((bf16[528,768]{1,0:T(8,128)(2,1)}, bf16[528,768]{1,0:T(8,128)(2,1)}, u32[]{:S(2)}, u32[]{:S(2)}) %collective-permute-start.2) | collective-permute-done | bytes 811040 | tf_op jit(solution)/shard_map/ppermute | solution.py:941
  25.0 1.7 collective-permute-start.5
  27.0 2.1 shard_map.198
  29.1 1.5 shard_map.199
  30.6 7.6 %shard_map.200 = (bf16[192,512]{1,0:T(8,128)(2,1)S(1)}, bf16[192,512]{1,0:T(8,128)(2,1)S(1)}, bf16[3,128,512]{2,1,0:T(8,128)(2,1)S(1)}, bf16[3,128,512]{2,1,0:T(8,128)(2,1)S(1)}) custom-call(s32[9]{0:T(128)S(1)} %pad_add_fusion.refs_0_, bf16[3,128,512]{2,1,0:T(8,128)(2,1)S(1)} %get-tuple-element.179.refs_1_, ...), custom_call_target="tpu_custom_call" | custom-call | flops 1320000000 | bytes 262144 | tf_op jit(solution)/shard_map/pallas_call | solution.py:46
  38.3 2.5 %collective-permute-done.5.refs_2_ = bf16[192,1536]{1,0:T(8,128)(2,1)S(1)} collective-permute-done((bf16[192,1536]{1,0:T(8,128)(2,1)S(1)}, bf16[192,1536]{1,0:T(8,128)(2,1)S(1)}, u32[]{:S(2)}, u32[]{:S(2)}) %collective-permute-start.5) | collective-permute-done | bytes 589856 | tf_op jit(solution)/shard_map/ppermute | solution.py:941
  40.7 1.8 collective-permute-start.6
  42.5 1.6 collective-permute-start.7
  44.1 1.5 collective-permute-start.8
  45.6 6.8 %shard_map.202 = (bf16[192,512]{1,0:T(8,128)(2,1)S(1)}, bf16[192,512]{1,0:T(8,128)(2,1)S(1)}, bf16[3,128,512]{2,1,0:T(8,128)(2,1)S(1)}, bf16[3,128,512]{2,1,0:T(8,128)(2,1)S(1)}) custom-call(s32[9]{0:T(128)S(1)} %pad_add_fusion.refs_0_, bf16[3,128,512]{2,1,0:T(8,128)(2,1)S(1)} %get-tuple-element.194.refs_1_, ...), custom_call_target="tpu_custom_call" | custom-call | flops 1320000000 | bytes 262144 | tf_op jit(solution)/shard_map/pallas_call | solution.py:46
  52.4 3.3 %collective-permute-done.6.refs_1_.refs_2_ = bf16[192,1536]{1,0:T(8,128)(2,1)S(1)} collective-permute-done((bf16[192,1536]{1,0:T(8,128)(2,1)S(1)}, bf16[192,1536]{1,0:T(8,128)(2,1)S(1)}, u32[]{:S(2)}, u32[]{:S(2)}) %collective-permute-start.6) | collective-permute-done | bytes 589856 | tf_op jit(solution)/shard_map/ppermute | solution.py:941
  59.5 1.5 collective-permute-start.11
  61.0 2.6 %shard_map.205.refs_2_.refs_16_ = bf16[768,2048]{1,0:T(8,128)(2,1)S(1)} custom-call(s32[8]{0:T(128)S(1)} %add_add_fusion.1.refs_0_.refs_1_, bf16[528,768]{1,0:T(8,128)(2,1)} %fusion.2.refs_2_.refs_1_, bf16[528,768]{1,0:T(8,128)(2,1)} %collective-permute-done.refs_2_, bf16[528,768]{1,0:T(8,128)(2,1)} %get-tuple-element.177.refs_2_.refs_3_, ...), custom_call_target="tpu_custom_call" | custom-call | flops 330000000 | bytes 262144 | tf_op jit(solution)/shard_map/pallas_call | solution.py:46
  63.8 2.6 %collective-permute-done.11.refs_0_.refs_2_.refs_10_ = bf16[192,512]{1,0:T(8,128)(2,1)S(1)} collective-permute-done((bf16[192,512]{1,0:T(8,128)(2,1)S(1)}, bf16[192,512]{1,0:T(8,128)(2,1)S(1)}, u32[]{:S(2)}, u32[]{:S(2)}) %collective-permute-start.11) | collective-permute-done | bytes 196640 | tf_op jit(solution)/shard_map/ppermute | solution.py:941
  66.4 2.0 collective-permute-done.12.refs_1_.refs_3_.refs_11_
  74.1 1.5 collective-permute-start.13
  77.6 5.3 %shard_map.209 = (f32[1024,768]{1,0:T(8,128)S(1)}, bf16[1024,768]{1,0:T(8,128)(2,1)S(1)}, bf16[1024,768]{1,0:T(8,128)(2,1)S(1)}, bf16[1024,768]{1,0:T(8,128)(2,1)S(1)}, bf16[512,768]{1,0:T(8,128)(2,1)S(1)}) custom-call(bf16[256,768]{1,0:T(8,128)(2,1)S(1)} %collective-permute-done.18.refs_0_, bf16[256,768]{1,0:T(8,128)(2,1)S(1)} %collective-permute-done.19.refs_1_, ...), custom_call_target="tpu_custom_call" | custom-call | flops 825000000 | bytes 262144 | tf_op jit(solution)/shard_map/pallas_call | solution.py:46
  82.9 3.6 %shard_map.210 = (bf16[3,128,512]{2,1,0:T(8,128)(2,1)S(1)}, bf16[3,128,512]{2,1,0:T(8,128)(2,1)S(1)}, bf16[3,128,512]{2,1,0:T(8,128)(2,1)S(1)}, bf16[3,128,512]{...) custom-call(bf16[3,128,512]{2,1,0:T(8,128)(2,1)S(1)} %get-tuple-elem, ...), custom_call_target="tpu_custom_call" | custom-call | flops 495000000 | bytes 262144 | tf_op jit(solution)/shard_map/pallas_call | solution.py:46
  86.5 4.0 %collective-permute-done.15.refs_9_ = bf16[192,768]{1,0:T(8,128)(2,1)S(1)} collective-permute-done((bf16[192,768]{1,0:T(8,128)(2,1)S(1)}, bf16[192,768]{1,0:T(8,128)(2,1)S(1)}, u32[]{:S(2)}, u32[]{:S(2)}) %collective-permute-start.15) | collective-permute-done | bytes 294944 | tf_op jit(solution)/shard_map/ppermute | solution.py:941
  90.6 3.3 %shard_map.211 = (bf16[256,768]{1,0:T(8,128)(2,1)S(1)}, bf16[256,768]{1,0:T(8,128)(2,1)S(1)}, bf16[512,768]{1,0:T(8,128)(2,1)S(1)}, bf16[512,768]{1,0:T(8,128)(2...) custom-call(s32[1]{0:T(128)} %bitcast.refs_0_, bf16[192,1536]{1,0:T(8,128)(2,1)S(1)} %get-tuple-element.193.refs_1_, ...), custom_call_target="tpu_custom_call" | custom-call | flops 660000000 | bytes 262144 | tf_op jit(solution)/shard_map/pallas_call | solution.py:46
  94.5 2.5 %shard_map.212 = (f32[512,768]{1,0:T(8,128)S(1)}, bf16[512,768]{1,0:T(8,128)(2,1)S(1)}, bf16[512,768]{1,0:T(8,128)(2,1)S(1)}) custom-call(bf16[512,768]{1,0:T(8,128)(2,1)S(1)} %get-tuple-element.217.refs_2_.refs_0_.refs_6_, f32[1024,768]{1,0:T(8,128)S(1)} %get-tuple-element.220.refs_11_.refs_1_, bf16[768,1536]{1,0:T(8,128)(2,1)S(1)} %get-tuple-element.233.refs_2_.refs_3_, ...), custom_call_target="tpu_custom_call" | custom-call | flops 495000000 | bytes 262144 | tf_op jit(solution)/shard_map/pallas_call | solution.py:46
  98.1 3.8 %shard_map.214 = (bf16[512,768]{1,0:T(8,128)(2,1)}, f32[512,768]{1,0:T(8,128)S(1)}, bf16[512,768]{1,0:T(8,128)(2,1)S(1)}, f32[2,768]{1,0:T(2,128)S(1)}) custom-call(bf16[256,768]{1,0:T(8,128)(2,1)S(1)} %collective-permute-done.20.refs_0_, bf16[256,768]{1,0:T(8,128)(2,1)S(1)} %collective-permute-done.21.refs_1_, ...), custom_call_target="tpu_custom_call" | custom-call | flops 495000000 | bytes 262144 | tf_op jit(solution)/shard_map/pallas_call | solution.py:46
  103.1 3.2 %shard_map.216 = (f32[512,768]{1,0:T(8,128)S(1)}, bf16[512,768]{1,0:T(8,128)(2,1)S(1)}, bf16[512,768]{1,0:T(8,128)(2,1)S(1)}) custom-call(bf16[512,768]{1,0:T(8,128)(2,1)S(1)} %get-tuple-element.254.refs_0_.refs_2_, bf16[768,1536]{1,0:T(8,128)(2,1)S(1)} %bitcast.12, bf16[768,768]{1,0:T(8,128)(2,1)S(1)} %copy-done, ...), custom_call_target="tpu_custom_call" | custom-call | flops 495000000 | bytes 262144 | tf_op jit(solution)/shard_map/pallas_call | solution.py:46
  106.4 6.0 %shard_map.217 = (bf16[256,768]{1,0:T(8,128)(2,1)S(1)}, bf16[256,768]{1,0:T(8,128)(2,1)S(1)}, bf16[512,768]{1,0:T(8,128)(2,1)S(1)}, bf16[512,768]{1,0:T(8,128)(2,1)S(1)}) custom-call(bf16[512,768]{1,0:T(8,128)(2,1)S(1)} %collective-permute-done.23.refs_0_.refs_3_, bf16[768,1536]{1,0:T(8,128)(2,1)S(1)} %bitcast.13, bf16[768,768]{1,0:T(8,128)(2,1)S(1)} %copy-done, ...), custom_call_target="tpu_custom_call" | custom-call | flops 990000000 | bytes 262144 | tf_op jit(solution)/shard_map/pallas_call | solution.py:46
  113.0 3.3 %shard_map.218.refs_3_.refs_17_ = f32[512,768]{1,0:T(8,128)S(1)} custom-call(bf16[512,768]{1,0:T(8,128)(2,1)S(1)} %get-tuple-element.254.refs_0_.refs_2_, f32[512,768]{1,0:T(8,128)S(1)} %get-tuple-element.260.refs_9_.refs_1_, bf16[768,1536]{1,0:T(8,128)(2,1)S(1)} %get-tuple-element.233.refs_2_.refs_3_, ...), custom_call_target="tpu_custom_call" | custom-call | flops 495000000 | bytes 262144 | tf_op jit(solution)/shard_map/pallas_call | solution.py:46
  116.3 4.2 %shard_map.219 = (f32[512,768]{1,0:T(8,128)S(1)}, bf16[208,512]{1,0:T(8,128)(2,1)S(1)}, bf16[784,512]{1,0:T(8,128)(2,1)S(1)}, bf16[208,512]{1,0:T(8,128)(2,1)S(1...) custom-call(bf16[256,768]{1,0:T(8,128)(2,1)S(1)} %collective-permute-done.24.refs_0_, ...), custom_call_target="tpu_custom_call" | custom-call | flops 825000000 | bytes 262144 | tf_op jit(solution)/shard_map/pallas_call | solution.py:46
  120.5 1.5 collective-permute-done.27.refs_4_
  124.3 8.6 %shard_map.221 = (bf16[384,384]{1,0:T(8,128)(2,1)S(1)}, bf16[384,384]{1,0:T(8,128)(2,1)S(1)}, bf16[384,384]{1,0:T(8,128)(2,1)S(1)}, bf16[384,384]{1,0:T(8,128)(2...) custom-call(s32[8]{0:T(128)S(1)} %add_add_fusion.1.refs_0_.refs_1_, s32[8]{0:T(128)S(1)} %add_add_fusion.refs_1_, ...), custom_call_target="tpu_custom_call" | custom-call | flops 1320000000 | bytes 262144 | tf_op jit(solution)/shard_map/pallas_call | solution.py:46
  133.3 7.8 %shard_map.223 = (bf16[384,1152]{1,0:T(8,128)(2,1)S(1)}, bf16[400,1152]{1,0:T(8,128)(2,1)S(1)}, bf16[384,1152]{1,0:T(8,128)(2,1)S(1)}, bf16[384,1152]{1,0:T(8,128)(2,1)S(1)}, f32[4,768]{1,0:T(4,128)S(1)}) custom-call(s32[8]{0:T(128)S(1)} %add_add_fusion.1.refs_0_.refs_1_, s32[8]{0:T(128)S(1)} %add_add_fusion.refs_1_, ...), custom_call_target="tpu_custom_call" | custom-call | flops 990000000 | bytes 262144 | tf_op jit(solution)/shard_map/pallas_call | solution.py:46
  141.1 1.6 collective-permute-start.32
  142.7 1.5 collective-permute-start.33
  144.8 13.0 %shard_map.225 = (bf16[192,512]{1,0:T(8,128)(2,1)S(1)}, bf16[672,512]{1,0:T(8,128)(2,1)S(1)}, bf16[192,512]{1,0:T(8,128)(2,1)S(1)}, bf16[768,192]{1,0:T(8,128)(2,1)S(1)}, bf16[192,768]{1,0:T(8,128)(2,1)S(1)}) custom-call(s32[9]{0:T(128)S(1)} %pad_add_fusion.refs_0_, s32[8]{0:T(128)S(1)} %add_add_fusion.1.refs_0_.refs_1_, ...), custom_call_target="tpu_custom_call" | custom-call | flops 1980000000 | bytes 262144 | tf_op jit(solution)/shard_map/pallas_call | solution.py:46
  157.8 7.0 %collective-permute-done.33.refs_3_ = bf16[384,1152]{1,0:T(8,128)(2,1)S(1)} collective-permute-done((bf16[384,1152]{1,0:T(8,128)(2,1)S(1)}, bf16[384,1152]{1,0:T(8,128)(2,1)S(1)}, u32[]{:S(2)}, u32[]{:S(2)}) %collective-permute-start.33) | collective-permute-done | bytes 884768 | tf_op jit(solution)/shard_map/ppermute | solution.py:941
  168.4 13.1 %shard_map.227 = (bf16[192,512]{1,0:T(8,128)(2,1)S(1)}, bf16[384,512]{1,0:T(8,128)(2,1)S(1)}, bf16[384,512]{1,0:T(8,128)(2,1)S(1)}, bf16[384,384]{1,0:T(8,128)(2,1)S(1)}, bf16[384,384]{1,0:T(8,128)(2,1)S(1)}) custom-call(s32[9]{0:T(128)S(1)} %pad_add_fusion.refs_0_, s32[8]{0:T(128)S(1)} %add_add_fusion.1.refs_0_.refs_1_, ...), custom_call_target="tpu_custom_call" | custom-call | flops 1980000000 | bytes 262144 | tf_op jit(solution)/shard_map/pallas_call | solution.py:46
  181.8 1.5 collective-permute-start.38
  184.3 3.1 %collective-permute-start.43 = (bf16[112,2304]{1,0:T(8,128)(2,1)S(1)}, bf16[112,2304]{1,0:T(8,128)(2,1)S(1)}, u32[]{:S(2)}, u32[]{:S(2)}) collective-permute-start(bf16[112,2304]{1,0:T(8,128)(2,1)S(1)} %fusion.3), channel_id=1, source_target_pairs={{0,16},{4,20},{8,24},{12,28},{16,0},{20,4},{24,8},{28,12},{1,17},{... | collective-permute-start | bytes 1548296 | tf_op jit(solution)/shard_map/ppermute | solution.py:941
  187.4 12.8 %shard_map.229 = (bf16[192,512]{1,0:T(8,128)(2,1)S(1)}, bf16[384,512]{1,0:T(8,128)(2,1)S(1)}, bf16[768,512]{1,0:T(8,128)(2,1)S(1)}, bf16[384,384]{1,0:T(8,128)(2,1)S(1)}, bf16[384,384]{1,0:T(8,128)(2,1)S(1)}) custom-call(s32[9]{0:T(128)S(1)} %pad_add_fusion.refs_0_, s32[8]{0:T(128)S(1)} %add_add_fusion.1.refs_0_.refs_1_, ...), custom_call_target="tpu_custom_call" | custom-call | flops 1980000000 | bytes 262144 | tf_op jit(solution)/shard_map/pallas_call | solution.py:46
  202.7 7.6 %collective-permute-done.43.refs_2_ = bf16[112,2304]{1,0:T(8,128)(2,1)S(1)} collective-permute-done((bf16[112,2304]{1,0:T(8,128)(2,1)S(1)}, bf16[112,2304]{1,0:T(8,128)(2,1)S(1)}, u32[]{:S(2)}, u32[]{:S(2)}) %collective-permute-start.43) | collective-permute-done | bytes 516128 | tf_op jit(solution)/shard_map/ppermute | solution.py:941
  211.9 2.8 %shard_map.233.refs_0_.refs_1_ = f32[512,768]{1,0:T(8,128)S(1)} custom-call(bf16[672,512]{1,0:T(8,128)(2,1)S(1)} %collective-permute-done.35.refs_32_.refs_0_, bf16[384,512]{1,0:T(8,128)(2,1)S(1)} %collective-permute-done.38.refs_0_.refs_1_, bf16[384,512]{1,0:T(8,128)(2,1)S(1)} %collective-permute-done.41.refs_2_, ...), custom_call_target="tpu_custom_call" | custom-call | flops 495000000 | bytes 262144 | tf_op jit(solution)/shard_map/pallas_call | solution.py:46
  214.7 1.8 collective-permute-done.45.refs_1_
  216.7 1.8 collective-permute-start.47
  219.1 3.7 %shard_map.235.refs_7_ = f32[512,768]{1,0:T(8,128)} custom-call(bf16[1152,512]{1,0:T(8,128)(2,1)S(1)} %collective-permute-done.44.refs_0_, f32[512,768]{1,0:T(8,128)S(1)} %shard_map.233.refs_0_.refs_1_, bf16[576,768]{1,0:T(8,128)(2,1)} %collective-permute-done.1.refs_6_.refs_2_, bf16[576,768]{1,0:T(8,128)(2,1)S(1)} %collective-permute-done.39.refs_1_.refs_3_, ...), custom_call_target="tpu_custom_call" | custom-call | flops 495000000 | bytes 262144 | tf_op jit(solution)/shard_map/pallas_call | solution.py:46
  224.2 3.1 %shard_map.236 = (f32[96,2,768]{2,1,0:T(2,128)}, f32[96,768]{1,0:T(8,128)}) custom-call(bf16[384,1152]{1,0:T(8,128)(2,1)S(1)} %get-tuple-element.308.refs_0_, bf16[400,1152]{1,0:T(8,128)(2,1)S(1)} %get-tuple-element.309.refs_1_, bf16[208,1152]{1,0:T(8,128)(2,1)S(1)} %get-tuple-element.324.refs_2_, bf16[384,1152]{1,0:T(8,128)(2,1)S(1)} %get-tuple-element.310.refs_3_, ...), custom_call_target="tpu_custom_call" | custom-call | flops 330000000 | bytes 262144 | tf_op jit(solution)/shard_map/pallas_call | solution.py:46
  228.3 1.7 shard_map.237
  (159 shorter events, 33.5 us)
Async XLA Ops:
  1.9 9.2 %collective-permute-start.1 = (bf16[576,768]{1,0:T(8,128)(2,1)S(1)}, bf16[576,768]{1,0:T(8,128)(2,1)}, u32[]{:S(2)}, u32[]{:S(2)}) collective-permute-start(bf16[576,768]{1,0:T(8,128)(2,1)S(1)} %bitcast.15), channel_id=1, source_target_pairs={{0,1},{1,0},{2,3},{3,2},{4,5},{5,4},{6,7},{7,6},{8,9},{9,8},{10,11... | collective-permute-start | bytes 2654216 | tf_op jit(solution)/shard_map/ppermute | solution.py:941
  3.3 7.7 %collective-permute-start = (bf16[528,768]{1,0:T(8,128)(2,1)}, bf16[528,768]{1,0:T(8,128)(2,1)}, u32[]{:S(2)}, u32[]{:S(2)}) collective-permute-start(bf16[528,768]{1,0:T(8,128)(2,1)} %fusion.2.refs_2_.refs_1_), channel_id=1, source_target_pairs={{0,1},{1,0},{2,3},{3,2},{4,5},{5,4},{6,7},{7,6},{8,9},{9,8},{10,11... | collective-permute-start | bytes 2433032 | tf_op jit(solution)/shard_map/ppermute | solution.py:941
  3.5 21.5 %collective-permute-start.2 = (bf16[528,768]{1,0:T(8,128)(2,1)}, bf16[528,768]{1,0:T(8,128)(2,1)}, u32[]{:S(2)}, u32[]{:S(2)}) collective-permute-start(bf16[528,768]{1,0:T(8,128)(2,1)} %fusion.2.refs_2_.refs_1_), channel_id=1, source_target_pairs={{0,2},{1,3},{2,0},{3,1},{4,6},{5,7},{6,4},{7,5},{8,10},{9,11},{10,... | collective-permute-start | bytes 2433032 | tf_op jit(solution)/shard_map/ppermute | solution.py:941
  25.0 4.1 %collective-permute-start.3 = (bf16[528,768]{1,0:T(8,128)(2,1)}, bf16[528,768]{1,0:T(8,128)(2,1)S(1)}, u32[]{:S(2)}, u32[]{:S(2)}) collective-permute-start(bf16[528,768]{1,0:T(8,128)(2,1)} %get-tuple-element.177.refs_2_.refs_3_), channel_id=1, source_target_pairs={{0,1},{1,0},{2,3},{3,2},{4,5},{5,4},{6,7},{7,6},{8,9},{9,8},{10,11... | collective-permute-start | bytes 2433032 | tf_op jit(solution)/shard_map/ppermute | solution.py:941
  25.0 15.7 %collective-permute-start.5 = (bf16[192,1536]{1,0:T(8,128)(2,1)S(1)}, bf16[192,1536]{1,0:T(8,128)(2,1)S(1)}, u32[]{:S(2)}, u32[]{:S(2)}) collective-permute-start(bf16[192,1536]{1,0:T(8,128)(2,1)S(1)} %get-tuple-element.192), channel_id=1, source_target_pairs={{0,2},{1,3},{2,0},{3,1},{4,6},{5,7},{6,4},{7,5},{8,10},{9,11},{10,... | collective-permute-start | bytes 1769480 | tf_op jit(solution)/shard_map/ppermute | solution.py:941
  26.7 3.9 %collective-permute-start.4 = (bf16[192,768]{1,0:T(8,128)(2,1)S(1)}, bf16[192,768]{1,0:T(8,128)(2,1)S(1)}, u32[]{:S(2)}, u32[]{:S(2)}) collective-permute-start(bf16[192,768]{1,0:T(8,128)(2,1)S(1)} %copy-done.4), channel_id=1, source_target_pairs={{0,1},{1,0},{2,3},{3,2},{4,5},{5,4},{6,7},{7,6},{8,9},{9,8},{10,11... | collective-permute-start | bytes 884744 | tf_op jit(solution)/shard_map/ppermute | solution.py:941
  40.7 15.0 %collective-permute-start.6 = (bf16[192,1536]{1,0:T(8,128)(2,1)S(1)}, bf16[192,1536]{1,0:T(8,128)(2,1)S(1)}, u32[]{:S(2)}, u32[]{:S(2)}) collective-permute-start(bf16[192,1536]{1,0:T(8,128)(2,1)S(1)} %get-tuple-element.193.refs_1_), channel_id=1, source_target_pairs={{0,4},{4,0},{8,12},{12,8},{16,20},{20,16},{24,28},{28,24},{1,5},{5... | collective-permute-start | bytes 1769480 | tf_op jit(solution)/shard_map/ppermute | solution.py:941
  42.5 14.7 %collective-permute-start.7 = (bf16[192,1536]{1,0:T(8,128)(2,1)S(1)}, bf16[192,1536]{1,0:T(8,128)(2,1)S(1)}, u32[]{:S(2)}, u32[]{:S(2)}) collective-permute-start(bf16[192,1536]{1,0:T(8,128)(2,1)S(1)} %get-tuple-element.193.refs_1_), channel_id=1, source_target_pairs={{0,8},{4,12},{8,0},{12,4},{16,24},{20,28},{24,16},{28,20},{1,9},{5... | collective-permute-start | bytes 1769480 | tf_op jit(solution)/shard_map/ppermute | solution.py:941
  44.1 14.4 %collective-permute-start.8 = (bf16[384,768]{1,0:T(8,128)(2,1)S(1)}, bf16[384,768]{1,0:T(8,128)(2,1)S(1)}, u32[]{:S(2)}, u32[]{:S(2)}) collective-permute-start(bf16[384,768]{1,0:T(8,128)(2,1)S(1)} %get-tuple-element.201), channel_id=1, source_target_pairs={{0,2},{1,3},{2,0},{3,1},{4,6},{5,7},{6,4},{7,5},{8,10},{9,11},{10,... | collective-permute-start | bytes 1769480 | tf_op jit(solution)/shard_map/ppermute | solution.py:941
  58.5 9.9 %collective-permute-start.10 = (bf16[96,1536]{1,0:T(8,128)(2,1)S(1)}, bf16[96,1536]{1,0:T(8,128)(2,1)S(1)}, u32[]{:S(2)}, u32[]{:S(2)}) collective-permute-start(bf16[96,1536]{1,0:T(8,128)(2,1)S(1)} %get-tuple-element.203), channel_id=1, source_target_pairs={{0,8},{4,12},{8,0},{12,4},{16,24},{20,28},{24,16},{28,20},{1,9},{5... | collective-permute-start | bytes 884744 | tf_op jit(solution)/shard_map/ppermute | solution.py:941
  59.0 9.4 %collective-permute-start.9 = (bf16[96,1536]{1,0:T(8,128)(2,1)S(1)}, bf16[96,1536]{1,0:T(8,128)(2,1)S(1)}, u32[]{:S(2)}, u32[]{:S(2)}) collective-permute-start(bf16[96,1536]{1,0:T(8,128)(2,1)S(1)} %get-tuple-element.202), channel_id=1, source_target_pairs={{0,4},{4,0},{8,12},{12,8},{16,20},{20,16},{24,28},{28,24},{1,5},{5... | collective-permute-start | bytes 884744 | tf_op jit(solution)/shard_map/ppermute | solution.py:941
  59.5 6.9 %collective-permute-start.11 = (bf16[192,512]{1,0:T(8,128)(2,1)S(1)}, bf16[192,512]{1,0:T(8,128)(2,1)S(1)}, u32[]{:S(2)}, u32[]{:S(2)}) collective-permute-start(bf16[192,512]{1,0:T(8,128)(2,1)S(1)} %get-tuple-element.204.refs_20_), channel_id=1, source_target_pairs={{0,2},{1,3},{2,0},{3,1},{4,6},{5,7},{6,4},{7,5},{8,10},{9,11},{10,... | collective-permute-start | bytes 589832 | tf_op jit(solution)/shard_map/ppermute | solution.py:941
  61.0 7.4 %collective-permute-start.12 = (bf16[192,512]{1,0:T(8,128)(2,1)S(1)}, bf16[192,512]{1,0:T(8,128)(2,1)S(1)}, u32[]{:S(2)}, u32[]{:S(2)}) collective-permute-start(bf16[192,512]{1,0:T(8,128)(2,1)S(1)} %get-tuple-element.205.refs_21_), channel_id=1, source_target_pairs={{0,3},{1,2},{2,1},{3,0},{4,7},{5,6},{6,5},{7,4},{8,11},{9,10},{10,... | collective-permute-start | bytes 589832 | tf_op jit(solution)/shard_map/ppermute | solution.py:941
  68.4 2.4 %collective-permute-start.17 = (bf16[192,768]{1,0:T(8,128)(2,1)S(1)}, bf16[192,768]{1,0:T(8,128)(2,1)S(1)}, u32[]{:S(2)}, u32[]{:S(2)}) collective-permute-start(bf16[192,768]{1,0:T(8,128)(2,1)S(1)} %get-tuple-element.213.refs_6_.refs_14_), channel_id=1, source_target_pairs={{0,1},{1,0},{2,3},{3,2},{4,5},{5,4},{6,7},{7,6},{8,9},{9,8},{10,11... | collective-permute-start | bytes 884744 | tf_op jit(solution)/shard_map/ppermute | solution.py:941
  69.3 1.5 collective-permute-start.16
  72.0 5.1 %collective-permute-start.18 = (bf16[256,768]{1,0:T(8,128)(2,1)S(1)}, bf16[256,768]{1,0:T(8,128)(2,1)S(1)}, u32[]{:S(2)}, u32[]{:S(2)}) collective-permute-start(bf16[256,768]{1,0:T(8,128)(2,1)S(1)} %get-tuple-element.215), channel_id=1, source_target_pairs={{0,1},{1,0},{2,3},{3,2},{4,5},{5,4},{6,7},{7,6},{8,9},{9,8},{10,11... | collective-permute-start | bytes 1179656 | tf_op jit(solution)/shard_map/ppermute | solution.py:941
  72.5 5.1 %collective-permute-start.19 = (bf16[256,768]{1,0:T(8,128)(2,1)S(1)}, bf16[256,768]{1,0:T(8,128)(2,1)S(1)}, u32[]{:S(2)}, u32[]{:S(2)}) collective-permute-start(bf16[256,768]{1,0:T(8,128)(2,1)S(1)} %get-tuple-element.216), channel_id=1, source_target_pairs={{0,1},{1,0},{2,3},{3,2},{4,5},{5,4},{6,7},{7,6},{8,9},{9,8},{10,11... | collective-permute-start | bytes 1179656 | tf_op jit(solution)/shard_map/ppermute | solution.py:941
  72.6 24.4 %collective-permute-start.22 = (bf16[512,768]{1,0:T(8,128)(2,1)S(1)}, bf16[512,768]{1,0:T(8,128)(2,1)S(1)}, u32[]{:S(2)}, u32[]{:S(2)}) collective-permute-start(bf16[512,768]{1,0:T(8,128)(2,1)S(1)} %get-tuple-element.217.refs_2_.refs_0_.refs_6_), channel_id=1, source_target_pairs={{0,2},{1,3},{2,0},{3,1},{4,6},{5,7},{6,4},{7,5},{8,10},{9,11},{10,... | collective-permute-start | bytes 2359304 | tf_op jit(solution)/shard_map/ppermute | solution.py:941
  74.1 12.4 %collective-permute-start.13 = (bf16[192,768]{1,0:T(8,128)(2,1)S(1)}, bf16[192,768]{1,0:T(8,128)(2,1)S(1)}, u32[]{:S(2)}, u32[]{:S(2)}) collective-permute-start(bf16[192,768]{1,0:T(8,128)(2,1)S(1)} %get-tuple-element.211.refs_6_), channel_id=1, source_target_pairs={{0,4},{4,0},{8,12},{12,8},{16,20},{20,16},{24,28},{28,24},{1,5},{5... | collective-permute-start | bytes 884744 | tf_op jit(solution)/shard_map/ppermute | solution.py:941
  75.6 10.9 %collective-permute-start.14 = (bf16[192,768]{1,0:T(8,128)(2,1)S(1)}, bf16[192,768]{1,0:T(8,128)(2,1)S(1)}, u32[]{:S(2)}, u32[]{:S(2)}) collective-permute-start(bf16[192,768]{1,0:T(8,128)(2,1)S(1)} %get-tuple-element.211.refs_6_), channel_id=1, source_target_pairs={{0,8},{4,12},{8,0},{12,4},{16,24},{20,28},{24,16},{28,20},{1,9},{5... | collective-permute-start | bytes 884744 | tf_op jit(solution)/shard_map/ppermute | solution.py:941
  77.1 13.5 %collective-permute-start.15 = (bf16[192,768]{1,0:T(8,128)(2,1)S(1)}, bf16[192,768]{1,0:T(8,128)(2,1)S(1)}, u32[]{:S(2)}, u32[]{:S(2)}) collective-permute-start(bf16[192,768]{1,0:T(8,128)(2,1)S(1)} %get-tuple-element.211.refs_6_), channel_id=1, source_target_pairs={{0,12},{4,8},{8,4},{12,0},{16,28},{20,24},{24,20},{28,16},{1,13},{... | collective-permute-start | bytes 884744 | tf_op jit(solution)/shard_map/ppermute | solution.py:941
  93.9 3.1 %collective-permute-start.20 = (bf16[256,768]{1,0:T(8,128)(2,1)S(1)}, bf16[256,768]{1,0:T(8,128)(2,1)S(1)}, u32[]{:S(2)}, u32[]{:S(2)}) collective-permute-start(bf16[256,768]{1,0:T(8,128)(2,1)S(1)} %get-tuple-element.230.refs_4_), channel_id=1, source_target_pairs={{0,1},{1,0},{2,3},{3,2},{4,5},{5,4},{6,7},{7,6},{8,9},{9,8},{10,11... | collective-permute-start | bytes 1179656 | tf_op jit(solution)/shard_map/ppermute | solution.py:941
  94.0 3.0 %collective-permute-start.21 = (bf16[256,768]{1,0:T(8,128)(2,1)S(1)}, bf16[256,768]{1,0:T(8,128)(2,1)S(1)}, u32[]{:S(2)}, u32[]{:S(2)}) collective-permute-start(bf16[256,768]{1,0:T(8,128)(2,1)S(1)} %get-tuple-element.231), channel_id=1, source_target_pairs={{0,1},{1,0},{2,3},{3,2},{4,5},{5,4},{6,7},{7,6},{8,9},{9,8},{10,11... | collective-permute-start | bytes 1179656 | tf_op jit(solution)/shard_map/ppermute | solution.py:941
  102.0 4.4 %collective-permute-start.23 = (bf16[512,768]{1,0:T(8,128)(2,1)S(1)}, bf16[512,768]{1,0:T(8,128)(2,1)S(1)}, u32[]{:S(2)}, u32[]{:S(2)}) collective-permute-start(bf16[512,768]{1,0:T(8,128)(2,1)S(1)} %get-tuple-element.254.refs_0_.refs_2_), channel_id=1, source_target_pairs={{0,1},{1,0},{2,3},{3,2},{4,5},{5,4},{6,7},{7,6},{8,9},{9,8},{10,11... | collective-permute-start | bytes 2359304 | tf_op jit(solution)/shard_map/ppermute | solution.py:941
  102.1 14.2 %collective-permute-start.26 = (bf16[512,768]{1,0:T(8,128)(2,1)S(1)}, bf16[512,768]{1,0:T(8,128)(2,1)S(1)}, u32[]{:S(2)}, u32[]{:S(2)}) collective-permute-start(bf16[512,768]{1,0:T(8,128)(2,1)S(1)} %get-tuple-element.266.refs_6_.refs_8_), channel_id=1, source_target_pairs={{0,1},{1,0},{2,3},{3,2},{4,5},{5,4},{6,7},{7,6},{8,9},{9,8},{10,11... | collective-permute-start | bytes 2359304 | tf_op jit(solution)/shard_map/ppermute | solution.py:941
  102.5 19.5 %collective-permute-start.27 = (bf16[512,768]{1,0:T(8,128)(2,1)S(1)}, bf16[512,768]{1,0:T(8,128)(2,1)S(1)}, u32[]{:S(2)}, u32[]{:S(2)}) collective-permute-start(bf16[512,768]{1,0:T(8,128)(2,1)S(1)} %get-tuple-element.254.refs_0_.refs_2_), channel_id=1, source_target_pairs={{0,2},{1,3},{2,0},{3,1},{4,6},{5,7},{6,4},{7,5},{8,10},{9,11},{10,... | collective-permute-start | bytes 2359304 | tf_op jit(solution)/shard_map/ppermute | solution.py:941
  112.4 3.9 %collective-permute-start.24 = (bf16[256,768]{1,0:T(8,128)(2,1)S(1)}, bf16[256,768]{1,0:T(8,128)(2,1)S(1)}, u32[]{:S(2)}, u32[]{:S(2)}) collective-permute-start(bf16[256,768]{1,0:T(8,128)(2,1)S(1)} %get-tuple-element.261.refs_6_), channel_id=1, source_target_pairs={{0,1},{1,0},{2,3},{3,2},{4,5},{5,4},{6,7},{7,6},{8,9},{9,8},{10,11... | collective-permute-start | bytes 1179656 | tf_op jit(solution)/shard_map/ppermute | solution.py:941
  112.5 3.8 %collective-permute-start.25 = (bf16[256,768]{1,0:T(8,128)(2,1)S(1)}, bf16[256,768]{1,0:T(8,128)(2,1)S(1)}, u32[]{:S(2)}, u32[]{:S(2)}) collective-permute-start(bf16[256,768]{1,0:T(8,128)(2,1)S(1)} %get-tuple-element.262), channel_id=1, source_target_pairs={{0,1},{1,0},{2,3},{3,2},{4,5},{5,4},{6,7},{7,6},{8,9},{9,8},{10,11... | collective-permute-start | bytes 1179656 | tf_op jit(solution)/shard_map/ppermute | solution.py:941
  122.1 2.3 collective-permute-start.31
  122.1 11.3 %collective-permute-start.28 = (bf16[784,512]{1,0:T(8,128)(2,1)S(1)}, bf16[784,512]{1,0:T(8,128)(2,1)S(1)}, u32[]{:S(2)}, u32[]{:S(2)}) collective-permute-start(bf16[784,512]{1,0:T(8,128)(2,1)S(1)} %get-tuple-element.271), channel_id=1, source_target_pairs={{0,1},{1,0},{2,3},{3,2},{4,5},{5,4},{6,7},{7,6},{8,9},{9,8},{10,11... | collective-permute-start | bytes 2408456 | tf_op jit(solution)/shard_map/ppermute | solution.py:941
  122.6 10.4 %collective-permute-start.29 = (bf16[208,512]{1,0:T(8,128)(2,1)S(1)}, bf16[208,512]{1,0:T(8,128)(2,1)S(1)}, u32[]{:S(2)}, u32[]{:S(2)}) collective-permute-start(bf16[208,512]{1,0:T(8,128)(2,1)S(1)} %get-tuple-element.272), channel_id=1, source_target_pairs={{0,2},{1,3},{2,0},{3,1},{4,6},{5,7},{6,4},{7,5},{8,10},{9,11},{10,... | collective-permute-start | bytes 638984 | tf_op jit(solution)/shard_map/ppermute | solution.py:941
  123.1 10.2 %collective-permute-start.30 = (bf16[208,512]{1,0:T(8,128)(2,1)S(1)}, bf16[208,512]{1,0:T(8,128)(2,1)S(1)}, u32[]{:S(2)}, u32[]{:S(2)}) collective-permute-start(bf16[208,512]{1,0:T(8,128)(2,1)S(1)} %get-tuple-element.273), channel_id=1, source_target_pairs={{0,3},{1,2},{2,1},{3,0},{4,7},{5,6},{6,5},{7,4},{8,11},{9,10},{10,... | collective-permute-start | bytes 638984 | tf_op jit(solution)/shard_map/ppermute | solution.py:941
  141.1 24.9 %collective-permute-start.32 = (bf16[400,1152]{1,0:T(8,128)(2,1)S(1)}, bf16[400,1152]{1,0:T(8,128)(2,1)S(1)}, u32[]{:S(2)}, u32[]{:S(2)}) collective-permute-start(bf16[400,1152]{1,0:T(8,128)(2,1)S(1)} %get-tuple-element.298), channel_id=1, source_target_pairs={{0,4},{4,0},{8,12},{12,8},{16,20},{20,16},{24,28},{28,24},{1,5},{5... | collective-permute-start | bytes 2764808 | tf_op jit(solution)/shard_map/ppermute | solution.py:941
  142.7 22.1 %collective-permute-start.33 = (bf16[384,1152]{1,0:T(8,128)(2,1)S(1)}, bf16[384,1152]{1,0:T(8,128)(2,1)S(1)}, u32[]{:S(2)}, u32[]{:S(2)}) collective-permute-start(bf16[384,1152]{1,0:T(8,128)(2,1)S(1)} %get-tuple-element.299), channel_id=1, source_target_pairs={{0,8},{4,12},{8,0},{12,4},{16,24},{20,28},{24,16},{28,20},{1,9},{5... | collective-permute-start | bytes 2654216 | tf_op jit(solution)/shard_map/ppermute | solution.py:941
  144.2 21.8 %collective-permute-start.34 = (bf16[576,768]{1,0:T(8,128)(2,1)S(1)}, bf16[576,768]{1,0:T(8,128)(2,1)S(1)}, u32[]{:S(2)}, u32[]{:S(2)}) collective-permute-start(bf16[576,768]{1,0:T(8,128)(2,1)S(1)} %get-tuple-element.300.refs_7_), channel_id=1, source_target_pairs={{0,2},{1,3},{2,0},{3,1},{4,6},{5,7},{6,4},{7,5},{8,10},{9,11},{10,... | collective-permute-start | bytes 2654216 | tf_op jit(solution)/shard_map/ppermute | solution.py:941
  166.2 15.3 %collective-permute-start.36 = (bf16[208,1152]{1,0:T(8,128)(2,1)S(1)}, bf16[208,1152]{1,0:T(8,128)(2,1)S(1)}, u32[]{:S(2)}, u32[]{:S(2)}) collective-permute-start(bf16[208,1152]{1,0:T(8,128)(2,1)S(1)} %pad_maximum_fusion.1), channel_id=1, source_target_pairs={{0,8},{4,12},{8,0},{12,4},{16,24},{20,28},{24,16},{28,20},{1,9},{5... | collective-permute-start | bytes 1437704 | tf_op jit(solution)/shard_map/ppermute | solution.py:941
  166.9 14.5 %collective-permute-start.37 = (bf16[192,1152]{1,0:T(8,128)(2,1)S(1)}, bf16[192,1152]{1,0:T(8,128)(2,1)S(1)}, u32[]{:S(2)}, u32[]{:S(2)}) collective-permute-start(bf16[192,1152]{1,0:T(8,128)(2,1)S(1)} %add_convert_fusion), channel_id=1, source_target_pairs={{0,4},{4,0},{8,12},{12,8},{16,20},{20,16},{24,28},{28,24},{1,5},{5... | collective-permute-start | bytes 1327112 | tf_op jit(solution)/shard_map/ppermute | solution.py:941
  167.8 19.6 %collective-permute-start.35 = (bf16[672,512]{1,0:T(8,128)(2,1)S(1)}, bf16[672,512]{1,0:T(8,128)(2,1)S(1)}, u32[]{:S(2)}, u32[]{:S(2)}) collective-permute-start(bf16[672,512]{1,0:T(8,128)(2,1)S(1)} %get-tuple-element.303), channel_id=1, source_target_pairs={{0,2},{1,3},{2,0},{3,1},{4,6},{5,7},{6,4},{7,5},{8,10},{9,11},{10,... | collective-permute-start | bytes 2064392 | tf_op jit(solution)/shard_map/ppermute | solution.py:941
  181.7 18.5 %collective-permute-start.39 = (bf16[576,768]{1,0:T(8,128)(2,1)S(1)}, bf16[576,768]{1,0:T(8,128)(2,1)S(1)}, u32[]{:S(2)}, u32[]{:S(2)}) collective-permute-start(bf16[576,768]{1,0:T(8,128)(2,1)S(1)} %get-tuple-element.316.refs_8_), channel_id=1, source_target_pairs={{0,1},{1,0},{2,3},{3,2},{4,5},{5,4},{6,7},{7,6},{8,9},{9,8},{10,11... | collective-permute-start | bytes 2654216 | tf_op jit(solution)/shard_map/ppermute | solution.py:941
  181.8 18.4 %collective-permute-start.38 = (bf16[384,512]{1,0:T(8,128)(2,1)S(1)}, bf16[384,512]{1,0:T(8,128)(2,1)S(1)}, u32[]{:S(2)}, u32[]{:S(2)}) collective-permute-start(bf16[384,512]{1,0:T(8,128)(2,1)S(1)} %get-tuple-element.315), channel_id=1, source_target_pairs={{0,2},{1,3},{2,0},{3,1},{4,6},{5,7},{6,4},{7,5},{8,10},{9,11},{10,... | collective-permute-start | bytes 1179656 | tf_op jit(solution)/shard_map/ppermute | solution.py:941
  183.3 16.9 %collective-permute-start.40 = (bf16[384,384]{1,0:T(8,128)(2,1)S(1)}, bf16[384,384]{1,0:T(8,128)(2,1)S(1)}, u32[]{:S(2)}, u32[]{:S(2)}) collective-permute-start(bf16[384,384]{1,0:T(8,128)(2,1)S(1)} %get-tuple-element.320), channel_id=1, source_target_pairs={{0,4},{4,0},{8,12},{12,8},{16,20},{20,16},{24,28},{28,24},{1,5},{5... | collective-permute-start | bytes 884744 | tf_op jit(solution)/shard_map/ppermute | solution.py:941
  184.3 26.0 %collective-permute-start.43 = (bf16[112,2304]{1,0:T(8,128)(2,1)S(1)}, bf16[112,2304]{1,0:T(8,128)(2,1)S(1)}, u32[]{:S(2)}, u32[]{:S(2)}) collective-permute-start(bf16[112,2304]{1,0:T(8,128)(2,1)S(1)} %fusion.3), channel_id=1, source_target_pairs={{0,16},{4,20},{8,24},{12,28},{16,0},{20,4},{24,8},{28,12},{1,17},{... | collective-permute-start | bytes 1548296 | tf_op jit(solution)/shard_map/ppermute | solution.py:941
  200.3 10.1 %collective-permute-start.42 = (bf16[384,384]{1,0:T(8,128)(2,1)S(1)}, bf16[384,384]{1,0:T(8,128)(2,1)S(1)}, u32[]{:S(2)}, u32[]{:S(2)}) collective-permute-start(bf16[384,384]{1,0:T(8,128)(2,1)S(1)} %get-tuple-element.323), channel_id=1, source_target_pairs={{0,4},{4,0},{8,12},{12,8},{16,20},{20,16},{24,28},{28,24},{1,5},{5... | collective-permute-start | bytes 884744 | tf_op jit(solution)/shard_map/ppermute | solution.py:941
  200.8 10.3 %collective-permute-start.41 = (bf16[384,512]{1,0:T(8,128)(2,1)S(1)}, bf16[384,512]{1,0:T(8,128)(2,1)S(1)}, u32[]{:S(2)}, u32[]{:S(2)}) collective-permute-start(bf16[384,512]{1,0:T(8,128)(2,1)S(1)} %get-tuple-element.321), channel_id=1, source_target_pairs={{0,2},{1,3},{2,0},{3,1},{4,6},{5,7},{6,4},{7,5},{8,10},{9,11},{10,... | collective-permute-start | bytes 1179656 | tf_op jit(solution)/shard_map/ppermute | solution.py:941
  201.4 13.3 %collective-permute-start.46 = (bf16[192,384]{1,0:T(8,128)(2,1)S(1)}, bf16[192,384]{1,0:T(8,128)(2,1)S(1)}, u32[]{:S(2)}, u32[]{:S(2)}) collective-permute-start(bf16[192,384]{1,0:T(8,128)(2,1)S(1)} %add_convert_fusion.4), channel_id=1, source_target_pairs={{0,8},{4,12},{8,0},{12,4},{16,24},{20,28},{24,16},{28,20},{1,9},{5... | collective-permute-start | bytes 442376 | tf_op jit(solution)/shard_map/ppermute | solution.py:941
  210.4 6.2 %collective-permute-start.45 = (bf16[192,384]{1,0:T(8,128)(2,1)S(1)}, bf16[192,384]{1,0:T(8,128)(2,1)S(1)}, u32[]{:S(2)}, u32[]{:S(2)}) collective-permute-start(bf16[192,384]{1,0:T(8,128)(2,1)S(1)} %add_convert_fusion.5), channel_id=1, source_target_pairs={{0,8},{4,12},{8,0},{12,4},{16,24},{20,28},{24,16},{28,20},{1,9},{5... | collective-permute-start | bytes 442376 | tf_op jit(solution)/shard_map/ppermute | solution.py:941
  211.8 7.4 %collective-permute-start.44 = (bf16[1152,512]{1,0:T(8,128)(2,1)S(1)}, bf16[1152,512]{1,0:T(8,128)(2,1)S(1)}, u32[]{:S(2)}, u32[]{:S(2)}) collective-permute-start(bf16[1152,512]{1,0:T(8,128)(2,1)S(1)} %shard_map.232.refs_9_), channel_id=1, source_target_pairs={{0,1},{1,0},{2,3},{3,2},{4,5},{5,4},{6,7},{7,6},{8,9},{9,8},{10,11... | collective-permute-start | bytes 3538952 | tf_op jit(solution)/shard_map/ppermute | solution.py:941
  216.7 10.7 %collective-permute-start.47 = (bf16[96,768]{1,0:T(8,128)(2,1)S(1)}, bf16[96,768]{1,0:T(8,128)(2,1)S(1)}, u32[]{:S(2)}, u32[]{:S(2)}) collective-permute-start(bf16[96,768]{1,0:T(8,128)(2,1)S(1)} %pad_maximum_fusion.2), channel_id=1, source_target_pairs={{0,16},{4,20},{8,24},{12,28},{16,0},{20,4},{24,8},{28,12},{1,17},{... | collective-permute-start | bytes 442376 | tf_op jit(solution)/shard_map/ppermute | solution.py:941
  (13 other events, 40.2 us)

commit v5 on v4

--- a/solution.py
+++ b/solution.py
@@ -1,4 +1,5 @@
 import functools
+import math
 
 import jax
 import jax.numpy as jnp
@@ -36,6 +37,16 @@
     in_vmem = pl.BlockSpec(memory_space=pltpu.VMEM)
     anywhere = pl.BlockSpec(memory_space=pl.ANY)
     awaits = (*awaits, *ORDER.last)
+    sizes = [math.prod(shape) for n, (shape, dtype) in enumerate(outs) if n not in hbm]
+    token = not sizes or min(sizes) > 1 << 15
+    if token:
+        inner, outs = kernel, [*outs, ((8, 128), F32)]
+
+        def kernel(*refs):
+            spot = n_in + len(outs) - 1
+            refs[spot][...] = jnp.zeros((8, 128), F32)
+            inner(*refs[:spot], *refs[spot + 1 :])
+
     n_in = len(scalars) + len(apart) + len(args)
     n_skip, n_out = len(awaits) + len(carry), len(outs)
 
@@ -57,7 +68,9 @@
         compiler_params=pltpu.CompilerParams(vmem_limit_bytes=mib << 20),
         cost_estimate=pl.CostEstimate(flops=int(us * SCALE * 1.1e9), bytes_accessed=1 << 18, transcendentals=0),
     )(*scalars, *apart, *args, *awaits, *carry)
-    ORDER.last = (min(results[:n_out], key=lambda r: r.size),)
+    ORDER.last = (min((r for n, r in enumerate(results[:n_out]) if n not in hbm), key=lambda r: r.size),)
+    if token:
+        results = [*results[: n_out - 1], *results[n_out:]]
     return results
 
 
@@ -459,19 +472,53 @@
     )
 
 
-PART_PLACES = ((0, 0, 0, 2), (0, 1, 0, 2), (0, 2, 0, 2), (0, 3, 0, 1), (0, 3, 1, 1)) + tuple((1, n, 0, 2) for n in range(4))
+def part_places(half):
+    places = [(n, 0, 2 * half, 0, 0, n, 0) for n in range(3)]
+    for n, quarter in ((3, 1), (4, 2)):
+        places.append((n, 0, half, 0, 0, 3, (n - 3) * half))
+        places += [(n, half, half, side, 1, quarter, side * half) for side in range(2)]
+    return places + [(5, 0, 2 * half, 0, 1, 0, 0), (6, 0, 2 * half, 0, 1, 3, 0)]
+
+
+N_PARTS, N_PLACES = 7, 11
 
 
 def gather_weights(at_ref, parts, wgu, wd, sem):
     copies = []
-    for n, (part, (which, quarter, first, count)) in enumerate(zip(parts, PART_PLACES)):
+    half, width = wgu.shape[0] // 8, wd.shape[1]
+    for n, (part, first, count, side, which, quarter, row) in enumerate(part_places(half)):
         dst = (wgu, wd)[which]
-        half = dst.shape[0] // 8
-        spot = pl.ds(pl.multiple_of((at_ref[0] ^ quarter) * (2 * half) + first * half, half), count * half)
-        copies.append(pltpu.make_async_copy(part, dst.at[spot, :], sem.at[n]))
+        spot = pl.multiple_of((at_ref[0] ^ quarter) * (2 * half) + row, half)
+        src = parts[part].at[pl.ds(first, count), pl.ds(side * width, dst.shape[1])]
+        copies.append(pltpu.make_async_copy(src, dst.at[pl.ds(spot, count), :], sem.at[n]))
     for c in copies:
         c.start()
     return copies
+
+
+def pack_kernel(pb1, pb2, pa, to_y, to_z, pa_out, wo_out, sem):
+    half, wide = to_y.shape[0] // 2, pa.shape[1]
+    pairs = [
+        (pb2.at[pl.ds(0, half), :], to_y.at[pl.ds(0, half), :]),
+        (pb1.at[pl.ds(half, half), :], to_z.at[pl.ds(0, half), :]),
+        (pa.at[pl.ds(0, 2 * half), :], pa_out),
+        (pa.at[pl.ds(2 * half, wo_out.shape[0]), :], wo_out),
+    ]
+    for dst in (to_y, to_z):
+        for side in range(2):
+            spot = dst.at[pl.ds(half, half), pl.ds(side * wide, wide)]
+            pairs.append((pa.at[pl.ds(side * half, half), :], spot))
+    copies = [pltpu.make_async_copy(src, dst, sem.at[n]) for n, (src, dst) in enumerate(pairs)]
+    for c in copies:
+        c.start()
+    for c in copies:
+        c.wait()
+
+
+def pack_parts(pb1, pb2, pa):
+    rows, wide = pb1.shape
+    outs = [(pb1.shape, BF16)] * 2 + [((rows, pa.shape[1]), BF16), ((pa.shape[0] - rows, pa.shape[1]), BF16)]
+    return run(pack_kernel, 1, 4, (), (), outs, [pltpu.SemaphoreType.DMA((8,))], apart=(pb1, pb2, pa))
 
 
 def mlp_rows(x, wg, wu, down, da, db, hid):
@@ -513,7 +560,7 @@
     saved = ((2 * rows, hidden), BF16)
     return run(
         mlp_own_kernel,
-        5,
+        0.1,
         10,
         (),
         (ml0, wgu, wd),
@@ -533,7 +580,7 @@
 
 
 def mlp_far_kernel(at_ref, *refs):
-    n_parts = len(PART_PLACES)
+    n_parts = N_PARTS
     ml1, acc, sib0, sib1, da, db, wgu, wd, sem = refs[n_parts:]
     rows = ml1.shape[0]
     for c in gather_weights(at_ref, refs[:n_parts], wgu, wd, sem):
@@ -555,7 +602,7 @@
         [((rows // 2, width), BF16)] * 2
         + [((rows, hidden), BF16)] * 2
         + [((width, 2 * hidden), BF16), ((hidden, width), BF16)],
-        [pltpu.SemaphoreType.DMA((len(parts),))],
+        [pltpu.SemaphoreType.DMA((N_PLACES,))],
         awaits,
         apart=parts,
     )
@@ -1108,7 +1155,7 @@
     part_b = quarter_of(wgu)
     part_a = jnp.concatenate([quarter_of(down_weight), wo0], axis=0)
 
-    proj = [project(0, sp, freqs, tok0, wt), project(1, sp, freqs, tok1, wt, awaits=(part_a, part_b, wt1))]
+    proj = [project(0, sp, freqs, tok0, wt), project(1, sp, freqs, tok1, wt, awaits=(part_a, part_b))]
     tok2, part_b = gate(tok2, part_b)
     tok3, pb0 = swap(tok2, 1), swap(part_b, 2)
     tok = (tok0, tok1, tok2, tok3)
@@ -1117,32 +1164,33 @@
     proj.append(more)
     pa0 = swap(part_a, 2)
     qt, kt, k, vt, cs = zip(*proj)
-    o2, o3, q2, q3 = attend(1, sp, qt, k, vt, (wo1,))
+    o2, o3, q2, q3 = attend(1, sp, qt, k, vt, (wo1, wt1))
     o2, pb0 = gate(o2, pb0)
     pb1, pb2, g2 = swap(pb0, 1, "dp"), swap(pb0, 2, "dp"), swap(o2, 2)
     o0, o1, q0, q1 = attend(0, sp, qt, k, vt)
-    half2, half1 = park((), ((pb2, 0), (pb1, 1)))
-    half2, half1, o3, pa0 = gate(half2, half1, o3, pa0)
-    g3, pb3 = swap(o3, 3), (swap(half2, 1, "dp"), swap(half1, 2, "dp"))
+    (o3,) = gate(o3, awaits=(pa0,))
+    g3 = swap(o3, 3)
     (tok_t,) = transposed(fast, (spots,), tok, rows)
     if not fast:
         tok_t = arranged(tok_t.T, spots).T
-    pa0, wo2 = park((), ((pa0, 0), (pa0, 1)))
-    o1, pa0, wo2 = gate(o1, pa0, wo2, awaits=(g2, g3, *pb3))
-    g1, wo3 = swap(o1, 1), swap(wo2, 1)
-    pa1, pa2, pa3 = swap(pa0, 1, "dp"), swap(pa0, 2, "dp"), swap(pa0, 3, "dp")
+    (o1,) = gate(o1)
+    g1 = swap(o1, 1)
+    to_y, to_z, pa0, wo2 = pack_parts(pb1, pb2, pa0)
+    (wo2,) = gate(wo2)
+    wo3 = swap(wo2, 1)
+    kept = park((*kt, *k, *vt, q0, q1, q2, q3, tok_t))
+    kt, k, vt, (q0, q1, q2, q3, tok_t) = kept[0:4], kept[4:8], kept[8:12], kept[12:17]
+    from_y, from_z, pa3 = swap(to_y, 1, "dp"), swap(to_z, 2, "dp"), swap(pa0, 3, "dp")
     wo = (wo0, wo1, wo2, wo3)
 
     gain1, bias1, gain2, bias2 = (u.reshape(1, width) for u in (norm1_gain, norm1_bias, norm2_gain, norm2_bias))
     ml0, xhat1, inv1, *halves = out_project((o0, g1, g2, g3), wo, tokens, gain1, bias1)
+    acc, da_o, db_o, hid_o, ml1 = mlp_own(ml0, [swap(u, 1) for u in halves], wgu, down_weight)
+    (ml0,) = gate(ml0, awaits=(from_y, from_z, pa3))
     ml2 = swap(ml0, 2)
-    acc, da_o, db_o, hid_o, ml1 = mlp_own(ml0, [swap(u, 1) for u in halves], wgu, down_weight)
-    parts = (pb0, pb1, pb2, *pb3, pa0, pa1, pa2, pa3)
-    kept = park((*kt, *k, *vt, q0, q1, q2, q3, tok_t))
-    kt, k, vt, (q0, q1, q2, q3, tok_t) = kept[0:4], kept[4:8], kept[8:12], kept[12:17]
+    parts = (pb0, pb1, pb2, from_y, from_z, pa0, pa3)
     sib0, sib1, da_1, db_1, wgu_p, wd_p = mlp_far(quarter, ml1, acc, parts)
     own, da_0, db_0 = mlp_last(ml0, acc, wgu_p, wd_p)
-    gate(awaits=(ml2,))
     output, dh2, dm0, sums2 = mid_norm(
         xhat1, own, (swap(sib0, 1), swap(sib1, 1)), out_grad, gain1, bias1, gain2, bias2
     )

time: 235 us -> 231 us (0.983)
  local copies, waits for them, and re-layouts: 7.71 us -> 4.34 us
    unnamed x31 -> x24, local copies, waits for them, and re-layouts: 6.91 us -> 3.54 us
    ppermute x48 -> x46, starting transfers between devices: 39.7 us -> 37.7 us  [swap(): return lax.ppermute(v, axis, [(i, i ^ bit) for i in range(n)])]
    ppermute x48 -> x46, waiting for transfers between devices: 50.2 us -> 51.9 us  [swap(): return lax.ppermute(v, axis, [(i, i ^ bit) for i in range(n)])]
  transfers between devices with their start and end apart: 48 -> 46, of which waited for: 17 -> 16; matrix products, arithmetic and copies ran while one was open for 2% -> 2% of each run, Pallas kernels for 50% -> 53%
where the time goes in v5:
time: 231 us; the launch traced here: 227 us
  Pallas kernels  129 us (56%)
  waiting for transfers between devices  51.9 us (22%)
  starting transfers between devices  37.7 us (16%)
  local copies, waits for them, and re-layouts  4.34 us (2%)
    pallas_call x43, Pallas kernels, run(): pl.pallas_call(body, in_specs=[pl.BlockSpec(memory_space=pltpu.SMEM)] * l...  129 us
    ppermute x46, waiting for transfers between devices, swap(): return lax.ppermute(v, axis, [(i, i ^ bit) for i in range(n)])  51.9 us
    ppermute x46, starting transfers between devices, swap(): return lax.ppermute(v, axis, [(i, i ^ bit) for i in range(n)])  37.7 us
  transfers between devices with their start and end apart: 46, of which 16 were waited for; matrix products, arithmetic and copies ran while one was open for 2% of the time, Pallas kernels for 53%

profile of v5, /device:TPU:0, one launch (start us, length us, event | category | flops | bytes accessed | tf_op | source)
XLA Modules:
  0.0 226.7 jit_solution(2342816775794729193)
XLA Ops:
  3.5 2.5 %collective-permute-start.1 = (bf16[528,768]{1,0:T(8,128)(2,1)}, bf16[528,768]{1,0:T(8,128)(2,1)}, u32[]{:S(2)}, u32[]{:S(2)}) collective-permute-start(bf16[528,768]{1,0:T(8,128)(2,1)} %fusion.2.refs_2_.refs_1_), channel_id=1, source_target_pairs={{0,2},{1,3},{2,0},{3,1},{4,6},{5,7},{6,4},{7,5},{8,10},{9,11},{10,... | collective-permute-start | bytes 2433032 | tf_op jit(solution)/shard_map/ppermute | solution.py:988
  6.2 2.1 copy.56
  8.5 2.3 shard_map.195
  10.9 2.1 shard_map.196
  13.1 11.9 %collective-permute-done.1.refs_1_ = bf16[528,768]{1,0:T(8,128)(2,1)} collective-permute-done((bf16[528,768]{1,0:T(8,128)(2,1)}, bf16[528,768]{1,0:T(8,128)(2,1)}, u32[]{:S(2)}, u32[]{:S(2)}) %collective-permute-start.1) | collective-permute-done | bytes 811040 | tf_op jit(solution)/shard_map/ppermute | solution.py:988
  25.0 1.7 collective-permute-start.5
  27.0 2.1 shard_map.198
  29.1 1.5 shard_map.199
  31.0 7.6 %shard_map.200 = (bf16[192,512]{1,0:T(8,128)(2,1)S(1)}, bf16[192,512]{1,0:T(8,128)(2,1)S(1)}, bf16[3,128,512]{2,1,0:T(8,128)(2,1)S(1)}, bf16[3,128,512]{2,1,0:T(8,128)(2,1)S(1)}, f32[8,128]{1,0:T(8,128)S(1)}) custom-call(s32[9]{0:T(128)S(1)} %pad_add_fusion.refs_0_, bf16[3,128,512]{2,1,0:T(8,128)(2,1)S(1)} %get-tuple-element.204.refs_1_, ...), custom_call_target="tpu_custom_call" | custom-call | flops 1320000000 | bytes 262144 | tf_op jit(solution)/shard_map/pallas_call | solution.py:57
  38.6 2.5 %collective-permute-done.5.refs_2_ = bf16[192,1536]{1,0:T(8,128)(2,1)S(1)} collective-permute-done((bf16[192,1536]{1,0:T(8,128)(2,1)S(1)}, bf16[192,1536]{1,0:T(8,128)(2,1)S(1)}, u32[]{:S(2)}, u32[]{:S(2)}) %collective-permute-start.5) | collective-permute-done | bytes 589856 | tf_op jit(solution)/shard_map/ppermute | solution.py:988
  41.1 1.8 collective-permute-start.6
  42.9 1.6 collective-permute-start.7
  44.5 1.5 collective-permute-start.13
  46.0 6.8 %shard_map.202 = (bf16[192,512]{1,0:T(8,128)(2,1)S(1)}, bf16[192,512]{1,0:T(8,128)(2,1)S(1)}, bf16[3,128,512]{2,1,0:T(8,128)(2,1)S(1)}, bf16[3,128,512]{2,1,0:T(8,128)(2,1)S(1)}, f32[8,128]{1,0:T(8,128)S(1)}) custom-call(s32[9]{0:T(128)S(1)} %pad_add_fusion.refs_0_, bf16[3,128,512]{2,1,0:T(8,128)(2,1)S(1)} %get-tuple-element.221.refs_1_, ...), custom_call_target="tpu_custom_call" | custom-call | flops 1320000000 | bytes 262144 | tf_op jit(solution)/shard_map/pallas_call | solution.py:57
  53.8 2.6 %shard_map.204 = (bf16[768,2048]{1,0:T(8,128)(2,1)S(1)}, f32[8,128]{1,0:T(8,128)S(1)}) custom-call(s32[8]{0:T(128)S(1)} %add_add_fusion.1.refs_0_.refs_1_, bf16[528,768]{1,0:T(8,128)(2,1)} %fusion.2.refs_2_.refs_1_, bf16[528,768]{1,0:T(8,128)(2,1)} %collective-permute-done.refs_2_, bf16[528,768]{1,0:T(8,128)(2,1)} %get-tuple-element.202.refs_2_.refs_3_, ...), custom_call_target="tpu_custom_call" | custom-call | flops 330000000 | bytes 262144 | tf_op jit(solution)/shard_map/pallas_call | solution.py:57
  59.4 1.6 collective-permute-start.10
  61.9 3.6 %shard_map.208 = (bf16[3,128,512]{2,1,0:T(8,128)(2,1)S(1)}, bf16[3,128,512]{2,1,0:T(8,128)(2,1)S(1)}, bf16[3,128,512]{2,1,0:T(8,128)(2,1)S(1)}, bf16[3,128,512]{...) custom-call(bf16[3,128,512]{2,1,0:T(8,128)(2,1)S(1)} %get-tuple-elem, ...), custom_call_target="tpu_custom_call" | custom-call | flops 495000000 | bytes 262144 | tf_op jit(solution)/shard_map/pallas_call | solution.py:57
  67.3 1.5 collective-permute-start.11
  69.1 5.3 %shard_map.210 = (f32[1024,768]{1,0:T(8,128)S(1)}, bf16[1024,768]{1,0:T(8,128)(2,1)S(1)}, bf16[1024,768]{1,0:T(8,128)(2,1)S(1)}, bf16[1024,768]{1,0:T(8,128)(2,1...) custom-call(bf16[256,768]{1,0:T(8,128)(2,1)S(1)} %collective-permute-done.16.refs_0_, ...), custom_call_target="tpu_custom_call" | custom-call | flops 16500000 | bytes 262144 | tf_op jit(solution)/shard_map/pallas_call | solution.py:57
  74.4 7.4 %collective-permute-done.11.refs_2_.refs_7_ = bf16[192,768]{1,0:T(8,128)(2,1)S(1)} collective-permute-done((bf16[192,768]{1,0:T(8,128)(2,1)S(1)}, bf16[192,768]{1,0:T(8,128)(2,1)S(1)}, u32[]{:S(2)}, u32[]{:S(2)}) %collective-permute-start.11) | collective-permute-done | bytes 294944 | tf_op jit(solution)/shard_map/ppermute | solution.py:988
  83.2 3.3 %shard_map.212 = (bf16[256,768]{1,0:T(8,128)(2,1)S(1)}, bf16[256,768]{1,0:T(8,128)(2,1)S(1)}, bf16[512,768]{1,0:T(8,128)(2,1)S(1)}, bf16[512,768]{1,0:T(8,128)(2...) custom-call(s32[1]{0:T(128)} %bitcast.refs_0_, ...), custom_call_target="tpu_custom_call" | custom-call | flops 660000000 | bytes 262144 | tf_op jit(solution)/shard_map/pallas_call | solution.py:57
  87.1 2.4 %shard_map.213 = (f32[512,768]{1,0:T(8,128)S(1)}, bf16[512,768]{1,0:T(8,128)(2,1)S(1)}, bf16[512,768]{1,0:T(8,128)(2,1)S(1)}, f32[8,128]{1,0:T(8,128)S(1)}) custom-call(bf16[512,768]{1,0:T(8,128)(2,1)S(1)} %get-tuple-element.262.refs_0_.refs_6_, f32[1024,768]{1,0:T(8,128)S(1)} %get-tuple-element.256.refs_9_.refs_1_, ...), custom_call_target="tpu_custom_call" | custom-call | flops 495000000 | bytes 262144 | tf_op jit(solution)/shard_map/pallas_call | solution.py:57
  89.5 3.9 %shard_map.214 = (bf16[512,768]{1,0:T(8,128)(2,1)}, f32[512,768]{1,0:T(8,128)S(1)}, bf16[512,768]{1,0:T(8,128)(2,1)S(1)}, f32[2,768]{1,0:T(2,128)S(1)}) custom-call(bf16[256,768]{1,0:T(8,128)(2,1)S(1)} %collective-permute-done.18.refs_0_, bf16[256,768]{1,0:T(8,128)(2,1)S(1)} %collective-permute-done.19.refs_1_, ...), custom_call_target="tpu_custom_call" | custom-call | flops 495000000 | bytes 262144 | tf_op jit(solution)/shard_map/pallas_call | solution.py:57
  93.5 8.0 %collective-permute-done.20.refs_2_ = bf16[512,768]{1,0:T(8,128)(2,1)S(1)} collective-permute-done((bf16[512,768]{1,0:T(8,128)(2,1)S(1)}, bf16[512,768]{1,0:T(8,128)(2,1)S(1)}, u32[]{:S(2)}, u32[]{:S(2)}) %collective-permute-start.20) | collective-permute-done | bytes 786464 | tf_op jit(solution)/shard_map/ppermute | solution.py:988
  102.5 3.2 %shard_map.216 = (f32[512,768]{1,0:T(8,128)S(1)}, bf16[512,768]{1,0:T(8,128)(2,1)S(1)}, bf16[512,768]{1,0:T(8,128)(2,1)S(1)}, f32[8,128]{1,0:T(8,128)S(1)}) custom-call(bf16[512,768]{1,0:T(8,128)(2,1)S(1)} %get-tuple-element.287.refs_0_.refs_2_, bf16[768,1536]{1,0:T(8,128)(2,1)S(1)} %bitcast.12, bf16[768,768]{1,0:T(8,128)(2,1)S(1)} %copy-done, ...), custom_call_target="tpu_custom_call" | custom-call | flops 495000000 | bytes 262144 | tf_op jit(solution)/shard_map/pallas_call | solution.py:57
  105.7 6.0 %shard_map.217 = (bf16[256,768]{1,0:T(8,128)(2,1)S(1)}, bf16[256,768]{1,0:T(8,128)(2,1)S(1)}, bf16[512,768]{1,0:T(8,128)(2,1)S(1)}, bf16[512,768]{1,0:T(8,128)(2,1)S(1)}, f32[8,128]{1,0:T(8,128)S(1)}) custom-call(bf16[512,768]{1,0:T(8,128)(2,1)S(1)} %collective-permute-done.21.refs_0_.refs_3_, bf16[768,1536]{1,0:T(8,128)(2,1)S(1)} %bitcast.13, ...), custom_call_target="tpu_custom_call" | custom-call | flops 990000000 | bytes 262144 | tf_op jit(solution)/shard_map/pallas_call | solution.py:57
  112.3 3.3 %shard_map.218 = (f32[512,768]{1,0:T(8,128)S(1)}, f32[8,128]{1,0:T(8,128)S(1)}) custom-call(bf16[512,768]{1,0:T(8,128)(2,1)S(1)} %get-tuple-element.287.refs_0_.refs_2_, f32[512,768]{1,0:T(8,128)S(1)} %get-tuple-element.297.refs_1_, bf16[768,1536]{1,0:T(8,128)(2,1)S(1)} %get-tuple-element.263.refs_2_.refs_3_, ...), custom_call_target="tpu_custom_call" | custom-call | flops 495000000 | bytes 262144 | tf_op jit(solution)/shard_map/pallas_call | solution.py:57
  115.7 4.2 %shard_map.219 = (f32[512,768]{1,0:T(8,128)S(1)}, bf16[208,512]{1,0:T(8,128)(2,1)S(1)}, bf16[784,512]{1,0:T(8,128)(2,1)S(1)}, bf16[208,512]{1,0:T(8,128)(2,1)S(1...) custom-call(bf16[256,768]{1,0:T(8,128)(2,1)S(1)} %collective-permute-done.22.refs_0_, ...), custom_call_target="tpu_custom_call" | custom-call | flops 825000000 | bytes 262144 | tf_op jit(solution)/shard_map/pallas_call | solution.py:57
  119.9 1.5 collective-permute-done.25.refs_4_
  123.7 8.5 %shard_map.221 = (bf16[384,384]{1,0:T(8,128)(2,1)S(1)}, bf16[384,384]{1,0:T(8,128)(2,1)S(1)}, bf16[384,384]{1,0:T(8,128)(2,1)S(1)}, bf16[384,384]{1,0:T(8,128)(2...) custom-call(s32[8]{0:T(128)S(1)} %add_add_fusion.1.refs_0_.refs_1_, ...), custom_call_target="tpu_custom_call" | custom-call | flops 1320000000 | bytes 262144 | tf_op jit(solution)/shard_map/pallas_call | solution.py:57
  132.7 7.8 %shard_map.223 = (bf16[384,1152]{1,0:T(8,128)(2,1)S(1)}, bf16[400,1152]{1,0:T(8,128)(2,1)S(1)}, bf16[384,1152]{1,0:T(8,128)(2,1)S(1)}, bf16[384,1152]{1,0:T(8,128)(2,1)S(1)}, f32[4,768]{1,0:T(4,128)S(1)}) custom-call(s32[8]{0:T(128)S(1)} %add_add_fusion.1.refs_0_.refs_1_, s32[8]{0:T(128)S(1)} %add_add_fusion.refs_1_, ...), custom_call_target="tpu_custom_call" | custom-call | flops 990000000 | bytes 262144 | tf_op jit(solution)/shard_map/pallas_call | solution.py:57
  141.2 1.5 collective-permute-start.31
  143.2 13.0 %shard_map.225 = (bf16[192,512]{1,0:T(8,128)(2,1)S(1)}, bf16[672,512]{1,0:T(8,128)(2,1)S(1)}, bf16[192,512]{1,0:T(8,128)(2,1)S(1)}, bf16[768,192]{1,0:T(8,128)(2...) custom-call(s32[9]{0:T(128)S(1)} %pad_add_fusion.refs_0_, s32[8]{0:T(128)S(1)} %add_add_fusion.1.refs_0_.refs_1_, ...), custom_call_target="tpu_custom_call" | custom-call | flops 1980000000 | bytes 262144 | tf_op jit(solution)/shard_map/pallas_call | solution.py:57
  156.2 7.0 %collective-permute-done.31.refs_3_ = bf16[384,1152]{1,0:T(8,128)(2,1)S(1)} collective-permute-done((bf16[384,1152]{1,0:T(8,128)(2,1)S(1)}, bf16[384,1152]{1,0:T(8,128)(2,1)S(1)}, u32[]{:S(2)}, u32[]{:S(2)}) %collective-permute-start.31) | collective-permute-done | bytes 884768 | tf_op jit(solution)/shard_map/ppermute | solution.py:988
  163.2 1.3 collective-permute-done.32.refs_4_
  165.4 1.5 collective-permute-start.35
  167.4 13.1 %shard_map.227 = (bf16[192,512]{1,0:T(8,128)(2,1)S(1)}, bf16[384,512]{1,0:T(8,128)(2,1)S(1)}, bf16[384,512]{1,0:T(8,128)(2,1)S(1)}, bf16[384,384]{1,0:T(8,128)(2...) custom-call(s32[9]{0:T(128)S(1)} %pad_add_fusion.refs_0_, s32[8]{0:T(128)S(1)} %add_add_fusion.1.refs_0_.refs_1_, ...), custom_call_target="tpu_custom_call" | custom-call | flops 1980000000 | bytes 262144 | tf_op jit(solution)/shard_map/pallas_call | solution.py:57
  180.8 1.6 collective-permute-start.36
  183.1 2.7 %collective-permute-start.41 = (bf16[112,2304]{1,0:T(8,128)(2,1)S(1)}, bf16[112,2304]{1,0:T(8,128)(2,1)S(1)}, u32[]{:S(2)}, u32[]{:S(2)}) collective-permute-start(bf16[112,2304]{1,0:T(8,128)(2,1)S(1)} %fusion.3), channel_id=1, source_target_pairs={{0,16},{4,20},{8,24},{12,28},{16,0},{20,4},{24,8},{28,12},{1,17},{... | collective-permute-start | bytes 1548296 | tf_op jit(solution)/shard_map/ppermute | solution.py:988
  185.7 12.8 %shard_map.229 = (bf16[192,512]{1,0:T(8,128)(2,1)S(1)}, bf16[384,512]{1,0:T(8,128)(2,1)S(1)}, bf16[768,512]{1,0:T(8,128)(2,1)S(1)}, bf16[384,384]{1,0:T(8,128)(2...) custom-call(s32[9]{0:T(128)S(1)} %pad_add_fusion.refs_0_, s32[8]{0:T(128)S(1)} %add_add_fusion.1.refs_0_.refs_1_, ...), custom_call_target="tpu_custom_call" | custom-call | flops 1980000000 | bytes 262144 | tf_op jit(solution)/shard_map/pallas_call | solution.py:57
  198.6 1.5 collective-permute-start.40
  200.6 1.4 collective-permute-start.44
  202.0 6.7 %collective-permute-done.41.refs_2_ = bf16[112,2304]{1,0:T(8,128)(2,1)S(1)} collective-permute-done((bf16[112,2304]{1,0:T(8,128)(2,1)S(1)}, bf16[112,2304]{1,0:T(8,128)(2,1)S(1)}, u32[]{:S(2)}, u32[]{:S(2)}) %collective-permute-start.41) | collective-permute-done | bytes 516128 | tf_op jit(solution)/shard_map/ppermute | solution.py:988
  211.1 2.8 %shard_map.233 = (f32[512,768]{1,0:T(8,128)S(1)}, f32[8,128]{1,0:T(8,128)S(1)}) custom-call(bf16[672,512]{1,0:T(8,128)(2,1)S(1)} %collective-permute-done.33.refs_32_.refs_0_, bf16[384,512]{1,0:T(8,128)(2,1)S(1)} %collective-permute-done.36.refs_0_.refs_1_, bf16[384,512]{1,0:T(8,128)(2,1)S(1)} %collective-permute-done.39.refs_2_, ...), custom_call_target="tpu_custom_call" | custom-call | flops 495000000 | bytes 262144 | tf_op jit(solution)/shard_map/pallas_call | solution.py:57
  215.0 2.0 collective-permute-start.45
  217.6 3.7 %shard_map.235 = (f32[512,768]{1,0:T(8,128)}, f32[8,128]{1,0:T(8,128)S(1)}) custom-call(bf16[1152,512]{1,0:T(8,128)(2,1)S(1)} %collective-permute-done.42.refs_0_, f32[512,768]{1,0:T(8,128)S(1)} %get-tuple-element.373.refs_1_, bf16[576,768]{1,0:T(8,128)(2,1)} %collective-permute-done.4.refs_12_.refs_2_, ...), custom_call_target="tpu_custom_call" | custom-call | flops 495000000 | bytes 262144 | tf_op jit(solution)/shard_map/pallas_call | solution.py:57
  221.3 3.2 %shard_map.236 = (f32[96,2,768]{2,1,0:T(2,128)}, f32[96,768]{1,0:T(8,128)}, f32[8,128]{1,0:T(8,128)S(1)}) custom-call(bf16[384,1152]{1,0:T(8,128)(2,1)S(1)} %get-tuple-element.348.refs_0_, bf16[400,1152]{1,0:T(8,128)(2,1)S(1)} %get-tuple-element.349.refs_1_, bf16[208,1152]{1,0:T(8,128)(2,1)S(1)} %get-tuple-element.364.refs_2_, ...), custom_call_target="tpu_custom_call" | custom-call | flops 330000000 | bytes 262144 | tf_op jit(solution)/shard_map/pallas_call | solution.py:57
  224.5 1.7 shard_map.237
  (148 shorter events, 25.3 us)
Async XLA Ops:
  3.0 7.9 %collective-permute-start = (bf16[528,768]{1,0:T(8,128)(2,1)}, bf16[528,768]{1,0:T(8,128)(2,1)}, u32[]{:S(2)}, u32[]{:S(2)}) collective-permute-start(bf16[528,768]{1,0:T(8,128)(2,1)} %fusion.2.refs_2_.refs_1_), channel_id=1, source_target_pairs={{0,1},{1,0},{2,3},{3,2},{4,5},{5,4},{6,7},{7,6},{8,9},{9,8},{10,11... | collective-permute-start | bytes 2433032 | tf_op jit(solution)/shard_map/ppermute | solution.py:988
  3.5 21.5 %collective-permute-start.1 = (bf16[528,768]{1,0:T(8,128)(2,1)}, bf16[528,768]{1,0:T(8,128)(2,1)}, u32[]{:S(2)}, u32[]{:S(2)}) collective-permute-start(bf16[528,768]{1,0:T(8,128)(2,1)} %fusion.2.refs_2_.refs_1_), channel_id=1, source_target_pairs={{0,2},{1,3},{2,0},{3,1},{4,6},{5,7},{6,4},{7,5},{8,10},{9,11},{10,... | collective-permute-start | bytes 2433032 | tf_op jit(solution)/shard_map/ppermute | solution.py:988
  5.9 25.0 %collective-permute-start.4 = (bf16[576,768]{1,0:T(8,128)(2,1)S(1)}, bf16[576,768]{1,0:T(8,128)(2,1)}, u32[]{:S(2)}, u32[]{:S(2)}) collective-permute-start(bf16[576,768]{1,0:T(8,128)(2,1)S(1)} %bitcast.15), channel_id=1, source_target_pairs={{0,1},{1,0},{2,3},{3,2},{4,5},{5,4},{6,7},{7,6},{8,9},{9,8},{10,11... | collective-permute-start | bytes 2654216 | tf_op jit(solution)/shard_map/ppermute | solution.py:988
  25.0 4.1 %collective-permute-start.2 = (bf16[528,768]{1,0:T(8,128)(2,1)}, bf16[528,768]{1,0:T(8,128)(2,1)S(1)}, u32[]{:S(2)}, u32[]{:S(2)}) collective-permute-start(bf16[528,768]{1,0:T(8,128)(2,1)} %get-tuple-element.202.refs_2_.refs_3_), channel_id=1, source_target_pairs={{0,1},{1,0},{2,3},{3,2},{4,5},{5,4},{6,7},{7,6},{8,9},{9,8},{10,11... | collective-permute-start | bytes 2433032 | tf_op jit(solution)/shard_map/ppermute | solution.py:988
  25.0 16.1 %collective-permute-start.5 = (bf16[192,1536]{1,0:T(8,128)(2,1)S(1)}, bf16[192,1536]{1,0:T(8,128)(2,1)S(1)}, u32[]{:S(2)}, u32[]{:S(2)}) collective-permute-start(bf16[192,1536]{1,0:T(8,128)(2,1)S(1)} %get-tuple-element.218), channel_id=1, source_target_pairs={{0,2},{1,3},{2,0},{3,1},{4,6},{5,7},{6,4},{7,5},{8,10},{9,11},{10,... | collective-permute-start | bytes 1769480 | tf_op jit(solution)/shard_map/ppermute | solution.py:988
  26.7 4.2 %collective-permute-start.3 = (bf16[192,768]{1,0:T(8,128)(2,1)S(1)}, bf16[192,768]{1,0:T(8,128)(2,1)S(1)}, u32[]{:S(2)}, u32[]{:S(2)}) collective-permute-start(bf16[192,768]{1,0:T(8,128)(2,1)S(1)} %copy-done.3), channel_id=1, source_target_pairs={{0,1},{1,0},{2,3},{3,2},{4,5},{5,4},{6,7},{7,6},{8,9},{9,8},{10,11... | collective-permute-start | bytes 884744 | tf_op jit(solution)/shard_map/ppermute | solution.py:988
  30.6 23.1 %collective-permute-start.8 = (bf16[384,768]{1,0:T(8,128)(2,1)S(1)}, bf16[384,768]{1,0:T(8,128)(2,1)S(1)}, u32[]{:S(2)}, u32[]{:S(2)}) collective-permute-start(bf16[384,768]{1,0:T(8,128)(2,1)S(1)} %get-tuple-element.220), channel_id=1, source_target_pairs={{0,2},{1,3},{2,0},{3,1},{4,6},{5,7},{6,4},{7,5},{8,10},{9,11},{10,... | collective-permute-start | bytes 1769480 | tf_op jit(solution)/shard_map/ppermute | solution.py:988
  41.1 15.3 %collective-permute-start.6 = (bf16[192,1536]{1,0:T(8,128)(2,1)S(1)}, bf16[192,1536]{1,0:T(8,128)(2,1)S(1)}, u32[]{:S(2)}, u32[]{:S(2)}) collective-permute-start(bf16[192,1536]{1,0:T(8,128)(2,1)S(1)} %get-tuple-element.219.refs_1_), channel_id=1, source_target_pairs={{0,4},{4,0},{8,12},{12,8},{16,20},{20,16},{24,28},{28,24},{1,5},{5... | collective-permute-start | bytes 1769480 | tf_op jit(solution)/shard_map/ppermute | solution.py:988
  42.9 14.3 %collective-permute-start.7 = (bf16[192,1536]{1,0:T(8,128)(2,1)S(1)}, bf16[192,1536]{1,0:T(8,128)(2,1)S(1)}, u32[]{:S(2)}, u32[]{:S(2)}) collective-permute-start(bf16[192,1536]{1,0:T(8,128)(2,1)S(1)} %get-tuple-element.219.refs_1_), channel_id=1, source_target_pairs={{0,8},{4,12},{8,0},{12,4},{16,24},{20,28},{24,16},{28,20},{1,9},{5... | collective-permute-start | bytes 1769480 | tf_op jit(solution)/shard_map/ppermute | solution.py:988
  44.5 16.4 %collective-permute-start.13 = (bf16[192,512]{1,0:T(8,128)(2,1)S(1)}, bf16[192,512]{1,0:T(8,128)(2,1)S(1)}, u32[]{:S(2)}, u32[]{:S(2)}) collective-permute-start(bf16[192,512]{1,0:T(8,128)(2,1)S(1)} %get-tuple-element.235.refs_20_), channel_id=1, source_target_pairs={{0,2},{1,3},{2,0},{3,1},{4,6},{5,7},{6,4},{7,5},{8,10},{9,11},{10,... | collective-permute-start | bytes 589832 | tf_op jit(solution)/shard_map/ppermute | solution.py:988
  56.3 5.6 %copy-start.5 = (f32[768]{0:T(1024)S(1)}, f32[768]{0:T(1024)}, u32[]{:S(2)}) copy-start(f32[768]{0:T(1024)} %param.19) | copy-start | bytes 9220
  56.4 5.6 %copy-start.6 = (f32[768]{0:T(1024)S(1)}, f32[768]{0:T(1024)}, u32[]{:S(2)}) copy-start(f32[768]{0:T(1024)} %param.20) | copy-start | bytes 9220
  57.6 8.0 %collective-permute-start.15 = (bf16[192,768]{1,0:T(8,128)(2,1)S(1)}, bf16[192,768]{1,0:T(8,128)(2,1)S(1)}, u32[]{:S(2)}, u32[]{:S(2)}) collective-permute-start(bf16[192,768]{1,0:T(8,128)(2,1)S(1)} %get-tuple-element.239.refs_6_.refs_14_), channel_id=1, source_target_pairs={{0,1},{1,0},{2,3},{3,2},{4,5},{5,4},{6,7},{7,6},{8,9},{9,8},{10,11... | collective-permute-start | bytes 884744 | tf_op jit(solution)/shard_map/ppermute | solution.py:988
  57.7 7.9 %collective-permute-start.12 = (bf16[192,512]{1,0:T(8,128)(2,1)S(1)}, bf16[192,512]{1,0:T(8,128)(2,1)S(1)}, u32[]{:S(2)}, u32[]{:S(2)}) collective-permute-start(bf16[192,512]{1,0:T(8,128)(2,1)S(1)} %get-tuple-element.234.refs_19_), channel_id=1, source_target_pairs={{0,1},{1,0},{2,3},{3,2},{4,5},{5,4},{6,7},{7,6},{8,9},{9,8},{10,11... | collective-permute-start | bytes 589832 | tf_op jit(solution)/shard_map/ppermute | solution.py:988
  58.2 7.4 %collective-permute-start.14 = (bf16[192,512]{1,0:T(8,128)(2,1)S(1)}, bf16[192,512]{1,0:T(8,128)(2,1)S(1)}, u32[]{:S(2)}, u32[]{:S(2)}) collective-permute-start(bf16[192,512]{1,0:T(8,128)(2,1)S(1)} %get-tuple-element.236.refs_21_), channel_id=1, source_target_pairs={{0,3},{1,2},{2,1},{3,0},{4,7},{5,6},{6,5},{7,4},{8,11},{9,10},{10,... | collective-permute-start | bytes 589832 | tf_op jit(solution)/shard_map/ppermute | solution.py:988
  59.4 22.5 %collective-permute-start.10 = (bf16[192,1536]{1,0:T(8,128)(2,1)S(1)}, bf16[192,1536]{1,0:T(8,128)(2,1)S(1)}, u32[]{:S(2)}, u32[]{:S(2)}) collective-permute-start(bf16[192,1536]{1,0:T(8,128)(2,1)S(1)} %get-tuple-element.231), channel_id=1, source_target_pairs={{0,8},{4,12},{8,0},{12,4},{16,24},{20,28},{24,16},{28,20},{1,9},{5... | collective-permute-start | bytes 1769480 | tf_op jit(solution)/shard_map/ppermute | solution.py:988
  60.9 21.7 %collective-permute-start.9 = (bf16[192,1536]{1,0:T(8,128)(2,1)S(1)}, bf16[192,1536]{1,0:T(8,128)(2,1)S(1)}, u32[]{:S(2)}, u32[]{:S(2)}) collective-permute-start(bf16[192,1536]{1,0:T(8,128)(2,1)S(1)} %get-tuple-element.230), channel_id=1, source_target_pairs={{0,4},{4,0},{8,12},{12,8},{16,20},{20,16},{24,28},{28,24},{1,5},{5... | collective-permute-start | bytes 1769480 | tf_op jit(solution)/shard_map/ppermute | solution.py:988
  66.8 2.1 collective-permute-start.16
  66.9 2.3 %collective-permute-start.17 = (bf16[256,768]{1,0:T(8,128)(2,1)S(1)}, bf16[256,768]{1,0:T(8,128)(2,1)S(1)}, u32[]{:S(2)}, u32[]{:S(2)}) collective-permute-start(bf16[256,768]{1,0:T(8,128)(2,1)S(1)} %get-tuple-element.252), channel_id=1, source_target_pairs={{0,1},{1,0},{2,3},{3,2},{4,5},{5,4},{6,7},{7,6},{8,9},{9,8},{10,11... | collective-permute-start | bytes 1179656 | tf_op jit(solution)/shard_map/ppermute | solution.py:988
  67.3 14.5 %collective-permute-start.11 = (bf16[192,768]{1,0:T(8,128)(2,1)S(1)}, bf16[192,768]{1,0:T(8,128)(2,1)S(1)}, u32[]{:S(2)}, u32[]{:S(2)}) collective-permute-start(bf16[192,768]{1,0:T(8,128)(2,1)S(1)} %get-tuple-element.232.refs_6_), channel_id=1, source_target_pairs={{0,12},{4,8},{8,4},{12,0},{16,28},{20,24},{24,20},{28,16},{1,13},{... | collective-permute-start | bytes 884744 | tf_op jit(solution)/shard_map/ppermute | solution.py:988
  82.7 18.8 %collective-permute-start.20 = (bf16[512,768]{1,0:T(8,128)(2,1)S(1)}, bf16[512,768]{1,0:T(8,128)(2,1)S(1)}, u32[]{:S(2)}, u32[]{:S(2)}) collective-permute-start(bf16[512,768]{1,0:T(8,128)(2,1)S(1)} %get-tuple-element.262.refs_0_.refs_6_), channel_id=1, source_target_pairs={{0,2},{1,3},{2,0},{3,1},{4,6},{5,7},{6,4},{7,5},{8,10},{9,11},{10,... | collective-permute-start | bytes 2359304 | tf_op jit(solution)/shard_map/ppermute | solution.py:988
  86.5 3.1 %collective-permute-start.18 = (bf16[256,768]{1,0:T(8,128)(2,1)S(1)}, bf16[256,768]{1,0:T(8,128)(2,1)S(1)}, u32[]{:S(2)}, u32[]{:S(2)}) collective-permute-start(bf16[256,768]{1,0:T(8,128)(2,1)S(1)} %get-tuple-element.259), channel_id=1, source_target_pairs={{0,1},{1,0},{2,3},{3,2},{4,5},{5,4},{6,7},{7,6},{8,9},{9,8},{10,11... | collective-permute-start | bytes 1179656 | tf_op jit(solution)/shard_map/ppermute | solution.py:988
  86.5 3.0 %collective-permute-start.19 = (bf16[256,768]{1,0:T(8,128)(2,1)S(1)}, bf16[256,768]{1,0:T(8,128)(2,1)S(1)}, u32[]{:S(2)}, u32[]{:S(2)}) collective-permute-start(bf16[256,768]{1,0:T(8,128)(2,1)S(1)} %get-tuple-element.260), channel_id=1, source_target_pairs={{0,1},{1,0},{2,3},{3,2},{4,5},{5,4},{6,7},{7,6},{8,9},{9,8},{10,11... | collective-permute-start | bytes 1179656 | tf_op jit(solution)/shard_map/ppermute | solution.py:988
  101.4 4.3 %collective-permute-start.21 = (bf16[512,768]{1,0:T(8,128)(2,1)S(1)}, bf16[512,768]{1,0:T(8,128)(2,1)S(1)}, u32[]{:S(2)}, u32[]{:S(2)}) collective-permute-start(bf16[512,768]{1,0:T(8,128)(2,1)S(1)} %get-tuple-element.287.refs_0_.refs_2_), channel_id=1, source_target_pairs={{0,1},{1,0},{2,3},{3,2},{4,5},{5,4},{6,7},{7,6},{8,9},{9,8},{10,11... | collective-permute-start | bytes 2359304 | tf_op jit(solution)/shard_map/ppermute | solution.py:988
  101.4 14.2 %collective-permute-start.24 = (bf16[512,768]{1,0:T(8,128)(2,1)S(1)}, bf16[512,768]{1,0:T(8,128)(2,1)S(1)}, u32[]{:S(2)}, u32[]{:S(2)}) collective-permute-start(bf16[512,768]{1,0:T(8,128)(2,1)S(1)} %get-tuple-element.303.refs_6_.refs_8_), channel_id=1, source_target_pairs={{0,1},{1,0},{2,3},{3,2},{4,5},{5,4},{6,7},{7,6},{8,9},{9,8},{10,11... | collective-permute-start | bytes 2359304 | tf_op jit(solution)/shard_map/ppermute | solution.py:988
  101.9 19.4 %collective-permute-start.25 = (bf16[512,768]{1,0:T(8,128)(2,1)S(1)}, bf16[512,768]{1,0:T(8,128)(2,1)S(1)}, u32[]{:S(2)}, u32[]{:S(2)}) collective-permute-start(bf16[512,768]{1,0:T(8,128)(2,1)S(1)} %get-tuple-element.287.refs_0_.refs_2_), channel_id=1, source_target_pairs={{0,2},{1,3},{2,0},{3,1},{4,6},{5,7},{6,4},{7,5},{8,10},{9,11},{10,... | collective-permute-start | bytes 2359304 | tf_op jit(solution)/shard_map/ppermute | solution.py:988
  111.8 3.9 %collective-permute-start.22 = (bf16[256,768]{1,0:T(8,128)(2,1)S(1)}, bf16[256,768]{1,0:T(8,128)(2,1)S(1)}, u32[]{:S(2)}, u32[]{:S(2)}) collective-permute-start(bf16[256,768]{1,0:T(8,128)(2,1)S(1)} %get-tuple-element.294), channel_id=1, source_target_pairs={{0,1},{1,0},{2,3},{3,2},{4,5},{5,4},{6,7},{7,6},{8,9},{9,8},{10,11... | collective-permute-start | bytes 1179656 | tf_op jit(solution)/shard_map/ppermute | solution.py:988
  111.8 3.8 %collective-permute-start.23 = (bf16[256,768]{1,0:T(8,128)(2,1)S(1)}, bf16[256,768]{1,0:T(8,128)(2,1)S(1)}, u32[]{:S(2)}, u32[]{:S(2)}) collective-permute-start(bf16[256,768]{1,0:T(8,128)(2,1)S(1)} %get-tuple-element.295), channel_id=1, source_target_pairs={{0,1},{1,0},{2,3},{3,2},{4,5},{5,4},{6,7},{7,6},{8,9},{9,8},{10,11... | collective-permute-start | bytes 1179656 | tf_op jit(solution)/shard_map/ppermute | solution.py:988
  121.4 2.3 %collective-permute-start.29 = (bf16[512,768]{1,0:T(8,128)(2,1)S(1)}, bf16[512,768]{1,0:T(8,128)(2,1)S(1)}, u32[]{:S(2)}, u32[]{:S(2)}) collective-permute-start(bf16[512,768]{1,0:T(8,128)(2,1)S(1)} %get-tuple-element.319.refs_4_), channel_id=1, source_target_pairs={{0,1},{1,0},{2,3},{3,2},{4,5},{5,4},{6,7},{7,6},{8,9},{9,8},{10,11... | collective-permute-start | bytes 2359304 | tf_op jit(solution)/shard_map/ppermute | solution.py:988
  121.4 11.3 %collective-permute-start.26 = (bf16[784,512]{1,0:T(8,128)(2,1)S(1)}, bf16[784,512]{1,0:T(8,128)(2,1)S(1)}, u32[]{:S(2)}, u32[]{:S(2)}) collective-permute-start(bf16[784,512]{1,0:T(8,128)(2,1)S(1)} %get-tuple-element.310), channel_id=1, source_target_pairs={{0,1},{1,0},{2,3},{3,2},{4,5},{5,4},{6,7},{7,6},{8,9},{9,8},{10,11... | collective-permute-start | bytes 2408456 | tf_op jit(solution)/shard_map/ppermute | solution.py:988
  121.9 10.3 %collective-permute-start.27 = (bf16[208,512]{1,0:T(8,128)(2,1)S(1)}, bf16[208,512]{1,0:T(8,128)(2,1)S(1)}, u32[]{:S(2)}, u32[]{:S(2)}) collective-permute-start(bf16[208,512]{1,0:T(8,128)(2,1)S(1)} %get-tuple-element.311), channel_id=1, source_target_pairs={{0,2},{1,3},{2,0},{3,1},{4,6},{5,7},{6,4},{7,5},{8,10},{9,11},{10,... | collective-permute-start | bytes 638984 | tf_op jit(solution)/shard_map/ppermute | solution.py:988
  122.4 10.2 %collective-permute-start.28 = (bf16[208,512]{1,0:T(8,128)(2,1)S(1)}, bf16[208,512]{1,0:T(8,128)(2,1)S(1)}, u32[]{:S(2)}, u32[]{:S(2)}) collective-permute-start(bf16[208,512]{1,0:T(8,128)(2,1)S(1)} %get-tuple-element.312), channel_id=1, source_target_pairs={{0,3},{1,2},{2,1},{3,0},{4,7},{5,6},{6,5},{7,4},{8,11},{9,10},{10,... | collective-permute-start | bytes 638984 | tf_op jit(solution)/shard_map/ppermute | solution.py:988
  140.5 24.0 %collective-permute-start.30 = (bf16[400,1152]{1,0:T(8,128)(2,1)S(1)}, bf16[400,1152]{1,0:T(8,128)(2,1)S(1)}, u32[]{:S(2)}, u32[]{:S(2)}) collective-permute-start(bf16[400,1152]{1,0:T(8,128)(2,1)S(1)} %get-tuple-element.338), channel_id=1, source_target_pairs={{0,4},{4,0},{8,12},{12,8},{16,20},{20,16},{24,28},{28,24},{1,5},{5... | collective-permute-start | bytes 2764808 | tf_op jit(solution)/shard_map/ppermute | solution.py:988
  141.2 22.1 %collective-permute-start.31 = (bf16[384,1152]{1,0:T(8,128)(2,1)S(1)}, bf16[384,1152]{1,0:T(8,128)(2,1)S(1)}, u32[]{:S(2)}, u32[]{:S(2)}) collective-permute-start(bf16[384,1152]{1,0:T(8,128)(2,1)S(1)} %get-tuple-element.339), channel_id=1, source_target_pairs={{0,8},{4,12},{8,0},{12,4},{16,24},{20,28},{24,16},{28,20},{1,9},{5... | collective-permute-start | bytes 2654216 | tf_op jit(solution)/shard_map/ppermute | solution.py:988
  142.7 21.8 %collective-permute-start.32 = (bf16[576,768]{1,0:T(8,128)(2,1)S(1)}, bf16[576,768]{1,0:T(8,128)(2,1)S(1)}, u32[]{:S(2)}, u32[]{:S(2)}) collective-permute-start(bf16[576,768]{1,0:T(8,128)(2,1)S(1)} %get-tuple-element.340.refs_7_), channel_id=1, source_target_pairs={{0,2},{1,3},{2,0},{3,1},{4,6},{5,7},{6,4},{7,5},{8,10},{9,11},{10,... | collective-permute-start | bytes 2654216 | tf_op jit(solution)/shard_map/ppermute | solution.py:988
  164.7 15.8 %collective-permute-start.34 = (bf16[208,1152]{1,0:T(8,128)(2,1)S(1)}, bf16[208,1152]{1,0:T(8,128)(2,1)S(1)}, u32[]{:S(2)}, u32[]{:S(2)}) collective-permute-start(bf16[208,1152]{1,0:T(8,128)(2,1)S(1)} %pad_maximum_fusion.1), channel_id=1, source_target_pairs={{0,8},{4,12},{8,0},{12,4},{16,24},{20,28},{24,16},{28,20},{1,9},{5... | collective-permute-start | bytes 1437704 | tf_op jit(solution)/shard_map/ppermute | solution.py:988
  165.4 15.1 %collective-permute-start.35 = (bf16[192,1152]{1,0:T(8,128)(2,1)S(1)}, bf16[192,1152]{1,0:T(8,128)(2,1)S(1)}, u32[]{:S(2)}, u32[]{:S(2)}) collective-permute-start(bf16[192,1152]{1,0:T(8,128)(2,1)S(1)} %add_convert_fusion), channel_id=1, source_target_pairs={{0,4},{4,0},{8,12},{12,8},{16,20},{20,16},{24,28},{28,24},{1,5},{5... | collective-permute-start | bytes 1327112 | tf_op jit(solution)/shard_map/ppermute | solution.py:988
  166.9 18.9 %collective-permute-start.33 = (bf16[672,512]{1,0:T(8,128)(2,1)S(1)}, bf16[672,512]{1,0:T(8,128)(2,1)S(1)}, u32[]{:S(2)}, u32[]{:S(2)}) collective-permute-start(bf16[672,512]{1,0:T(8,128)(2,1)S(1)} %get-tuple-element.343), channel_id=1, source_target_pairs={{0,2},{1,3},{2,0},{3,1},{4,6},{5,7},{6,4},{7,5},{8,10},{9,11},{10,... | collective-permute-start | bytes 2064392 | tf_op jit(solution)/shard_map/ppermute | solution.py:988
  180.7 17.8 %collective-permute-start.37 = (bf16[576,768]{1,0:T(8,128)(2,1)S(1)}, bf16[576,768]{1,0:T(8,128)(2,1)S(1)}, u32[]{:S(2)}, u32[]{:S(2)}) collective-permute-start(bf16[576,768]{1,0:T(8,128)(2,1)S(1)} %get-tuple-element.356.refs_8_), channel_id=1, source_target_pairs={{0,1},{1,0},{2,3},{3,2},{4,5},{5,4},{6,7},{7,6},{8,9},{9,8},{10,11... | collective-permute-start | bytes 2654216 | tf_op jit(solution)/shard_map/ppermute | solution.py:988
  180.8 17.7 %collective-permute-start.36 = (bf16[384,512]{1,0:T(8,128)(2,1)S(1)}, bf16[384,512]{1,0:T(8,128)(2,1)S(1)}, u32[]{:S(2)}, u32[]{:S(2)}) collective-permute-start(bf16[384,512]{1,0:T(8,128)(2,1)S(1)} %get-tuple-element.355), channel_id=1, source_target_pairs={{0,2},{1,3},{2,0},{3,1},{4,6},{5,7},{6,4},{7,5},{8,10},{9,11},{10,... | collective-permute-start | bytes 1179656 | tf_op jit(solution)/shard_map/ppermute | solution.py:988
  182.4 16.1 %collective-permute-start.38 = (bf16[384,384]{1,0:T(8,128)(2,1)S(1)}, bf16[384,384]{1,0:T(8,128)(2,1)S(1)}, u32[]{:S(2)}, u32[]{:S(2)}) collective-permute-start(bf16[384,384]{1,0:T(8,128)(2,1)S(1)} %get-tuple-element.360), channel_id=1, source_target_pairs={{0,4},{4,0},{8,12},{12,8},{16,20},{20,16},{24,28},{28,24},{1,5},{5... | collective-permute-start | bytes 884744 | tf_op jit(solution)/shard_map/ppermute | solution.py:988
  183.1 25.7 %collective-permute-start.41 = (bf16[112,2304]{1,0:T(8,128)(2,1)S(1)}, bf16[112,2304]{1,0:T(8,128)(2,1)S(1)}, u32[]{:S(2)}, u32[]{:S(2)}) collective-permute-start(bf16[112,2304]{1,0:T(8,128)(2,1)S(1)} %fusion.3), channel_id=1, source_target_pairs={{0,16},{4,20},{8,24},{12,28},{16,0},{20,4},{24,8},{28,12},{1,17},{... | collective-permute-start | bytes 1548296 | tf_op jit(solution)/shard_map/ppermute | solution.py:988
  198.6 10.1 %collective-permute-start.40 = (bf16[384,384]{1,0:T(8,128)(2,1)S(1)}, bf16[384,384]{1,0:T(8,128)(2,1)S(1)}, u32[]{:S(2)}, u32[]{:S(2)}) collective-permute-start(bf16[384,384]{1,0:T(8,128)(2,1)S(1)} %get-tuple-element.363), channel_id=1, source_target_pairs={{0,4},{4,0},{8,12},{12,8},{16,20},{20,16},{24,28},{28,24},{1,5},{5... | collective-permute-start | bytes 884744 | tf_op jit(solution)/shard_map/ppermute | solution.py:988
  200.0 10.3 %collective-permute-start.39 = (bf16[384,512]{1,0:T(8,128)(2,1)S(1)}, bf16[384,512]{1,0:T(8,128)(2,1)S(1)}, u32[]{:S(2)}, u32[]{:S(2)}) collective-permute-start(bf16[384,512]{1,0:T(8,128)(2,1)S(1)} %get-tuple-element.361), channel_id=1, source_target_pairs={{0,2},{1,3},{2,0},{3,1},{4,6},{5,7},{6,4},{7,5},{8,10},{9,11},{10,... | collective-permute-start | bytes 1179656 | tf_op jit(solution)/shard_map/ppermute | solution.py:988
  200.6 13.3 %collective-permute-start.44 = (bf16[192,384]{1,0:T(8,128)(2,1)S(1)}, bf16[192,384]{1,0:T(8,128)(2,1)S(1)}, u32[]{:S(2)}, u32[]{:S(2)}) collective-permute-start(bf16[192,384]{1,0:T(8,128)(2,1)S(1)} %add_convert_fusion.4), channel_id=1, source_target_pairs={{0,8},{4,12},{8,0},{12,4},{16,24},{20,28},{24,16},{28,20},{1,9},{5... | collective-permute-start | bytes 442376 | tf_op jit(solution)/shard_map/ppermute | solution.py:988
  208.8 6.2 %collective-permute-start.43 = (bf16[192,384]{1,0:T(8,128)(2,1)S(1)}, bf16[192,384]{1,0:T(8,128)(2,1)S(1)}, u32[]{:S(2)}, u32[]{:S(2)}) collective-permute-start(bf16[192,384]{1,0:T(8,128)(2,1)S(1)} %add_convert_fusion.5), channel_id=1, source_target_pairs={{0,8},{4,12},{8,0},{12,4},{16,24},{20,28},{24,16},{28,20},{1,9},{5... | collective-permute-start | bytes 442376 | tf_op jit(solution)/shard_map/ppermute | solution.py:988
  210.9 6.7 %collective-permute-start.42 = (bf16[1152,512]{1,0:T(8,128)(2,1)S(1)}, bf16[1152,512]{1,0:T(8,128)(2,1)S(1)}, u32[]{:S(2)}, u32[]{:S(2)}) collective-permute-start(bf16[1152,512]{1,0:T(8,128)(2,1)S(1)} %get-tuple-element.367), channel_id=1, source_target_pairs={{0,1},{1,0},{2,3},{3,2},{4,5},{5,4},{6,7},{7,6},{8,9},{9,8},{10,11... | collective-permute-start | bytes 3538952 | tf_op jit(solution)/shard_map/ppermute | solution.py:988
  215.0 9.5 %collective-permute-start.45 = (bf16[96,768]{1,0:T(8,128)(2,1)S(1)}, bf16[96,768]{1,0:T(8,128)(2,1)S(1)}, u32[]{:S(2)}, u32[]{:S(2)}) collective-permute-start(bf16[96,768]{1,0:T(8,128)(2,1)S(1)} %pad_maximum_fusion.2), channel_id=1, source_target_pairs={{0,16},{4,20},{8,24},{12,28},{16,0},{20,4},{24,8},{28,12},{1,17},{... | collective-permute-start | bytes 442376 | tf_op jit(solution)/shard_map/ppermute | solution.py:988
  (9 other events, 23.6 us)

commit v6 on v5

--- a/solution.py
+++ b/solution.py
@@ -654,7 +654,7 @@
     rows, width = xhat.shape
     return run(
         mid_kernel,
-        3,
+        10,
         8,
         (),
         (xhat, own, out_grad, g1, b1, g2, b2),
@@ -1186,8 +1186,9 @@
     gain1, bias1, gain2, bias2 = (u.reshape(1, width) for u in (norm1_gain, norm1_bias, norm2_gain, norm2_bias))
     ml0, xhat1, inv1, *halves = out_project((o0, g1, g2, g3), wo, tokens, gain1, bias1)
     acc, da_o, db_o, hid_o, ml1 = mlp_own(ml0, [swap(u, 1) for u in halves], wgu, down_weight)
-    (ml0,) = gate(ml0, awaits=(from_y, from_z, pa3))
+    (ml0,) = gate(ml0)
     ml2 = swap(ml0, 2)
+    gate(awaits=(from_y, from_z, pa3))
     parts = (pb0, pb1, pb2, from_y, from_z, pa0, pa3)
     sib0, sib1, da_1, db_1, wgu_p, wd_p = mlp_far(quarter, ml1, acc, parts)
     own, da_0, db_0 = mlp_last(ml0, acc, wgu_p, wd_p)

time: 231 us -> 227 us (0.983)
  waiting for transfers between devices: 51.9 us -> 45.4 us
  starting transfers between devices: 37.7 us -> 40.6 us
    ppermute x46, waiting for transfers between devices: 51.9 us -> 45.4 us  [swap(): return lax.ppermute(v, axis, [(i, i ^ bit) for i in range(n)])]
    ppermute x46, starting transfers between devices: 37.7 us -> 40.6 us  [swap(): return lax.ppermute(v, axis, [(i, i ^ bit) for i in range(n)])]
    pallas_call x43 -> x44, Pallas kernels: 129 us -> 129 us  [run(): pl.pallas_call(body, in_specs=[pl.BlockSpec(memory_space=pltpu.SMEM)] * l...]
  transfers between devices with their start and end apart: 46 -> 46, of which waited for: 16 -> 18; matrix products, arithmetic and copies ran while one was open for 2% -> 2% of each run, Pallas kernels for 53% -> 53%
where the time goes in v6:
time: 227 us; the launch traced here: 223 us
  Pallas kernels  129 us (57%)
  waiting for transfers between devices  45.4 us (20%)
  starting transfers between devices  40.6 us (18%)
  local copies, waits for them, and re-layouts  4.34 us (2%)
    pallas_call x44, Pallas kernels, run(): pl.pallas_call(body, in_specs=[pl.BlockSpec(memory_space=pltpu.SMEM)] * l...  129 us
    ppermute x46, waiting for transfers between devices, swap(): return lax.ppermute(v, axis, [(i, i ^ bit) for i in range(n)])  45.4 us
    ppermute x46, starting transfers between devices, swap(): return lax.ppermute(v, axis, [(i, i ^ bit) for i in range(n)])  40.6 us
  transfers between devices with their start and end apart: 46, of which 18 were waited for; matrix products, arithmetic and copies ran while one was open for 2% of the time, Pallas kernels for 53%

profile of v6, /device:TPU:0, one launch (start us, length us, event | category | flops | bytes accessed | tf_op | source)
XLA Modules:
  0.0 223.1 jit_solution(16310168759580460833)
XLA Ops:
  3.5 2.5 %collective-permute-start.1 = (bf16[528,768]{1,0:T(8,128)(2,1)}, bf16[528,768]{1,0:T(8,128)(2,1)}, u32[]{:S(2)}, u32[]{:S(2)}) collective-permute-start(bf16[528,768]{1,0:T(8,128)(2,1)} %fusion.2.refs_2_.refs_1_), channel_id=1, source_target_pairs={{0,2},{1,3},{2,0},{3,1},{4,6},{5,7},{6,4},{7,5},{8,10},{9,11},{10,... | collective-permute-start | bytes 2433032 | tf_op jit(solution)/shard_map/ppermute | solution.py:988
  6.2 2.1 copy.56
  8.5 2.3 %shard_map.195 = (bf16[3,128,512]{2,1,0:T(8,128)(2,1)S(1)}, bf16[3,128,512]{2,1,0:T(8,128)(2,1)S(1)}, bf16[3,512,128]{2,1,0:T(8,128)(2,1)S(1)}, bf16[3,128,512]{2,1,0:T(8,128)(2,1)S(1)}, f32[64,512]{1,0:T(8,128)S(1)}) custom-call(s32[9]{0:T(128)S(1)} %pad_add_fusion.refs_0_, f32[32,128]{1,0:T(8,128)S(1)} %broadcast_in_dim.15.refs_1_, ...), custom_call_target="tpu_custom_call" | custom-call | flops 412500000 | bytes 262144 | tf_op jit(solution)/shard_map/pallas_call | solution.py:57
  10.9 2.1 shard_map.196
  13.1 11.9 %collective-permute-done.1.refs_1_ = bf16[528,768]{1,0:T(8,128)(2,1)} collective-permute-done((bf16[528,768]{1,0:T(8,128)(2,1)}, bf16[528,768]{1,0:T(8,128)(2,1)}, u32[]{:S(2)}, u32[]{:S(2)}) %collective-permute-start.1) | collective-permute-done | bytes 811040 | tf_op jit(solution)/shard_map/ppermute | solution.py:988
  25.0 1.7 collective-permute-start.5
  27.0 2.1 shard_map.198
  29.1 1.5 shard_map.199
  31.0 7.6 %shard_map.200 = (bf16[192,512]{1,0:T(8,128)(2,1)S(1)}, bf16[192,512]{1,0:T(8,128)(2,1)S(1)}, bf16[3,128,512]{2,1,0:T(8,128)(2,1)S(1)}, bf16[3,128,512]{2,1,0:T(8,128)(2,1)S(1)}, f32[8,128]{1,0:T(8,128)S(1)}) custom-call(s32[9]{0:T(128)S(1)} %pad_add_fusion.refs_0_, bf16[3,128,512]{2,1,0:T(8,128)(2,1)S(1)} %get-tuple-element.204.refs_1_, ...), custom_call_target="tpu_custom_call" | custom-call | flops 1320000000 | bytes 262144 | tf_op jit(solution)/shard_map/pallas_call | solution.py:57
  38.6 2.5 %collective-permute-done.5.refs_2_ = bf16[192,1536]{1,0:T(8,128)(2,1)S(1)} collective-permute-done((bf16[192,1536]{1,0:T(8,128)(2,1)S(1)}, bf16[192,1536]{1,0:T(8,128)(2,1)S(1)}, u32[]{:S(2)}, u32[]{:S(2)}) %collective-permute-start.5) | collective-permute-done | bytes 589856 | tf_op jit(solution)/shard_map/ppermute | solution.py:988
  41.1 1.8 collective-permute-start.6
  42.9 1.6 collective-permute-start.7
  44.5 6.8 %shard_map.202 = (bf16[192,512]{1,0:T(8,128)(2,1)S(1)}, bf16[192,512]{1,0:T(8,128)(2,1)S(1)}, bf16[3,128,512]{2,1,0:T(8,128)(2,1)S(1)}, bf16[3,128,512]{2,1,0:T(8,128)(2,1)S(1)}, f32[8,128]{1,0:T(8,128)S(1)}) custom-call(s32[9]{0:T(128)S(1)} %pad_add_fusion.refs_0_, bf16[3,128,512]{2,1,0:T(8,128)(2,1)S(1)} %get-tuple-element.221.refs_1_, ...), custom_call_target="tpu_custom_call" | custom-call | flops 1320000000 | bytes 262144 | tf_op jit(solution)/shard_map/pallas_call | solution.py:57
  51.3 2.0 collective-permute-done.8.refs_0_.refs_2_
  53.4 2.6 %shard_map.204 = (bf16[768,2048]{1,0:T(8,128)(2,1)S(1)}, f32[8,128]{1,0:T(8,128)S(1)}) custom-call(s32[8]{0:T(128)S(1)} %add_add_fusion.1.refs_0_.refs_1_, bf16[528,768]{1,0:T(8,128)(2,1)} %fusion.2.refs_2_.refs_1_, bf16[528,768]{1,0:T(8,128)(2,1)} %collective-permute-done.refs_2_, bf16[528,768]{1,0:T(8,128)(2,1)} %get-tuple-element.202.refs_2_.refs_3_, ...), custom_call_target="tpu_custom_call" | custom-call | flops 330000000 | bytes 262144 | tf_op jit(solution)/shard_map/pallas_call | solution.py:57
  57.7 1.6 collective-permute-start.13
  59.9 1.6 collective-permute-start.10
  61.6 3.5 %shard_map.208 = (bf16[3,128,512]{2,1,0:T(8,128)(2,1)S(1)}, bf16[3,128,512]{2,1,0:T(8,128)(2,1)S(1)}, bf16[3,128,512]{2,1,0:T(8,128)(2,1)S(1)}, bf16[3,128,512]{...) custom-call(bf16[3,128,512]{2,1,0:T(8,128)(2,1)S(1)} %get-tuple-elem, ...), custom_call_target="tpu_custom_call" | custom-call | flops 495000000 | bytes 262144 | tf_op jit(solution)/shard_map/pallas_call | solution.py:57
  66.0 2.7 %collective-permute-done.14.refs_3_.refs_11_ = bf16[192,512]{1,0:T(8,128)(2,1)S(1)} collective-permute-done((bf16[192,512]{1,0:T(8,128)(2,1)S(1)}, bf16[192,512]{1,0:T(8,128)(2,1)S(1)}, u32[]{:S(2)}, u32[]{:S(2)}) %collective-permute-start.14) | collective-permute-done | bytes 196640 | tf_op jit(solution)/shard_map/ppermute | solution.py:988
  70.6 1.6 collective-permute-start.11
  72.5 5.3 %shard_map.210 = (f32[1024,768]{1,0:T(8,128)S(1)}, bf16[1024,768]{1,0:T(8,128)(2,1)S(1)}, bf16[1024,768]{1,0:T(8,128)(2,1)S(1)}, bf16[1024,768]{1,0:T(8,128)(2,1...) custom-call(bf16[256,768]{1,0:T(8,128)(2,1)S(1)} %collective-permute-done.16.refs_0_, ...), custom_call_target="tpu_custom_call" | custom-call | flops 16500000 | bytes 262144 | tf_op jit(solution)/shard_map/pallas_call | solution.py:57
  77.8 1.6 collective-permute-start.20
  79.4 2.5 %collective-permute-done.11.refs_2_.refs_7_ = bf16[192,768]{1,0:T(8,128)(2,1)S(1)} collective-permute-done((bf16[192,768]{1,0:T(8,128)(2,1)S(1)}, bf16[192,768]{1,0:T(8,128)(2,1)S(1)}, u32[]{:S(2)}, u32[]{:S(2)}) %collective-permute-start.11) | collective-permute-done | bytes 294944 | tf_op jit(solution)/shard_map/ppermute | solution.py:988
  81.8 4.8 %collective-permute-done.9.refs_0_.refs_4_ = bf16[192,1536]{1,0:T(8,128)(2,1)S(1)} collective-permute-done((bf16[192,1536]{1,0:T(8,128)(2,1)S(1)}, bf16[192,1536]{1,0:T(8,128)(2,1)S(1)}, u32[]{:S(2)}, u32[]{:S(2)}) %collective-permute-start.9) | collective-permute-done | bytes 589856 | tf_op jit(solution)/shard_map/ppermute | solution.py:988
  86.6 3.3 %shard_map.213 = (bf16[256,768]{1,0:T(8,128)(2,1)S(1)}, bf16[256,768]{1,0:T(8,128)(2,1)S(1)}, bf16[512,768]{1,0:T(8,128)(2,1)S(1)}, bf16[512,768]{1,0:T(8,128)(2...) custom-call(s32[1]{0:T(128)} %bitcast.refs_0_, ...), custom_call_target="tpu_custom_call" | custom-call | flops 660000000 | bytes 262144 | tf_op jit(solution)/shard_map/pallas_call | solution.py:57
  90.5 2.4 %shard_map.214 = (f32[512,768]{1,0:T(8,128)S(1)}, bf16[512,768]{1,0:T(8,128)(2,1)S(1)}, bf16[512,768]{1,0:T(8,128)(2,1)S(1)}, f32[8,128]{1,0:T(8,128)S(1)}) custom-call(bf16[512,768]{1,0:T(8,128)(2,1)S(1)} %get-tuple-element.262.refs_0_.refs_6_, f32[1024,768]{1,0:T(8,128)S(1)} %get-tuple-element.256.refs_9_.refs_1_, ...), custom_call_target="tpu_custom_call" | custom-call | flops 495000000 | bytes 262144 | tf_op jit(solution)/shard_map/pallas_call | solution.py:57
  93.0 3.9 %shard_map.215 = (bf16[512,768]{1,0:T(8,128)(2,1)}, f32[512,768]{1,0:T(8,128)S(1)}, bf16[512,768]{1,0:T(8,128)(2,1)S(1)}, f32[2,768]{1,0:T(2,128)S(1)}) custom-call(bf16[256,768]{1,0:T(8,128)(2,1)S(1)} %collective-permute-done.18.refs_0_, bf16[256,768]{1,0:T(8,128)(2,1)S(1)} %collective-permute-done.19.refs_1_, ...), custom_call_target="tpu_custom_call" | custom-call | flops 1650000000 | bytes 262144 | tf_op jit(solution)/shard_map/pallas_call | solution.py:57
  98.2 1.5 collective-permute-start.25
  99.7 3.2 %shard_map.217 = (f32[512,768]{1,0:T(8,128)S(1)}, bf16[512,768]{1,0:T(8,128)(2,1)S(1)}, bf16[512,768]{1,0:T(8,128)(2,1)S(1)}, f32[8,128]{1,0:T(8,128)S(1)}) custom-call(bf16[512,768]{1,0:T(8,128)(2,1)S(1)} %get-tuple-element.287.refs_0_.refs_2_, bf16[768,1536]{1,0:T(8,128)(2,1)S(1)} %bitcast.12, bf16[768,768]{1,0:T(8,128)(2,1)S(1)} %copy-done, ...), custom_call_target="tpu_custom_call" | custom-call | flops 495000000 | bytes 262144 | tf_op jit(solution)/shard_map/pallas_call | solution.py:57
  103.0 6.0 %shard_map.218 = (bf16[256,768]{1,0:T(8,128)(2,1)S(1)}, bf16[256,768]{1,0:T(8,128)(2,1)S(1)}, bf16[512,768]{1,0:T(8,128)(2,1)S(1)}, bf16[512,768]{1,0:T(8,128)(2,1)S(1)}, f32[8,128]{1,0:T(8,128)S(1)}) custom-call(bf16[512,768]{1,0:T(8,128)(2,1)S(1)} %collective-permute-done.21.refs_0_.refs_3_, bf16[768,1536]{1,0:T(8,128)(2,1)S(1)} %bitcast.13, ...), custom_call_target="tpu_custom_call" | custom-call | flops 990000000 | bytes 262144 | tf_op jit(solution)/shard_map/pallas_call | solution.py:57
  109.5 3.3 %shard_map.219 = (f32[512,768]{1,0:T(8,128)S(1)}, f32[8,128]{1,0:T(8,128)S(1)}) custom-call(bf16[512,768]{1,0:T(8,128)(2,1)S(1)} %get-tuple-element.287.refs_0_.refs_2_, f32[512,768]{1,0:T(8,128)S(1)} %get-tuple-element.297.refs_1_, bf16[768,1536]{1,0:T(8,128)(2,1)S(1)} %get-tuple-element.263.refs_2_.refs_3_, ...), custom_call_target="tpu_custom_call" | custom-call | flops 495000000 | bytes 262144 | tf_op jit(solution)/shard_map/pallas_call | solution.py:57
  112.9 4.2 %shard_map.220 = (f32[512,768]{1,0:T(8,128)S(1)}, bf16[208,512]{1,0:T(8,128)(2,1)S(1)}, bf16[784,512]{1,0:T(8,128)(2,1)S(1)}, bf16[208,512]{1,0:T(8,128)(2,1)S(1...) custom-call(bf16[256,768]{1,0:T(8,128)(2,1)S(1)} %collective-permute-done.22.refs_0_, ...), custom_call_target="tpu_custom_call" | custom-call | flops 825000000 | bytes 262144 | tf_op jit(solution)/shard_map/pallas_call | solution.py:57
  118.2 1.5 collective-permute-start.27
  119.9 8.5 %shard_map.222 = (bf16[384,384]{1,0:T(8,128)(2,1)S(1)}, bf16[384,384]{1,0:T(8,128)(2,1)S(1)}, bf16[384,384]{1,0:T(8,128)(2,1)S(1)}, bf16[384,384]{1,0:T(8,128)(2...) custom-call(s32[8]{0:T(128)S(1)} %add_add_fusion.1.refs_0_.refs_1_, ...), custom_call_target="tpu_custom_call" | custom-call | flops 1320000000 | bytes 262144 | tf_op jit(solution)/shard_map/pallas_call | solution.py:57
  128.9 7.8 %shard_map.224 = (bf16[384,1152]{1,0:T(8,128)(2,1)S(1)}, bf16[400,1152]{1,0:T(8,128)(2,1)S(1)}, bf16[384,1152]{1,0:T(8,128)(2,1)S(1)}, bf16[384,1152]{1,0:T(8,128)(2,1)S(1)}, f32[4,768]{1,0:T(4,128)S(1)}) custom-call(s32[8]{0:T(128)S(1)} %add_add_fusion.1.refs_0_.refs_1_, s32[8]{0:T(128)S(1)} %add_add_fusion.refs_1_, ...), custom_call_target="tpu_custom_call" | custom-call | flops 990000000 | bytes 262144 | tf_op jit(solution)/shard_map/pallas_call | solution.py:57
  140.5 13.0 %shard_map.226 = (bf16[192,512]{1,0:T(8,128)(2,1)S(1)}, bf16[672,512]{1,0:T(8,128)(2,1)S(1)}, bf16[192,512]{1,0:T(8,128)(2,1)S(1)}, bf16[768,192]{1,0:T(8,128)(2...) custom-call(s32[9]{0:T(128)S(1)} %pad_add_fusion.refs_0_, s32[8]{0:T(128)S(1)} %add_add_fusion.1.refs_0_.refs_1_, ...), custom_call_target="tpu_custom_call" | custom-call | flops 1980000000 | bytes 262144 | tf_op jit(solution)/shard_map/pallas_call | solution.py:57
  153.5 6.4 %collective-permute-done.31.refs_3_ = bf16[384,1152]{1,0:T(8,128)(2,1)S(1)} collective-permute-done((bf16[384,1152]{1,0:T(8,128)(2,1)S(1)}, bf16[384,1152]{1,0:T(8,128)(2,1)S(1)}, u32[]{:S(2)}, u32[]{:S(2)}) %collective-permute-start.31) | collective-permute-done | bytes 884768 | tf_op jit(solution)/shard_map/ppermute | solution.py:988
  163.1 1.5 collective-permute-start.33
  164.6 13.1 %shard_map.228 = (bf16[192,512]{1,0:T(8,128)(2,1)S(1)}, bf16[384,512]{1,0:T(8,128)(2,1)S(1)}, bf16[384,512]{1,0:T(8,128)(2,1)S(1)}, bf16[384,384]{1,0:T(8,128)(2...) custom-call(s32[9]{0:T(128)S(1)} %pad_add_fusion.refs_0_, s32[8]{0:T(128)S(1)} %add_add_fusion.1.refs_0_.refs_1_, ...), custom_call_target="tpu_custom_call" | custom-call | flops 1980000000 | bytes 262144 | tf_op jit(solution)/shard_map/pallas_call | solution.py:57
  179.4 2.6 %collective-permute-start.41 = (bf16[112,2304]{1,0:T(8,128)(2,1)S(1)}, bf16[112,2304]{1,0:T(8,128)(2,1)S(1)}, u32[]{:S(2)}, u32[]{:S(2)}) collective-permute-start(bf16[112,2304]{1,0:T(8,128)(2,1)S(1)} %fusion.3), channel_id=1, source_target_pairs={{0,16},{4,20},{8,24},{12,28},{16,0},{20,4},{24,8},{28,12},{1,17},{... | collective-permute-start | bytes 1548296 | tf_op jit(solution)/shard_map/ppermute | solution.py:988
  182.1 12.8 %shard_map.230 = (bf16[192,512]{1,0:T(8,128)(2,1)S(1)}, bf16[384,512]{1,0:T(8,128)(2,1)S(1)}, bf16[768,512]{1,0:T(8,128)(2,1)S(1)}, bf16[384,384]{1,0:T(8,128)(2...) custom-call(s32[9]{0:T(128)S(1)} %pad_add_fusion.refs_0_, s32[8]{0:T(128)S(1)} %add_add_fusion.1.refs_0_.refs_1_, ...), custom_call_target="tpu_custom_call" | custom-call | flops 1980000000 | bytes 262144 | tf_op jit(solution)/shard_map/pallas_call | solution.py:57
  196.2 1.5 collective-permute-start.39
  199.2 5.9 %collective-permute-done.41.refs_2_ = bf16[112,2304]{1,0:T(8,128)(2,1)S(1)} collective-permute-done((bf16[112,2304]{1,0:T(8,128)(2,1)S(1)}, bf16[112,2304]{1,0:T(8,128)(2,1)S(1)}, u32[]{:S(2)}, u32[]{:S(2)}) %collective-permute-start.41) | collective-permute-done | bytes 516128 | tf_op jit(solution)/shard_map/ppermute | solution.py:988
  207.2 2.8 %shard_map.234 = (f32[512,768]{1,0:T(8,128)S(1)}, f32[8,128]{1,0:T(8,128)S(1)}) custom-call(bf16[672,512]{1,0:T(8,128)(2,1)S(1)} %collective-permute-done.33.refs_32_.refs_0_, bf16[384,512]{1,0:T(8,128)(2,1)S(1)} %collective-permute-done.36.refs_0_.refs_1_, bf16[384,512]{1,0:T(8,128)(2,1)S(1)} %collective-permute-done.39.refs_2_, ...), custom_call_target="tpu_custom_call" | custom-call | flops 495000000 | bytes 262144 | tf_op jit(solution)/shard_map/pallas_call | solution.py:57
  211.4 2.0 collective-permute-start.45
  214.0 3.7 %shard_map.236 = (f32[512,768]{1,0:T(8,128)}, f32[8,128]{1,0:T(8,128)S(1)}) custom-call(bf16[1152,512]{1,0:T(8,128)(2,1)S(1)} %collective-permute-done.42.refs_0_, f32[512,768]{1,0:T(8,128)S(1)} %get-tuple-element.373.refs_1_, bf16[576,768]{1,0:T(8,128)(2,1)} %collective-permute-done.4.refs_12_.refs_2_, ...), custom_call_target="tpu_custom_call" | custom-call | flops 495000000 | bytes 262144 | tf_op jit(solution)/shard_map/pallas_call | solution.py:57
  217.7 3.2 %shard_map.237 = (f32[96,2,768]{2,1,0:T(2,128)}, f32[96,768]{1,0:T(8,128)}, f32[8,128]{1,0:T(8,128)S(1)}) custom-call(bf16[384,1152]{1,0:T(8,128)(2,1)S(1)} %get-tuple-element.348.refs_0_, bf16[400,1152]{1,0:T(8,128)(2,1)S(1)} %get-tuple-element.349.refs_1_, bf16[208,1152]{1,0:T(8,128)(2,1)S(1)} %get-tuple-element.364.refs_2_, ...), custom_call_target="tpu_custom_call" | custom-call | flops 330000000 | bytes 262144 | tf_op jit(solution)/shard_map/pallas_call | solution.py:57
  220.9 1.7 shard_map.238
  (149 shorter events, 28.9 us)
Async XLA Ops:
  3.0 7.9 %collective-permute-start = (bf16[528,768]{1,0:T(8,128)(2,1)}, bf16[528,768]{1,0:T(8,128)(2,1)}, u32[]{:S(2)}, u32[]{:S(2)}) collective-permute-start(bf16[528,768]{1,0:T(8,128)(2,1)} %fusion.2.refs_2_.refs_1_), channel_id=1, source_target_pairs={{0,1},{1,0},{2,3},{3,2},{4,5},{5,4},{6,7},{7,6},{8,9},{9,8},{10,11... | collective-permute-start | bytes 2433032 | tf_op jit(solution)/shard_map/ppermute | solution.py:988
  3.5 21.5 %collective-permute-start.1 = (bf16[528,768]{1,0:T(8,128)(2,1)}, bf16[528,768]{1,0:T(8,128)(2,1)}, u32[]{:S(2)}, u32[]{:S(2)}) collective-permute-start(bf16[528,768]{1,0:T(8,128)(2,1)} %fusion.2.refs_2_.refs_1_), channel_id=1, source_target_pairs={{0,2},{1,3},{2,0},{3,1},{4,6},{5,7},{6,4},{7,5},{8,10},{9,11},{10,... | collective-permute-start | bytes 2433032 | tf_op jit(solution)/shard_map/ppermute | solution.py:988
  5.9 25.0 %collective-permute-start.4 = (bf16[576,768]{1,0:T(8,128)(2,1)S(1)}, bf16[576,768]{1,0:T(8,128)(2,1)}, u32[]{:S(2)}, u32[]{:S(2)}) collective-permute-start(bf16[576,768]{1,0:T(8,128)(2,1)S(1)} %bitcast.15), channel_id=1, source_target_pairs={{0,1},{1,0},{2,3},{3,2},{4,5},{5,4},{6,7},{7,6},{8,9},{9,8},{10,11... | collective-permute-start | bytes 2654216 | tf_op jit(solution)/shard_map/ppermute | solution.py:988
  25.0 4.1 %collective-permute-start.2 = (bf16[528,768]{1,0:T(8,128)(2,1)}, bf16[528,768]{1,0:T(8,128)(2,1)S(1)}, u32[]{:S(2)}, u32[]{:S(2)}) collective-permute-start(bf16[528,768]{1,0:T(8,128)(2,1)} %get-tuple-element.202.refs_2_.refs_3_), channel_id=1, source_target_pairs={{0,1},{1,0},{2,3},{3,2},{4,5},{5,4},{6,7},{7,6},{8,9},{9,8},{10,11... | collective-permute-start | bytes 2433032 | tf_op jit(solution)/shard_map/ppermute | solution.py:988
  25.0 16.1 %collective-permute-start.5 = (bf16[192,1536]{1,0:T(8,128)(2,1)S(1)}, bf16[192,1536]{1,0:T(8,128)(2,1)S(1)}, u32[]{:S(2)}, u32[]{:S(2)}) collective-permute-start(bf16[192,1536]{1,0:T(8,128)(2,1)S(1)} %get-tuple-element.218), channel_id=1, source_target_pairs={{0,2},{1,3},{2,0},{3,1},{4,6},{5,7},{6,4},{7,5},{8,10},{9,11},{10,... | collective-permute-start | bytes 1769480 | tf_op jit(solution)/shard_map/ppermute | solution.py:988
  26.7 4.2 %collective-permute-start.3 = (bf16[192,768]{1,0:T(8,128)(2,1)S(1)}, bf16[192,768]{1,0:T(8,128)(2,1)S(1)}, u32[]{:S(2)}, u32[]{:S(2)}) collective-permute-start(bf16[192,768]{1,0:T(8,128)(2,1)S(1)} %copy-done.3), channel_id=1, source_target_pairs={{0,1},{1,0},{2,3},{3,2},{4,5},{5,4},{6,7},{7,6},{8,9},{9,8},{10,11... | collective-permute-start | bytes 884744 | tf_op jit(solution)/shard_map/ppermute | solution.py:988
  30.6 22.8 %collective-permute-start.8 = (bf16[384,768]{1,0:T(8,128)(2,1)S(1)}, bf16[384,768]{1,0:T(8,128)(2,1)S(1)}, u32[]{:S(2)}, u32[]{:S(2)}) collective-permute-start(bf16[384,768]{1,0:T(8,128)(2,1)S(1)} %get-tuple-element.220), channel_id=1, source_target_pairs={{0,2},{1,3},{2,0},{3,1},{4,6},{5,7},{6,4},{7,5},{8,10},{9,11},{10,... | collective-permute-start | bytes 1769480 | tf_op jit(solution)/shard_map/ppermute | solution.py:988
  41.1 14.9 %collective-permute-start.6 = (bf16[192,1536]{1,0:T(8,128)(2,1)S(1)}, bf16[192,1536]{1,0:T(8,128)(2,1)S(1)}, u32[]{:S(2)}, u32[]{:S(2)}) collective-permute-start(bf16[192,1536]{1,0:T(8,128)(2,1)S(1)} %get-tuple-element.219.refs_1_), channel_id=1, source_target_pairs={{0,4},{4,0},{8,12},{12,8},{16,20},{20,16},{24,28},{28,24},{1,5},{5... | collective-permute-start | bytes 1769480 | tf_op jit(solution)/shard_map/ppermute | solution.py:988
  42.9 14.3 %collective-permute-start.7 = (bf16[192,1536]{1,0:T(8,128)(2,1)S(1)}, bf16[192,1536]{1,0:T(8,128)(2,1)S(1)}, u32[]{:S(2)}, u32[]{:S(2)}) collective-permute-start(bf16[192,1536]{1,0:T(8,128)(2,1)S(1)} %get-tuple-element.219.refs_1_), channel_id=1, source_target_pairs={{0,8},{4,12},{8,0},{12,4},{16,24},{20,28},{24,16},{28,20},{1,9},{5... | collective-permute-start | bytes 1769480 | tf_op jit(solution)/shard_map/ppermute | solution.py:988
  56.0 3.9 %copy-start.5 = (f32[768]{0:T(1024)S(1)}, f32[768]{0:T(1024)}, u32[]{:S(2)}) copy-start(f32[768]{0:T(1024)} %param.19) | copy-start | bytes 9220
  57.6 11.2 %collective-permute-start.15 = (bf16[192,768]{1,0:T(8,128)(2,1)S(1)}, bf16[192,768]{1,0:T(8,128)(2,1)S(1)}, u32[]{:S(2)}, u32[]{:S(2)}) collective-permute-start(bf16[192,768]{1,0:T(8,128)(2,1)S(1)} %get-tuple-element.239.refs_6_.refs_14_), channel_id=1, source_target_pairs={{0,1},{1,0},{2,3},{3,2},{4,5},{5,4},{6,7},{7,6},{8,9},{9,8},{10,11... | collective-permute-start | bytes 884744 | tf_op jit(solution)/shard_map/ppermute | solution.py:988
  57.7 7.8 %collective-permute-start.13 = (bf16[192,512]{1,0:T(8,128)(2,1)S(1)}, bf16[192,512]{1,0:T(8,128)(2,1)S(1)}, u32[]{:S(2)}, u32[]{:S(2)}) collective-permute-start(bf16[192,512]{1,0:T(8,128)(2,1)S(1)} %get-tuple-element.235.refs_20_), channel_id=1, source_target_pairs={{0,2},{1,3},{2,0},{3,1},{4,6},{5,7},{6,4},{7,5},{8,10},{9,11},{10,... | collective-permute-start | bytes 589832 | tf_op jit(solution)/shard_map/ppermute | solution.py:988
  59.2 6.8 %collective-permute-start.12 = (bf16[192,512]{1,0:T(8,128)(2,1)S(1)}, bf16[192,512]{1,0:T(8,128)(2,1)S(1)}, u32[]{:S(2)}, u32[]{:S(2)}) collective-permute-start(bf16[192,512]{1,0:T(8,128)(2,1)S(1)} %get-tuple-element.234.refs_19_), channel_id=1, source_target_pairs={{0,1},{1,0},{2,3},{3,2},{4,5},{5,4},{6,7},{7,6},{8,9},{9,8},{10,11... | collective-permute-start | bytes 589832 | tf_op jit(solution)/shard_map/ppermute | solution.py:988
  59.4 9.4 %collective-permute-start.14 = (bf16[192,512]{1,0:T(8,128)(2,1)S(1)}, bf16[192,512]{1,0:T(8,128)(2,1)S(1)}, u32[]{:S(2)}, u32[]{:S(2)}) collective-permute-start(bf16[192,512]{1,0:T(8,128)(2,1)S(1)} %get-tuple-element.236.refs_21_), channel_id=1, source_target_pairs={{0,3},{1,2},{2,1},{3,0},{4,7},{5,6},{6,5},{7,4},{8,11},{9,10},{10,... | collective-permute-start | bytes 589832 | tf_op jit(solution)/shard_map/ppermute | solution.py:988
  59.9 21.9 %collective-permute-start.10 = (bf16[192,1536]{1,0:T(8,128)(2,1)S(1)}, bf16[192,1536]{1,0:T(8,128)(2,1)S(1)}, u32[]{:S(2)}, u32[]{:S(2)}) collective-permute-start(bf16[192,1536]{1,0:T(8,128)(2,1)S(1)} %get-tuple-element.231), channel_id=1, source_target_pairs={{0,8},{4,12},{8,0},{12,4},{16,24},{20,28},{24,16},{28,20},{1,9},{5... | collective-permute-start | bytes 1769480 | tf_op jit(solution)/shard_map/ppermute | solution.py:988
  61.6 7.2 %copy-start.2 = (bf16[512,768]{1,0:T(8,128)(2,1)S(1)}, bf16[512,768]{1,0:T(8,128)(2,1)}, u32[]{:S(2)}) copy-start(bf16[512,768]{1,0:T(8,128)(2,1)} %refs_8_.1) | copy-start | bytes 2359300
  65.4 21.2 %collective-permute-start.9 = (bf16[192,1536]{1,0:T(8,128)(2,1)S(1)}, bf16[192,1536]{1,0:T(8,128)(2,1)S(1)}, u32[]{:S(2)}, u32[]{:S(2)}) collective-permute-start(bf16[192,1536]{1,0:T(8,128)(2,1)S(1)} %get-tuple-element.230), channel_id=1, source_target_pairs={{0,4},{4,0},{8,12},{12,8},{16,20},{20,16},{24,28},{28,24},{1,5},{5... | collective-permute-start | bytes 1769480 | tf_op jit(solution)/shard_map/ppermute | solution.py:988
  69.9 2.3 %collective-permute-start.16 = (bf16[256,768]{1,0:T(8,128)(2,1)S(1)}, bf16[256,768]{1,0:T(8,128)(2,1)S(1)}, u32[]{:S(2)}, u32[]{:S(2)}) collective-permute-start(bf16[256,768]{1,0:T(8,128)(2,1)S(1)} %get-tuple-element.251), channel_id=1, source_target_pairs={{0,1},{1,0},{2,3},{3,2},{4,5},{5,4},{6,7},{7,6},{8,9},{9,8},{10,11... | collective-permute-start | bytes 1179656 | tf_op jit(solution)/shard_map/ppermute | solution.py:988
  70.6 1.9 collective-permute-start.17
  70.6 11.2 %collective-permute-start.11 = (bf16[192,768]{1,0:T(8,128)(2,1)S(1)}, bf16[192,768]{1,0:T(8,128)(2,1)S(1)}, u32[]{:S(2)}, u32[]{:S(2)}) collective-permute-start(bf16[192,768]{1,0:T(8,128)(2,1)S(1)} %get-tuple-element.232.refs_6_), channel_id=1, source_target_pairs={{0,12},{4,8},{8,4},{12,0},{16,28},{20,24},{24,20},{28,16},{1,13},{... | collective-permute-start | bytes 884744 | tf_op jit(solution)/shard_map/ppermute | solution.py:988
  77.8 19.9 %collective-permute-start.20 = (bf16[512,768]{1,0:T(8,128)(2,1)S(1)}, bf16[512,768]{1,0:T(8,128)(2,1)S(1)}, u32[]{:S(2)}, u32[]{:S(2)}) collective-permute-start(bf16[512,768]{1,0:T(8,128)(2,1)S(1)} %get-tuple-element.262.refs_0_.refs_6_), channel_id=1, source_target_pairs={{0,2},{1,3},{2,0},{3,1},{4,6},{5,7},{6,4},{7,5},{8,10},{9,11},{10,... | collective-permute-start | bytes 2359304 | tf_op jit(solution)/shard_map/ppermute | solution.py:988
  89.9 3.1 %collective-permute-start.18 = (bf16[256,768]{1,0:T(8,128)(2,1)S(1)}, bf16[256,768]{1,0:T(8,128)(2,1)S(1)}, u32[]{:S(2)}, u32[]{:S(2)}) collective-permute-start(bf16[256,768]{1,0:T(8,128)(2,1)S(1)} %get-tuple-element.259), channel_id=1, source_target_pairs={{0,1},{1,0},{2,3},{3,2},{4,5},{5,4},{6,7},{7,6},{8,9},{9,8},{10,11... | collective-permute-start | bytes 1179656 | tf_op jit(solution)/shard_map/ppermute | solution.py:988
  90.0 3.0 %collective-permute-start.19 = (bf16[256,768]{1,0:T(8,128)(2,1)S(1)}, bf16[256,768]{1,0:T(8,128)(2,1)S(1)}, u32[]{:S(2)}, u32[]{:S(2)}) collective-permute-start(bf16[256,768]{1,0:T(8,128)(2,1)S(1)} %get-tuple-element.260), channel_id=1, source_target_pairs={{0,1},{1,0},{2,3},{3,2},{4,5},{5,4},{6,7},{7,6},{8,9},{9,8},{10,11... | collective-permute-start | bytes 1179656 | tf_op jit(solution)/shard_map/ppermute | solution.py:988
  97.7 5.3 %collective-permute-start.21 = (bf16[512,768]{1,0:T(8,128)(2,1)S(1)}, bf16[512,768]{1,0:T(8,128)(2,1)S(1)}, u32[]{:S(2)}, u32[]{:S(2)}) collective-permute-start(bf16[512,768]{1,0:T(8,128)(2,1)S(1)} %get-tuple-element.287.refs_0_.refs_2_), channel_id=1, source_target_pairs={{0,1},{1,0},{2,3},{3,2},{4,5},{5,4},{6,7},{7,6},{8,9},{9,8},{10,11... | collective-permute-start | bytes 2359304 | tf_op jit(solution)/shard_map/ppermute | solution.py:988
  97.7 15.2 %collective-permute-start.24 = (bf16[512,768]{1,0:T(8,128)(2,1)S(1)}, bf16[512,768]{1,0:T(8,128)(2,1)S(1)}, u32[]{:S(2)}, u32[]{:S(2)}) collective-permute-start(bf16[512,768]{1,0:T(8,128)(2,1)S(1)} %get-tuple-element.303.refs_6_.refs_8_), channel_id=1, source_target_pairs={{0,1},{1,0},{2,3},{3,2},{4,5},{5,4},{6,7},{7,6},{8,9},{9,8},{10,11... | collective-permute-start | bytes 2359304 | tf_op jit(solution)/shard_map/ppermute | solution.py:988
  98.2 19.4 %collective-permute-start.25 = (bf16[512,768]{1,0:T(8,128)(2,1)S(1)}, bf16[512,768]{1,0:T(8,128)(2,1)S(1)}, u32[]{:S(2)}, u32[]{:S(2)}) collective-permute-start(bf16[512,768]{1,0:T(8,128)(2,1)S(1)} %get-tuple-element.287.refs_0_.refs_2_), channel_id=1, source_target_pairs={{0,2},{1,3},{2,0},{3,1},{4,6},{5,7},{6,4},{7,5},{8,10},{9,11},{10,... | collective-permute-start | bytes 2359304 | tf_op jit(solution)/shard_map/ppermute | solution.py:988
  109.0 3.9 %collective-permute-start.22 = (bf16[256,768]{1,0:T(8,128)(2,1)S(1)}, bf16[256,768]{1,0:T(8,128)(2,1)S(1)}, u32[]{:S(2)}, u32[]{:S(2)}) collective-permute-start(bf16[256,768]{1,0:T(8,128)(2,1)S(1)} %get-tuple-element.294), channel_id=1, source_target_pairs={{0,1},{1,0},{2,3},{3,2},{4,5},{5,4},{6,7},{7,6},{8,9},{9,8},{10,11... | collective-permute-start | bytes 1179656 | tf_op jit(solution)/shard_map/ppermute | solution.py:988
  109.0 3.8 %collective-permute-start.23 = (bf16[256,768]{1,0:T(8,128)(2,1)S(1)}, bf16[256,768]{1,0:T(8,128)(2,1)S(1)}, u32[]{:S(2)}, u32[]{:S(2)}) collective-permute-start(bf16[256,768]{1,0:T(8,128)(2,1)S(1)} %get-tuple-element.295), channel_id=1, source_target_pairs={{0,1},{1,0},{2,3},{3,2},{4,5},{5,4},{6,7},{7,6},{8,9},{9,8},{10,11... | collective-permute-start | bytes 1179656 | tf_op jit(solution)/shard_map/ppermute | solution.py:988
  117.6 2.3 %collective-permute-start.29 = (bf16[512,768]{1,0:T(8,128)(2,1)S(1)}, bf16[512,768]{1,0:T(8,128)(2,1)S(1)}, u32[]{:S(2)}, u32[]{:S(2)}) collective-permute-start(bf16[512,768]{1,0:T(8,128)(2,1)S(1)} %get-tuple-element.319.refs_4_), channel_id=1, source_target_pairs={{0,1},{1,0},{2,3},{3,2},{4,5},{5,4},{6,7},{7,6},{8,9},{9,8},{10,11... | collective-permute-start | bytes 2359304 | tf_op jit(solution)/shard_map/ppermute | solution.py:988
  117.7 11.3 %collective-permute-start.26 = (bf16[784,512]{1,0:T(8,128)(2,1)S(1)}, bf16[784,512]{1,0:T(8,128)(2,1)S(1)}, u32[]{:S(2)}, u32[]{:S(2)}) collective-permute-start(bf16[784,512]{1,0:T(8,128)(2,1)S(1)} %get-tuple-element.310), channel_id=1, source_target_pairs={{0,1},{1,0},{2,3},{3,2},{4,5},{5,4},{6,7},{7,6},{8,9},{9,8},{10,11... | collective-permute-start | bytes 2408456 | tf_op jit(solution)/shard_map/ppermute | solution.py:988
  118.2 10.3 %collective-permute-start.27 = (bf16[208,512]{1,0:T(8,128)(2,1)S(1)}, bf16[208,512]{1,0:T(8,128)(2,1)S(1)}, u32[]{:S(2)}, u32[]{:S(2)}) collective-permute-start(bf16[208,512]{1,0:T(8,128)(2,1)S(1)} %get-tuple-element.311), channel_id=1, source_target_pairs={{0,2},{1,3},{2,0},{3,1},{4,6},{5,7},{6,4},{7,5},{8,10},{9,11},{10,... | collective-permute-start | bytes 638984 | tf_op jit(solution)/shard_map/ppermute | solution.py:988
  119.7 9.3 %collective-permute-start.28 = (bf16[208,512]{1,0:T(8,128)(2,1)S(1)}, bf16[208,512]{1,0:T(8,128)(2,1)S(1)}, u32[]{:S(2)}, u32[]{:S(2)}) collective-permute-start(bf16[208,512]{1,0:T(8,128)(2,1)S(1)} %get-tuple-element.312), channel_id=1, source_target_pairs={{0,3},{1,2},{2,1},{3,0},{4,7},{5,6},{6,5},{7,4},{8,11},{9,10},{10,... | collective-permute-start | bytes 638984 | tf_op jit(solution)/shard_map/ppermute | solution.py:988
  136.7 24.0 %collective-permute-start.30 = (bf16[400,1152]{1,0:T(8,128)(2,1)S(1)}, bf16[400,1152]{1,0:T(8,128)(2,1)S(1)}, u32[]{:S(2)}, u32[]{:S(2)}) collective-permute-start(bf16[400,1152]{1,0:T(8,128)(2,1)S(1)} %get-tuple-element.338), channel_id=1, source_target_pairs={{0,4},{4,0},{8,12},{12,8},{16,20},{20,16},{24,28},{28,24},{1,5},{5... | collective-permute-start | bytes 2764808 | tf_op jit(solution)/shard_map/ppermute | solution.py:988
  137.8 22.1 %collective-permute-start.31 = (bf16[384,1152]{1,0:T(8,128)(2,1)S(1)}, bf16[384,1152]{1,0:T(8,128)(2,1)S(1)}, u32[]{:S(2)}, u32[]{:S(2)}) collective-permute-start(bf16[384,1152]{1,0:T(8,128)(2,1)S(1)} %get-tuple-element.339), channel_id=1, source_target_pairs={{0,8},{4,12},{8,0},{12,4},{16,24},{20,28},{24,16},{28,20},{1,9},{5... | collective-permute-start | bytes 2654216 | tf_op jit(solution)/shard_map/ppermute | solution.py:988
  139.0 21.8 %collective-permute-start.32 = (bf16[576,768]{1,0:T(8,128)(2,1)S(1)}, bf16[576,768]{1,0:T(8,128)(2,1)S(1)}, u32[]{:S(2)}, u32[]{:S(2)}) collective-permute-start(bf16[576,768]{1,0:T(8,128)(2,1)S(1)} %get-tuple-element.340.refs_7_), channel_id=1, source_target_pairs={{0,2},{1,3},{2,0},{3,1},{4,6},{5,7},{6,4},{7,5},{8,10},{9,11},{10,... | collective-permute-start | bytes 2654216 | tf_op jit(solution)/shard_map/ppermute | solution.py:988
  161.0 16.7 %collective-permute-start.34 = (bf16[208,1152]{1,0:T(8,128)(2,1)S(1)}, bf16[208,1152]{1,0:T(8,128)(2,1)S(1)}, u32[]{:S(2)}, u32[]{:S(2)}) collective-permute-start(bf16[208,1152]{1,0:T(8,128)(2,1)S(1)} %pad_maximum_fusion.1), channel_id=1, source_target_pairs={{0,8},{4,12},{8,0},{12,4},{16,24},{20,28},{24,16},{28,20},{1,9},{5... | collective-permute-start | bytes 1437704 | tf_op jit(solution)/shard_map/ppermute | solution.py:988
  162.0 15.7 %collective-permute-start.35 = (bf16[192,1152]{1,0:T(8,128)(2,1)S(1)}, bf16[192,1152]{1,0:T(8,128)(2,1)S(1)}, u32[]{:S(2)}, u32[]{:S(2)}) collective-permute-start(bf16[192,1152]{1,0:T(8,128)(2,1)S(1)} %add_convert_fusion), channel_id=1, source_target_pairs={{0,4},{4,0},{8,12},{12,8},{16,20},{20,16},{24,28},{28,24},{1,5},{5... | collective-permute-start | bytes 1327112 | tf_op jit(solution)/shard_map/ppermute | solution.py:988
  163.1 18.9 %collective-permute-start.33 = (bf16[672,512]{1,0:T(8,128)(2,1)S(1)}, bf16[672,512]{1,0:T(8,128)(2,1)S(1)}, u32[]{:S(2)}, u32[]{:S(2)}) collective-permute-start(bf16[672,512]{1,0:T(8,128)(2,1)S(1)} %get-tuple-element.343), channel_id=1, source_target_pairs={{0,2},{1,3},{2,0},{3,1},{4,6},{5,7},{6,4},{7,5},{8,10},{9,11},{10,... | collective-permute-start | bytes 2064392 | tf_op jit(solution)/shard_map/ppermute | solution.py:988
  177.9 16.9 %collective-permute-start.37 = (bf16[576,768]{1,0:T(8,128)(2,1)S(1)}, bf16[576,768]{1,0:T(8,128)(2,1)S(1)}, u32[]{:S(2)}, u32[]{:S(2)}) collective-permute-start(bf16[576,768]{1,0:T(8,128)(2,1)S(1)} %get-tuple-element.356.refs_8_), channel_id=1, source_target_pairs={{0,1},{1,0},{2,3},{3,2},{4,5},{5,4},{6,7},{7,6},{8,9},{9,8},{10,11... | collective-permute-start | bytes 2654216 | tf_op jit(solution)/shard_map/ppermute | solution.py:988
  178.0 16.8 %collective-permute-start.36 = (bf16[384,512]{1,0:T(8,128)(2,1)S(1)}, bf16[384,512]{1,0:T(8,128)(2,1)S(1)}, u32[]{:S(2)}, u32[]{:S(2)}) collective-permute-start(bf16[384,512]{1,0:T(8,128)(2,1)S(1)} %get-tuple-element.355), channel_id=1, source_target_pairs={{0,2},{1,3},{2,0},{3,1},{4,6},{5,7},{6,4},{7,5},{8,10},{9,11},{10,... | collective-permute-start | bytes 1179656 | tf_op jit(solution)/shard_map/ppermute | solution.py:988
  178.6 16.2 %collective-permute-start.38 = (bf16[384,384]{1,0:T(8,128)(2,1)S(1)}, bf16[384,384]{1,0:T(8,128)(2,1)S(1)}, u32[]{:S(2)}, u32[]{:S(2)}) collective-permute-start(bf16[384,384]{1,0:T(8,128)(2,1)S(1)} %get-tuple-element.360), channel_id=1, source_target_pairs={{0,4},{4,0},{8,12},{12,8},{16,20},{20,16},{24,28},{28,24},{1,5},{5... | collective-permute-start | bytes 884744 | tf_op jit(solution)/shard_map/ppermute | solution.py:988
  179.4 25.7 %collective-permute-start.41 = (bf16[112,2304]{1,0:T(8,128)(2,1)S(1)}, bf16[112,2304]{1,0:T(8,128)(2,1)S(1)}, u32[]{:S(2)}, u32[]{:S(2)}) collective-permute-start(bf16[112,2304]{1,0:T(8,128)(2,1)S(1)} %fusion.3), channel_id=1, source_target_pairs={{0,16},{4,20},{8,24},{12,28},{16,0},{20,4},{24,8},{28,12},{1,17},{... | collective-permute-start | bytes 1548296 | tf_op jit(solution)/shard_map/ppermute | solution.py:988
  194.9 10.2 %collective-permute-start.40 = (bf16[384,384]{1,0:T(8,128)(2,1)S(1)}, bf16[384,384]{1,0:T(8,128)(2,1)S(1)}, u32[]{:S(2)}, u32[]{:S(2)}) collective-permute-start(bf16[384,384]{1,0:T(8,128)(2,1)S(1)} %get-tuple-element.363), channel_id=1, source_target_pairs={{0,4},{4,0},{8,12},{12,8},{16,20},{20,16},{24,28},{28,24},{1,5},{5... | collective-permute-start | bytes 884744 | tf_op jit(solution)/shard_map/ppermute | solution.py:988
  196.2 10.3 %collective-permute-start.39 = (bf16[384,512]{1,0:T(8,128)(2,1)S(1)}, bf16[384,512]{1,0:T(8,128)(2,1)S(1)}, u32[]{:S(2)}, u32[]{:S(2)}) collective-permute-start(bf16[384,512]{1,0:T(8,128)(2,1)S(1)} %get-tuple-element.361), channel_id=1, source_target_pairs={{0,2},{1,3},{2,0},{3,1},{4,6},{5,7},{6,4},{7,5},{8,10},{9,11},{10,... | collective-permute-start | bytes 1179656 | tf_op jit(solution)/shard_map/ppermute | solution.py:988
  197.7 12.3 %collective-permute-start.44 = (bf16[192,384]{1,0:T(8,128)(2,1)S(1)}, bf16[192,384]{1,0:T(8,128)(2,1)S(1)}, u32[]{:S(2)}, u32[]{:S(2)}) collective-permute-start(bf16[192,384]{1,0:T(8,128)(2,1)S(1)} %add_convert_fusion.4), channel_id=1, source_target_pairs={{0,8},{4,12},{8,0},{12,4},{16,24},{20,28},{24,16},{28,20},{1,9},{5... | collective-permute-start | bytes 442376 | tf_op jit(solution)/shard_map/ppermute | solution.py:988
  205.1 6.2 %collective-permute-start.43 = (bf16[192,384]{1,0:T(8,128)(2,1)S(1)}, bf16[192,384]{1,0:T(8,128)(2,1)S(1)}, u32[]{:S(2)}, u32[]{:S(2)}) collective-permute-start(bf16[192,384]{1,0:T(8,128)(2,1)S(1)} %add_convert_fusion.5), channel_id=1, source_target_pairs={{0,8},{4,12},{8,0},{12,4},{16,24},{20,28},{24,16},{28,20},{1,9},{5... | collective-permute-start | bytes 442376 | tf_op jit(solution)/shard_map/ppermute | solution.py:988
  207.1 6.9 %collective-permute-start.42 = (bf16[1152,512]{1,0:T(8,128)(2,1)S(1)}, bf16[1152,512]{1,0:T(8,128)(2,1)S(1)}, u32[]{:S(2)}, u32[]{:S(2)}) collective-permute-start(bf16[1152,512]{1,0:T(8,128)(2,1)S(1)} %get-tuple-element.367), channel_id=1, source_target_pairs={{0,1},{1,0},{2,3},{3,2},{4,5},{5,4},{6,7},{7,6},{8,9},{9,8},{10,11... | collective-permute-start | bytes 3538952 | tf_op jit(solution)/shard_map/ppermute | solution.py:988
  211.4 9.5 %collective-permute-start.45 = (bf16[96,768]{1,0:T(8,128)(2,1)S(1)}, bf16[96,768]{1,0:T(8,128)(2,1)S(1)}, u32[]{:S(2)}, u32[]{:S(2)}) collective-permute-start(bf16[96,768]{1,0:T(8,128)(2,1)S(1)} %pad_maximum_fusion.2), channel_id=1, source_target_pairs={{0,16},{4,20},{8,24},{12,28},{16,0},{20,4},{24,8},{28,12},{1,17},{... | collective-permute-start | bytes 442376 | tf_op jit(solution)/shard_map/ppermute | solution.py:988
  (9 other events, 23.9 us)
